TPU v7x, 512 devices: a whole 4x4x16 slice. The times are simulated.
512 devices in a mesh: ctx: 64 (over x, z_hi, y, core), head: 8 (over z_lo).
Axes of the slice: x: 4, y: 4, z: 16 (z_hi: 2, z_lo: 8; z = z_hi * 8 + z_lo), core: 2. Of those that a mesh axis runs over, the one named last changes fastest.
Arguments:
- queries: bfloat16 [64, 2, 512, 1024], P('ctx', None, None, 'head'), may hold values from -8 to 8
- key_states: bfloat16 [64, 2, 512, 128], P('ctx', None, 'head'), may hold values from -6 to 6
- value_states: bfloat16 [64, 2, 512, 128], P('ctx', None, 'head'), may hold values from -6 to 6
- out_grad: bfloat16 [64, 2, 512, 1024], P('ctx', None, None, 'head'), may hold values from -6 to 6
- segments: int32 [65536], replicated, may hold values from 0 to 169, never falling along the last dimension, each value on 1 to 1536 neighbouring positions
Outputs:
- attended: bfloat16 [64, 2, 512, 1024], P('ctx', None, None, 'head')
- query_grad: bfloat16 [64, 2, 512, 1024], P('ctx', None, None, 'head')
- key_grad: bfloat16 [64, 2, 512, 128], P('ctx', None, 'head')
- value_grad: bfloat16 [64, 2, 512, 128], P('ctx', None, 'head')
Inputs may be any that keep to these rules, and one draw needn't show every extreme that they name: `segments`: document numbers never fall along the sequence; every document covers at most 1536 positions, and one covers exactly that many.
All inputs are finite; a program needn't handle non-finite values.
Results may differ from a plain program's by a relative error of at most 0.017.
Values may be sent and summed in bfloat16 or wider, within the bound.
No kernel may reach another device: no remote copies, remote signals or barrier semaphores. Data moves between devices by JAX's collectives and lax.ppermute only.
A program may use at most 64 MiB of HBM per device.

v0:
```python
import jax
import jax.numpy as jnp
from jax import lax
from jax.sharding import PartitionSpec as P

REACH = 3


NEG_FILL = -1e30


def shifted(array, axis, by):
    peers = lax.axis_size(axis)
    pairs = [(i, i + by) for i in range(peers) if 0 <= i + by < peers]
    return lax.ppermute(array, axis, pairs)


def advance_whole(lower, upper, last_device):
    moved_lower = shifted(lower, "ctx", 1)
    moved_upper = shifted(upper, "ctx", -1)
    return (moved_lower, jnp.where(last_device, lower, moved_upper))


def retreat_whole(stacked, last_device):
    moved_lower = shifted(stacked[0], "ctx", -1)
    moved_upper = shifted(stacked[1], "ctx", 1)
    return jnp.stack([jnp.where(last_device, stacked[1], moved_lower), moved_upper])


def tile_allowed(segments, query_block, key_block, width):
    query_seg = lax.dynamic_slice_in_dim(segments, query_block * width, width)
    key_seg = lax.dynamic_slice_in_dim(segments, jnp.maximum(key_block, 0) * width, width)
    offsets = jnp.arange(width, dtype=jnp.int32)
    query_pos = query_block * width + offsets
    key_pos = key_block * width + offsets
    same_doc = query_seg[:, None] == key_seg[None, :]
    causal = key_pos[None, :] <= query_pos[:, None]
    return same_doc & causal & (key_block >= 0)


def tile_live(segments, query_block, key_block, width, offset):
    if offset == 0:
        return jnp.array(True)
    last_key = segments[jnp.maximum(key_block, 0) * width + width - 1]
    first_query = segments[query_block * width]
    return (key_block >= 0) & (last_key == first_query)


def tile_scores(query_tile, key_tile, allowed, score_scale):
    raw = (
        jnp.einsum("qhd,kd->hqk", query_tile, key_tile, preferred_element_type=jnp.float32)
        * score_scale
    )
    return jnp.where(allowed[None], raw, NEG_FILL)


def body(queries, key_states, value_states, out_grad, segments):
    devices = lax.axis_size("ctx")
    position = lax.axis_index("ctx")
    last_device = position == devices - 1
    width = queries.shape[2]
    head_dim = key_states.shape[3]
    head_count = queries.shape[3] // head_dim
    score_scale = head_dim ** (-0.5)
    query_blocks = [position, 2 * devices - 1 - position]
    key_blocks = []
    whole_keys, whole_values = (
        lax.all_gather(key_states, "head", axis=2, tiled=True),
        lax.all_gather(value_states, "head", axis=2, tiled=True),
    )
    lower = jnp.stack([whole_keys[0, 0], whole_values[0, 0]])
    upper = jnp.stack([whole_keys[0, 1], whole_values[0, 1]])
    for offset in range(REACH + 1):
        if offset > 0:
            lower, upper = advance_whole(lower, upper, last_device)
        key_blocks.append(jnp.stack([lower, upper]))
    query_tiles = [queries[0, half].reshape(width, head_count, head_dim) for half in range(2)]
    grad_tiles = [out_grad[0, half].reshape(width, head_count, head_dim) for half in range(2)]
    allowed_tiles = []
    live_tiles = []
    for offset in range(REACH + 1):
        allowed_tiles.append(
            [
                tile_allowed(segments, query_blocks[half], query_blocks[half] - offset, width)
                for half in range(2)
            ]
        )
        live_tiles.append(
            [
                tile_live(segments, query_blocks[half], query_blocks[half] - offset, width, offset)
                for half in range(2)
            ]
        )
    blank_scores = jnp.full((head_count, width, width), NEG_FILL, jnp.float32)
    score_tiles = [[blank_scores, blank_scores] for offset in range(REACH + 1)]
    log_totals = []
    for half in range(2):
        running_max = jnp.full((head_count, width), NEG_FILL, jnp.float32)
        running_sum = jnp.zeros((head_count, width), jnp.float32)
        for offset in range(REACH + 1):

            def first_pass(carried, offset=offset, half=half):
                old_max, old_sum, unused = carried
                scores = tile_scores(
                    query_tiles[half],
                    key_blocks[offset][half][0],
                    allowed_tiles[offset][half],
                    score_scale,
                )
                new_max = jnp.maximum(old_max, jnp.max(scores, axis=-1))
                new_sum = old_sum * jnp.exp(old_max - new_max) + jnp.sum(
                    jnp.exp(scores - new_max[:, :, None]), axis=-1
                )
                return (new_max, new_sum, scores)

            running_max, running_sum, kept_scores = first_pass(
                (running_max, running_sum, blank_scores)
            )
            score_tiles[offset][half] = kept_scores
        log_totals.append(running_max + jnp.log(running_sum))
    attended_tiles = []
    deltas = []
    for half in range(2):
        output_acc = jnp.zeros((width, head_count, head_dim), jnp.float32)
        for offset in range(REACH + 1):

            def second_pass(carried, offset=offset, half=half):
                weights = jnp.exp(score_tiles[offset][half] - log_totals[half][:, :, None]).astype(
                    jnp.bfloat16
                )
                return carried + jnp.einsum(
                    "hqk,kd->qhd",
                    weights,
                    key_blocks[offset][half][1],
                    preferred_element_type=jnp.float32,
                )

            output_acc = second_pass(output_acc)
        attended_tile = output_acc.astype(jnp.bfloat16)
        attended_tiles.append(attended_tile)
        deltas.append(
            jnp.einsum(
                "qhd,qhd->hq", grad_tiles[half], attended_tile, preferred_element_type=jnp.float32
            )
        )
    query_accs = [jnp.zeros((width, head_count, head_dim), jnp.float32) for half in range(2)]
    returned = None
    for offset in reversed(range(REACH + 1)):
        parts = []
        for half in range(2):
            key_tile = key_blocks[offset][half][0]
            value_tile = key_blocks[offset][half][1]

            def backward_tile(
                carried, half=half, key_tile=key_tile, value_tile=value_tile, offset=offset
            ):
                query_acc = carried[0]
                probs = jnp.exp(score_tiles[offset][half] - log_totals[half][:, :, None])
                weights = probs.astype(jnp.bfloat16)
                value_part = jnp.einsum(
                    "hqk,qhd->kd", weights, grad_tiles[half], preferred_element_type=jnp.float32
                )
                dot_grad = jnp.einsum(
                    "qhd,kd->hqk", grad_tiles[half], value_tile, preferred_element_type=jnp.float32
                )
                score_grad = (probs * (dot_grad - deltas[half][:, :, None])).astype(jnp.bfloat16)
                query_acc = (
                    query_acc
                    + jnp.einsum(
                        "hqk,kd->qhd", score_grad, key_tile, preferred_element_type=jnp.float32
                    )
                    * score_scale
                )
                key_part = (
                    jnp.einsum(
                        "hqk,qhd->kd",
                        score_grad,
                        query_tiles[half],
                        preferred_element_type=jnp.float32,
                    )
                    * score_scale
                )
                return (query_acc, key_part, value_part)

            empty_part = jnp.zeros((width, head_dim), jnp.float32)
            query_accs[half], key_part, value_part = backward_tile(
                (query_accs[half], empty_part, empty_part)
            )
            parts.append(jnp.stack([key_part, value_part]))
        contrib = jnp.stack(parts)
        if returned is not None:
            returned = retreat_whole(returned, last_device) + contrib
        else:
            returned = contrib
    returned = lax.psum_scatter(returned, "head", scatter_dimension=2, tiled=True)
    attended = jnp.stack([tile.reshape(width, head_count * head_dim) for tile in attended_tiles])[
        None
    ]
    query_grad = jnp.stack([acc.reshape(width, head_count * head_dim) for acc in query_accs])[
        None
    ].astype(jnp.bfloat16)
    key_grad = returned[:, 0][None].astype(jnp.bfloat16)
    value_grad = returned[:, 1][None].astype(jnp.bfloat16)
    return (attended, query_grad, key_grad, value_grad)


def solution(mesh):
    return jax.shard_map(
        body,
        mesh=mesh,
        in_specs=(
            P("ctx", None, None, "head"),
            P("ctx", None, "head", None),
            P("ctx", None, "head", None),
            P("ctx", None, None, "head"),
            P(),
        ),
        out_specs=(
            P("ctx", None, None, "head"),
            P("ctx", None, None, "head"),
            P("ctx", None, "head", None),
            P("ctx", None, "head", None),
        ),
        check_vma=False,
    )
```

profile of v0, /device:TPU:6, one launch (start us, length us, event | category | flops | bytes accessed | tf_op | source)
XLA Modules:
  0.0 428.4 jit_solution(10861266887282181746)
XLA Ops:
  1.4 49.6 %all_gather.6 = bf16[1,2,512,128]{3,1,0,2:T(2,128)(2,1)S(1)} all-gather(bf16[1,2,64,128]{3,1,0,2:T(2,128)(2,1)S(1)} %copy.72), channel_id=1, replica_groups=mesh['ctx'=64,'head'=8] {'head'}, dimensions={2}, use_global_device_ids=true | all-gather | bytes 294912 | tf_op jit(solution)/shard_map/all_gather | solution.py:68
  52.2 47.0 %all_gather.7 = bf16[1,2,512,128]{3,1,0,2:T(2,128)(2,1)S(1)} all-gather(bf16[1,2,64,128]{3,1,0,2:T(2,128)(2,1)S(1)} %copy.74), channel_id=1, replica_groups=mesh['ctx'=64,'head'=8] {'head'}, dimensions={2}, use_global_device_ids=true | all-gather | bytes 294912 | tf_op jit(solution)/shard_map/all_gather | solution.py:69
  100.4 3.0 collective-permute-start.3
  105.8 1.5 fusion.196
  109.3 3.9 collective-permute-done.3
  114.2 1.9 collective-permute-start
  116.1 15.5 %collective-permute-start.4 = (bf16[2,512,128]{1,2,0:T(8,128)(2,1)S(1)}, bf16[2,512,128]{1,2,0:T(8,128)(2,1)}, u32[]{:S(2)}, u32[]{:S(2)}) collective-permute-start(bf16[2,512,128]{1,2,0:T(8,128)(2,1)S(1)} %get-tuple-element.40), channel_id=1, source_target_pairs={{8,0},{16,8},{24,16},{32,24},{40,32},{48,40},{56,48},{64,56},{72,6... | collective-permute-start | bytes 786440 | tf_op jit(solution)/shard_map/ppermute | solution.py:15
  132.3 1.3 dynamic-slice
  134.2 1.2 fusion.201
  135.5 2.2 collective-permute-done
  138.8 15.7 %collective-permute-start.5 = (bf16[2,512,128]{1,2,0:T(8,128)(2,1)S(1)}, bf16[2,512,128]{1,2,0:T(8,128)(2,1)S(1)}, u32[]{:S(2)}, u32[]{:S(2)}) collective-permute-start(bf16[2,512,128]{1,2,0:T(8,128)(2,1)S(1)} %broadcast_select_fusion.1), channel_id=1, source_target_pairs={{8,0},{16,8},{24,16},{32,24},{40,32},{48,40},{56,48},{64,56},{72,6... | collective-permute-start | bytes 786440 | tf_op jit(solution)/shard_map/ppermute | solution.py:15
  154.6 1.9 collective-permute-start.1
  157.8 16.6 %collective-permute-done.1 = bf16[2,512,128]{1,2,0:T(8,128)(2,1)S(1)} collective-permute-done((bf16[2,512,128]{1,2,0:T(8,128)(2,1)S(1)}, bf16[2,512,128]{1,2,0:T(8,128)(2,1)S(1)}, u32[]{:S(2)}, u32[]{:S(2)}) %collective-permute-start.1) | collective-permute-done | bytes 262176 | tf_op jit(solution)/shard_map/ppermute | solution.py:15
  177.8 1.0 convolution_bitcast_fusion.8
  179.2 2.1 collective-permute-start.2
  182.2 17.4 %collective-permute-done.2 = bf16[2,512,128]{1,2,0:T(8,128)(2,1)S(1)} collective-permute-done((bf16[2,512,128]{1,2,0:T(8,128)(2,1)S(1)}, bf16[2,512,128]{1,2,0:T(8,128)(2,1)S(1)}, u32[]{:S(2)}, u32[]{:S(2)}) %collective-permute-start.2) | collective-permute-done | bytes 262176 | tf_op jit(solution)/shard_map/ppermute | solution.py:15
  202.5 1.1 fusion.96
  204.9 1.0 convolution_bitcast_fusion.9
  210.4 1.9 collective-permute-start.6
  213.5 11.7 %collective-permute-done.6 = f32[2,512,128]{1,2,0:T(8,128)S(1)} collective-permute-done((f32[2,512,128]{1,2,0:T(8,128)S(1)}, f32[2,512,128]{1,2,0:T(8,128)S(1)}, u32[]{:S(2)}, u32[]{:S(2)}) %collective-permute-start.6) | collective-permute-done | bytes 524320 | tf_op jit(solution)/shard_map/ppermute | solution.py:15
  225.4 2.1 collective-permute-start.7
  228.0 26.2 %collective-permute-done.7 = f32[2,512,128]{1,2,0:T(8,128)S(1)} collective-permute-done((f32[2,512,128]{1,2,0:T(8,128)S(1)}, f32[2,512,128]{1,2,0:T(8,128)S(1)}, u32[]{:S(2)}, u32[]{:S(2)}) %collective-permute-start.7) | collective-permute-done | bytes 524320 | tf_op jit(solution)/shard_map/ppermute | solution.py:15
  254.4 1.9 collective-permute-start.8
  256.6 2.4 collective-permute-start.9
  259.3 3.9 collective-permute-done.8
  263.3 21.3 %collective-permute-done.9 = f32[2,512,128]{1,2,0:T(8,128)S(1)} collective-permute-done((f32[2,512,128]{1,2,0:T(8,128)S(1)}, f32[2,512,128]{1,2,0:T(8,128)S(1)}, u32[]{:S(2)}, u32[]{:S(2)}) %collective-permute-start.9) | collective-permute-done | bytes 524320 | tf_op jit(solution)/shard_map/ppermute | solution.py:15
  284.8 1.0 slice_bitcast_fusion
  285.9 1.9 collective-permute-start.10
  290.9 2.5 collective-permute-start.11
  294.8 1.1 select_bitcast_fusion
  295.9 17.6 %collective-permute-done.11 = f32[2,512,128]{1,2,0:T(8,128)S(1)} collective-permute-done((f32[2,512,128]{1,2,0:T(8,128)S(1)}, f32[2,512,128]{1,2,0:T(8,128)S(1)}, u32[]{:S(2)}, u32[]{:S(2)}) %collective-permute-start.11) | collective-permute-done | bytes 524320 | tf_op jit(solution)/shard_map/ppermute | solution.py:15
  314.5 113.2 %all-reduce.2 = bf16[2,2,512,128]{3,1,0,2:T(2,128)(2,1)S(1)} all-reduce(f32[2,2,512,128]{3,1,0,2:T(2,128)S(1)} %copy.102), channel_id=2, replica_groups=mesh['ctx'=64,'head'=8] {'head'}, use_global_device_ids=true, to_apply=%region_16.17.clone | all-reduce | flops 262144 | bytes 1572864
  (151 shorter events, 33.4 us)
Async XLA Ops:
  99.7 7.7 %copy-start.1 = (bf16[1,2,512,128]{3,2,1,0:T(8,128)(2,1)S(1)}, bf16[1,2,512,128]{3,2,1,0:T(8,128)(2,1)}, u32[]{:S(2)}) copy-start(bf16[1,2,512,128]{3,2,1,0:T(8,128)(2,1)} %param.5) | copy-start | bytes 786436
  100.4 12.8 %collective-permute-start.3 = (bf16[2,512,128]{1,2,0:T(8,128)(2,1)}, bf16[2,512,128]{1,2,0:T(8,128)(2,1)}, u32[]{:S(2)}, u32[]{:S(2)}) collective-permute-start(bf16[2,512,128]{1,2,0:T(8,128)(2,1)} %pad_maximum_fusion.3), channel_id=1, source_target_pairs={{8,0},{16,8},{24,16},{32,24},{40,32},{48,40},{56,48},{64,56},{72,6... | collective-permute-start | bytes 786440 | tf_op jit(solution)/shard_map/ppermute | solution.py:15
  103.4 5.3 %copy-start.19 = (s32[512]{0:T(512)}, s32[512]{0:T(512)S(1)}, u32[]{:S(2)}) copy-start(s32[512]{0:T(512)S(1)} %iota_add_fusion.7) | copy-start | bytes 6148
  103.5 3.9 copy-start.23
  108.6 4.6 %copy-start.6 = (bf16[1,1,512,128]{2,3,1,0:T(8,128)(2,1)}, bf16[1,1,512,128]{2,3,1,0:T(8,128)(2,1)S(1)}, u32[]{:S(2)}) copy-start(bf16[1,1,512,128]{2,3,1,0:T(8,128)(2,1)S(1)} %copy.139) | copy-start | bytes 393220
  114.2 23.4 %collective-permute-start = (bf16[2,512,128]{1,2,0:T(8,128)(2,1)S(1)}, bf16[2,512,128]{1,2,0:T(8,128)(2,1)S(1)}, u32[]{:S(2)}, u32[]{:S(2)}) collective-permute-start(bf16[2,512,128]{1,2,0:T(8,128)(2,1)S(1)} %get-tuple-element.41), channel_id=1, source_target_pairs={{0,8},{8,16},{16,24},{24,32},{32,40},{40,48},{48,56},{56,64},{64,7... | collective-permute-start | bytes 786440 | tf_op jit(solution)/shard_map/ppermute | solution.py:15
  116.1 21.7 %collective-permute-start.4 = (bf16[2,512,128]{1,2,0:T(8,128)(2,1)S(1)}, bf16[2,512,128]{1,2,0:T(8,128)(2,1)}, u32[]{:S(2)}, u32[]{:S(2)}) collective-permute-start(bf16[2,512,128]{1,2,0:T(8,128)(2,1)S(1)} %get-tuple-element.40), channel_id=1, source_target_pairs={{8,0},{16,8},{24,16},{32,24},{40,32},{48,40},{56,48},{64,56},{72,6... | collective-permute-start | bytes 786440 | tf_op jit(solution)/shard_map/ppermute | solution.py:15
  135.4 21.1 %copy-start.15 = (s32[512]{0:T(512)S(1)}, s32[512]{0:T(512)}, u32[]{:S(2)}) copy-start(s32[512]{0:T(512)} %copy-done.14) | copy-start | bytes 6148
  135.4 21.1 %copy-start.18 = (s32[512]{0:T(512)S(1)}, s32[512]{0:T(512)}, u32[]{:S(2)}) copy-start(s32[512]{0:T(512)} %get-tuple-element.39) | copy-start | bytes 6148
  135.4 21.1 %copy-start.24 = (s32[512]{0:T(512)S(1)}, s32[512]{0:T(512)}, u32[]{:S(2)}) copy-start(s32[512]{0:T(512)} %copy-done.23) | copy-start | bytes 6148
  135.4 21.1 %copy-start.27 = (s32[512]{0:T(512)S(1)}, s32[512]{0:T(512)}, u32[]{:S(2)}) copy-start(s32[512]{0:T(512)} %iota_add_fusion.1) | copy-start | bytes 6148
  137.6 64.1 %copy-start.2 = (bf16[2,512,128]{1,2,0:T(8,128)(2,1)}, bf16[2,512,128]{1,2,0:T(8,128)(2,1)S(1)}, u32[]{:S(2)}) copy-start(bf16[2,512,128]{1,2,0:T(8,128)(2,1)S(1)} %collective-permute-done) | copy-start | bytes 786436
  138.8 35.5 %collective-permute-start.5 = (bf16[2,512,128]{1,2,0:T(8,128)(2,1)S(1)}, bf16[2,512,128]{1,2,0:T(8,128)(2,1)S(1)}, u32[]{:S(2)}, u32[]{:S(2)}) collective-permute-start(bf16[2,512,128]{1,2,0:T(8,128)(2,1)S(1)} %broadcast_select_fusion.1), channel_id=1, source_target_pairs={{8,0},{16,8},{24,16},{32,24},{40,32},{48,40},{56,48},{64,56},{72,6... | collective-permute-start | bytes 786440 | tf_op jit(solution)/shard_map/ppermute | solution.py:15
  154.6 19.8 %collective-permute-start.1 = (bf16[2,512,128]{1,2,0:T(8,128)(2,1)S(1)}, bf16[2,512,128]{1,2,0:T(8,128)(2,1)S(1)}, u32[]{:S(2)}, u32[]{:S(2)}) collective-permute-start(bf16[2,512,128]{1,2,0:T(8,128)(2,1)S(1)} %collective-permute-done), channel_id=1, source_target_pairs={{0,8},{8,16},{16,24},{24,32},{32,40},{40,48},{48,56},{56,64},{64,7... | collective-permute-start | bytes 786440 | tf_op jit(solution)/shard_map/ppermute | solution.py:15
  157.8 16.6 %copy-start.16 = (s32[512]{0:T(512)S(1)}, s32[512]{0:T(512)}, u32[]{:S(2)}) copy-start(s32[512]{0:T(512)} %get-tuple-element.38) | copy-start | bytes 6148
  157.8 16.6 %copy-start.25 = (s32[512]{0:T(512)S(1)}, s32[512]{0:T(512)}, u32[]{:S(2)}) copy-start(s32[512]{0:T(512)} %iota_add_fusion) | copy-start | bytes 6148
  178.8 2.5 copy-start.13
  178.8 2.5 copy-start.22
  179.2 20.4 %collective-permute-start.2 = (bf16[2,512,128]{1,2,0:T(8,128)(2,1)S(1)}, bf16[2,512,128]{1,2,0:T(8,128)(2,1)S(1)}, u32[]{:S(2)}, u32[]{:S(2)}) collective-permute-start(bf16[2,512,128]{1,2,0:T(8,128)(2,1)S(1)} %collective-permute-done.1), channel_id=1, source_target_pairs={{0,8},{8,16},{16,24},{24,32},{32,40},{40,48},{48,56},{56,64},{64,7... | collective-permute-start | bytes 786440 | tf_op jit(solution)/shard_map/ppermute | solution.py:15
  181.8 17.8 %copy-start.21 = (s32[512]{0:T(512)S(1)}, s32[512]{0:T(512)}, u32[]{:S(2)}) copy-start(s32[512]{0:T(512)} %iota_add_fusion.4) | copy-start | bytes 6148
  182.2 20.3 %copy-start.4 = (bf16[128,512]{0,1:T(8,128)(2,1)}, bf16[128,512]{0,1:T(8,128)(2,1)S(1)}, u32[]{:S(2)}) copy-start(bf16[128,512]{0,1:T(8,128)(2,1)S(1)} %fusion.74) | copy-start | bytes 393220
  210.4 14.9 %collective-permute-start.6 = (f32[2,512,128]{1,2,0:T(8,128)S(1)}, f32[2,512,128]{1,2,0:T(8,128)S(1)}, u32[]{:S(2)}, u32[]{:S(2)}) collective-permute-start(f32[2,512,128]{1,2,0:T(8,128)S(1)} %pad_maximum_fusion.1), channel_id=1, source_target_pairs={{8,0},{16,8},{24,16},{32,24},{40,32},{48,40},{56,48},{64,56},{72,6... | collective-permute-start | bytes 1572872 | tf_op jit(solution)/shard_map/ppermute | solution.py:15
  225.4 2.1 copy-start.7
  225.4 28.8 %collective-permute-start.7 = (f32[2,512,128]{1,2,0:T(8,128)S(1)}, f32[2,512,128]{1,2,0:T(8,128)S(1)}, u32[]{:S(2)}, u32[]{:S(2)}) collective-permute-start(f32[2,512,128]{1,2,0:T(8,128)S(1)} %get-tuple-element.29), channel_id=1, source_target_pairs={{0,8},{8,16},{16,24},{24,32},{32,40},{40,48},{48,56},{56,64},{64,7... | collective-permute-start | bytes 1572872 | tf_op jit(solution)/shard_map/ppermute | solution.py:15
  254.4 8.8 %collective-permute-start.8 = (f32[2,512,128]{1,2,0:T(8,128)S(1)}, f32[2,512,128]{1,2,0:T(8,128)S(1)}, u32[]{:S(2)}, u32[]{:S(2)}) collective-permute-start(f32[2,512,128]{1,2,0:T(8,128)S(1)} %get-tuple-element.26), channel_id=1, source_target_pairs={{8,0},{16,8},{24,16},{32,24},{40,32},{48,40},{56,48},{64,56},{72,6... | collective-permute-start | bytes 1572872 | tf_op jit(solution)/shard_map/ppermute | solution.py:15
  256.6 28.0 %collective-permute-start.9 = (f32[2,512,128]{1,2,0:T(8,128)S(1)}, f32[2,512,128]{1,2,0:T(8,128)S(1)}, u32[]{:S(2)}, u32[]{:S(2)}) collective-permute-start(f32[2,512,128]{1,2,0:T(8,128)S(1)} %get-tuple-element.27), channel_id=1, source_target_pairs={{0,8},{8,16},{16,24},{24,32},{32,40},{40,48},{48,56},{56,64},{64,7... | collective-permute-start | bytes 1572872 | tf_op jit(solution)/shard_map/ppermute | solution.py:15
  285.9 8.9 %collective-permute-start.10 = (f32[2,512,128]{1,2,0:T(8,128)}, f32[2,512,128]{1,2,0:T(8,128)}, u32[]{:S(2)}, u32[]{:S(2)}) collective-permute-start(f32[2,512,128]{1,2,0:T(8,128)} %get-tuple-element.24), channel_id=1, source_target_pairs={{8,0},{16,8},{24,16},{32,24},{40,32},{48,40},{56,48},{64,56},{72,6... | collective-permute-start | bytes 1572872 | tf_op jit(solution)/shard_map/ppermute | solution.py:15
  287.8 1.0 copy-start.10
  288.8 1.0 copy-start.9
  289.8 1.0 copy-start.11
  290.9 2.9 copy-start.8
  290.9 22.6 %collective-permute-start.11 = (f32[2,512,128]{1,2,0:T(8,128)S(1)}, f32[2,512,128]{1,2,0:T(8,128)S(1)}, u32[]{:S(2)}, u32[]{:S(2)}) collective-permute-start(f32[2,512,128]{1,2,0:T(8,128)S(1)} %copy-done.11), channel_id=1, source_target_pairs={{0,8},{8,16},{16,24},{24,32},{32,40},{40,48},{48,56},{56,64},{64,7... | collective-permute-start | bytes 1572872 | tf_op jit(solution)/shard_map/ppermute | solution.py:15
  (8 other events, 6.2 us)
where the time goes:
time: 434 us; the launch traced here: 428 us
  blocking collectives  210 us (48%)
  waiting for transfers between devices  122 us (28%)
  starting transfers between devices  52.9 us (12%)
  matrix products  19.2 us (4%)
  local copies, waits for them, and re-layouts  11.8 us (3%)
  other arithmetic  10.4 us (2%)
    ppermute x12, waiting for transfers between devices, shifted(): return lax.ppermute(array, axis, pairs)  122 us
    unnamed x1, blocking collectives  113 us
    ppermute x12, starting transfers between devices, shifted(): return lax.ppermute(array, axis, pairs)  52.9 us
    all_gather x1, blocking collectives, body(): lax.all_gather(key_states, 'head', axis=2, tiled=True)  49.6 us
    all_gather x1, blocking collectives, body(): lax.all_gather(value_states, 'head', axis=2, tiled=True)  47 us
  transfers between devices with their start and end apart: 12, of which 11 were waited for; matrix products, arithmetic and copies ran while one was open for 4% of the time, Pallas kernels for 0%

commit v1 on v0

v1 whole, which is shorter than its diff:
```python
import jax
import jax.numpy as jnp
from jax import lax
from jax.experimental import pallas as pl
from jax.experimental.pallas import tpu as pltpu
from jax.sharding import PartitionSpec as P

REACH = 3
GROUP = 8
NEG_FILL = -1e30


def ring_pairs(ctx, step_even, step_odd):
    pairs = []
    for base in range(0, ctx, GROUP):
        for r in range(GROUP):
            chip, core = divmod(r, 2)
            move, target = (step_even, step_odd)[core]
            pairs.append((base + r, base + ((chip + move) % (GROUP // 2)) * 2 + target))
    return pairs


def halo_pairs(ctx):
    pairs = []
    for base in range(0, ctx, GROUP):
        for k in range(REACH):
            high = base + GROUP - 1 - k
            pairs.append((high, high + GROUP if base + GROUP < ctx else base + k))
            if base > 0:
                pairs.append((base + k, base + k - GROUP))
    return pairs


def inverse(pairs):
    return [(b, a) for a, b in pairs]


def attention_kernel(
    lo_ref, core_ref, seg_row, seg_col, q_own, g_own, qg_far, kv_own, kv_a, kv_b, kv_c, kv_d,
    out_own, out_far, p_own, p_a, p_b, p_c, p_d,
    keys, values, keys_t, values_t, scores, key_acc, value_acc, sems,
):
    tile = scores.shape[1]
    width = q_own.shape[1]
    shard = kv_a.shape[2]
    head_dim = q_own.shape[2]
    per_span = width // tile
    shards = kv_a.shape[0]
    scale = head_dim ** -0.5
    core = core_ref[0]
    f32, bf16 = jnp.float32, jnp.bfloat16

    copies = []
    for slot, source in enumerate((kv_d, kv_b, kv_c, kv_own, kv_a)):
        for which, target in enumerate((keys, values)):
            if source is kv_own:
                view = source.at[:, core, which]
            else:
                view = source.at[:, which]
            copy = pltpu.make_async_copy(
                view, target.at[pl.ds(slot * shards, shards)], sems.at[slot, which]
            )
            copy.start()
            copies.append(copy)
    key_acc[...] = jnp.zeros_like(key_acc)
    value_acc[...] = jnp.zeros_like(value_acc)
    for copy in copies:
        copy.wait()

    tile_shards = tile // shard

    def tile_of(ref, j):
        return ref[pl.ds(j * tile_shards, tile_shards)].reshape(tile, head_dim)

    key_tiles = keys.shape[0] // tile_shards
    for j in range(key_tiles):
        keys_t[j] = tile_of(keys, j).T
        values_t[j] = tile_of(values, j).T

    nt = (((1,), (1,)), ((), ()))
    nn = (((1,), (0,)), ((), ()))
    for i in range(2 * per_span):
        span, part = divmod(i, per_span)
        rows = pl.ds(part * tile, tile)
        if span == 0:
            query = q_own[core, rows]
            grad = g_own[core, rows]
        else:
            query = qg_far[0, rows]
            grad = qg_far[1, rows]
        diagonal = REACH * per_span + i
        lo = lo_ref[i]
        query_seg = seg_row[:, pl.ds(diagonal * tile, tile)]

        def score_tile(j, causal):
            raw = lax.dot_general(tile_of(keys, j), query, nt, preferred_element_type=f32) * scale
            if causal:
                allowed = seg_col[pl.ds(j * tile, tile), :] == query_seg
                at_key = lax.broadcasted_iota(jnp.int32, (tile, tile), 0)
                at_query = lax.broadcasted_iota(jnp.int32, (tile, tile), 1)
                allowed = allowed & (at_key <= at_query)
            else:
                start = pl.multiple_of(j * tile, tile)
                allowed = seg_col[pl.ds(start, tile), :] == query_seg
            raw = jnp.where(allowed, raw, NEG_FILL)
            scores[j] = raw
            return jnp.max(raw, axis=0, keepdims=True)

        top = score_tile(diagonal, True)
        top = lax.fori_loop(
            lo, diagonal, lambda j, m: jnp.maximum(m, score_tile(j, False)), top
        )

        def forward(j, carry):
            total, acc = carry
            prob = jnp.exp(scores[j] - top)
            scores[j] = prob
            total = total + jnp.sum(prob, axis=0, keepdims=True)
            acc = acc + lax.dot_general(
                values_t[j], prob.astype(bf16), nn, preferred_element_type=f32
            )
            return total, acc

        total, acc = lax.fori_loop(
            lo,
            diagonal + 1,
            forward,
            (jnp.zeros((1, tile), f32), jnp.zeros((head_dim, tile), f32)),
        )
        inv = 1.0 / total
        attended_t = (acc * inv).astype(bf16).astype(f32)
        attended = attended_t.T.astype(bf16)
        delta = jnp.sum(grad.astype(f32).T * attended_t, axis=0, keepdims=True)

        def backward(j, acc):
            prob = scores[j] * inv
            start = pl.multiple_of(j * tile, tile)
            here = pl.ds(start, tile)
            value_acc[here] += lax.dot_general(
                prob.astype(bf16), grad, nn, preferred_element_type=f32
            )
            dot_grad = lax.dot_general(tile_of(values, j), grad, nt, preferred_element_type=f32)
            score_grad = (prob * (dot_grad - delta)).astype(bf16)
            key_acc[here] += lax.dot_general(score_grad, query, nn, preferred_element_type=f32)
            return acc + lax.dot_general(keys_t[j], score_grad, nn, preferred_element_type=f32)

        acc = lax.fori_loop(lo, diagonal + 1, backward, jnp.zeros((head_dim, tile), f32))
        query_grad = (acc.T * scale).astype(bf16)
        target = out_own if span == 0 else out_far
        target[0, rows] = attended
        target[1, rows] = query_grad

    for slot, target in enumerate((p_d, p_b, p_c, p_own, p_a)):
        here = pl.ds(slot * width, width)
        target[0] = (key_acc[here] * scale).astype(target.dtype)
        target[1] = value_acc[here].astype(target.dtype)


def attention(lo, core, seg_window, queries, out_grad, far, kv_own, kv_a, kv_b, kv_c, kv_d):
    width, head_dim = queries.shape[1:]
    shards, _, shard, _ = kv_a.shape
    tile = max(min(256, width // 2), shard)
    window = (REACH + 2) * width
    part = jax.ShapeDtypeStruct((2, width, head_dim), jnp.bfloat16)
    own_part = jax.ShapeDtypeStruct((2, width, head_dim), jnp.float32)
    vmem = pl.BlockSpec(memory_space=pltpu.VMEM)
    smem = pl.BlockSpec(memory_space=pltpu.SMEM)
    hbm = pl.BlockSpec(memory_space=pl.ANY)
    return pl.pallas_call(
        attention_kernel,
        out_shape=(part, part, own_part, part, part, part, part),
        in_specs=[smem, smem] + [vmem] * 5 + [hbm] * 5,
        out_specs=[vmem] * 7,
        scratch_shapes=[
            pltpu.VMEM(((REACH + 2) * shards, shard, head_dim), jnp.bfloat16),
            pltpu.VMEM(((REACH + 2) * shards, shard, head_dim), jnp.bfloat16),
            pltpu.VMEM((window // tile, head_dim, tile), jnp.bfloat16),
            pltpu.VMEM((window // tile, head_dim, tile), jnp.bfloat16),
            pltpu.VMEM((window // tile, tile, tile), jnp.float32),
            pltpu.VMEM((window, head_dim), jnp.float32),
            pltpu.VMEM((window, head_dim), jnp.float32),
            pltpu.SemaphoreType.DMA((REACH + 2, 2)),
        ],
        compiler_params=pltpu.CompilerParams(vmem_limit_bytes=40 * 1024 * 1024),
        cost_estimate=pl.CostEstimate(
            flops=6 * 2 * 8 * width * width * head_dim,
            bytes_accessed=8 * 1024 * 1024,
            transcendentals=8 * width * width,
        ),
        name="attention",
    )(
        lo, core, seg_window[None, :], seg_window[:, None],
        queries, out_grad, far, kv_own, kv_a, kv_b, kv_c, kv_d,
    )


def body(queries, key_states, value_states, out_grad, segments):
    ctx = lax.axis_size("ctx")
    position = lax.axis_index("ctx")
    ring_place = position % GROUP
    chip, core = ring_place // 2, ring_place % 2
    chips = GROUP // 2
    width = queries.shape[2]
    heads = lax.axis_size("head")
    shard = key_states.shape[2]
    head_dim = key_states.shape[3]

    swap = ring_pairs(ctx, (0, 1), (0, 0))
    pairs_b = ring_pairs(ctx, (1, 0), (-1, 1))
    pairs_c = ring_pairs(ctx, (-1, 1), (1, 0))
    pairs_d = ring_pairs(ctx, (-2, 1), (2, 0))
    halo = halo_pairs(ctx)

    own = jnp.stack([key_states[0], value_states[0]], axis=1)
    sent = jnp.where(ring_place >= GROUP - REACH, own[0], own[1])
    edge = lax.ppermute(sent, "ctx", halo)
    mine = jnp.concatenate([own, edge[None]], axis=0)
    gathered = lax.all_to_all(
        jnp.broadcast_to(mine[None], (heads,) + mine.shape), "head", 0, 0, tiled=False
    )

    queries, out_grad = queries[0], out_grad[0]
    even = core == 0
    far = lax.ppermute(
        jnp.where(
            even,
            jnp.stack([queries[1], out_grad[1]]),
            jnp.stack([queries[0], out_grad[0]]),
        ),
        "ctx",
        swap,
    )

    own_half = jnp.where(even, gathered[:, 0], gathered[:, 1])
    far_half = jnp.where(even, gathered[:, 1], gathered[:, 0])
    kv_edge = gathered[:, 2]
    wrap_b = jnp.where(even, chip == chips - 1, chip == 0)
    wrap_c = jnp.where(even, chip == 0, chip == chips - 1)
    wrap_d = jnp.where(even, chip <= 1, chip >= chips - 2)
    kv_d = lax.ppermute(jnp.where(wrap_d, kv_edge, far_half), "ctx", pairs_d)
    kv_c = lax.ppermute(jnp.where(wrap_c, kv_edge, far_half), "ctx", pairs_c)
    kv_b = lax.ppermute(jnp.where(wrap_b, kv_edge, own_half), "ctx", pairs_b)
    kv_a = lax.ppermute(far_half, "ctx", swap)

    first = jnp.where(even, position, 2 * ctx - 1 - position)
    window = (REACH + 2) * width
    padded = jnp.concatenate([jnp.full((REACH * width,), -1, jnp.int32), segments])
    seg_window = lax.dynamic_slice_in_dim(padded, first * width, window)
    tile = max(min(256, width // 2), shard)
    heads_of_tiles = seg_window[REACH * width :: tile]
    lo = jnp.sum(seg_window[None, :] < heads_of_tiles[:, None], axis=1, dtype=jnp.int32) // tile

    out_own, out_far, p_own, p_a, p_b, p_c, p_d = attention(
        lo, core[None].astype(jnp.int32), seg_window, queries, out_grad, far,
        gathered, kv_a, kv_b, kv_c, kv_d,
    )

    r_d = lax.ppermute(p_d, "ctx", inverse(pairs_d)).astype(jnp.float32)
    r_c = lax.ppermute(p_c, "ctx", inverse(pairs_c)).astype(jnp.float32)
    r_b = lax.ppermute(p_b, "ctx", inverse(pairs_b)).astype(jnp.float32)
    r_a = lax.ppermute(p_a, "ctx", swap).astype(jnp.float32)
    back = lax.ppermute(out_far, "ctx", swap)

    own_sum = p_own + jnp.where(wrap_b, 0.0, r_b)
    far_sum = r_a + jnp.where(wrap_c, 0.0, r_c) + jnp.where(wrap_d, 0.0, r_d)
    edge_sum = (
        jnp.where(wrap_b, r_b, 0.0) + jnp.where(wrap_c, r_c, 0.0) + jnp.where(wrap_d, r_d, 0.0)
    )
    sums = jnp.stack(
        [jnp.where(even, own_sum, far_sum), jnp.where(even, far_sum, own_sum), edge_sum]
    ).astype(jnp.bfloat16)
    sums = sums.reshape(3, 2, heads, shard, head_dim).transpose(2, 0, 1, 3, 4)
    spread = lax.all_to_all(sums, "head", 0, 0, tiled=False)
    total = jnp.sum(spread.astype(jnp.float32), axis=0)
    returned = lax.ppermute(total[2].astype(jnp.bfloat16), "ctx", inverse(halo)).astype(jnp.float32)
    late = ring_place >= GROUP - REACH
    lower = total[0] + jnp.where(late, returned, 0.0)
    upper = total[1] + jnp.where(late, 0.0, returned)
    grads = jnp.stack([lower, upper]).astype(jnp.bfloat16)

    results = []
    for k in range(2):
        results.append(
            jnp.where(
                even, jnp.stack([out_own[k], back[k]]), jnp.stack([back[k], out_own[k]])
            )[None]
        )
    return results[0], results[1], grads[:, 0][None], grads[:, 1][None]


def solution(mesh):
    return jax.shard_map(
        body,
        mesh=mesh,
        in_specs=(
            P("ctx", None, None, "head"),
            P("ctx", None, "head", None),
            P("ctx", None, "head", None),
            P("ctx", None, None, "head"),
            P(),
        ),
        out_specs=(
            P("ctx", None, None, "head"),
            P("ctx", None, None, "head"),
            P("ctx", None, "head", None),
            P("ctx", None, "head", None),
        ),
        check_vma=False,
    )
```

time: 434 us -> 188 us (0.43); the launches traced: 428 us -> 187 us
  blocking collectives: 210 us -> 0 us
  waiting for transfers between devices: 122 us -> 102 us
  matrix products: 19.2 us -> 0 us
  starting transfers between devices: 52.9 us -> 67.8 us
  Pallas kernels: 0 us -> 10.4 us
  local copies, waits for them, and re-layouts: 11.8 us -> 1.75 us
  other arithmetic: 10.4 us -> 4.86 us
    unnamed x1 -> x0, blocking collectives: 113 us -> none
    all_gather x2 -> x0, blocking collectives: 96.6 us -> none  [the longest x1 49.6 us: body(): lax.all_gather(key_states, 'head', axis=2, tiled=True)]
    ppermute x12, waiting for transfers between devices: 122 us -> 28.3 us  [the longest x1 10.1 us: body(): r_c = lax.ppermute(p_c, 'ctx', inverse(pairs_c)).astype(jnp.float32)]
    all_to_all x0 -> x2, waiting for transfers between devices: none -> 73.2 us  [the longest x1 37.1 us: body(): lax.all_to_all(jnp.broadcast_to(mine[None], (heads,) + mine.shape), 'head...]
    dot_general x48 -> x0, matrix products: 19.2 us -> none  [the longest x8 4.69 us: tile_scores(): jnp.einsum('qhd,kd->hqk', query_tile, key_tile, preferred_element_type=jn...]
    all_to_all x0 -> x2, starting transfers between devices: none -> 13.7 us  [the longest x1 9.44 us: body(): lax.all_to_all(jnp.broadcast_to(mine[None], (heads,) + mine.shape), 'head...]
    pallas_call x0 -> x1, Pallas kernels: none -> 10.4 us  [attention(): pl.pallas_call(attention_kernel, out_shape=(part, part, own_part, part, p...]
    unnamed x65 -> x6, local copies, waits for them, and re-layouts: 7.08 us -> 0.02 us
  transfers between devices with their start and end apart: 12 -> 14, of which waited for: 11 -> 8; matrix products, arithmetic and copies ran while one was open for 4% -> 1% of each run, Pallas kernels for 0% -> 0%
where the time goes in v1:
time: 188 us; the launch traced here: 187 us
  waiting for transfers between devices  102 us (54%)
  starting transfers between devices  67.8 us (36%)
  Pallas kernels  10.4 us (6%)
  other arithmetic  4.86 us (3%)
    all_to_all x1, waiting for transfers between devices, body(): lax.all_to_all(jnp.broadcast_to(mine[None], (heads,) + mine.shape), 'head...  37.1 us
    all_to_all x1, waiting for transfers between devices, body(): spread = lax.all_to_all(sums, 'head', 0, 0, tiled=False)  36 us
    ppermute x1, starting transfers between devices, body(): edge = lax.ppermute(sent, 'ctx', halo)  16 us
    pallas_call x1, Pallas kernels, attention(): pl.pallas_call(attention_kernel, out_shape=(part, part, own_part, part, p...  10.4 us
    ppermute x1, waiting for transfers between devices, body(): r_c = lax.ppermute(p_c, 'ctx', inverse(pairs_c)).astype(jnp.float32)  10.1 us
    ppermute x1, starting transfers between devices, body(): r_a = lax.ppermute(p_a, 'ctx', swap).astype(jnp.float32)  10 us
    all_to_all x1, starting transfers between devices, body(): lax.all_to_all(jnp.broadcast_to(mine[None], (heads,) + mine.shape), 'head...  9.44 us
    ppermute x1, waiting for transfers between devices, body(): lax.ppermute(total[2].astype(jnp.bfloat16), 'ctx', inverse(halo))  9.13 us
  transfers between devices with their start and end apart: 14, of which 8 were waited for; matrix products, arithmetic and copies ran while one was open for 1% of the time, Pallas kernels for 0%

profile of v1, /device:TPU:6, one launch (start us, length us, event | category | flops | bytes accessed | tf_op | source)
XLA Modules:
  0.0 187.4 jit_solution(16227729255350063319)
XLA Ops:
  0.6 0.8 fusion.15
  1.4 16.0 %collective-permute-start.1 = (bf16[2,64,128]{2,1,0:T(8,128)(2,1)S(1)}, bf16[2,64,128]{2,1,0:T(8,128)(2,1)S(1)}, u32[]{:S(2)}, u32[]{:S(2)}) collective-permute-start(bf16[2,64,128]{2,1,0:T(8,128)(2,1)S(1)} %fusion.15), channel_id=1, source_target_pairs={{56,120},{48,112},{40,104},{120,184},{64,0},{112,176},{72,8},{104,... | collective-permute-start | bytes 98312 | tf_op jit(solution)/shard_map/ppermute | solution.py:216
  17.4 1.6 collective-permute-done.1
  19.0 0.8 pad_maximum_fusion.1
  19.9 1.1 broadcast_in_dim.43
  20.9 9.4 %all-to-all-start = ((bf16[8,3,2,64,128]{4,3,2,1,0:T(8,128)(2,1)}), bf16[8,3,2,64,128]{4,3,2,1,0:T(8,128)(2,1)S(1)}, u32[]{:S(2)}, u32[]{:S(2)}) async-start(bf16[8,3,2,64,128]{4,3,2,1,0:T(8,128)(2,1)} %broadcast_in_dim.43), calls=%async_computation | async-start | bytes 1572864 | tf_op jit(solution)/shard_map/all_to_all | solution.py:218
  30.5 1.9 %collective-permute-start = (bf16[2,512,128]{2,1,0:T(8,128)(2,1)S(1)}, bf16[2,512,128]{2,1,0:T(8,128)(2,1)S(1)}, u32[]{:S(2)}, u32[]{:S(2)}) collective-permute-start(bf16[2,512,128]{2,1,0:T(8,128)(2,1)S(1)} %maximum_select_fusion), channel_id=1, source_target_pairs={{0,8},{8,0},{16,24},{24,16},{32,40},{40,32},{48,56},{56,48},{64,72... | collective-permute-start | bytes 786440 | tf_op jit(solution)/shard_map/ppermute | solution.py:224
  32.7 37.1 %all-to-all-done.kv_own = bf16[8,3,2,64,128]{4,3,2,1,0:T(8,128)(2,1)S(1)} async-done(((bf16[8,3,2,64,128]{4,3,2,1,0:T(8,128)(2,1)}), bf16[8,3,2,64,128]{4,3,2,1,0:T(8,128)(2,1)S(1)}, u32[]{:S(2)}, u32[]{:S(2)}) %all-to-all-start) | async-done | bytes 786464 | tf_op jit(solution)/shard_map/all_to_all | solution.py:218
  69.9 1.9 %collective-permute-start.5 = (bf16[8,2,64,128]{3,2,1,0:T(8,128)(2,1)S(1)}, bf16[8,2,64,128]{3,2,1,0:T(8,128)(2,1)S(1)}, u32[]{:S(2)}, u32[]{:S(2)}) collective-permute-start(bf16[8,2,64,128]{3,2,1,0:T(8,128)(2,1)S(1)} %get-tuple-element.18), channel_id=1, source_target_pairs={{0,40},{8,32},{16,56},{24,48},{32,8},{40,0},{48,24},{56,16},{64,10... | collective-permute-start | bytes 786440 | tf_op jit(solution)/shard_map/ppermute | solution.py:240
  71.8 1.9 %collective-permute-start.2 = (bf16[8,2,64,128]{3,2,1,0:T(8,128)(2,1)S(1)}, bf16[8,2,64,128]{3,2,1,0:T(8,128)(2,1)S(1)}, u32[]{:S(2)}, u32[]{:S(2)}) collective-permute-start(bf16[8,2,64,128]{3,2,1,0:T(8,128)(2,1)S(1)} %get-tuple-element.19), channel_id=1, source_target_pairs={{0,8},{8,0},{16,24},{24,16},{32,40},{40,32},{48,56},{56,48},{64,72... | collective-permute-start | bytes 786440 | tf_op jit(solution)/shard_map/ppermute | solution.py:243
  73.8 5.9 %collective-permute-start.4 = (bf16[8,2,64,128]{3,2,1,0:T(8,128)(2,1)S(1)}, bf16[8,2,64,128]{3,2,1,0:T(8,128)(2,1)S(1)}, u32[]{:S(2)}, u32[]{:S(2)}) collective-permute-start(bf16[8,2,64,128]{3,2,1,0:T(8,128)(2,1)S(1)} %get-tuple-element.23), channel_id=1, source_target_pairs={{0,56},{8,16},{16,8},{24,32},{32,24},{40,48},{48,40},{56,0},{64,12... | collective-permute-start | bytes 786440 | tf_op jit(solution)/shard_map/ppermute | solution.py:241
  79.7 2.8 %collective-permute-start.3 = (bf16[8,2,64,128]{3,2,1,0:T(8,128)(2,1)S(1)}, bf16[8,2,64,128]{3,2,1,0:T(8,128)(2,1)S(1)}, u32[]{:S(2)}, u32[]{:S(2)}) collective-permute-start(bf16[8,2,64,128]{3,2,1,0:T(8,128)(2,1)S(1)} %get-tuple-element.24), channel_id=1, source_target_pairs={{0,16},{8,56},{16,32},{24,8},{32,48},{40,24},{48,0},{56,40},{64,80... | collective-permute-start | bytes 786440 | tf_op jit(solution)/shard_map/ppermute | solution.py:242
  82.5 0.2 convert_reduce_fusion.1
  82.7 0.4 broadcast_in_dim.46.seg_col
  83.1 1.0 collective-permute-done.4.kv_c
  84.1 5.1 %collective-permute-done.3.kv_b = bf16[8,2,64,128]{3,2,1,0:T(8,128)(2,1)S(1)} collective-permute-done((bf16[8,2,64,128]{3,2,1,0:T(8,128)(2,1)S(1)}, bf16[8,2,64,128]{3,2,1,0:T(8,128)(2,1)S(1)}, u32[]{:S(2)}, u32[]{:S(2)}) %collective-permute-start.3) | collective-permute-done | bytes 262176 | tf_op jit(solution)/shard_map/ppermute | solution.py:242
  89.2 10.4 %attention.1 = (bf16[2,512,128]{2,1,0:T(8,128)(2,1)S(1)}, bf16[2,512,128]{2,1,0:T(8,128)(2,1)S(1)}, f32[2,512,128]{2,1,0:T(8,128)S(1)}, bf16[2,512,128]{2,1,0:T(...) custom-call(s32[4]{0:T(128)S(1)} %and_select_fusion.lo_ref, ...), custom_call_target="tpu_custom_call" | custom-call | flops 3221225472 | bytes 8388608 | tf_op jit(solution)/shard_map/attention/pallas_call | solution.py:169
  99.6 1.9 %collective-permute-start.7 = (bf16[2,512,128]{2,1,0:T(8,128)(2,1)S(1)}, bf16[2,512,128]{2,1,0:T(8,128)(2,1)S(1)}, u32[]{:S(2)}, u32[]{:S(2)}) collective-permute-start(bf16[2,512,128]{2,1,0:T(8,128)(2,1)S(1)} %get-tuple-element.14), channel_id=1, source_target_pairs={{16,0},{56,8},{32,16},{8,24},{48,32},{24,40},{0,48},{40,56},{80,64... | collective-permute-start | bytes 786440 | tf_op jit(solution)/shard_map/ppermute | solution.py:260
  101.5 10.0 %collective-permute-start.8 = (bf16[2,512,128]{2,1,0:T(8,128)(2,1)S(1)}, bf16[2,512,128]{2,1,0:T(8,128)(2,1)S(1)}, u32[]{:S(2)}, u32[]{:S(2)}) collective-permute-start(bf16[2,512,128]{2,1,0:T(8,128)(2,1)S(1)} %get-tuple-element.15), channel_id=1, source_target_pairs={{0,8},{8,0},{16,24},{24,16},{32,40},{40,32},{48,56},{56,48},{64,72... | collective-permute-start | bytes 786440 | tf_op jit(solution)/shard_map/ppermute | solution.py:261
  111.6 1.9 %collective-permute-start.9 = (bf16[2,512,128]{2,1,0:T(8,128)(2,1)S(1)}, bf16[2,512,128]{2,1,0:T(8,128)(2,1)S(1)}, u32[]{:S(2)}, u32[]{:S(2)}) collective-permute-start(bf16[2,512,128]{2,1,0:T(8,128)(2,1)S(1)} %get-tuple-element.16), channel_id=1, source_target_pairs={{56,0},{16,8},{8,16},{32,24},{24,32},{48,40},{40,48},{0,56},{120,6... | collective-permute-start | bytes 786440 | tf_op jit(solution)/shard_map/ppermute | solution.py:259
  113.5 2.5 %collective-permute-start.10 = (bf16[2,512,128]{2,1,0:T(8,128)(2,1)S(1)}, bf16[2,512,128]{2,1,0:T(8,128)(2,1)S(1)}, u32[]{:S(2)}, u32[]{:S(2)}) collective-permute-start(bf16[2,512,128]{2,1,0:T(8,128)(2,1)S(1)} %get-tuple-element.17), channel_id=1, source_target_pairs={{40,0},{32,8},{56,16},{48,24},{8,32},{0,40},{24,48},{16,56},{104,6... | collective-permute-start | bytes 786440 | tf_op jit(solution)/shard_map/ppermute | solution.py:258
  116.0 10.1 %collective-permute-done.9 = bf16[2,512,128]{2,1,0:T(8,128)(2,1)S(1)} collective-permute-done((bf16[2,512,128]{2,1,0:T(8,128)(2,1)S(1)}, bf16[2,512,128]{2,1,0:T(8,128)(2,1)S(1)}, u32[]{:S(2)}, u32[]{:S(2)}) %collective-permute-start.9) | collective-permute-done | bytes 262176 | tf_op jit(solution)/shard_map/ppermute | solution.py:259
  126.1 0.3 select_convert_fusion.1
  126.5 1.0 copy_bitcast_fusion
  127.4 4.3 %all-to-all-start.1 = ((bf16[8,3,2,64,128]{4,3,2,1,0:T(8,128)(2,1)}), bf16[8,3,2,64,128]{4,3,2,1,0:T(8,128)(2,1)S(1)}, u32[]{:S(2)}, u32[]{:S(2)}) async-start(bf16[8,3,2,64,128]{4,3,2,1,0:T(8,128)(2,1)} %copy_bitcast_fusion), calls=%async_computation.1 | async-start | bytes 1572864 | tf_op jit(solution)/shard_map/all_to_all | solution.py:273
  131.7 1.9 %collective-permute-start.6 = (bf16[2,512,128]{2,1,0:T(8,128)(2,1)S(1)}, bf16[2,512,128]{2,1,0:T(8,128)(2,1)S(1)}, u32[]{:S(2)}, u32[]{:S(2)}) collective-permute-start(bf16[2,512,128]{2,1,0:T(8,128)(2,1)S(1)} %get-tuple-element.12), channel_id=1, source_target_pairs={{0,8},{8,0},{16,24},{24,16},{32,40},{40,32},{48,56},{56,48},{64,72... | collective-permute-start | bytes 786440 | tf_op jit(solution)/shard_map/ppermute | solution.py:262
  133.6 1.5 collective-permute-done.6
  135.1 36.0 %all-to-all-done.1 = bf16[8,3,2,64,128]{4,3,2,1,0:T(8,128)(2,1)S(1)} async-done(((bf16[8,3,2,64,128]{4,3,2,1,0:T(8,128)(2,1)}), bf16[8,3,2,64,128]{4,3,2,1,0:T(8,128)(2,1)S(1)}, u32[]{:S(2)}, u32[]{:S(2)}) %all-to-all-start.1) | async-done | bytes 786464 | tf_op jit(solution)/shard_map/all_to_all | solution.py:273
  171.3 5.4 %collective-permute-start.11 = (bf16[2,64,128]{2,1,0:T(8,128)(2,1)S(1)}, bf16[2,64,128]{2,1,0:T(8,128)(2,1)S(1)}, u32[]{:S(2)}, u32[]{:S(2)}) collective-permute-start(bf16[2,64,128]{2,1,0:T(8,128)(2,1)S(1)} %fusion.16), channel_id=1, source_target_pairs={{120,56},{112,48},{104,40},{184,120},{0,64},{176,112},{8,72},{168,... | collective-permute-start | bytes 98312 | tf_op jit(solution)/shard_map/ppermute | solution.py:275
  176.7 0.9 maximum_select_fusion.1
  177.6 9.1 %collective-permute-done.11 = bf16[2,64,128]{2,1,0:T(8,128)(2,1)S(1)} collective-permute-done((bf16[2,64,128]{2,1,0:T(8,128)(2,1)S(1)}, bf16[2,64,128]{2,1,0:T(8,128)(2,1)S(1)}, u32[]{:S(2)}, u32[]{:S(2)}) %collective-permute-start.11) | collective-permute-done | bytes 32800 | tf_op jit(solution)/shard_map/ppermute | solution.py:275
  186.7 0.6 fusion.19
  (27 shorter events, 0.6 us)
Async XLA Ops:
  1.4 17.6 %collective-permute-start.1 = (bf16[2,64,128]{2,1,0:T(8,128)(2,1)S(1)}, bf16[2,64,128]{2,1,0:T(8,128)(2,1)S(1)}, u32[]{:S(2)}, u32[]{:S(2)}) collective-permute-start(bf16[2,64,128]{2,1,0:T(8,128)(2,1)S(1)} %fusion.15), channel_id=1, source_target_pairs={{56,120},{48,112},{40,104},{120,184},{64,0},{112,176},{72,8},{104,... | collective-permute-start | bytes 98312 | tf_op jit(solution)/shard_map/ppermute | solution.py:216
  19.8 10.6 %copy-start = (bf16[1,2,512,128]{3,2,1,0:T(8,128)(2,1)S(1)}, bf16[1,2,512,128]{3,2,1,0:T(8,128)(2,1)}, u32[]{:S(2)}) copy-start(bf16[1,2,512,128]{3,2,1,0:T(8,128)(2,1)} %param.5) | copy-start | bytes 786436
  19.8 10.6 %copy-start.1 = (bf16[1,2,512,128]{3,2,1,0:T(8,128)(2,1)S(1)}, bf16[1,2,512,128]{3,2,1,0:T(8,128)(2,1)}, u32[]{:S(2)}) copy-start(bf16[1,2,512,128]{3,2,1,0:T(8,128)(2,1)} %param.8) | copy-start | bytes 786436
  20.9 48.9 %all-to-all-start = ((bf16[8,3,2,64,128]{4,3,2,1,0:T(8,128)(2,1)}), bf16[8,3,2,64,128]{4,3,2,1,0:T(8,128)(2,1)S(1)}, u32[]{:S(2)}, u32[]{:S(2)}) async-start(bf16[8,3,2,64,128]{4,3,2,1,0:T(8,128)(2,1)} %broadcast_in_dim.43), calls=%async_computation | async-start | bytes 1572864 | tf_op jit(solution)/shard_map/all_to_all | solution.py:218
  30.4 2.1 %copy-start.2 = (s32[65536]{0:T(1024)S(1)}, s32[65536]{0:T(1024)}, u32[]{:S(2)}) copy-start(s32[65536]{0:T(1024)} %param.9) | copy-start | bytes 786436
  30.5 52.6 %collective-permute-start = (bf16[2,512,128]{2,1,0:T(8,128)(2,1)S(1)}, bf16[2,512,128]{2,1,0:T(8,128)(2,1)S(1)}, u32[]{:S(2)}, u32[]{:S(2)}) collective-permute-start(bf16[2,512,128]{2,1,0:T(8,128)(2,1)S(1)} %maximum_select_fusion), channel_id=1, source_target_pairs={{0,8},{8,0},{16,24},{24,16},{32,40},{40,32},{48,56},{56,48},{64,72... | collective-permute-start | bytes 786440 | tf_op jit(solution)/shard_map/ppermute | solution.py:224
  69.9 13.2 %collective-permute-start.5 = (bf16[8,2,64,128]{3,2,1,0:T(8,128)(2,1)S(1)}, bf16[8,2,64,128]{3,2,1,0:T(8,128)(2,1)S(1)}, u32[]{:S(2)}, u32[]{:S(2)}) collective-permute-start(bf16[8,2,64,128]{3,2,1,0:T(8,128)(2,1)S(1)} %get-tuple-element.18), channel_id=1, source_target_pairs={{0,40},{8,32},{16,56},{24,48},{32,8},{40,0},{48,24},{56,16},{64,10... | collective-permute-start | bytes 786440 | tf_op jit(solution)/shard_map/ppermute | solution.py:240
  71.8 11.3 %collective-permute-start.2 = (bf16[8,2,64,128]{3,2,1,0:T(8,128)(2,1)S(1)}, bf16[8,2,64,128]{3,2,1,0:T(8,128)(2,1)S(1)}, u32[]{:S(2)}, u32[]{:S(2)}) collective-permute-start(bf16[8,2,64,128]{3,2,1,0:T(8,128)(2,1)S(1)} %get-tuple-element.19), channel_id=1, source_target_pairs={{0,8},{8,0},{16,24},{24,16},{32,40},{40,32},{48,56},{56,48},{64,72... | collective-permute-start | bytes 786440 | tf_op jit(solution)/shard_map/ppermute | solution.py:243
  73.8 10.3 %collective-permute-start.4 = (bf16[8,2,64,128]{3,2,1,0:T(8,128)(2,1)S(1)}, bf16[8,2,64,128]{3,2,1,0:T(8,128)(2,1)S(1)}, u32[]{:S(2)}, u32[]{:S(2)}) collective-permute-start(bf16[8,2,64,128]{3,2,1,0:T(8,128)(2,1)S(1)} %get-tuple-element.23), channel_id=1, source_target_pairs={{0,56},{8,16},{16,8},{24,32},{32,24},{40,48},{48,40},{56,0},{64,12... | collective-permute-start | bytes 786440 | tf_op jit(solution)/shard_map/ppermute | solution.py:241
  79.7 9.5 %collective-permute-start.3 = (bf16[8,2,64,128]{3,2,1,0:T(8,128)(2,1)S(1)}, bf16[8,2,64,128]{3,2,1,0:T(8,128)(2,1)S(1)}, u32[]{:S(2)}, u32[]{:S(2)}) collective-permute-start(bf16[8,2,64,128]{3,2,1,0:T(8,128)(2,1)S(1)} %get-tuple-element.24), channel_id=1, source_target_pairs={{0,16},{8,56},{16,32},{24,8},{32,48},{40,24},{48,0},{56,40},{64,80... | collective-permute-start | bytes 786440 | tf_op jit(solution)/shard_map/ppermute | solution.py:242
  99.6 16.4 %collective-permute-start.7 = (bf16[2,512,128]{2,1,0:T(8,128)(2,1)S(1)}, bf16[2,512,128]{2,1,0:T(8,128)(2,1)S(1)}, u32[]{:S(2)}, u32[]{:S(2)}) collective-permute-start(bf16[2,512,128]{2,1,0:T(8,128)(2,1)S(1)} %get-tuple-element.14), channel_id=1, source_target_pairs={{16,0},{56,8},{32,16},{8,24},{48,32},{24,40},{0,48},{40,56},{80,64... | collective-permute-start | bytes 786440 | tf_op jit(solution)/shard_map/ppermute | solution.py:260
  101.5 14.5 %collective-permute-start.8 = (bf16[2,512,128]{2,1,0:T(8,128)(2,1)S(1)}, bf16[2,512,128]{2,1,0:T(8,128)(2,1)S(1)}, u32[]{:S(2)}, u32[]{:S(2)}) collective-permute-start(bf16[2,512,128]{2,1,0:T(8,128)(2,1)S(1)} %get-tuple-element.15), channel_id=1, source_target_pairs={{0,8},{8,0},{16,24},{24,16},{32,40},{40,32},{48,56},{56,48},{64,72... | collective-permute-start | bytes 786440 | tf_op jit(solution)/shard_map/ppermute | solution.py:261
  111.6 14.5 %collective-permute-start.9 = (bf16[2,512,128]{2,1,0:T(8,128)(2,1)S(1)}, bf16[2,512,128]{2,1,0:T(8,128)(2,1)S(1)}, u32[]{:S(2)}, u32[]{:S(2)}) collective-permute-start(bf16[2,512,128]{2,1,0:T(8,128)(2,1)S(1)} %get-tuple-element.16), channel_id=1, source_target_pairs={{56,0},{16,8},{8,16},{32,24},{24,32},{48,40},{40,48},{0,56},{120,6... | collective-permute-start | bytes 786440 | tf_op jit(solution)/shard_map/ppermute | solution.py:259
  113.5 12.6 %collective-permute-start.10 = (bf16[2,512,128]{2,1,0:T(8,128)(2,1)S(1)}, bf16[2,512,128]{2,1,0:T(8,128)(2,1)S(1)}, u32[]{:S(2)}, u32[]{:S(2)}) collective-permute-start(bf16[2,512,128]{2,1,0:T(8,128)(2,1)S(1)} %get-tuple-element.17), channel_id=1, source_target_pairs={{40,0},{32,8},{56,16},{48,24},{8,32},{0,40},{24,48},{16,56},{104,6... | collective-permute-start | bytes 786440 | tf_op jit(solution)/shard_map/ppermute | solution.py:258
  127.4 43.7 %all-to-all-start.1 = ((bf16[8,3,2,64,128]{4,3,2,1,0:T(8,128)(2,1)}), bf16[8,3,2,64,128]{4,3,2,1,0:T(8,128)(2,1)S(1)}, u32[]{:S(2)}, u32[]{:S(2)}) async-start(bf16[8,3,2,64,128]{4,3,2,1,0:T(8,128)(2,1)} %copy_bitcast_fusion), calls=%async_computation.1 | async-start | bytes 1572864 | tf_op jit(solution)/shard_map/all_to_all | solution.py:273
  131.7 3.4 %collective-permute-start.6 = (bf16[2,512,128]{2,1,0:T(8,128)(2,1)S(1)}, bf16[2,512,128]{2,1,0:T(8,128)(2,1)S(1)}, u32[]{:S(2)}, u32[]{:S(2)}) collective-permute-start(bf16[2,512,128]{2,1,0:T(8,128)(2,1)S(1)} %get-tuple-element.12), channel_id=1, source_target_pairs={{0,8},{8,0},{16,24},{24,16},{32,40},{40,32},{48,56},{56,48},{64,72... | collective-permute-start | bytes 786440 | tf_op jit(solution)/shard_map/ppermute | solution.py:262
  171.3 15.4 %collective-permute-start.11 = (bf16[2,64,128]{2,1,0:T(8,128)(2,1)S(1)}, bf16[2,64,128]{2,1,0:T(8,128)(2,1)S(1)}, u32[]{:S(2)}, u32[]{:S(2)}) collective-permute-start(bf16[2,64,128]{2,1,0:T(8,128)(2,1)S(1)} %fusion.16), channel_id=1, source_target_pairs={{120,56},{112,48},{104,40},{184,120},{0,64},{176,112},{8,72},{168,... | collective-permute-start | bytes 98312 | tf_op jit(solution)/shard_map/ppermute | solution.py:275

commit v2 on v1

v2 whole, which is shorter than its diff:
```python
import math

import jax
import jax.numpy as jnp
from jax import lax
from jax.experimental import pallas as pl
from jax.experimental.pallas import tpu as pltpu
from jax.sharding import Mesh
from jax.sharding import PartitionSpec as P

REACH = 3
GROUP = 8
NEG_FILL = -1e30
CTX = ("pair", "core")


def within(ctx, moves):
    return [(base + a, base + b) for base in range(0, ctx, GROUP) for a, b in moves]


def swap_pairs(ctx):
    return within(ctx, [(r, r ^ 1) for r in range(GROUP)])


def near_pairs(ctx):
    forth = [(r, r + 2) for r in range(0, GROUP - 2, 2)]
    return within(ctx, forth + [(r, r - 2) for r in range(3, GROUP, 2)])


def next_pairs(ctx):
    forth = [(r, r + 4) for r in range(0, GROUP - 4, 2)]
    return within(ctx, forth + [(r, r - 4) for r in range(5, GROUP, 2)])


def edge_pairs(ctx, heads):
    moves = []
    for base in range(0, ctx, GROUP):
        for k in range(REACH):
            top = base + GROUP - 1 - k
            if base + GROUP < ctx:
                moves.append((top, base + GROUP + REACH - 1 - k))
            else:
                moves.append((top, base + GROUP - REACH + k))
            if base > 0:
                moves.append((base + k, base - REACH + k))
    return [
        (a * heads + h, b * heads + heads - 1 - h) for a, b in moves for h in range(heads)
    ]


def inverse(pairs):
    return [(b, a) for a, b in pairs]


def attention_kernel(
    lo_ref, place_ref, start_row, q_own, g_own, qg_far, kv_own, kv_near, kv_next, kv_edge,
    kv_edge1, kv_edge2, out_own, out_far, p_own, p_near, p_next,
    keys, values, keys_t, values_t, scores, key_acc, value_acc, sems,
):
    tile = scores.shape[1]
    width = q_own.shape[1]
    shard = kv_own.shape[3]
    head_dim = q_own.shape[2]
    per_span = width // tile
    shards = kv_own.shape[1]
    scale = head_dim ** -0.5
    core = place_ref[0]
    f32, bf16 = jnp.float32, jnp.bfloat16

    def copies(slot, source):
        return [
            pltpu.make_async_copy(
                source.at[:, which], target.at[pl.ds(slot * shards, shards)], sems.at[slot, which]
            )
            for which, target in enumerate((keys, values))
        ]

    def fetch(slot, source):
        for copy in copies(slot, source):
            copy.start()

    fetch(3, kv_own.at[core])
    fetch(4, kv_own.at[1 - core])

    @pl.when(place_ref[1] == 1)
    def _():
        fetch(0, kv_edge)

    @pl.when(place_ref[1] == 0)
    def _():
        fetch(0, kv_next)

    @pl.when(place_ref[2] == 1)
    def _():
        fetch(1, kv_edge2)
        fetch(2, kv_edge1)

    @pl.when(place_ref[2] == 0)
    def _():
        fetch(1, kv_near.at[core])
        fetch(2, kv_near.at[1 - core])

    key_acc[...] = jnp.zeros_like(key_acc)
    value_acc[...] = jnp.zeros_like(value_acc)
    for slot in range(REACH + 2):
        for copy in copies(slot, kv_edge):
            copy.wait()

    tile_shards = tile // shard

    def tile_of(ref, j):
        return ref[pl.ds(j * tile_shards, tile_shards)].reshape(tile, head_dim)

    key_tiles = keys.shape[0] // tile_shards
    for j in range(key_tiles):
        keys_t[j] = tile_of(keys, j).T
        values_t[j] = tile_of(values, j).T

    nt = (((1,), (1,)), ((), ()))
    nn = (((1,), (0,)), ((), ()))
    for i in range(2 * per_span):
        span, part = divmod(i, per_span)
        rows = pl.ds(part * tile, tile)
        if span == 0:
            query = q_own[core, rows]
            grad = g_own[core, rows]
        else:
            query = qg_far[0, rows]
            grad = qg_far[1, rows]
        diagonal = REACH * per_span + i
        lo = lo_ref[i]
        start = start_row[:, pl.ds(i * tile, tile)]

        def score_tile(j, causal):
            raw = lax.dot_general(
                tile_of(keys, j), query, nt, preferred_element_type=f32
            ) * (scale * math.log2(math.e))
            at_key = lax.broadcasted_iota(jnp.int32, (tile, tile), 0)
            allowed = at_key >= start - j * tile
            if causal:
                at_query = lax.broadcasted_iota(jnp.int32, (tile, tile), 1)
                allowed = allowed & (at_key <= at_query)
            raw = jnp.where(allowed, raw, NEG_FILL)
            scores[j] = raw
            return jnp.max(raw, axis=0, keepdims=True)

        top = score_tile(diagonal, True)
        top = lax.fori_loop(
            lo, diagonal, lambda j, m: jnp.maximum(m, score_tile(j, False)), top
        )

        def forward(j, carry):
            total, acc = carry
            prob = jnp.exp2(scores[j] - top)
            scores[j] = prob
            total = total + jnp.sum(prob, axis=0, keepdims=True)
            acc = acc + lax.dot_general(
                values_t[j], prob.astype(bf16), nn, preferred_element_type=f32
            )
            return total, acc

        total, acc = lax.fori_loop(
            lo,
            diagonal + 1,
            forward,
            (jnp.zeros((1, tile), f32), jnp.zeros((head_dim, tile), f32)),
        )
        inv = 1.0 / total
        attended_t = (acc * inv).astype(bf16).astype(f32)
        attended = attended_t.T.astype(bf16)
        delta = jnp.sum(grad.astype(f32).T * attended_t, axis=0, keepdims=True)

        def backward(j, acc):
            prob = scores[j] * inv
            here = pl.ds(pl.multiple_of(j * tile, tile), tile)
            value_acc[here] += lax.dot_general(
                prob.astype(bf16), grad, nn, preferred_element_type=f32
            )
            dot_grad = lax.dot_general(tile_of(values, j), grad, nt, preferred_element_type=f32)
            score_grad = (prob * (dot_grad - delta)).astype(bf16)
            key_acc[here] += lax.dot_general(score_grad, query, nn, preferred_element_type=f32)
            return acc + lax.dot_general(keys_t[j], score_grad, nn, preferred_element_type=f32)

        acc = lax.fori_loop(lo, diagonal + 1, backward, jnp.zeros((head_dim, tile), f32))
        query_grad = (acc.T * scale).astype(bf16)
        target = out_own if span == 0 else out_far
        target[0, rows] = attended
        target[1, rows] = query_grad

    targets = (p_next, p_near.at[0], p_near.at[1], p_own.at[0], p_own.at[1])
    for slot, target in enumerate(targets):
        here = pl.ds(slot * width, width)
        target[0] = (key_acc[here] * scale).astype(target.dtype)
        target[1] = value_acc[here].astype(target.dtype)


def attention(lo, place, start, queries, out_grad, far, kv_own, *kv_others):
    width, head_dim = queries.shape[1:]
    _, shards, _, shard, _ = kv_own.shape
    tile = max(min(256, width // 2), shard)
    window = (REACH + 2) * width
    part = (2, width, head_dim)
    vmem = pl.BlockSpec(memory_space=pltpu.VMEM)
    smem = pl.BlockSpec(memory_space=pltpu.SMEM)
    hbm = pl.BlockSpec(memory_space=pl.ANY)
    return pl.pallas_call(
        attention_kernel,
        out_shape=(
            jax.ShapeDtypeStruct(part, jnp.bfloat16),
            jax.ShapeDtypeStruct(part, jnp.bfloat16),
            jax.ShapeDtypeStruct((2,) + part, jnp.float32),
            jax.ShapeDtypeStruct((2,) + part, jnp.bfloat16),
            jax.ShapeDtypeStruct(part, jnp.bfloat16),
        ),
        in_specs=[smem, smem] + [vmem] * 4 + [hbm] * 6,
        out_specs=[vmem] * 5,
        scratch_shapes=[
            pltpu.VMEM(((REACH + 2) * shards, shard, head_dim), jnp.bfloat16),
            pltpu.VMEM(((REACH + 2) * shards, shard, head_dim), jnp.bfloat16),
            pltpu.VMEM((window // tile, head_dim, tile), jnp.bfloat16),
            pltpu.VMEM((window // tile, head_dim, tile), jnp.bfloat16),
            pltpu.VMEM((window // tile, tile, tile), jnp.float32),
            pltpu.VMEM((window, head_dim), jnp.float32),
            pltpu.VMEM((window, head_dim), jnp.float32),
            pltpu.SemaphoreType.DMA((REACH + 2, 2)),
        ],
        compiler_params=pltpu.CompilerParams(vmem_limit_bytes=40 * 1024 * 1024),
        cost_estimate=pl.CostEstimate(
            flops=6 * 2 * 8 * width * width * head_dim,
            bytes_accessed=8 * 1024 * 1024,
            transcendentals=8 * width * width,
        ),
        name="attention",
    )(lo, place, start[None, :], queries, out_grad, far, kv_own, *kv_others)


def body(queries, key_states, value_states, out_grad, segments):
    ctx = lax.axis_size("pair") * 2
    core = lax.axis_index("core")
    position = lax.axis_index("pair") * 2 + core
    place = position % GROUP
    width = queries.shape[2]
    heads = lax.axis_size("head")
    shard = key_states.shape[2]
    head_dim = key_states.shape[3]
    bf16, f32 = jnp.bfloat16, jnp.float32

    swap, near, far_chip = swap_pairs(ctx), near_pairs(ctx), next_pairs(ctx)
    edge1 = within(ctx, [(2, 0), (GROUP - 3, GROUP - 1)])
    edge2 = within(ctx, [(1, 0), (GROUP - 2, GROUP - 1)])
    edge = edge_pairs(ctx, heads)
    even = core == 0
    sends_lower = place >= GROUP - REACH

    own = jnp.stack([key_states[0], value_states[0]], axis=1)
    crossed = lax.ppermute(jnp.where(sends_lower, own[0], own[1]), CTX + ("head",), edge)

    spread = jnp.broadcast_to(own[:, None], (2, heads) + own.shape[1:])
    kv_own = lax.all_to_all(
        spread.reshape((2 * heads,) + own.shape[1:]), ("core", "head"), 0, 0, tiled=True
    ).reshape(spread.shape)
    crossed, kv_own = lax.optimization_barrier((crossed, kv_own))
    kv_edge = lax.all_to_all(
        jnp.broadcast_to(crossed[None], (heads,) + crossed.shape), "head", 0, 0, tiled=True
    )[::-1]

    queries, out_grad = queries[0], out_grad[0]
    far = lax.ppermute(
        jnp.where(
            even,
            jnp.stack([queries[1], out_grad[1]]),
            jnp.stack([queries[0], out_grad[0]]),
        ),
        CTX,
        swap,
    )

    kv_next = lax.ppermute(jnp.where(even, kv_own[1], kv_own[0]), CTX, far_chip)
    kv_near = lax.ppermute(kv_own, CTX, near)
    kv_edge1 = lax.ppermute(kv_edge, CTX, edge1)
    kv_edge2 = lax.ppermute(kv_edge, CTX, edge2)

    first = jnp.where(even, position, 2 * ctx - 1 - position)
    window = (REACH + 2) * width
    padded = jnp.concatenate([jnp.full((REACH * width,), -1, jnp.int32), segments])
    seg_window = lax.dynamic_slice_in_dim(padded, first * width, window)
    start = jnp.sum(
        seg_window[:, None] < seg_window[None, REACH * width :], axis=0, dtype=jnp.int32
    )
    tile = max(min(256, width // 2), shard)
    lo = start[::tile] // tile
    edge_next = jnp.where(even, place <= 2, place >= GROUP - 3)
    edge_near = jnp.where(even, place == 0, place == GROUP - 1)
    places = jnp.stack([core, edge_next, edge_near]).astype(jnp.int32)

    out_own, out_far, p_own, p_near, p_next = attention(
        lo, places, start, queries, out_grad, far,
        kv_own, kv_near, kv_next, kv_edge, kv_edge1, kv_edge2,
    )

    r_edge1 = lax.ppermute(p_near[1], CTX, inverse(edge1)).astype(f32)
    r_edge2 = lax.ppermute(p_near[0], CTX, inverse(edge2)).astype(f32)
    r_next = lax.ppermute(p_next, CTX, inverse(far_chip)).astype(f32)
    r_near = lax.ppermute(p_near, CTX, inverse(near)).astype(f32)

    edge_sum = jnp.where(edge_next, p_next.astype(f32), 0.0) + r_edge1 + r_edge2
    edge_sum = edge_sum.astype(bf16).reshape(2, heads, shard, head_dim)
    edge_heads = lax.all_to_all(
        edge_sum.transpose(1, 0, 2, 3)[::-1], "head", 0, 0, tiled=True
    )
    edge_total = jnp.sum(edge_heads.astype(f32), axis=0).astype(bf16)
    returned = lax.ppermute(edge_total, CTX + ("head",), inverse(edge)).astype(f32)

    sums = p_own + r_near
    sums = jnp.stack([sums[0], sums[1] + r_next])
    sums = jnp.where(even, sums, sums[::-1]).astype(bf16)
    sums = sums.reshape(2, 2, heads, shard, head_dim).transpose(0, 2, 1, 3, 4)
    by_head = lax.all_to_all(
        sums.reshape((2 * heads,) + own.shape[1:]), ("core", "head"), 0, 0, tiled=True
    ).reshape(spread.shape)
    total = jnp.sum(by_head.astype(f32), axis=1)
    lower = total[0] + jnp.where(sends_lower, returned, 0.0)
    upper = total[1] + jnp.where(sends_lower, 0.0, returned)
    grads = jnp.stack([lower, upper]).astype(bf16)

    back = lax.ppermute(out_far, CTX, swap)
    results = []
    for k in range(2):
        results.append(
            jnp.where(
                even, jnp.stack([out_own[k], back[k]]), jnp.stack([back[k], out_own[k]])
            )[None]
        )
    return results[0], results[1], grads[:, 0][None], grads[:, 1][None]


def solution(mesh):
    ctx, heads = mesh.devices.shape
    mesh = Mesh(mesh.devices.reshape(ctx // 2, 2, heads), CTX + ("head",))
    by_head = P(CTX, None, None, "head")
    by_row = P(CTX, None, "head", None)
    return jax.shard_map(
        body,
        mesh=mesh,
        in_specs=(by_head, by_row, by_row, by_head, P()),
        out_specs=(by_head, by_head, by_row, by_row),
        check_vma=False,
    )
```

time: 188 us -> 165 us (0.88)
  waiting for transfers between devices: 102 us -> 60.6 us
  local copies, waits for them, and re-layouts: 1.75 us -> 12.1 us
  starting transfers between devices: 67.8 us -> 71.6 us
  Pallas kernels: 10.4 us -> 12.7 us
    all_to_all x2 -> x4, waiting for transfers between devices: 73.2 us -> 42.8 us  [the longest x1 17.1 us: body(): lax.all_to_all(sums.reshape((2 * heads,) + own.shape[1:]), ('core', 'head...]
    all_to_all x2 -> x4, starting transfers between devices: 13.7 us -> 31.4 us  [the longest x1 12.8 us: body(): lax.all_to_all(spread.reshape((2 * heads,) + own.shape[1:]), ('core', 'he...]
    ppermute x11, starting transfers between devices: 52.2 us -> 37.1 us  [the longest x1 11.3 us: body(): lax.ppermute(jnp.where(sends_lower, own[0], own[1]), CTX + ('head',), edge)]
    ppermute x11, waiting for transfers between devices: 28.3 us -> 17.8 us  [the longest x1 8.32 us: body(): r_next = lax.ppermute(p_next, CTX, inverse(far_chip)).astype(f32)]
    unnamed x6 -> x34, local copies, waits for them, and re-layouts: 0.02 us -> 8.46 us
    pallas_call x1, Pallas kernels: 10.4 us -> 12.7 us  [attention(): pl.pallas_call(attention_kernel, out_shape=(jax.ShapeDtypeStruct(part, jn...]
  transfers between devices with their start and end apart: 14 -> 16, of which waited for: 8 -> 9; matrix products, arithmetic and copies ran while one was open for 1% -> 3% of each run, Pallas kernels for 0% -> 0%
where the time goes in v2:
time: 165 us; the launch traced here: 163 us
  starting transfers between devices  71.6 us (43%)
  waiting for transfers between devices  60.6 us (37%)
  Pallas kernels  12.7 us (8%)
  local copies, waits for them, and re-layouts  12.1 us (7%)
  other arithmetic  4.5 us (3%)
    all_to_all x1, waiting for transfers between devices, body(): lax.all_to_all(sums.reshape((2 * heads,) + own.shape[1:]), ('core', 'head...  17.1 us
    all_to_all x1, waiting for transfers between devices, body(): lax.all_to_all(spread.reshape((2 * heads,) + own.shape[1:]), ('core', 'he...  15.4 us
    all_to_all x1, starting transfers between devices, body(): lax.all_to_all(spread.reshape((2 * heads,) + own.shape[1:]), ('core', 'he...  12.8 us
    pallas_call x1, Pallas kernels, attention(): pl.pallas_call(attention_kernel, out_shape=(jax.ShapeDtypeStruct(part, jn...  12.7 us
    ppermute x1, starting transfers between devices, body(): lax.ppermute(jnp.where(sends_lower, own[0], own[1]), CTX + ('head',), edge)  11.3 us
    unnamed x34, local copies, waits for them, and re-layouts  8.46 us
    ppermute x1, waiting for transfers between devices, body(): r_next = lax.ppermute(p_next, CTX, inverse(far_chip)).astype(f32)  8.32 us
    all_to_all x1, starting transfers between devices, body(): lax.all_to_all(edge_sum.transpose(1, 0, 2, 3)[::-1], 'head', 0, 0, tiled=...  7.47 us
  transfers between devices with their start and end apart: 16, of which 9 were waited for; matrix products, arithmetic and copies ran while one was open for 3% of the time, Pallas kernels for 0%

profile of v2, /device:TPU:6, one launch (start us, length us, event | category | flops | bytes accessed | tf_op | source)
XLA Modules:
  0.0 162.6 jit_solution(617081787634309047)
XLA Ops:
  2.4 12.8 %all-to-all-start = ((bf16[16,2,64,128]{3,2,1,0:T(8,128)(2,1)}), bf16[16,2,64,128]{3,2,1,0:T(8,128)(2,1)S(1)}, u32[]{:S(2)}, u32[]{:S(2)}) async-start(bf16[16,2,64,128]{3,2,1,0:T(8,128)(2,1)} %bitcast.13), calls=%async_computation | async-start | bytes 1048576 | tf_op jit(solution)/shard_map/all_to_all | solution.py:259
  15.2 11.3 %collective-permute-start.1 = (bf16[2,64,128]{2,1,0:T(8,128)(2,1)S(1)}, bf16[2,64,128]{2,1,0:T(8,128)(2,1)S(1)}, u32[]{:S(2)}, u32[]{:S(2)}) collective-permute-start(bf16[2,64,128]{2,1,0:T(8,128)(2,1)S(1)} %fusion.13), channel_id=1, source_target_pairs={{56,87},{57,86},{58,85},{59,84},{60,83},{61,82},{62,81},{63,80},{4... | collective-permute-start | bytes 98312 | tf_op jit(solution)/shard_map/ppermute | solution.py:256
  26.6 2.0 %collective-permute-done.1 = bf16[2,64,128]{2,1,0:T(8,128)(2,1)S(1)} collective-permute-done((bf16[2,64,128]{2,1,0:T(8,128)(2,1)S(1)}, bf16[2,64,128]{2,1,0:T(8,128)(2,1)S(1)}, u32[]{:S(2)}, u32[]{:S(2)}) %collective-permute-start.1) | collective-permute-done | bytes 32800 | tf_op jit(solution)/shard_map/ppermute | solution.py:256
  28.6 15.4 %all-to-all-done = bf16[16,2,64,128]{3,2,1,0:T(8,128)(2,1)S(1)} async-done(((bf16[16,2,64,128]{3,2,1,0:T(8,128)(2,1)}), bf16[16,2,64,128]{3,2,1,0:T(8,128)(2,1)S(1)}, u32[]{:S(2)}, u32[]{:S(2)}) %all-to-all-start) | async-done | bytes 524320 | tf_op jit(solution)/shard_map/all_to_all | solution.py:259
  44.8 5.3 %all-to-all-start.1 = ((bf16[8,2,64,128]{3,2,1,0:T(8,128)(2,1)}), bf16[8,2,64,128]{3,2,1,0:T(8,128)(2,1)S(1)}, u32[]{:S(2)}, u32[]{:S(2)}) async-start(bf16[8,2,64,128]{3,2,1,0:T(8,128)(2,1)} %broadcast_in_dim.18), calls=%async_computation.1 | async-start | bytes 524288 | tf_op jit(solution)/shard_map/all_to_all | solution.py:263
  50.1 3.1 %collective-permute-start = (bf16[2,512,128]{2,1,0:T(8,128)(2,1)S(1)}, bf16[2,512,128]{2,1,0:T(8,128)(2,1)S(1)}, u32[]{:S(2)}, u32[]{:S(2)}) collective-permute-start(bf16[2,512,128]{2,1,0:T(8,128)(2,1)S(1)} %maximum_select_fusion), channel_id=1, source_target_pairs={{0,8},{8,0},{16,24},{24,16},{32,40},{40,32},{48,56},{56,48},{64,72... | collective-permute-start | bytes 786440 | tf_op jit(solution)/shard_map/ppermute | solution.py:268
  53.4 1.4 convert_reduce_fusion
  54.9 1.4 collective-permute-start.2
  56.3 3.8 %collective-permute-start.3 = (bf16[8,2,64,128]{3,2,1,0:T(8,128)(2,1)S(1)}, bf16[8,2,64,128]{3,2,1,0:T(8,128)(2,1)S(1)}, u32[]{:S(2)}, u32[]{:S(2)}) collective-permute-start(bf16[8,2,64,128]{3,2,1,0:T(8,128)(2,1)S(1)} %select_bitcast_fusion), channel_id=1, source_target_pairs={{0,32},{16,48},{40,8},{56,24},{64,96},{80,112},{104,72},{120,88},{... | collective-permute-start | bytes 786440 | tf_op jit(solution)/shard_map/ppermute | solution.py:278
  60.2 6.2 %all-to-all-done.1 = bf16[8,2,64,128]{3,2,1,0:T(8,128)(2,1)S(1)} async-done(((bf16[8,2,64,128]{3,2,1,0:T(8,128)(2,1)}), bf16[8,2,64,128]{3,2,1,0:T(8,128)(2,1)S(1)}, u32[]{:S(2)}, u32[]{:S(2)}) %all-to-all-start.1) | async-done | bytes 262176 | tf_op jit(solution)/shard_map/all_to_all | solution.py:263
  66.4 1.3 collective-permute-start.5
  67.7 1.3 collective-permute-start.4
  72.1 3.9 %collective-permute-done.4.kv_edge1 = bf16[8,2,64,128]{3,2,1,0:T(8,128)(2,1)S(1)} collective-permute-done((bf16[8,2,64,128]{3,2,1,0:T(8,128)(2,1)S(1)}, bf16[8,2,64,128]{3,2,1,0:T(8,128)(2,1)S(1)}, u32[]{:S(2)}, u32[]{:S(2)}) %collective-permute-start.4) | collective-permute-done | bytes 262176 | tf_op jit(solution)/shard_map/ppermute | solution.py:280
  76.6 1.0 copy-done.3
  77.7 0.9 copy-done.5
  78.6 0.9 copy-done.9
  79.6 0.9 copy-done.11
  80.5 0.9 copy-done.13
  81.5 12.7 %attention.1 = (bf16[2,512,128]{2,1,0:T(8,128)(2,1)S(1)}, bf16[2,512,128]{2,1,0:T(8,128)(2,1)S(1)}, f32[2,2,512,128]{3,2,1,0:T(8,128)S(1)}, bf16[2,2,512,128]{3,2,1,0:T(8,128)(2,1)S(1)}, bf16[2,512,128]{2,1,0:T(8,128)(2,1)S(1)}) custom-call(s32[4]{0:T(128)S(1)} %and_select_fusion.lo_ref, s32[3]{0:T(128)S(1)} %pad_add_fusion.place_ref, ...), custom_call_target="tpu_custom_call" | custom-call | flops 3221225472 | bytes 8388608 | tf_op jit(solution)/shard_map/attention/pallas_call | solution.py:206
  94.2 1.3 collective-permute-start.7
  95.5 4.6 %collective-permute-start.9 = (bf16[2,512,128]{2,1,0:T(8,128)(2,1)S(1)}, bf16[2,512,128]{2,1,0:T(8,128)(2,1)S(1)}, u32[]{:S(2)}, u32[]{:S(2)}) collective-permute-start(bf16[2,512,128]{2,1,0:T(8,128)(2,1)S(1)} %get-tuple-element.18), channel_id=1, source_target_pairs={{0,16},{56,40},{64,80},{120,104},{128,144},{184,168},{192,208},{24... | collective-permute-start | bytes 786440 | tf_op jit(solution)/shard_map/ppermute | solution.py:301
  100.1 1.3 collective-permute-start.10
  101.4 2.5 %collective-permute-done.9 = bf16[2,512,128]{2,1,0:T(8,128)(2,1)S(1)} collective-permute-done((bf16[2,512,128]{2,1,0:T(8,128)(2,1)S(1)}, bf16[2,512,128]{2,1,0:T(8,128)(2,1)S(1)}, u32[]{:S(2)}, u32[]{:S(2)}) %collective-permute-start.9) | collective-permute-done | bytes 262176 | tf_op jit(solution)/shard_map/ppermute | solution.py:301
  104.9 7.5 %all-to-all-start.3 = ((bf16[8,2,64,128]{3,2,1,0:T(8,128)(2,1)}), bf16[8,2,64,128]{3,2,1,0:T(8,128)(2,1)S(1)}, u32[]{:S(2)}, u32[]{:S(2)}) async-start(bf16[8,2,64,128]{3,2,1,0:T(8,128)(2,1)} %rev.11), calls=%async_computation.3 | async-start | bytes 524288 | tf_op jit(solution)/shard_map/all_to_all | solution.py:308
  112.3 1.3 collective-permute-start.8
  113.8 8.3 %collective-permute-done.8 = bf16[2,512,128]{2,1,0:T(8,128)(2,1)S(1)} collective-permute-done((bf16[2,512,128]{2,1,0:T(8,128)(2,1)S(1)}, bf16[2,512,128]{2,1,0:T(8,128)(2,1)S(1)}, u32[]{:S(2)}, u32[]{:S(2)}) %collective-permute-start.8) | collective-permute-done | bytes 262176 | tf_op jit(solution)/shard_map/ppermute | solution.py:303
  123.2 4.1 %all-to-all-done.3 = bf16[8,2,64,128]{3,2,1,0:T(8,128)(2,1)S(1)} async-done(((bf16[8,2,64,128]{3,2,1,0:T(8,128)(2,1)}), bf16[8,2,64,128]{3,2,1,0:T(8,128)(2,1)S(1)}, u32[]{:S(2)}, u32[]{:S(2)}) %all-to-all-start.3) | async-done | bytes 262176 | tf_op jit(solution)/shard_map/all_to_all | solution.py:308
  127.3 5.9 %all-to-all-start.2 = ((bf16[16,2,64,128]{3,2,1,0:T(8,128)(2,1)}), bf16[16,2,64,128]{3,2,1,0:T(8,128)(2,1)S(1)}, u32[]{:S(2)}, u32[]{:S(2)}) async-start(bf16[16,2,64,128]{3,2,1,0:T(8,128)(2,1)} %bitcast.24), calls=%async_computation.2 | async-start | bytes 1048576 | tf_op jit(solution)/shard_map/all_to_all | solution.py:318
  133.2 2.3 %collective-permute-start.6 = (bf16[2,512,128]{2,1,0:T(8,128)(2,1)S(1)}, bf16[2,512,128]{2,1,0:T(8,128)(2,1)S(1)}, u32[]{:S(2)}, u32[]{:S(2)}) collective-permute-start(bf16[2,512,128]{2,1,0:T(8,128)(2,1)S(1)} %copy-done.7), channel_id=1, source_target_pairs={{0,8},{8,0},{16,24},{24,16},{32,40},{40,32},{48,56},{56,48},{64,72... | collective-permute-start | bytes 786440 | tf_op jit(solution)/shard_map/ppermute | solution.py:326
  135.6 1.1 collective-permute-done.6
  137.6 7.2 %collective-permute-start.11 = (bf16[2,64,128]{2,1,0:T(8,128)(2,1)S(1)}, bf16[2,64,128]{2,1,0:T(8,128)(2,1)S(1)}, u32[]{:S(2)}, u32[]{:S(2)}) collective-permute-start(bf16[2,64,128]{2,1,0:T(8,128)(2,1)S(1)} %reduce_sum.32), channel_id=1, source_target_pairs={{87,56},{86,57},{85,58},{84,59},{83,60},{82,61},{81,62},{80,63},{7... | collective-permute-start | bytes 98312 | tf_op jit(solution)/shard_map/ppermute | solution.py:312
  144.8 17.1 %all-to-all-done.2 = bf16[16,2,64,128]{3,2,1,0:T(8,128)(2,1)S(1)} async-done(((bf16[16,2,64,128]{3,2,1,0:T(8,128)(2,1)}), bf16[16,2,64,128]{3,2,1,0:T(8,128)(2,1)S(1)}, u32[]{:S(2)}, u32[]{:S(2)}) %all-to-all-start.2) | async-done | bytes 524320 | tf_op jit(solution)/shard_map/all_to_all | solution.py:318
  (68 shorter events, 10.4 us)
Async XLA Ops:
  0.6 14.6 %copy-start.15 = (bf16[1,2,64,128]{3,2,1,0:T(8,128)(2,1)S(1)}, bf16[1,2,64,128]{3,2,1,0:T(8,128)(2,1)}, u32[]{:S(2)}) copy-start(bf16[1,2,64,128]{3,2,1,0:T(8,128)(2,1)} %param.7) | copy-start | bytes 98308
  0.6 14.6 %copy-start.16 = (bf16[1,2,64,128]{3,2,1,0:T(8,128)(2,1)S(1)}, bf16[1,2,64,128]{3,2,1,0:T(8,128)(2,1)}, u32[]{:S(2)}) copy-start(bf16[1,2,64,128]{3,2,1,0:T(8,128)(2,1)} %param.6) | copy-start | bytes 98308
  0.7 25.9 %copy-start = (bf16[1,2,512,128]{3,2,1,0:T(8,128)(2,1)S(1)}, bf16[1,2,512,128]{3,2,1,0:T(8,128)(2,1)}, u32[]{:S(2)}) copy-start(bf16[1,2,512,128]{3,2,1,0:T(8,128)(2,1)} %param.5) | copy-start | bytes 786436
  2.4 47.6 %copy-start.1 = (bf16[1,2,512,128]{3,2,1,0:T(8,128)(2,1)S(1)}, bf16[1,2,512,128]{3,2,1,0:T(8,128)(2,1)}, u32[]{:S(2)}) copy-start(bf16[1,2,512,128]{3,2,1,0:T(8,128)(2,1)} %param.8) | copy-start | bytes 786436
  2.4 41.6 %all-to-all-start = ((bf16[16,2,64,128]{3,2,1,0:T(8,128)(2,1)}), bf16[16,2,64,128]{3,2,1,0:T(8,128)(2,1)S(1)}, u32[]{:S(2)}, u32[]{:S(2)}) async-start(bf16[16,2,64,128]{3,2,1,0:T(8,128)(2,1)} %bitcast.13), calls=%async_computation | async-start | bytes 1048576 | tf_op jit(solution)/shard_map/all_to_all | solution.py:259
  15.2 13.3 %collective-permute-start.1 = (bf16[2,64,128]{2,1,0:T(8,128)(2,1)S(1)}, bf16[2,64,128]{2,1,0:T(8,128)(2,1)S(1)}, u32[]{:S(2)}, u32[]{:S(2)}) collective-permute-start(bf16[2,64,128]{2,1,0:T(8,128)(2,1)S(1)} %fusion.13), channel_id=1, source_target_pairs={{56,87},{57,86},{58,85},{59,84},{60,83},{61,82},{62,81},{63,80},{4... | collective-permute-start | bytes 98312 | tf_op jit(solution)/shard_map/ppermute | solution.py:256
  44.0 9.3 %copy-start.14 = (s32[65536]{0:T(1024)S(1)}, s32[65536]{0:T(1024)}, u32[]{:S(2)}) copy-start(s32[65536]{0:T(1024)} %param.9) | copy-start | bytes 786436
  44.8 21.6 %all-to-all-start.1 = ((bf16[8,2,64,128]{3,2,1,0:T(8,128)(2,1)}), bf16[8,2,64,128]{3,2,1,0:T(8,128)(2,1)S(1)}, u32[]{:S(2)}, u32[]{:S(2)}) async-start(bf16[8,2,64,128]{3,2,1,0:T(8,128)(2,1)} %broadcast_in_dim.18), calls=%async_computation.1 | async-start | bytes 524288 | tf_op jit(solution)/shard_map/all_to_all | solution.py:263
  50.1 19.1 %collective-permute-start = (bf16[2,512,128]{2,1,0:T(8,128)(2,1)S(1)}, bf16[2,512,128]{2,1,0:T(8,128)(2,1)S(1)}, u32[]{:S(2)}, u32[]{:S(2)}) collective-permute-start(bf16[2,512,128]{2,1,0:T(8,128)(2,1)S(1)} %maximum_select_fusion), channel_id=1, source_target_pairs={{0,8},{8,0},{16,24},{24,16},{32,40},{40,32},{48,56},{56,48},{64,72... | collective-permute-start | bytes 786440 | tf_op jit(solution)/shard_map/ppermute | solution.py:268
  54.9 15.7 %collective-permute-start.2 = (bf16[2,8,2,64,128]{4,3,2,1,0:T(8,128)(2,1)S(1)}, bf16[2,8,2,64,128]{4,3,2,1,0:T(8,128)(2,1)S(1)}, u32[]{:S(2)}, u32[]{:S(2)}) collective-permute-start(bf16[2,8,2,64,128]{4,3,2,1,0:T(8,128)(2,1)S(1)} %bitcast.75), channel_id=1, source_target_pairs={{0,16},{16,32},{32,48},{24,8},{40,24},{56,40},{64,80},{80,96},{96,... | collective-permute-start | bytes 1572872 | tf_op jit(solution)/shard_map/ppermute | solution.py:279
  56.3 13.5 %collective-permute-start.3 = (bf16[8,2,64,128]{3,2,1,0:T(8,128)(2,1)S(1)}, bf16[8,2,64,128]{3,2,1,0:T(8,128)(2,1)S(1)}, u32[]{:S(2)}, u32[]{:S(2)}) collective-permute-start(bf16[8,2,64,128]{3,2,1,0:T(8,128)(2,1)S(1)} %select_bitcast_fusion), channel_id=1, source_target_pairs={{0,32},{16,48},{40,8},{56,24},{64,96},{80,112},{104,72},{120,88},{... | collective-permute-start | bytes 786440 | tf_op jit(solution)/shard_map/ppermute | solution.py:278
  66.4 5.0 %collective-permute-start.5 = (bf16[8,2,64,128]{3,2,1,0:T(8,128)(2,1)S(1)}, bf16[8,2,64,128]{3,2,1,0:T(8,128)(2,1)S(1)}, u32[]{:S(2)}, u32[]{:S(2)}) collective-permute-start(bf16[8,2,64,128]{3,2,1,0:T(8,128)(2,1)S(1)} %rev.9.kv_edge), channel_id=1, source_target_pairs={{8,0},{48,56},{72,64},{112,120},{136,128},{176,184},{200,192},{240... | collective-permute-start | bytes 786440 | tf_op jit(solution)/shard_map/ppermute | solution.py:281
  67.7 8.3 %collective-permute-start.4 = (bf16[8,2,64,128]{3,2,1,0:T(8,128)(2,1)S(1)}, bf16[8,2,64,128]{3,2,1,0:T(8,128)(2,1)S(1)}, u32[]{:S(2)}, u32[]{:S(2)}) collective-permute-start(bf16[8,2,64,128]{3,2,1,0:T(8,128)(2,1)S(1)} %rev.9.kv_edge), channel_id=1, source_target_pairs={{16,0},{40,56},{80,64},{104,120},{144,128},{168,184},{208,192},{23... | collective-permute-start | bytes 786440 | tf_op jit(solution)/shard_map/ppermute | solution.py:280
  69.2 0.7 copy-start.4
  69.9 0.7 copy-start.8
  70.6 0.8 copy-start.2
  71.4 0.7 copy-start.10
  76.6 1.0 copy-start.3
  77.7 0.9 copy-start.5
  78.6 0.9 copy-start.9
  79.6 0.9 copy-start.11
  80.5 0.9 copy-start.13
  94.2 9.9 %copy-start.6 = (bf16[2,512,128]{2,1,0:T(8,128)(2,1)}, bf16[2,512,128]{2,1,0:T(8,128)(2,1)S(1)}, u32[]{:S(2)}) copy-start(bf16[2,512,128]{2,1,0:T(8,128)(2,1)S(1)} %get-tuple-element.14) | copy-start | bytes 786436
  94.2 19.4 %collective-permute-start.7 = (bf16[2,2,512,128]{3,2,1,0:T(8,128)(2,1)S(1)}, bf16[2,2,512,128]{3,2,1,0:T(8,128)(2,1)S(1)}, u32[]{:S(2)}, u32[]{:S(2)}) collective-permute-start(bf16[2,2,512,128]{3,2,1,0:T(8,128)(2,1)S(1)} %get-tuple-element.16), channel_id=1, source_target_pairs={{16,0},{32,16},{48,32},{8,24},{24,40},{40,56},{80,64},{96,80},{112... | collective-permute-start | bytes 1572872 | tf_op jit(solution)/shard_map/ppermute | solution.py:304
  95.5 8.4 %collective-permute-start.9 = (bf16[2,512,128]{2,1,0:T(8,128)(2,1)S(1)}, bf16[2,512,128]{2,1,0:T(8,128)(2,1)S(1)}, u32[]{:S(2)}, u32[]{:S(2)}) collective-permute-start(bf16[2,512,128]{2,1,0:T(8,128)(2,1)S(1)} %get-tuple-element.18), channel_id=1, source_target_pairs={{0,16},{56,40},{64,80},{120,104},{128,144},{184,168},{192,208},{24... | collective-permute-start | bytes 786440 | tf_op jit(solution)/shard_map/ppermute | solution.py:301
  100.1 3.9 %collective-permute-start.10 = (bf16[2,512,128]{2,1,0:T(8,128)(2,1)S(1)}, bf16[2,512,128]{2,1,0:T(8,128)(2,1)S(1)}, u32[]{:S(2)}, u32[]{:S(2)}) collective-permute-start(bf16[2,512,128]{2,1,0:T(8,128)(2,1)S(1)} %get-tuple-element.19), channel_id=1, source_target_pairs={{0,8},{56,48},{64,72},{120,112},{128,136},{184,176},{192,200},{248... | collective-permute-start | bytes 786440 | tf_op jit(solution)/shard_map/ppermute | solution.py:302
  104.9 22.4 %all-to-all-start.3 = ((bf16[8,2,64,128]{3,2,1,0:T(8,128)(2,1)}), bf16[8,2,64,128]{3,2,1,0:T(8,128)(2,1)S(1)}, u32[]{:S(2)}, u32[]{:S(2)}) async-start(bf16[8,2,64,128]{3,2,1,0:T(8,128)(2,1)} %rev.11), calls=%async_computation.3 | async-start | bytes 524288 | tf_op jit(solution)/shard_map/all_to_all | solution.py:308
  112.3 9.8 %collective-permute-start.8 = (bf16[2,512,128]{2,1,0:T(8,128)(2,1)S(1)}, bf16[2,512,128]{2,1,0:T(8,128)(2,1)S(1)}, u32[]{:S(2)}, u32[]{:S(2)}) collective-permute-start(bf16[2,512,128]{2,1,0:T(8,128)(2,1)S(1)} %get-tuple-element.17), channel_id=1, source_target_pairs={{32,0},{48,16},{8,40},{24,56},{96,64},{112,80},{72,104},{88,120},{... | collective-permute-start | bytes 786440 | tf_op jit(solution)/shard_map/ppermute | solution.py:303
  122.3 10.9 %copy-start.7 = (bf16[2,512,128]{2,1,0:T(8,128)(2,1)S(1)}, bf16[2,512,128]{2,1,0:T(8,128)(2,1)}, u32[]{:S(2)}) copy-start(bf16[2,512,128]{2,1,0:T(8,128)(2,1)} %copy-done.6) | copy-start | bytes 786436
  127.3 34.6 %all-to-all-start.2 = ((bf16[16,2,64,128]{3,2,1,0:T(8,128)(2,1)}), bf16[16,2,64,128]{3,2,1,0:T(8,128)(2,1)S(1)}, u32[]{:S(2)}, u32[]{:S(2)}) async-start(bf16[16,2,64,128]{3,2,1,0:T(8,128)(2,1)} %bitcast.24), calls=%async_computation.2 | async-start | bytes 1048576 | tf_op jit(solution)/shard_map/all_to_all | solution.py:318
  133.2 3.5 %collective-permute-start.6 = (bf16[2,512,128]{2,1,0:T(8,128)(2,1)S(1)}, bf16[2,512,128]{2,1,0:T(8,128)(2,1)S(1)}, u32[]{:S(2)}, u32[]{:S(2)}) collective-permute-start(bf16[2,512,128]{2,1,0:T(8,128)(2,1)S(1)} %copy-done.7), channel_id=1, source_target_pairs={{0,8},{8,0},{16,24},{24,16},{32,40},{40,32},{48,56},{56,48},{64,72... | collective-permute-start | bytes 786440 | tf_op jit(solution)/shard_map/ppermute | solution.py:326
  137.6 24.4 %collective-permute-start.11 = (bf16[2,64,128]{2,1,0:T(8,128)(2,1)S(1)}, bf16[2,64,128]{2,1,0:T(8,128)(2,1)S(1)}, u32[]{:S(2)}, u32[]{:S(2)}) collective-permute-start(bf16[2,64,128]{2,1,0:T(8,128)(2,1)S(1)} %reduce_sum.32), channel_id=1, source_target_pairs={{87,56},{86,57},{85,58},{84,59},{83,60},{82,61},{81,62},{80,63},{7... | collective-permute-start | bytes 98312 | tf_op jit(solution)/shard_map/ppermute | solution.py:312
  (1 other events, 0.7 us)

commit v3 on v2

--- a/solution.py
+++ b/solution.py
@@ -48,6 +48,26 @@
     ]
 
 
+def partners(ctx, heads, places, bit):
+    return [
+        ((base + r) * heads + h, (base + r) * heads + (h ^ bit))
+        for base in range(0, ctx, GROUP)
+        for r in places
+        for h in range(heads)
+    ]
+
+
+def folds(heads):
+    return [1 << k for k in reversed(range(heads.bit_length() - 1))]
+
+
+def edge_order(heads):
+    order = [0]
+    for bit in folds(heads):
+        order = order + [k | bit for k in order]
+    return [heads - 1 - k for k in order]
+
+
 def inverse(pairs):
     return [(b, a) for a, b in pairs]
 
@@ -79,12 +99,19 @@
         for copy in copies(slot, source):
             copy.start()
 
+    def fetch_edge(slot, source):
+        for place, row in enumerate(edge_order(shards)):
+            for which, target in enumerate((keys, values)):
+                pltpu.make_async_copy(
+                    source.at[place, which], target.at[slot * shards + row], sems.at[slot, which]
+                ).start()
+
     fetch(3, kv_own.at[core])
     fetch(4, kv_own.at[1 - core])
 
     @pl.when(place_ref[1] == 1)
     def _():
-        fetch(0, kv_edge)
+        fetch_edge(0, kv_edge)
 
     @pl.when(place_ref[1] == 0)
     def _():
@@ -92,8 +119,8 @@
 
     @pl.when(place_ref[2] == 1)
     def _():
-        fetch(1, kv_edge2)
-        fetch(2, kv_edge1)
+        fetch_edge(1, kv_edge2)
+        fetch_edge(2, kv_edge1)
 
     @pl.when(place_ref[2] == 0)
     def _():
@@ -202,7 +229,6 @@
     part = (2, width, head_dim)
     vmem = pl.BlockSpec(memory_space=pltpu.VMEM)
     smem = pl.BlockSpec(memory_space=pltpu.SMEM)
-    hbm = pl.BlockSpec(memory_space=pl.ANY)
     return pl.pallas_call(
         attention_kernel,
         out_shape=(
@@ -212,7 +238,7 @@
             jax.ShapeDtypeStruct((2,) + part, jnp.bfloat16),
             jax.ShapeDtypeStruct(part, jnp.bfloat16),
         ),
-        in_specs=[smem, smem] + [vmem] * 4 + [hbm] * 6,
+        in_specs=[smem, smem] + [vmem] * 10,
         out_specs=[vmem] * 5,
         scratch_shapes=[
             pltpu.VMEM(((REACH + 2) * shards, shard, head_dim), jnp.bfloat16),
@@ -224,7 +250,7 @@
             pltpu.VMEM((window, head_dim), jnp.float32),
             pltpu.SemaphoreType.DMA((REACH + 2, 2)),
         ],
-        compiler_params=pltpu.CompilerParams(vmem_limit_bytes=40 * 1024 * 1024),
+        compiler_params=pltpu.CompilerParams(vmem_limit_bytes=24 * 1024 * 1024),
         cost_estimate=pl.CostEstimate(
             flops=6 * 2 * 8 * width * width * head_dim,
             bytes_accessed=8 * 1024 * 1024,
@@ -259,10 +285,15 @@
     kv_own = lax.all_to_all(
         spread.reshape((2 * heads,) + own.shape[1:]), ("core", "head"), 0, 0, tiled=True
     ).reshape(spread.shape)
-    crossed, kv_own = lax.optimization_barrier((crossed, kv_own))
-    kv_edge = lax.all_to_all(
-        jnp.broadcast_to(crossed[None], (heads,) + crossed.shape), "head", 0, 0, tiled=True
-    )[::-1]
+    head = lax.axis_index("head")
+    holders = [r for r in range(GROUP) if r < REACH or r >= GROUP - REACH]
+    kv_edge = crossed[None]
+    for bit in folds(heads):
+        other = lax.ppermute(kv_edge, CTX + ("head",), partners(ctx, heads, holders, bit))
+        high = (head & bit) != 0
+        kv_edge = jnp.concatenate(
+            [jnp.where(high, other, kv_edge), jnp.where(high, kv_edge, other)]
+        )
 
     queries, out_grad = queries[0], out_grad[0]
     far = lax.ppermute(
@@ -304,11 +335,15 @@
     r_near = lax.ppermute(p_near, CTX, inverse(near)).astype(f32)
 
     edge_sum = jnp.where(edge_next, p_next.astype(f32), 0.0) + r_edge1 + r_edge2
-    edge_sum = edge_sum.astype(bf16).reshape(2, heads, shard, head_dim)
-    edge_heads = lax.all_to_all(
-        edge_sum.transpose(1, 0, 2, 3)[::-1], "head", 0, 0, tiled=True
-    )
-    edge_total = jnp.sum(edge_heads.astype(f32), axis=0).astype(bf16)
+    edge_sum = edge_sum.reshape(2, heads, shard, head_dim).transpose(1, 0, 2, 3)[::-1]
+    for bit in reversed(folds(heads)):
+        halves = edge_sum.reshape((-1, 2) + edge_sum.shape[1:])
+        lower, upper = halves[:, 0], halves[:, 1]
+        high = (head & bit) != 0
+        away = jnp.where(high, lower, upper).astype(bf16)
+        other = lax.ppermute(away, CTX + ("head",), partners(ctx, heads, holders, bit))
+        edge_sum = jnp.where(high, upper, lower) + other.astype(f32)
+    edge_total = edge_sum[0].astype(bf16)
     returned = lax.ppermute(edge_total, CTX + ("head",), inverse(edge)).astype(f32)
 
     sums = p_own + r_near

time: 165 us -> 196 us (1.19)
  the two profiles are of different devices: /device:TPU:6 before, /device:TPU:130 now
where the time goes in v3:
time: 196 us; the launch traced here: 195 us
  waiting for transfers between devices  90 us (46%)
  starting transfers between devices  66.9 us (34%)
  Pallas kernels  17.2 us (9%)
  local copies, waits for them, and re-layouts  12.5 us (6%)
  other arithmetic  7.45 us (4%)
    ppermute x3, waiting for transfers between devices, body(): lax.ppermute(away, CTX + ('head',), partners(ctx, heads, holders, bit))  35.9 us
    ppermute x3, waiting for transfers between devices, body(): lax.ppermute(kv_edge, CTX + ('head',), partners(ctx, heads, holders, bit))  29.8 us
    pallas_call x1, Pallas kernels, attention(): pl.pallas_call(attention_kernel, out_shape=(jax.ShapeDtypeStruct(part, jn...  17.2 us
    ppermute x1, waiting for transfers between devices, body(): lax.ppermute(edge_total, CTX + ('head',), inverse(edge)).astype(f32)  13.1 us
    ppermute x1, starting transfers between devices, body(): lax.ppermute(jnp.where(sends_lower, own[0], own[1]), CTX + ('head',), edge)  12.5 us
    all_to_all x1, starting transfers between devices, body(): lax.all_to_all(sums.reshape((2 * heads,) + own.shape[1:]), ('core', 'head...  9.3 us
    unnamed x26, local copies, waits for them, and re-layouts  8.44 us
    ppermute x3, starting transfers between devices, body(): lax.ppermute(kv_edge, CTX + ('head',), partners(ctx, heads, holders, bit))  7.64 us
  transfers between devices with their start and end apart: 20, of which 11 were waited for; matrix products, arithmetic and copies ran while one was open for 5% of the time, Pallas kernels for 0%

profile of v3, /device:TPU:130, one launch (start us, length us, event | category | flops | bytes accessed | tf_op | source)
XLA Modules:
  0.0 195.2 jit_solution(7209304801637754295)
XLA Ops:
  1.5 12.5 %collective-permute-start.3 = (bf16[2,64,128]{2,1,0:T(8,128)(2,1)S(1)}, bf16[2,64,128]{2,1,0:T(8,128)(2,1)S(1)}, u32[]{:S(2)}, u32[]{:S(2)}) collective-permute-start(bf16[2,64,128]{2,1,0:T(8,128)(2,1)S(1)} %fusion.23), channel_id=1, source_target_pairs={{56,87},{57,86},{58,85},{59,84},{60,83},{61,82},{62,81},{63,80},{4... | collective-permute-start | bytes 98312 | tf_op jit(solution)/shard_map/ppermute | solution.py:282
  15.7 7.3 %all-to-all-start = ((bf16[16,2,64,128]{3,2,1,0:T(8,128)(2,1)}), bf16[16,2,64,128]{3,2,1,0:T(8,128)(2,1)S(1)}, u32[]{:S(2)}, u32[]{:S(2)}) async-start(bf16[16,2,64,128]{3,2,1,0:T(8,128)(2,1)} %bitcast.12), calls=%async_computation | async-start | bytes 1048576 | tf_op jit(solution)/shard_map/all_to_all | solution.py:285
  23.1 2.1 %collective-permute-start = (bf16[2,512,128]{2,1,0:T(8,128)(2,1)S(1)}, bf16[2,512,128]{2,1,0:T(8,128)(2,1)S(1)}, u32[]{:S(2)}, u32[]{:S(2)}) collective-permute-start(bf16[2,512,128]{2,1,0:T(8,128)(2,1)S(1)} %maximum_select_fusion), channel_id=1, source_target_pairs={{0,8},{8,0},{16,24},{24,16},{32,40},{40,32},{48,56},{56,48},{64,72... | collective-permute-start | bytes 786440 | tf_op jit(solution)/shard_map/ppermute | solution.py:299
  25.2 2.3 %collective-permute-start.4 = (bf16[1,2,64,128]{3,2,1,0:T(8,128)(2,1)S(1)}, bf16[1,2,64,128]{3,2,1,0:T(8,128)(2,1)S(1)}, u32[]{:S(2)}, u32[]{:S(2)}) collective-permute-start(bf16[1,2,64,128]{3,2,1,0:T(8,128)(2,1)S(1)} %bitcast.148), channel_id=1, source_target_pairs={{0,4},{1,5},{2,6},{3,7},{4,0},{5,1},{6,2},{7,3},{8,12},{9,13},{10,... | collective-permute-start | bytes 98312 | tf_op jit(solution)/shard_map/ppermute | solution.py:292
  27.6 21.4 %collective-permute-done.4 = bf16[1,2,64,128]{3,2,1,0:T(8,128)(2,1)S(1)} collective-permute-done((bf16[1,2,64,128]{3,2,1,0:T(8,128)(2,1)S(1)}, bf16[1,2,64,128]{3,2,1,0:T(8,128)(2,1)S(1)}, u32[]{:S(2)}, u32[]{:S(2)}) %collective-permute-start.4) | collective-permute-done | bytes 32800 | tf_op jit(solution)/shard_map/ppermute | solution.py:292
  49.1 3.0 %collective-permute-start.5 = (bf16[2,2,64,128]{3,2,1,0:T(8,128)(2,1)S(1)}, bf16[2,2,64,128]{3,2,1,0:T(8,128)(2,1)S(1)}, u32[]{:S(2)}, u32[]{:S(2)}) collective-permute-start(bf16[2,2,64,128]{3,2,1,0:T(8,128)(2,1)S(1)} %pad_maximum_fusion.4), channel_id=1, source_target_pairs={{0,2},{1,3},{2,0},{3,1},{4,6},{5,7},{6,4},{7,5},{8,10},{9,11},{10,... | collective-permute-start | bytes 196616 | tf_op jit(solution)/shard_map/ppermute | solution.py:292
  52.2 5.4 %collective-permute-done.5 = bf16[2,2,64,128]{3,2,1,0:T(8,128)(2,1)S(1)} collective-permute-done((bf16[2,2,64,128]{3,2,1,0:T(8,128)(2,1)S(1)}, bf16[2,2,64,128]{3,2,1,0:T(8,128)(2,1)S(1)}, u32[]{:S(2)}, u32[]{:S(2)}) %collective-permute-start.5) | collective-permute-done | bytes 65568 | tf_op jit(solution)/shard_map/ppermute | solution.py:292
  57.6 2.4 %collective-permute-start.6 = (bf16[4,2,64,128]{3,2,1,0:T(8,128)(2,1)S(1)}, bf16[4,2,64,128]{3,2,1,0:T(8,128)(2,1)S(1)}, u32[]{:S(2)}, u32[]{:S(2)}) collective-permute-start(bf16[4,2,64,128]{3,2,1,0:T(8,128)(2,1)S(1)} %pad_maximum_fusion.2), channel_id=1, source_target_pairs={{0,1},{1,0},{2,3},{3,2},{4,5},{5,4},{6,7},{7,6},{8,9},{9,8},{10,11... | collective-permute-start | bytes 393224 | tf_op jit(solution)/shard_map/ppermute | solution.py:292
  60.0 1.5 convert_reduce_fusion
  61.4 3.0 %collective-permute-done.6 = bf16[4,2,64,128]{3,2,1,0:T(8,128)(2,1)S(1)} collective-permute-done((bf16[4,2,64,128]{3,2,1,0:T(8,128)(2,1)S(1)}, bf16[4,2,64,128]{3,2,1,0:T(8,128)(2,1)S(1)}, u32[]{:S(2)}, u32[]{:S(2)}) %collective-permute-start.6) | collective-permute-done | bytes 131104 | tf_op jit(solution)/shard_map/ppermute | solution.py:292
  64.5 1.3 collective-permute-start.8
  65.8 1.3 collective-permute-start.7
  67.1 4.6 %collective-permute-start.1 = (bf16[2,8,2,64,128]{4,3,2,1,0:T(8,128)(2,1)S(1)}, bf16[2,8,2,64,128]{4,3,2,1,0:T(8,128)(2,1)S(1)}, u32[]{:S(2)}, u32[]{:S(2)}) collective-permute-start(bf16[2,8,2,64,128]{4,3,2,1,0:T(8,128)(2,1)S(1)} %bitcast.132), channel_id=1, source_target_pairs={{0,16},{16,32},{32,48},{24,8},{40,24},{56,40},{64,80},{80,96},{96,... | collective-permute-start | bytes 1572872 | tf_op jit(solution)/shard_map/ppermute | solution.py:310
  71.8 1.4 collective-permute-start.2
  74.7 1.3 collective-permute-done.7.kv_edge1
  76.8 4.4 %collective-permute-done.2.kv_next = bf16[8,2,64,128]{3,2,1,0:T(8,128)(2,1)S(1)} collective-permute-done((bf16[8,2,64,128]{3,2,1,0:T(8,128)(2,1)S(1)}, bf16[8,2,64,128]{3,2,1,0:T(8,128)(2,1)S(1)}, u32[]{:S(2)}, u32[]{:S(2)}) %collective-permute-start.2) | collective-permute-done | bytes 262176 | tf_op jit(solution)/shard_map/ppermute | solution.py:309
  87.5 17.2 %attention.1 = (bf16[2,512,128]{2,1,0:T(8,128)(2,1)S(1)}, bf16[2,512,128]{2,1,0:T(8,128)(2,1)}, f32[2,2,512,128]{3,2,1,0:T(8,128)S(1)}, bf16[2,2,512,128]{3,2,1,0:T(8,128)(2,1)S(1)}, bf16[2,512,128]{2,1,0:T(8,128)(2,1)S(1)}) custom-call(s32[4]{0:T(128)S(1)} %and_select_fusion.lo_ref, s32[3]{0:T(128)S(1)} %pad_add_fusion.place_ref, s32[1,1024]{1,0:T(1,128)S(1)} %bitcast.136, ...), custom_call_target="tpu_custom_call" | custom-call | flops 3221225472 | bytes 8388608 | tf_op jit(solution)/shard_map/attention/pallas_call | solution.py:232
  104.8 1.3 collective-permute-start.10
  106.1 4.6 %collective-permute-start.12 = (bf16[2,512,128]{2,1,0:T(8,128)(2,1)S(1)}, bf16[2,512,128]{2,1,0:T(8,128)(2,1)S(1)}, u32[]{:S(2)}, u32[]{:S(2)}) collective-permute-start(bf16[2,512,128]{2,1,0:T(8,128)(2,1)S(1)} %get-tuple-element.14), channel_id=1, source_target_pairs={{0,16},{56,40},{64,80},{120,104},{128,144},{184,168},{192,208},{24... | collective-permute-start | bytes 786440 | tf_op jit(solution)/shard_map/ppermute | solution.py:332
  110.7 1.3 collective-permute-start.13
  112.0 1.9 collective-permute-start.9
  113.9 1.3 collective-permute-start.11
  119.3 4.5 %collective-permute-done.11 = bf16[2,512,128]{2,1,0:T(8,128)(2,1)} collective-permute-done((bf16[2,512,128]{2,1,0:T(8,128)(2,1)S(1)}, bf16[2,512,128]{2,1,0:T(8,128)(2,1)}, u32[]{:S(2)}, u32[]{:S(2)}) %collective-permute-start.11) | collective-permute-done | bytes 262176 | tf_op jit(solution)/shard_map/ppermute | solution.py:334
  125.8 9.3 %all-to-all-start.1 = ((bf16[16,2,64,128]{3,2,1,0:T(8,128)(2,1)}), bf16[16,2,64,128]{3,2,1,0:T(8,128)(2,1)S(1)}, u32[]{:S(2)}, u32[]{:S(2)}) async-start(bf16[16,2,64,128]{3,2,1,0:T(8,128)(2,1)} %bitcast.24), calls=%async_computation.1 | async-start | bytes 1048576 | tf_op jit(solution)/shard_map/all_to_all | solution.py:353
  135.1 3.4 %collective-permute-start.14 = (bf16[4,2,64,128]{3,2,1,0:T(8,128)(2,1)S(1)}, bf16[4,2,64,128]{3,2,1,0:T(8,128)(2,1)S(1)}, u32[]{:S(2)}, u32[]{:S(2)}) collective-permute-start(bf16[4,2,64,128]{3,2,1,0:T(8,128)(2,1)S(1)} %fusion.5), channel_id=1, source_target_pairs={{0,1},{1,0},{2,3},{3,2},{4,5},{5,4},{6,7},{7,6},{8,9},{9,8},{10,11... | collective-permute-start | bytes 393224 | tf_op jit(solution)/shard_map/ppermute | solution.py:344
  138.5 23.1 %collective-permute-done.14 = bf16[4,2,64,128]{3,2,1,0:T(8,128)(2,1)S(1)} collective-permute-done((bf16[4,2,64,128]{3,2,1,0:T(8,128)(2,1)S(1)}, bf16[4,2,64,128]{3,2,1,0:T(8,128)(2,1)S(1)}, u32[]{:S(2)}, u32[]{:S(2)}) %collective-permute-start.14) | collective-permute-done | bytes 131104 | tf_op jit(solution)/shard_map/ppermute | solution.py:344
  161.8 1.9 collective-permute-start.15
  163.7 5.9 %collective-permute-done.15 = bf16[2,2,64,128]{3,2,1,0:T(8,128)(2,1)S(1)} collective-permute-done((bf16[2,2,64,128]{3,2,1,0:T(8,128)(2,1)S(1)}, bf16[2,2,64,128]{3,2,1,0:T(8,128)(2,1)S(1)}, u32[]{:S(2)}, u32[]{:S(2)}) %collective-permute-start.15) | collective-permute-done | bytes 65568 | tf_op jit(solution)/shard_map/ppermute | solution.py:344
  169.6 1.9 collective-permute-start.16
  172.4 6.9 %collective-permute-done.16 = bf16[1,2,64,128]{3,2,1,0:T(8,128)(2,1)S(1)} collective-permute-done((bf16[1,2,64,128]{3,2,1,0:T(8,128)(2,1)S(1)}, bf16[1,2,64,128]{3,2,1,0:T(8,128)(2,1)S(1)}, u32[]{:S(2)}, u32[]{:S(2)}) %collective-permute-start.16) | collective-permute-done | bytes 32800 | tf_op jit(solution)/shard_map/ppermute | solution.py:344
  179.4 1.9 collective-permute-start.17
  181.4 13.1 %collective-permute-done.17 = bf16[2,64,128]{2,1,0:T(8,128)(2,1)S(1)} collective-permute-done((bf16[2,64,128]{2,1,0:T(8,128)(2,1)S(1)}, bf16[2,64,128]{2,1,0:T(8,128)(2,1)S(1)}, u32[]{:S(2)}, u32[]{:S(2)}) %collective-permute-start.17) | collective-permute-done | bytes 32800 | tf_op jit(solution)/shard_map/ppermute | solution.py:347
  (76 shorter events, 19.4 us)
Async XLA Ops:
  0.6 22.4 %copy-start = (bf16[1,2,512,128]{3,2,1,0:T(8,128)(2,1)S(1)}, bf16[1,2,512,128]{3,2,1,0:T(8,128)(2,1)}, u32[]{:S(2)}) copy-start(bf16[1,2,512,128]{3,2,1,0:T(8,128)(2,1)} %param.5) | copy-start | bytes 786436
  1.5 23.7 %collective-permute-start.3 = (bf16[2,64,128]{2,1,0:T(8,128)(2,1)S(1)}, bf16[2,64,128]{2,1,0:T(8,128)(2,1)S(1)}, u32[]{:S(2)}, u32[]{:S(2)}) collective-permute-start(bf16[2,64,128]{2,1,0:T(8,128)(2,1)S(1)} %fusion.23), channel_id=1, source_target_pairs={{56,87},{57,86},{58,85},{59,84},{60,83},{61,82},{62,81},{63,80},{4... | collective-permute-start | bytes 98312 | tf_op jit(solution)/shard_map/ppermute | solution.py:282
  14.8 8.3 %copy-start.1 = (bf16[1,2,512,128]{3,2,1,0:T(8,128)(2,1)S(1)}, bf16[1,2,512,128]{3,2,1,0:T(8,128)(2,1)}, u32[]{:S(2)}) copy-start(bf16[1,2,512,128]{3,2,1,0:T(8,128)(2,1)} %param.8) | copy-start | bytes 786436
  15.7 51.4 %all-to-all-start = ((bf16[16,2,64,128]{3,2,1,0:T(8,128)(2,1)}), bf16[16,2,64,128]{3,2,1,0:T(8,128)(2,1)S(1)}, u32[]{:S(2)}, u32[]{:S(2)}) async-start(bf16[16,2,64,128]{3,2,1,0:T(8,128)(2,1)} %bitcast.12), calls=%async_computation | async-start | bytes 1048576 | tf_op jit(solution)/shard_map/all_to_all | solution.py:285
  23.0 4.5 %copy-start.12 = (s32[65536]{0:T(1024)S(1)}, s32[65536]{0:T(1024)}, u32[]{:S(2)}) copy-start(s32[65536]{0:T(1024)} %param.9) | copy-start | bytes 786436
  23.1 50.2 %collective-permute-start = (bf16[2,512,128]{2,1,0:T(8,128)(2,1)S(1)}, bf16[2,512,128]{2,1,0:T(8,128)(2,1)S(1)}, u32[]{:S(2)}, u32[]{:S(2)}) collective-permute-start(bf16[2,512,128]{2,1,0:T(8,128)(2,1)S(1)} %maximum_select_fusion), channel_id=1, source_target_pairs={{0,8},{8,0},{16,24},{24,16},{32,40},{40,32},{48,56},{56,48},{64,72... | collective-permute-start | bytes 786440 | tf_op jit(solution)/shard_map/ppermute | solution.py:299
  25.2 23.8 %collective-permute-start.4 = (bf16[1,2,64,128]{3,2,1,0:T(8,128)(2,1)S(1)}, bf16[1,2,64,128]{3,2,1,0:T(8,128)(2,1)S(1)}, u32[]{:S(2)}, u32[]{:S(2)}) collective-permute-start(bf16[1,2,64,128]{3,2,1,0:T(8,128)(2,1)S(1)} %bitcast.148), channel_id=1, source_target_pairs={{0,4},{1,5},{2,6},{3,7},{4,0},{5,1},{6,2},{7,3},{8,12},{9,13},{10,... | collective-permute-start | bytes 98312 | tf_op jit(solution)/shard_map/ppermute | solution.py:292
  49.1 8.5 %collective-permute-start.5 = (bf16[2,2,64,128]{3,2,1,0:T(8,128)(2,1)S(1)}, bf16[2,2,64,128]{3,2,1,0:T(8,128)(2,1)S(1)}, u32[]{:S(2)}, u32[]{:S(2)}) collective-permute-start(bf16[2,2,64,128]{3,2,1,0:T(8,128)(2,1)S(1)} %pad_maximum_fusion.4), channel_id=1, source_target_pairs={{0,2},{1,3},{2,0},{3,1},{4,6},{5,7},{6,4},{7,5},{8,10},{9,11},{10,... | collective-permute-start | bytes 196616 | tf_op jit(solution)/shard_map/ppermute | solution.py:292
  57.6 6.9 %collective-permute-start.6 = (bf16[4,2,64,128]{3,2,1,0:T(8,128)(2,1)S(1)}, bf16[4,2,64,128]{3,2,1,0:T(8,128)(2,1)S(1)}, u32[]{:S(2)}, u32[]{:S(2)}) collective-permute-start(bf16[4,2,64,128]{3,2,1,0:T(8,128)(2,1)S(1)} %pad_maximum_fusion.2), channel_id=1, source_target_pairs={{0,1},{1,0},{2,3},{3,2},{4,5},{5,4},{6,7},{7,6},{8,9},{9,8},{10,11... | collective-permute-start | bytes 393224 | tf_op jit(solution)/shard_map/ppermute | solution.py:292
  64.5 9.5 %collective-permute-start.8 = (bf16[8,2,64,128]{3,2,1,0:T(8,128)(2,1)S(1)}, bf16[8,2,64,128]{3,2,1,0:T(8,128)(2,1)S(1)}, u32[]{:S(2)}, u32[]{:S(2)}) collective-permute-start(bf16[8,2,64,128]{3,2,1,0:T(8,128)(2,1)S(1)} %pad_maximum_fusion.1.kv_edge), channel_id=1, source_target_pairs={{8,0},{48,56},{72,64},{112,120},{136,128},{176,184},{200,192},{240... | collective-permute-start | bytes 786440 | tf_op jit(solution)/shard_map/ppermute | solution.py:312
  65.8 10.2 %collective-permute-start.7 = (bf16[8,2,64,128]{3,2,1,0:T(8,128)(2,1)S(1)}, bf16[8,2,64,128]{3,2,1,0:T(8,128)(2,1)S(1)}, u32[]{:S(2)}, u32[]{:S(2)}) collective-permute-start(bf16[8,2,64,128]{3,2,1,0:T(8,128)(2,1)S(1)} %pad_maximum_fusion.1.kv_edge), channel_id=1, source_target_pairs={{16,0},{40,56},{80,64},{104,120},{144,128},{168,184},{208,192},{23... | collective-permute-start | bytes 786440 | tf_op jit(solution)/shard_map/ppermute | solution.py:311
  67.1 14.8 %collective-permute-start.1 = (bf16[2,8,2,64,128]{4,3,2,1,0:T(8,128)(2,1)S(1)}, bf16[2,8,2,64,128]{4,3,2,1,0:T(8,128)(2,1)S(1)}, u32[]{:S(2)}, u32[]{:S(2)}) collective-permute-start(bf16[2,8,2,64,128]{4,3,2,1,0:T(8,128)(2,1)S(1)} %bitcast.132), channel_id=1, source_target_pairs={{0,16},{16,32},{32,48},{24,8},{40,24},{56,40},{64,80},{80,96},{96,... | collective-permute-start | bytes 1572872 | tf_op jit(solution)/shard_map/ppermute | solution.py:310
  71.8 9.4 %collective-permute-start.2 = (bf16[8,2,64,128]{3,2,1,0:T(8,128)(2,1)S(1)}, bf16[8,2,64,128]{3,2,1,0:T(8,128)(2,1)S(1)}, u32[]{:S(2)}, u32[]{:S(2)}) collective-permute-start(bf16[8,2,64,128]{3,2,1,0:T(8,128)(2,1)S(1)} %slice_select_fusion), channel_id=1, source_target_pairs={{0,32},{16,48},{40,8},{56,24},{64,96},{80,112},{104,72},{120,88},{... | collective-permute-start | bytes 786440 | tf_op jit(solution)/shard_map/ppermute | solution.py:309
  73.3 0.7 copy-start.4
  76.0 0.7 copy-start.8
  81.2 0.7 copy-start.10
  81.9 0.8 copy-start.2
  82.7 1.0 copy-start.3
  83.7 0.9 copy-start.5
  84.7 0.9 copy-start.7
  85.6 0.9 copy-start.9
  86.6 0.9 copy-start.11
  104.8 13.4 %collective-permute-start.10 = (bf16[2,2,512,128]{3,2,1,0:T(8,128)(2,1)S(1)}, bf16[2,2,512,128]{3,2,1,0:T(8,128)(2,1)}, u32[]{:S(2)}, u32[]{:S(2)}) collective-permute-start(bf16[2,2,512,128]{3,2,1,0:T(8,128)(2,1)S(1)} %get-tuple-element.12), channel_id=1, source_target_pairs={{16,0},{32,16},{48,32},{8,24},{24,40},{40,56},{80,64},{96,80},{112... | collective-permute-start | bytes 1572872 | tf_op jit(solution)/shard_map/ppermute | solution.py:335
  106.1 10.0 %collective-permute-start.12 = (bf16[2,512,128]{2,1,0:T(8,128)(2,1)S(1)}, bf16[2,512,128]{2,1,0:T(8,128)(2,1)S(1)}, u32[]{:S(2)}, u32[]{:S(2)}) collective-permute-start(bf16[2,512,128]{2,1,0:T(8,128)(2,1)S(1)} %get-tuple-element.14), channel_id=1, source_target_pairs={{0,16},{56,40},{64,80},{120,104},{128,144},{184,168},{192,208},{24... | collective-permute-start | bytes 786440 | tf_op jit(solution)/shard_map/ppermute | solution.py:332
  110.7 5.4 %collective-permute-start.13 = (bf16[2,512,128]{2,1,0:T(8,128)(2,1)S(1)}, bf16[2,512,128]{2,1,0:T(8,128)(2,1)S(1)}, u32[]{:S(2)}, u32[]{:S(2)}) collective-permute-start(bf16[2,512,128]{2,1,0:T(8,128)(2,1)S(1)} %get-tuple-element.15), channel_id=1, source_target_pairs={{0,8},{56,48},{64,72},{120,112},{128,136},{184,176},{192,200},{248... | collective-permute-start | bytes 786440 | tf_op jit(solution)/shard_map/ppermute | solution.py:333
  112.0 51.7 %collective-permute-start.9 = (bf16[2,512,128]{2,1,0:T(8,128)(2,1)}, bf16[2,512,128]{2,1,0:T(8,128)(2,1)S(1)}, u32[]{:S(2)}, u32[]{:S(2)}) collective-permute-start(bf16[2,512,128]{2,1,0:T(8,128)(2,1)} %get-tuple-element.10), channel_id=1, source_target_pairs={{0,8},{8,0},{16,24},{24,16},{32,40},{40,32},{48,56},{56,48},{64,72... | collective-permute-start | bytes 786440 | tf_op jit(solution)/shard_map/ppermute | solution.py:361
  113.9 9.9 %collective-permute-start.11 = (bf16[2,512,128]{2,1,0:T(8,128)(2,1)S(1)}, bf16[2,512,128]{2,1,0:T(8,128)(2,1)}, u32[]{:S(2)}, u32[]{:S(2)}) collective-permute-start(bf16[2,512,128]{2,1,0:T(8,128)(2,1)S(1)} %get-tuple-element.13), channel_id=1, source_target_pairs={{32,0},{48,16},{8,40},{24,56},{96,64},{112,80},{72,104},{88,120},{... | collective-permute-start | bytes 786440 | tf_op jit(solution)/shard_map/ppermute | solution.py:334
  125.8 55.5 %all-to-all-start.1 = ((bf16[16,2,64,128]{3,2,1,0:T(8,128)(2,1)}), bf16[16,2,64,128]{3,2,1,0:T(8,128)(2,1)S(1)}, u32[]{:S(2)}, u32[]{:S(2)}) async-start(bf16[16,2,64,128]{3,2,1,0:T(8,128)(2,1)} %bitcast.24), calls=%async_computation.1 | async-start | bytes 1048576 | tf_op jit(solution)/shard_map/all_to_all | solution.py:353
  135.1 26.6 %collective-permute-start.14 = (bf16[4,2,64,128]{3,2,1,0:T(8,128)(2,1)S(1)}, bf16[4,2,64,128]{3,2,1,0:T(8,128)(2,1)S(1)}, u32[]{:S(2)}, u32[]{:S(2)}) collective-permute-start(bf16[4,2,64,128]{3,2,1,0:T(8,128)(2,1)S(1)} %fusion.5), channel_id=1, source_target_pairs={{0,1},{1,0},{2,3},{3,2},{4,5},{5,4},{6,7},{7,6},{8,9},{9,8},{10,11... | collective-permute-start | bytes 393224 | tf_op jit(solution)/shard_map/ppermute | solution.py:344
  161.8 7.8 %collective-permute-start.15 = (bf16[2,2,64,128]{3,2,1,0:T(8,128)(2,1)S(1)}, bf16[2,2,64,128]{3,2,1,0:T(8,128)(2,1)S(1)}, u32[]{:S(2)}, u32[]{:S(2)}) collective-permute-start(bf16[2,2,64,128]{3,2,1,0:T(8,128)(2,1)S(1)} %fusion.13), channel_id=1, source_target_pairs={{0,2},{1,3},{2,0},{3,1},{4,6},{5,7},{6,4},{7,5},{8,10},{9,11},{10,... | collective-permute-start | bytes 196616 | tf_op jit(solution)/shard_map/ppermute | solution.py:344
  169.6 9.7 %collective-permute-start.16 = (bf16[1,2,64,128]{3,2,1,0:T(8,128)(2,1)S(1)}, bf16[1,2,64,128]{3,2,1,0:T(8,128)(2,1)S(1)}, u32[]{:S(2)}, u32[]{:S(2)}) collective-permute-start(bf16[1,2,64,128]{3,2,1,0:T(8,128)(2,1)S(1)} %fusion.15), channel_id=1, source_target_pairs={{0,4},{1,5},{2,6},{3,7},{4,0},{5,1},{6,2},{7,3},{8,12},{9,13},{10,... | collective-permute-start | bytes 98312 | tf_op jit(solution)/shard_map/ppermute | solution.py:344
  179.4 15.1 %collective-permute-start.17 = (bf16[2,64,128]{2,1,0:T(8,128)(2,1)S(1)}, bf16[2,64,128]{2,1,0:T(8,128)(2,1)S(1)}, u32[]{:S(2)}, u32[]{:S(2)}) collective-permute-start(bf16[2,64,128]{2,1,0:T(8,128)(2,1)S(1)} %fusion.16), channel_id=1, source_target_pairs={{87,56},{86,57},{85,58},{84,59},{83,60},{82,61},{81,62},{80,63},{7... | collective-permute-start | bytes 98312 | tf_op jit(solution)/shard_map/ppermute | solution.py:347
  (1 other events, 0.7 us)

commit v4 on v2

v4 whole, which is shorter than its diff:
```python
import math

import jax
import jax.numpy as jnp
from jax import lax
from jax.experimental import pallas as pl
from jax.experimental.pallas import tpu as pltpu
from jax.sharding import Mesh
from jax.sharding import PartitionSpec as P

REACH = 3
GROUP = 8
NEG_FILL = -1e30
CTX = ("pair", "core")


def within(ctx, moves):
    return [(base + a, base + b) for base in range(0, ctx, GROUP) for a, b in moves]


def swap_pairs(ctx):
    return within(ctx, [(r, r ^ 1) for r in range(GROUP)])


def near_pairs(ctx):
    forth = [(r, r + 2) for r in range(0, GROUP - 2, 2)]
    return within(ctx, forth + [(r, r - 2) for r in range(3, GROUP, 2)])


def next_pairs(ctx):
    forth = [(r, r + 4) for r in range(0, GROUP - 4, 2)]
    return within(ctx, forth + [(r, r - 4) for r in range(5, GROUP, 2)])


def edge_pairs(ctx, heads):
    moves = []
    for base in range(0, ctx, GROUP):
        for k in range(REACH):
            top = base + GROUP - 1 - k
            if base + GROUP < ctx:
                moves.append((top, base + GROUP + REACH - 1 - k))
            else:
                moves.append((top, base + GROUP - REACH + k))
            if base > 0:
                moves.append((base + k, base - REACH + k))
    return [
        (a * heads + h, b * heads + h) for a, b in moves for h in range(heads)
    ]


def inverse(pairs):
    return [(b, a) for a, b in pairs]


NT = (((1,), (1,)), ((), ()))
NN = (((1,), (0,)), ((), ()))


def matmul(a, b, dims=NN):
    return lax.dot_general(a, b, dims, preferred_element_type=jnp.float32)


def key_tile(ref, j, which, tile):
    _, shards, _, shard, head_dim = ref.shape
    per_span = shards * shard // tile
    rows = pl.ds((j % per_span) * (tile // shard), tile // shard)
    return ref[j // per_span, rows, which].reshape(tile, head_dim)


def query_tile(own_ref, far_ref, far_index, core, i, tile):
    width = far_ref.shape[1]
    span, part = divmod(i, width // tile)
    rows = pl.ds(part * tile, tile)
    return own_ref[core, rows] if span == 0 else far_ref[far_index, rows]


def masked_scores(keys, query, start, j, tile, causal):
    raw = matmul(keys, query, NT) * (query.shape[1] ** -0.5 * math.log2(math.e))
    at_key = lax.broadcasted_iota(jnp.int32, raw.shape, 0)
    allowed = at_key >= start - j * tile
    if causal:
        allowed = allowed & (at_key <= lax.broadcasted_iota(jnp.int32, raw.shape, 1))
    return jnp.where(allowed, raw, NEG_FILL)


def column_max(a):
    return jnp.max(a, axis=0, keepdims=True)


def column_sum(a):
    return jnp.sum(a, axis=0, keepdims=True)


def own_forward_kernel(
    lo_ref, place_ref, start_row, queries, far, kv_own, top_row, total_row, acc_out,
    keys, values, values_t, scores,
):
    tile, tiles = scores.shape[1], scores.shape[0]
    core = place_ref[0]
    before = REACH * tiles // 2
    for j in range(tiles):
        span = core if j < tiles // 2 else 1 - core
        rows = pl.ds(j % (tiles // 2) * (tile // kv_own.shape[3]), tile // kv_own.shape[3])
        keys[j] = kv_own[span, rows, 0].reshape(keys.shape[1:])
        values_t[j] = kv_own[span, rows, 1].reshape(keys.shape[1:]).T
    for i in range(tiles):
        columns = pl.ds(i * tile, tile)
        query = query_tile(queries, far, 0, core, i, tile)
        start = start_row[:, columns]
        lo = jnp.maximum(lo_ref[i] - before, 0)

        def score_tile(j, causal):
            raw = masked_scores(keys[j], query, start, j + before, tile, causal)
            scores[j] = raw
            return column_max(raw)

        top = lax.fori_loop(
            lo, i, lambda j, m: jnp.maximum(m, score_tile(j, False)), score_tile(i, True)
        )

        def forward(j, carry):
            total, acc = carry
            prob = jnp.exp2(scores[j] - top)
            return total + column_sum(prob), acc + matmul(values_t[j], prob.astype(jnp.bfloat16))

        total, acc = lax.fori_loop(
            lo, i + 1, forward, (jnp.zeros_like(top), jnp.zeros(acc_out.shape[1:], jnp.float32))
        )
        top_row[:, columns] = top
        total_row[:, columns] = total
        acc_out[i] = acc


def earlier_kernel(
    lo_ref, place_ref, start_row, queries, out_grad, far, top_row, total_row, acc_in, kv_prev,
    attended_out, lse_row, delta_row, acc_out, p_near, p_next,
    keys_t, values_t, scores, key_acc, value_acc,
):
    tile, before = scores.shape[1], scores.shape[0]
    tiles = acc_in.shape[0]
    scale = queries.shape[2] ** -0.5
    core = place_ref[0]
    bf16, f32 = jnp.bfloat16, jnp.float32
    first = lo_ref[0]

    @pl.when(first < before)
    def _():
        key_acc[...] = jnp.zeros_like(key_acc)
        value_acc[...] = jnp.zeros_like(value_acc)

        def turn(j, carry):
            keys_t[j] = key_tile(kv_prev, j, 0, tile).T
            values_t[j] = key_tile(kv_prev, j, 1, tile).T
            return carry

        lax.fori_loop(first, before, turn, 0)

    for i in range(tiles):
        columns = pl.ds(i * tile, tile)
        query = query_tile(queries, far, 0, core, i, tile)
        grad = query_tile(out_grad, far, 1, core, i, tile)
        start = start_row[:, columns]
        lo = jnp.minimum(lo_ref[i], before)
        own_top = top_row[:, columns]

        def score_tile(j, top):
            raw = masked_scores(key_tile(kv_prev, j, 0, tile), query, start, j, tile, False)
            scores[j] = raw
            return jnp.maximum(top, column_max(raw))

        top = lax.fori_loop(lo, before, score_tile, own_top)
        shrink = jnp.exp2(own_top - top)

        def forward(j, carry):
            total, acc = carry
            prob = jnp.exp2(scores[j] - top)
            scores[j] = prob
            return total + column_sum(prob), acc + matmul(values_t[j], prob.astype(bf16))

        total, acc = lax.fori_loop(
            lo, before, forward, (total_row[:, columns] * shrink, acc_in[i] * shrink)
        )
        inv = 1.0 / total
        attended_t = (acc * inv).astype(bf16).astype(f32)
        delta = column_sum(grad.astype(f32).T * attended_t)
        half, part = divmod(i, tiles // 2)
        attended_out[half, pl.ds(part * tile, tile)] = attended_t.T.astype(bf16)
        lse_row[:, columns] = top + jnp.log2(total)
        delta_row[:, columns] = delta

        def backward(j, acc):
            prob = scores[j] * inv
            here = pl.ds(pl.multiple_of(j * tile, tile), tile)
            value_acc[here] += matmul(prob.astype(bf16), grad)
            dot_grad = matmul(key_tile(kv_prev, j, 1, tile), grad, NT)
            score_grad = (prob * (dot_grad - delta)).astype(bf16)
            key_acc[here] += matmul(score_grad, query)
            return acc + matmul(keys_t[j], score_grad)

        acc_out[i] = lax.fori_loop(lo, before, backward, jnp.zeros(acc_out.shape[1:], f32))

    shards, shard = kv_prev.shape[1], kv_prev.shape[3]

    @pl.when(first < before)
    def _():
        for slot, target in enumerate((p_next, p_near.at[0], p_near.at[1])):
            for row in range(shards):
                here = pl.ds((slot * shards + row) * shard, shard)
                target[row, 0] = (key_acc[here] * scale).astype(bf16)
                target[row, 1] = value_acc[here].astype(bf16)

    @pl.when(first >= before)
    def _():
        p_next[...] = jnp.zeros_like(p_next)
        p_near[...] = jnp.zeros_like(p_near)


def own_backward_kernel(
    lo_ref, place_ref, start_row, queries, out_grad, far, kv_own, attended, lse_row, delta_row,
    acc_in, out_own, out_far, p_own,
    keys, values, keys_t, key_acc, value_acc,
):
    tiles, tile = keys.shape[0], keys.shape[1]
    scale = queries.shape[2] ** -0.5
    core = place_ref[0]
    bf16, f32 = jnp.bfloat16, jnp.float32
    before = REACH * tiles // 2
    for j in range(tiles):
        span = core if j < tiles // 2 else 1 - core
        rows = pl.ds(j % (tiles // 2) * (tile // kv_own.shape[3]), tile // kv_own.shape[3])
        block = kv_own[span, rows, 0].reshape(keys.shape[1:])
        keys[j] = block
        keys_t[j] = block.T
        values[j] = kv_own[span, rows, 1].reshape(keys.shape[1:])
    key_acc[...] = jnp.zeros_like(key_acc)
    value_acc[...] = jnp.zeros_like(value_acc)
    for i in range(tiles):
        columns = pl.ds(i * tile, tile)
        query = query_tile(queries, far, 0, core, i, tile)
        grad = query_tile(out_grad, far, 1, core, i, tile)
        start = start_row[:, columns]
        lse, delta = lse_row[:, columns], delta_row[:, columns]

        def backward(j, acc, causal):
            raw = masked_scores(keys[j], query, start, j + before, tile, causal)
            prob = jnp.exp2(raw - lse)
            value_acc[j] += matmul(prob.astype(bf16), grad)
            score_grad = (prob * (matmul(values[j], grad, NT) - delta)).astype(bf16)
            key_acc[j] += matmul(score_grad, query)
            return acc + matmul(keys_t[j], score_grad)

        acc = backward(i, acc_in[i], True)
        acc = lax.fori_loop(
            jnp.maximum(lo_ref[i] - before, 0), i, lambda j, acc: backward(j, acc, False), acc
        )
        half, part = divmod(i, tiles // 2)
        rows = pl.ds(part * tile, tile)
        (out_own, out_far)[half][1, rows] = (acc.T * scale).astype(bf16)
    out_own[0] = attended[0]
    out_far[0] = attended[1]
    shards, shard = kv_own.shape[1], kv_own.shape[3]
    for span in range(2):
        for row in range(shards):
            j, part = divmod((span * shards + row) * shard, tile)
            here = pl.ds(part, shard)
            p_own[span, row, 0] = key_acc[j, here] * scale
            p_own[span, row, 1] = value_acc[j, here]


def vmem_kernel(kernel, name, outputs, scratch, tiles, tile, head_dim, matmuls):
    def call(*operands):
        rest = [pl.BlockSpec(memory_space=pltpu.VMEM)] * (len(operands) - 2)
        return pl.pallas_call(
            kernel,
            out_shape=outputs,
            in_specs=[pl.BlockSpec(memory_space=pltpu.SMEM)] * 2 + rest,
            out_specs=[pl.BlockSpec(memory_space=pltpu.VMEM)] * len(outputs),
            scratch_shapes=[pltpu.VMEM(shape, dtype) for shape, dtype in scratch],
            compiler_params=pltpu.CompilerParams(vmem_limit_bytes=24 * 1024 * 1024),
            cost_estimate=pl.CostEstimate(
                flops=2 * matmuls * tiles * tile * tile * head_dim,
                bytes_accessed=4 * 1024 * 1024,
                transcendentals=tiles * tile * tile,
            ),
            name=name,
        )(*operands)

    return call


def body(queries, key_states, value_states, out_grad, segments):
    ctx = lax.axis_size("pair") * 2
    core = lax.axis_index("core")
    position = lax.axis_index("pair") * 2 + core
    place = position % GROUP
    width = queries.shape[2]
    heads = lax.axis_size("head")
    shard = key_states.shape[2]
    head_dim = key_states.shape[3]
    bf16, f32 = jnp.bfloat16, jnp.float32

    swap, near, far_chip = swap_pairs(ctx), near_pairs(ctx), next_pairs(ctx)
    edge1 = within(ctx, [(2, 0), (GROUP - 3, GROUP - 1)])
    edge2 = within(ctx, [(1, 0), (GROUP - 2, GROUP - 1)])
    edge = edge_pairs(ctx, heads)
    even = core == 0
    sends_lower = place >= GROUP - REACH

    own = jnp.stack([key_states[0], value_states[0]], axis=1)
    crossed = lax.ppermute(jnp.where(sends_lower, own[0], own[1]), CTX + ("head",), edge)

    spread = jnp.broadcast_to(own[:, None], (2, heads) + own.shape[1:])
    kv_own = lax.all_to_all(
        spread.reshape((2 * heads,) + own.shape[1:]), ("core", "head"), 0, 0, tiled=True
    ).reshape(spread.shape)
    crossed, kv_own = lax.optimization_barrier((crossed, kv_own))
    kv_edge = lax.all_to_all(
        jnp.broadcast_to(crossed[None], (heads,) + crossed.shape), "head", 0, 0, tiled=True
    )

    queries, out_grad = queries[0], out_grad[0]
    far = lax.ppermute(
        jnp.where(
            even,
            jnp.stack([queries[1], out_grad[1]]),
            jnp.stack([queries[0], out_grad[0]]),
        ),
        CTX,
        swap,
    )

    kv_next = lax.ppermute(jnp.where(even, kv_own[1], kv_own[0]), CTX, far_chip)
    kv_near = lax.ppermute(kv_own, CTX, near)
    kv_edge1 = lax.ppermute(kv_edge, CTX, edge1)
    kv_edge2 = lax.ppermute(kv_edge, CTX, edge2)

    first = jnp.where(even, position, 2 * ctx - 1 - position)
    window = (REACH + 2) * width
    padded = jnp.concatenate([jnp.full((REACH * width,), -1, jnp.int32), segments])
    seg_window = lax.dynamic_slice_in_dim(padded, first * width, window)
    start = jnp.sum(
        seg_window[:, None] < seg_window[None, REACH * width :], axis=0, dtype=jnp.int32
    )
    tile = max(min(256, width // 2), shard)
    tiles, earlier = 2 * width // tile, REACH * width // tile
    lo = start[::tile] // tile
    edge_next = jnp.where(even, place <= 2, place >= GROUP - 3)
    edge_near = jnp.where(even, place == 0, place == GROUP - 1)
    places = core[None].astype(jnp.int32)
    start = start[None, :]

    near_ordered = jnp.where(even, kv_near, kv_near[::-1])
    kv_prev = jnp.stack(
        [
            jnp.where(edge_next, kv_edge, kv_next),
            jnp.where(edge_near, kv_edge2, near_ordered[0]),
            jnp.where(edge_near, kv_edge1, near_ordered[1]),
        ]
    )

    row = jax.ShapeDtypeStruct((1, 2 * width), f32)
    turned = jax.ShapeDtypeStruct((tiles, head_dim, tile), f32)
    part = jax.ShapeDtypeStruct((2, width, head_dim), bf16)
    span_like = kv_next.shape
    natural = ((tiles, tile, head_dim), bf16)
    top, total, acc = vmem_kernel(
        own_forward_kernel, "own_forward", (row, row, turned),
        [natural, natural, ((tiles, head_dim, tile), bf16), ((tiles, tile, tile), f32)],
        6, tile, head_dim, 2,
    )(lo, places, start, queries, far, kv_own)
    attended, lse, delta, acc, p_near, p_next = vmem_kernel(
        earlier_kernel, "earlier",
        (
            part, row, row, turned,
            jax.ShapeDtypeStruct((2,) + span_like, bf16),
            jax.ShapeDtypeStruct(span_like, bf16),
        ),
        [
            ((earlier, head_dim, tile), bf16),
            ((earlier, head_dim, tile), bf16),
            ((earlier, tile, tile), f32),
            ((earlier * tile, head_dim), f32),
            ((earlier * tile, head_dim), f32),
        ],
        6, tile, head_dim, 6,
    )(lo, places, start, queries, out_grad, far, top, total, acc, kv_prev)

    r_edge1 = lax.ppermute(p_near[1], CTX, inverse(edge1)).astype(f32)
    r_edge2 = lax.ppermute(p_near[0], CTX, inverse(edge2)).astype(f32)
    r_next = lax.ppermute(p_next, CTX, inverse(far_chip)).astype(f32)
    r_near = lax.ppermute(p_near, CTX, inverse(near)).astype(f32)

    out_own, out_far, p_own = vmem_kernel(
        own_backward_kernel, "own_backward",
        (part, part, jax.ShapeDtypeStruct((2,) + span_like, f32)),
        [natural, natural, ((tiles, head_dim, tile), bf16)]
        + [((tiles, tile, head_dim), f32)] * 2,
        6, tile, head_dim, 5,
    )(lo, places, start, queries, out_grad, far, kv_own, attended, lse, delta, acc)

    edge_sum = jnp.where(edge_next, p_next.astype(f32), 0.0) + r_edge1 + r_edge2
    edge_heads = lax.all_to_all(edge_sum.astype(bf16), "head", 0, 0, tiled=True)
    edge_total = jnp.sum(edge_heads.astype(f32), axis=0).astype(bf16)
    returned = lax.ppermute(edge_total, CTX + ("head",), inverse(edge)).astype(f32)

    sums = p_own + r_near
    sums = jnp.stack([sums[0], sums[1] + r_next])
    sums = jnp.where(even, sums, sums[::-1]).astype(bf16)
    by_head = lax.all_to_all(
        sums.reshape((2 * heads,) + own.shape[1:]), ("core", "head"), 0, 0, tiled=True
    ).reshape(spread.shape)
    total = jnp.sum(by_head.astype(f32), axis=1)
    lower = total[0] + jnp.where(sends_lower, returned, 0.0)
    upper = total[1] + jnp.where(sends_lower, 0.0, returned)
    grads = jnp.stack([lower, upper]).astype(bf16)

    back = lax.ppermute(out_far, CTX, swap)
    results = []
    for k in range(2):
        results.append(
            jnp.where(
                even, jnp.stack([out_own[k], back[k]]), jnp.stack([back[k], out_own[k]])
            )[None]
        )
    return results[0], results[1], grads[:, 0][None], grads[:, 1][None]


def solution(mesh):
    ctx, heads = mesh.devices.shape
    mesh = Mesh(mesh.devices.reshape(ctx // 2, 2, heads), CTX + ("head",))
    by_head = P(CTX, None, None, "head")
    by_row = P(CTX, None, "head", None)
    return jax.shard_map(
        body,
        mesh=mesh,
        in_specs=(by_head, by_row, by_row, by_head, P()),
        out_specs=(by_head, by_head, by_row, by_row),
        check_vma=False,
    )
```

time: 165 us -> 160 us (0.970)
  starting transfers between devices: 71.6 us -> 82 us
  waiting for transfers between devices: 60.6 us -> 51.4 us
  local copies, waits for them, and re-layouts: 12.1 us -> 3.89 us
  other arithmetic: 4.5 us -> 9.36 us
  Pallas kernels: 12.7 us -> 10.7 us
    ppermute x1, waiting for transfers between devices: 8.32 us -> 0.01 us  [body(): r_next = lax.ppermute(p_next, CTX, inverse(far_chip)).astype(f32)]
    unnamed x34 -> x14, local copies, waits for them, and re-layouts: 8.46 us -> 1.78 us
    all_to_all x1, waiting for transfers between devices: 15.4 us -> 9.22 us  [body(): lax.all_to_all(spread.reshape((2 * heads,) + own.shape[1:]), ('core', 'he...]
    all_to_all x1, starting transfers between devices: 5.9 us -> 11.7 us  [body(): lax.all_to_all(sums.reshape((2 * heads,) + own.shape[1:]), ('core', 'head...]
    ppermute x1, waiting for transfers between devices: 1.96 us -> 7.73 us  [body(): lax.ppermute(jnp.where(sends_lower, own[0], own[1]), CTX + ('head',), edge)]
    all_to_all x1, starting transfers between devices: 5.26 us -> 10.6 us  [body(): lax.all_to_all(jnp.broadcast_to(crossed[None], (heads,) + crossed.shape),...]
    ppermute x1, starting transfers between devices: 1.31 us -> 6.4 us  [body(): r_edge2 = lax.ppermute(p_near[0], CTX, inverse(edge2)).astype(f32)]
    ppermute x1, starting transfers between devices: 4.56 us -> 1.46 us  [body(): r_edge1 = lax.ppermute(p_near[1], CTX, inverse(edge1)).astype(f32)]
  transfers between devices with their start and end apart: 16 -> 16, of which waited for: 9 -> 7; matrix products, arithmetic and copies ran while one was open for 3% -> 6% of each run, Pallas kernels for 0% -> 5%
where the time goes in v4:
time: 160 us; the launch traced here: 158 us
  starting transfers between devices  82 us (51%)
  waiting for transfers between devices  51.4 us (32%)
  Pallas kernels  10.7 us (7%)
  other arithmetic  9.36 us (6%)
  local copies, waits for them, and re-layouts  3.89 us (2%)
    all_to_all x1, waiting for transfers between devices, body(): lax.all_to_all(sums.reshape((2 * heads,) + own.shape[1:]), ('core', 'head...  18.7 us
    all_to_all x1, starting transfers between devices, body(): lax.all_to_all(spread.reshape((2 * heads,) + own.shape[1:]), ('core', 'he...  12.6 us
    all_to_all x1, starting transfers between devices, body(): lax.all_to_all(sums.reshape((2 * heads,) + own.shape[1:]), ('core', 'head...  11.7 us
    ppermute x1, starting transfers between devices, body(): lax.ppermute(jnp.where(sends_lower, own[0], own[1]), CTX + ('head',), edge)  11.1 us
    pallas_call x3, Pallas kernels, call(): pl.pallas_call(kernel, out_shape=outputs, in_specs=[pl.BlockSpec(memory_s...  10.7 us
    all_to_all x1, starting transfers between devices, body(): lax.all_to_all(jnp.broadcast_to(crossed[None], (heads,) + crossed.shape),...  10.6 us
    all_to_all x1, waiting for transfers between devices, body(): lax.all_to_all(spread.reshape((2 * heads,) + own.shape[1:]), ('core', 'he...  9.22 us
    ppermute x1, waiting for transfers between devices, body(): lax.ppermute(jnp.where(sends_lower, own[0], own[1]), CTX + ('head',), edge)  7.73 us
  transfers between devices with their start and end apart: 16, of which 7 were waited for; matrix products, arithmetic and copies ran while one was open for 6% of the time, Pallas kernels for 5%

profile of v4, /device:TPU:6, one launch (start us, length us, event | category | flops | bytes accessed | tf_op | source)
XLA Modules:
  0.0 158.4 jit_solution(15512071292082229448)
XLA Ops:
  1.5 0.9 broadcast_in_dim.20
  2.5 12.6 %all-to-all-start = ((bf16[16,2,64,128]{3,2,1,0:T(8,128)(2,1)}), bf16[16,2,64,128]{3,2,1,0:T(8,128)(2,1)S(1)}, u32[]{:S(2)}, u32[]{:S(2)}) async-start(bf16[16,2,64,128]{3,2,1,0:T(8,128)(2,1)} %bitcast.11), calls=%async_computation | async-start | bytes 1048576 | tf_op jit(solution)/shard_map/all_to_all | solution.py:313
  15.1 11.1 %collective-permute-start.1 = (bf16[2,64,128]{2,1,0:T(8,128)(2,1)S(1)}, bf16[2,64,128]{2,1,0:T(8,128)(2,1)S(1)}, u32[]{:S(2)}, u32[]{:S(2)}) collective-permute-start(bf16[2,64,128]{2,1,0:T(8,128)(2,1)S(1)} %fusion.17), channel_id=1, source_target_pairs={{56,80},{57,81},{58,82},{59,83},{60,84},{61,85},{62,86},{63,87},{4... | collective-permute-start | bytes 98312 | tf_op jit(solution)/shard_map/ppermute | solution.py:310
  26.4 1.9 %collective-permute-start = (bf16[2,512,128]{2,1,0:T(8,128)(2,1)S(1)}, bf16[2,512,128]{2,1,0:T(8,128)(2,1)S(1)}, u32[]{:S(2)}, u32[]{:S(2)}) collective-permute-start(bf16[2,512,128]{2,1,0:T(8,128)(2,1)S(1)} %maximum_select_fusion), channel_id=1, source_target_pairs={{0,8},{8,0},{16,24},{24,16},{32,40},{40,32},{48,56},{56,48},{64,72... | collective-permute-start | bytes 786440 | tf_op jit(solution)/shard_map/ppermute | solution.py:322
  28.4 7.7 %collective-permute-done.1 = bf16[2,64,128]{2,1,0:T(8,128)(2,1)S(1)} collective-permute-done((bf16[2,64,128]{2,1,0:T(8,128)(2,1)S(1)}, bf16[2,64,128]{2,1,0:T(8,128)(2,1)S(1)}, u32[]{:S(2)}, u32[]{:S(2)}) %collective-permute-start.1) | collective-permute-done | bytes 32800 | tf_op jit(solution)/shard_map/ppermute | solution.py:310
  36.1 9.2 %all-to-all-done = bf16[16,2,64,128]{3,2,1,0:T(8,128)(2,1)S(1)} async-done(((bf16[16,2,64,128]{3,2,1,0:T(8,128)(2,1)}), bf16[16,2,64,128]{3,2,1,0:T(8,128)(2,1)S(1)}, u32[]{:S(2)}, u32[]{:S(2)}) %all-to-all-start) | async-done | bytes 524320 | tf_op jit(solution)/shard_map/all_to_all | solution.py:313
  46.1 10.6 %all-to-all-start.1 = ((bf16[8,2,64,128]{3,2,1,0:T(8,128)(2,1)}), bf16[8,2,64,128]{3,2,1,0:T(8,128)(2,1)S(1)}, u32[]{:S(2)}, u32[]{:S(2)}) async-start(bf16[8,2,64,128]{3,2,1,0:T(8,128)(2,1)} %broadcast_in_dim.36), calls=%async_computation.1 | async-start | bytes 524288 | tf_op jit(solution)/shard_map/all_to_all | solution.py:317
  56.8 3.7 %collective-permute-start.4 = (bf16[2,8,2,64,128]{4,3,2,1,0:T(8,128)(2,1)S(1)}, bf16[2,8,2,64,128]{4,3,2,1,0:T(8,128)(2,1)S(1)}, u32[]{:S(2)}, u32[]{:S(2)}) collective-permute-start(bf16[2,8,2,64,128]{4,3,2,1,0:T(8,128)(2,1)S(1)} %bitcast.84), channel_id=1, source_target_pairs={{0,16},{16,32},{32,48},{24,8},{40,24},{56,40},{64,80},{80,96},{96,... | collective-permute-start | bytes 1572872 | tf_op jit(solution)/shard_map/ppermute | solution.py:333
  60.5 1.5 convert_reduce_fusion
  62.1 2.6 %collective-permute-start.2 = (bf16[8,2,64,128]{3,2,1,0:T(8,128)(2,1)S(1)}, bf16[8,2,64,128]{3,2,1,0:T(8,128)(2,1)S(1)}, u32[]{:S(2)}, u32[]{:S(2)}) collective-permute-start(bf16[8,2,64,128]{3,2,1,0:T(8,128)(2,1)S(1)} %select_bitcast_fusion.1), channel_id=1, source_target_pairs={{0,32},{16,48},{40,8},{56,24},{64,96},{80,112},{104,72},{120,88},{... | collective-permute-start | bytes 786440 | tf_op jit(solution)/shard_map/ppermute | solution.py:332
  64.7 3.7 %own_forward.1 = (f32[1,1024]{1,0:T(1,128)S(1)}, f32[1,1024]{1,0:T(1,128)S(1)}, f32[4,128,256]{2,1,0:T(8,128)S(1)}) custom-call(s32[4]{0:T(128)S(1)} %and_select_fusion.lo_ref, s32[1]{0:T(128)} %bitcast.place_ref, s32[1,1024]{1,0:T(1,128)S(1)} %bitcast.93, bf16[2,512,128]{2,1,0:T(8,128)(2,1)S(1)} %bitcast.88, ...), custom_call_target="tpu_custom_call" | custom-call | flops 201326592 | bytes 4194304 | tf_op jit(solution)/shard_map/own_forward/pallas_call | solution.py:273
  69.2 4.1 %all-to-all-done.1 = bf16[8,2,64,128]{3,2,1,0:T(8,128)(2,1)S(1)} async-done(((bf16[8,2,64,128]{3,2,1,0:T(8,128)(2,1)}), bf16[8,2,64,128]{3,2,1,0:T(8,128)(2,1)S(1)}, u32[]{:S(2)}, u32[]{:S(2)}) %all-to-all-start.1) | async-done | bytes 262176 | tf_op jit(solution)/shard_map/all_to_all | solution.py:317
  73.3 1.3 collective-permute-start.5
  74.6 1.3 collective-permute-start.3
  76.1 5.5 %collective-permute-done.5 = bf16[8,2,64,128]{3,2,1,0:T(8,128)(2,1)S(1)} collective-permute-done((bf16[8,2,64,128]{3,2,1,0:T(8,128)(2,1)S(1)}, bf16[8,2,64,128]{3,2,1,0:T(8,128)(2,1)S(1)}, u32[]{:S(2)}, u32[]{:S(2)}) %collective-permute-start.5) | collective-permute-done | bytes 262176 | tf_op jit(solution)/shard_map/ppermute | solution.py:334
  82.7 2.2 %earlier.1 = (bf16[2,512,128]{2,1,0:T(8,128)(2,1)S(1)}, f32[1,1024]{1,0:T(1,128)S(1)}, f32[1,1024]{1,0:T(1,128)S(1)}, f32[4,128,256]{2,1,0:T(8,128)S(1)}, bf16[2...) custom-call(s32[4]{0:T(128)S(1)} %and_select_fusion.lo_ref, s32[1]{0:T(128)} %bitcast.place_ref, ...), custom_call_target="tpu_custom_call" | custom-call | flops 603979776 | bytes 4194304 | tf_op jit(solution)/shard_map/earlier/pallas_call | solution.py:273
  85.0 1.5 collective-permute-start.9
  86.5 6.4 %collective-permute-start.10 = (bf16[8,2,64,128]{3,2,1,0:T(8,128)(2,1)S(1)}, bf16[8,2,64,128]{3,2,1,0:T(8,128)(2,1)S(1)}, u32[]{:S(2)}, u32[]{:S(2)}) collective-permute-start(bf16[8,2,64,128]{3,2,1,0:T(8,128)(2,1)S(1)} %get-tuple-element.33), channel_id=1, source_target_pairs={{0,8},{56,48},{64,72},{120,112},{128,136},{184,176},{192,200},{248... | collective-permute-start | bytes 786440 | tf_op jit(solution)/shard_map/ppermute | solution.py:389
  92.9 1.3 collective-permute-start.7
  94.2 1.3 collective-permute-start.8
  96.3 6.2 %all-to-all-start.3 = ((bf16[8,2,64,128]{3,2,1,0:T(8,128)(2,1)}), bf16[8,2,64,128]{3,2,1,0:T(8,128)(2,1)}, u32[]{:S(2)}, u32[]{:S(2)}) async-start(bf16[8,2,64,128]{3,2,1,0:T(8,128)(2,1)} %add_convert_fusion), calls=%async_computation.3 | async-start | bytes 524288 | tf_op jit(solution)/shard_map/all_to_all | solution.py:402
  102.5 4.8 %own_backward.1 = (bf16[2,512,128]{2,1,0:T(8,128)(2,1)S(1)}, bf16[2,512,128]{2,1,0:T(8,128)(2,1)S(1)}, f32[2,8,2,64,128]{4,3,2,1,0:T(8,128)S(1)}) custom-call(s32[4]{0:T(128)S(1)} %and_select_fusion.lo_ref, s32[1]{0:T(128)} %bitcast.place_ref, s32[1,1024]{1,0:T(1,128)S(1)} %bitcast.95, bf16[2,512,128]{2,1,0:T(8,128)(2,1)S(1)} %bitcast.90, ...), custom_call_target="tpu_custom_call" | custom-call | flops 503316480 | bytes 4194304 | tf_op jit(solution)/shard_map/own_backward/pallas_call | solution.py:273
  107.4 1.2 convert_add_fusion
  108.6 1.0 fusion.2
  109.7 1.0 fusion
  110.7 5.0 %all-to-all-done.3 = bf16[8,2,64,128]{3,2,1,0:T(8,128)(2,1)} async-done(((bf16[8,2,64,128]{3,2,1,0:T(8,128)(2,1)}), bf16[8,2,64,128]{3,2,1,0:T(8,128)(2,1)}, u32[]{:S(2)}, u32[]{:S(2)}) %all-to-all-start.3) | async-done | bytes 262176 | tf_op jit(solution)/shard_map/all_to_all | solution.py:402
  115.7 11.7 %all-to-all-start.2 = ((bf16[16,2,64,128]{3,2,1,0:T(8,128)(2,1)}), bf16[16,2,64,128]{3,2,1,0:T(8,128)(2,1)S(1)}, u32[]{:S(2)}, u32[]{:S(2)}) async-start(bf16[16,2,64,128]{3,2,1,0:T(8,128)(2,1)} %bitcast.25), calls=%async_computation.2 | async-start | bytes 1048576 | tf_op jit(solution)/shard_map/all_to_all | solution.py:409
  127.5 2.3 %collective-permute-start.6 = (bf16[2,512,128]{2,1,0:T(8,128)(2,1)S(1)}, bf16[2,512,128]{2,1,0:T(8,128)(2,1)S(1)}, u32[]{:S(2)}, u32[]{:S(2)}) collective-permute-start(bf16[2,512,128]{2,1,0:T(8,128)(2,1)S(1)} %get-tuple-element.28), channel_id=1, source_target_pairs={{0,8},{8,0},{16,24},{24,16},{32,40},{40,32},{48,56},{56,48},{64,72... | collective-permute-start | bytes 786440 | tf_op jit(solution)/shard_map/ppermute | solution.py:417
  129.8 1.1 collective-permute-done.6
  131.8 1.0 reduce_sum.32
  132.8 6.2 %collective-permute-start.11 = (bf16[2,64,128]{2,1,0:T(8,128)(2,1)S(1)}, bf16[2,64,128]{2,1,0:T(8,128)(2,1)S(1)}, u32[]{:S(2)}, u32[]{:S(2)}) collective-permute-start(bf16[2,64,128]{2,1,0:T(8,128)(2,1)S(1)} %reduce_sum.32), channel_id=1, source_target_pairs={{80,56},{81,57},{82,58},{83,59},{84,60},{85,61},{86,62},{87,63},{7... | collective-permute-start | bytes 98312 | tf_op jit(solution)/shard_map/ppermute | solution.py:404
  139.0 18.7 %all-to-all-done.2 = bf16[16,2,64,128]{3,2,1,0:T(8,128)(2,1)S(1)} async-done(((bf16[16,2,64,128]{3,2,1,0:T(8,128)(2,1)}), bf16[16,2,64,128]{3,2,1,0:T(8,128)(2,1)S(1)}, u32[]{:S(2)}, u32[]{:S(2)}) %all-to-all-start.2) | async-done | bytes 524320 | tf_op jit(solution)/shard_map/all_to_all | solution.py:409
  (49 shorter events, 6.7 us)
Async XLA Ops:
  0.6 14.5 %copy-start.5 = (bf16[1,2,64,128]{3,2,1,0:T(8,128)(2,1)S(1)}, bf16[1,2,64,128]{3,2,1,0:T(8,128)(2,1)}, u32[]{:S(2)}) copy-start(bf16[1,2,64,128]{3,2,1,0:T(8,128)(2,1)} %param.7) | copy-start | bytes 98308
  0.6 14.5 %copy-start.6 = (bf16[1,2,64,128]{3,2,1,0:T(8,128)(2,1)S(1)}, bf16[1,2,64,128]{3,2,1,0:T(8,128)(2,1)}, u32[]{:S(2)}) copy-start(bf16[1,2,64,128]{3,2,1,0:T(8,128)(2,1)} %param.6) | copy-start | bytes 98308
  0.7 25.6 %copy-start = (bf16[1,2,512,128]{3,2,1,0:T(8,128)(2,1)S(1)}, bf16[1,2,512,128]{3,2,1,0:T(8,128)(2,1)}, u32[]{:S(2)}) copy-start(bf16[1,2,512,128]{3,2,1,0:T(8,128)(2,1)} %param.5) | copy-start | bytes 786436
  1.5 24.8 %copy-start.1 = (bf16[1,2,512,128]{3,2,1,0:T(8,128)(2,1)S(1)}, bf16[1,2,512,128]{3,2,1,0:T(8,128)(2,1)}, u32[]{:S(2)}) copy-start(bf16[1,2,512,128]{3,2,1,0:T(8,128)(2,1)} %param.8) | copy-start | bytes 786436
  2.5 42.9 %all-to-all-start = ((bf16[16,2,64,128]{3,2,1,0:T(8,128)(2,1)}), bf16[16,2,64,128]{3,2,1,0:T(8,128)(2,1)S(1)}, u32[]{:S(2)}, u32[]{:S(2)}) async-start(bf16[16,2,64,128]{3,2,1,0:T(8,128)(2,1)} %bitcast.11), calls=%async_computation | async-start | bytes 1048576 | tf_op jit(solution)/shard_map/all_to_all | solution.py:313
  15.1 20.9 %collective-permute-start.1 = (bf16[2,64,128]{2,1,0:T(8,128)(2,1)S(1)}, bf16[2,64,128]{2,1,0:T(8,128)(2,1)S(1)}, u32[]{:S(2)}, u32[]{:S(2)}) collective-permute-start(bf16[2,64,128]{2,1,0:T(8,128)(2,1)S(1)} %fusion.17), channel_id=1, source_target_pairs={{56,80},{57,81},{58,82},{59,83},{60,84},{61,85},{62,86},{63,87},{4... | collective-permute-start | bytes 98312 | tf_op jit(solution)/shard_map/ppermute | solution.py:310
  26.3 30.3 %copy-start.4 = (s32[65536]{0:T(1024)S(1)}, s32[65536]{0:T(1024)}, u32[]{:S(2)}) copy-start(s32[65536]{0:T(1024)} %param.9) | copy-start | bytes 786436
  26.4 38.3 %collective-permute-start = (bf16[2,512,128]{2,1,0:T(8,128)(2,1)S(1)}, bf16[2,512,128]{2,1,0:T(8,128)(2,1)S(1)}, u32[]{:S(2)}, u32[]{:S(2)}) collective-permute-start(bf16[2,512,128]{2,1,0:T(8,128)(2,1)S(1)} %maximum_select_fusion), channel_id=1, source_target_pairs={{0,8},{8,0},{16,24},{24,16},{32,40},{40,32},{48,56},{56,48},{64,72... | collective-permute-start | bytes 786440 | tf_op jit(solution)/shard_map/ppermute | solution.py:322
  46.1 27.3 %all-to-all-start.1 = ((bf16[8,2,64,128]{3,2,1,0:T(8,128)(2,1)}), bf16[8,2,64,128]{3,2,1,0:T(8,128)(2,1)S(1)}, u32[]{:S(2)}, u32[]{:S(2)}) async-start(bf16[8,2,64,128]{3,2,1,0:T(8,128)(2,1)} %broadcast_in_dim.36), calls=%async_computation.1 | async-start | bytes 524288 | tf_op jit(solution)/shard_map/all_to_all | solution.py:317
  56.8 19.1 %collective-permute-start.4 = (bf16[2,8,2,64,128]{4,3,2,1,0:T(8,128)(2,1)S(1)}, bf16[2,8,2,64,128]{4,3,2,1,0:T(8,128)(2,1)S(1)}, u32[]{:S(2)}, u32[]{:S(2)}) collective-permute-start(bf16[2,8,2,64,128]{4,3,2,1,0:T(8,128)(2,1)S(1)} %bitcast.84), channel_id=1, source_target_pairs={{0,16},{16,32},{32,48},{24,8},{40,24},{56,40},{64,80},{80,96},{96,... | collective-permute-start | bytes 1572872 | tf_op jit(solution)/shard_map/ppermute | solution.py:333
  62.1 14.0 %collective-permute-start.2 = (bf16[8,2,64,128]{3,2,1,0:T(8,128)(2,1)S(1)}, bf16[8,2,64,128]{3,2,1,0:T(8,128)(2,1)S(1)}, u32[]{:S(2)}, u32[]{:S(2)}) collective-permute-start(bf16[8,2,64,128]{3,2,1,0:T(8,128)(2,1)S(1)} %select_bitcast_fusion.1), channel_id=1, source_target_pairs={{0,32},{16,48},{40,8},{56,24},{64,96},{80,112},{104,72},{120,88},{... | collective-permute-start | bytes 786440 | tf_op jit(solution)/shard_map/ppermute | solution.py:332
  68.4 0.8 copy-start.2
  73.3 8.3 %collective-permute-start.5 = (bf16[8,2,64,128]{3,2,1,0:T(8,128)(2,1)S(1)}, bf16[8,2,64,128]{3,2,1,0:T(8,128)(2,1)S(1)}, u32[]{:S(2)}, u32[]{:S(2)}) collective-permute-start(bf16[8,2,64,128]{3,2,1,0:T(8,128)(2,1)S(1)} %all-to-all-done.1), channel_id=1, source_target_pairs={{16,0},{40,56},{80,64},{104,120},{144,128},{168,184},{208,192},{23... | collective-permute-start | bytes 786440 | tf_op jit(solution)/shard_map/ppermute | solution.py:334
  74.6 7.0 %collective-permute-start.3 = (bf16[8,2,64,128]{3,2,1,0:T(8,128)(2,1)S(1)}, bf16[8,2,64,128]{3,2,1,0:T(8,128)(2,1)S(1)}, u32[]{:S(2)}, u32[]{:S(2)}) collective-permute-start(bf16[8,2,64,128]{3,2,1,0:T(8,128)(2,1)S(1)} %all-to-all-done.1), channel_id=1, source_target_pairs={{8,0},{48,56},{72,64},{112,120},{136,128},{176,184},{200,192},{240... | collective-permute-start | bytes 786440 | tf_op jit(solution)/shard_map/ppermute | solution.py:335
  81.7 1.0 copy-start.3
  85.0 10.5 %collective-permute-start.9 = (bf16[8,2,64,128]{3,2,1,0:T(8,128)(2,1)S(1)}, bf16[8,2,64,128]{3,2,1,0:T(8,128)(2,1)S(1)}, u32[]{:S(2)}, u32[]{:S(2)}) collective-permute-start(bf16[8,2,64,128]{3,2,1,0:T(8,128)(2,1)S(1)} %get-tuple-element.32), channel_id=1, source_target_pairs={{0,16},{56,40},{64,80},{120,104},{128,144},{184,168},{192,208},{24... | collective-permute-start | bytes 786440 | tf_op jit(solution)/shard_map/ppermute | solution.py:388
  86.5 9.0 %collective-permute-start.10 = (bf16[8,2,64,128]{3,2,1,0:T(8,128)(2,1)S(1)}, bf16[8,2,64,128]{3,2,1,0:T(8,128)(2,1)S(1)}, u32[]{:S(2)}, u32[]{:S(2)}) collective-permute-start(bf16[8,2,64,128]{3,2,1,0:T(8,128)(2,1)S(1)} %get-tuple-element.33), channel_id=1, source_target_pairs={{0,8},{56,48},{64,72},{120,112},{128,136},{184,176},{192,200},{248... | collective-permute-start | bytes 786440 | tf_op jit(solution)/shard_map/ppermute | solution.py:389
  92.9 14.5 %collective-permute-start.7 = (bf16[2,8,2,64,128]{4,3,2,1,0:T(8,128)(2,1)S(1)}, bf16[2,8,2,64,128]{4,3,2,1,0:T(8,128)(2,1)}, u32[]{:S(2)}, u32[]{:S(2)}) collective-permute-start(bf16[2,8,2,64,128]{4,3,2,1,0:T(8,128)(2,1)S(1)} %get-tuple-element.30), channel_id=1, source_target_pairs={{16,0},{32,16},{48,32},{8,24},{24,40},{40,56},{80,64},{96,80},{112... | collective-permute-start | bytes 1572872 | tf_op jit(solution)/shard_map/ppermute | solution.py:391
  94.2 14.5 %collective-permute-start.8 = (bf16[8,2,64,128]{3,2,1,0:T(8,128)(2,1)S(1)}, bf16[8,2,64,128]{3,2,1,0:T(8,128)(2,1)}, u32[]{:S(2)}, u32[]{:S(2)}) collective-permute-start(bf16[8,2,64,128]{3,2,1,0:T(8,128)(2,1)S(1)} %get-tuple-element.31), channel_id=1, source_target_pairs={{32,0},{48,16},{8,40},{24,56},{96,64},{112,80},{72,104},{88,120},{... | collective-permute-start | bytes 786440 | tf_op jit(solution)/shard_map/ppermute | solution.py:390
  96.3 19.4 %all-to-all-start.3 = ((bf16[8,2,64,128]{3,2,1,0:T(8,128)(2,1)}), bf16[8,2,64,128]{3,2,1,0:T(8,128)(2,1)}, u32[]{:S(2)}, u32[]{:S(2)}) async-start(bf16[8,2,64,128]{3,2,1,0:T(8,128)(2,1)} %add_convert_fusion), calls=%async_computation.3 | async-start | bytes 524288 | tf_op jit(solution)/shard_map/all_to_all | solution.py:402
  115.7 42.0 %all-to-all-start.2 = ((bf16[16,2,64,128]{3,2,1,0:T(8,128)(2,1)}), bf16[16,2,64,128]{3,2,1,0:T(8,128)(2,1)S(1)}, u32[]{:S(2)}, u32[]{:S(2)}) async-start(bf16[16,2,64,128]{3,2,1,0:T(8,128)(2,1)} %bitcast.25), calls=%async_computation.2 | async-start | bytes 1048576 | tf_op jit(solution)/shard_map/all_to_all | solution.py:409
  127.5 3.5 %collective-permute-start.6 = (bf16[2,512,128]{2,1,0:T(8,128)(2,1)S(1)}, bf16[2,512,128]{2,1,0:T(8,128)(2,1)S(1)}, u32[]{:S(2)}, u32[]{:S(2)}) collective-permute-start(bf16[2,512,128]{2,1,0:T(8,128)(2,1)S(1)} %get-tuple-element.28), channel_id=1, source_target_pairs={{0,8},{8,0},{16,24},{24,16},{32,40},{40,32},{48,56},{56,48},{64,72... | collective-permute-start | bytes 786440 | tf_op jit(solution)/shard_map/ppermute | solution.py:417
  132.8 25.0 %collective-permute-start.11 = (bf16[2,64,128]{2,1,0:T(8,128)(2,1)S(1)}, bf16[2,64,128]{2,1,0:T(8,128)(2,1)S(1)}, u32[]{:S(2)}, u32[]{:S(2)}) collective-permute-start(bf16[2,64,128]{2,1,0:T(8,128)(2,1)S(1)} %reduce_sum.32), channel_id=1, source_target_pairs={{80,56},{81,57},{82,58},{83,59},{84,60},{85,61},{86,62},{87,63},{7... | collective-permute-start | bytes 98312 | tf_op jit(solution)/shard_map/ppermute | solution.py:404

commit v5 on v4

--- a/solution.py
+++ b/solution.py
@@ -32,7 +32,11 @@
     return within(ctx, forth + [(r, r - 4) for r in range(5, GROUP, 2)])
 
 
-def edge_pairs(ctx, heads):
+def head_pairs(ctx, heads, bit):
+    return [(d, d ^ bit) for d in range(ctx * heads)]
+
+
+def edge_pairs(ctx, heads, flip):
     moves = []
     for base in range(0, ctx, GROUP):
         for k in range(REACH):
@@ -44,8 +48,22 @@
             if base > 0:
                 moves.append((base + k, base - REACH + k))
     return [
-        (a * heads + h, b * heads + h) for a, b in moves for h in range(heads)
+        (a * heads + h, b * heads + (h ^ flip)) for a, b in moves for h in range(heads)
     ]
+
+
+def folds(heads):
+    return [1 << k for k in reversed(range(heads.bit_length() - 1))]
+
+
+def pick(bit, low, high):
+    return jnp.where(bit, high, low)
+
+
+def by_bit(bit, mine, other, axis):
+    mine, other = jnp.expand_dims(mine, axis), jnp.expand_dims(other, axis)
+    place = lax.broadcasted_iota(jnp.int32, (2,) + (1,) * (mine.ndim - axis - 1), 0)
+    return jnp.where(place == bit.astype(jnp.int32), mine, other)
 
 
 def inverse(pairs):
@@ -302,21 +320,32 @@
     swap, near, far_chip = swap_pairs(ctx), near_pairs(ctx), next_pairs(ctx)
     edge1 = within(ctx, [(2, 0), (GROUP - 3, GROUP - 1)])
     edge2 = within(ctx, [(1, 0), (GROUP - 2, GROUP - 1)])
-    edge = edge_pairs(ctx, heads)
+    everywhere = CTX + ("head",)
     even = core == 0
     sends_lower = place >= GROUP - REACH
-
-    own = jnp.stack([key_states[0], value_states[0]], axis=1)
-    crossed = lax.ppermute(jnp.where(sends_lower, own[0], own[1]), CTX + ("head",), edge)
-
-    spread = jnp.broadcast_to(own[:, None], (2, heads) + own.shape[1:])
-    kv_own = lax.all_to_all(
-        spread.reshape((2 * heads,) + own.shape[1:]), ("core", "head"), 0, 0, tiled=True
-    ).reshape(spread.shape)
-    crossed, kv_own = lax.optimization_barrier((crossed, kv_own))
-    kv_edge = lax.all_to_all(
-        jnp.broadcast_to(crossed[None], (heads,) + crossed.shape), "head", 0, 0, tiled=True
-    )
+    head = lax.axis_index("head")
+    bits = folds(heads)
+    far_bit = bits[0]
+    high = {bit: (head & bit) != 0 for bit in bits}
+    straight, crossing = edge_pairs(ctx, heads, 0), edge_pairs(ctx, heads, far_bit)
+
+    lower = jnp.stack([key_states[0, 0], value_states[0, 0]])
+    upper = jnp.stack([key_states[0, 1], value_states[0, 1]])
+    leaving = pick(sends_lower, upper, lower)
+    half = by_bit(core, pick(even, upper, lower), lax.ppermute(pick(even, lower, upper), CTX, swap), 0)
+    kv_own = by_bit(high[far_bit], half, lax.ppermute(half, everywhere, head_pairs(ctx, heads, far_bit)), 1)
+    kv_edge = by_bit(
+        high[far_bit],
+        lax.ppermute(leaving, everywhere, straight),
+        lax.ppermute(leaving, everywhere, crossing),
+        0,
+    )
+    kv_all = jnp.concatenate([kv_own, kv_edge[None]])
+    for k, bit in enumerate(bits[1:]):
+        other = lax.ppermute(kv_all, everywhere, head_pairs(ctx, heads, bit))
+        kv_all = by_bit(high[bit], kv_all, other, 2 + k)
+    kv_all = kv_all.reshape((3, heads) + half.shape[1:])
+    kv_own, kv_edge = kv_all[:2], kv_all[2]
 
     queries, out_grad = queries[0], out_grad[0]
     far = lax.ppermute(
@@ -399,19 +428,28 @@
     )(lo, places, start, queries, out_grad, far, kv_own, attended, lse, delta, acc)
 
     edge_sum = jnp.where(edge_next, p_next.astype(f32), 0.0) + r_edge1 + r_edge2
-    edge_heads = lax.all_to_all(edge_sum.astype(bf16), "head", 0, 0, tiled=True)
-    edge_total = jnp.sum(edge_heads.astype(f32), axis=0).astype(bf16)
-    returned = lax.ppermute(edge_total, CTX + ("head",), inverse(edge)).astype(f32)
-
     sums = p_own + r_near
-    sums = jnp.stack([sums[0], sums[1] + r_next])
-    sums = jnp.where(even, sums, sums[::-1]).astype(bf16)
-    by_head = lax.all_to_all(
-        sums.reshape((2 * heads,) + own.shape[1:]), ("core", "head"), 0, 0, tiled=True
-    ).reshape(spread.shape)
-    total = jnp.sum(by_head.astype(f32), axis=1)
-    lower = total[0] + jnp.where(sends_lower, returned, 0.0)
-    upper = total[1] + jnp.where(sends_lower, 0.0, returned)
+    first_sum, second_sum = sums[0], sums[1] + r_next
+    sums = jnp.stack(
+        [pick(even, second_sum, first_sum), pick(even, first_sum, second_sum), edge_sum]
+    )
+    for bit in reversed(bits[1:]):
+        halves = sums.reshape((3, -1, 2) + half.shape[1:])
+        away = pick(high[bit], halves[:, :, 1], halves[:, :, 0]).astype(bf16)
+        other = lax.ppermute(away, everywhere, head_pairs(ctx, heads, bit))
+        sums = pick(high[bit], halves[:, :, 0], halves[:, :, 1]) + other.astype(f32)
+    stays, away = pick(high[far_bit], sums[:, 0], sums[:, 1]), pick(high[far_bit], sums[:, 1], sums[:, 0])
+    away = away.astype(bf16)
+    other = lax.ppermute(away[:2], everywhere, head_pairs(ctx, heads, far_bit))
+    returned = lax.ppermute(stays[2].astype(bf16), everywhere, inverse(straight)).astype(f32)
+    returned += lax.ppermute(away[2], everywhere, inverse(crossing)).astype(f32)
+    stays = stays[:2] + other.astype(f32)
+    own_half = pick(even, stays[1], stays[0])
+    far_half = lax.ppermute(
+        pick(even, stays[0], stays[1]).astype(bf16), CTX, swap
+    ).astype(f32)
+    lower = pick(even, far_half, own_half) + jnp.where(sends_lower, returned, 0.0)
+    upper = pick(even, own_half, far_half) + jnp.where(sends_lower, 0.0, returned)
     grads = jnp.stack([lower, upper]).astype(bf16)
 
     back = lax.ppermute(out_far, CTX, swap)

time: 160 us -> 163 us (1.019)
  the two profiles are of different devices: /device:TPU:6 before, /device:TPU:7 now
where the time goes in v5:
time: 163 us; the launch traced here: 162 us
  starting transfers between devices  109 us (67%)
  waiting for transfers between devices  33.5 us (21%)
  Pallas kernels  10.7 us (7%)
  other arithmetic  4.99 us (3%)
  local copies, waits for them, and re-layouts  2.93 us (2%)
    ppermute x1, starting transfers between devices, body(): lax.ppermute(stays[2].astype(bf16), everywhere, inverse(straight))  21.8 us
    ppermute x1, starting transfers between devices, body(): lax.ppermute(leaving, everywhere, crossing)  15.7 us
    ppermute x2, waiting for transfers between devices, body(): other = lax.ppermute(kv_all, everywhere, head_pairs(ctx, heads, bit))  13.1 us
    pallas_call x3, Pallas kernels, call(): pl.pallas_call(kernel, out_shape=outputs, in_specs=[pl.BlockSpec(memory_s...  10.7 us
    ppermute x2, starting transfers between devices, body(): other = lax.ppermute(away, everywhere, head_pairs(ctx, heads, bit))  9.88 us
    ppermute x1, starting transfers between devices, body(): r_near = lax.ppermute(p_near, CTX, inverse(near)).astype(f32)  9.34 us
    ppermute x2, starting transfers between devices, body(): other = lax.ppermute(kv_all, everywhere, head_pairs(ctx, heads, bit))  8.39 us
    ppermute x1, starting transfers between devices, body(): kv_edge2 = lax.ppermute(kv_edge, CTX, edge2)  7.95 us
  transfers between devices with their start and end apart: 22, of which 8 were waited for; matrix products, arithmetic and copies ran while one was open for 3% of the time, Pallas kernels for 5%

profile of v5, /device:TPU:7, one launch (start us, length us, event | category | flops | bytes accessed | tf_op | source)
XLA Modules:
  0.0 162.3 jit_solution(5910202047472060066)
XLA Ops:
  2.2 15.7 %collective-permute-start.4 = (bf16[2,64,128]{2,1,0:T(8,128)(2,1)S(1)}, bf16[2,64,128]{2,1,0:T(8,128)(2,1)S(1)}, u32[]{:S(2)}, u32[]{:S(2)}) collective-permute-start(bf16[2,64,128]{2,1,0:T(8,128)(2,1)S(1)} %get-tuple-element.49), channel_id=1, source_target_pairs={{56,84},{57,85},{58,86},{59,87},{60,80},{61,81},{62,82},{63,83},{4... | collective-permute-start | bytes 98312 | tf_op jit(solution)/shard_map/ppermute | solution.py:340
  17.9 4.9 %collective-permute-start.3 = (bf16[2,64,128]{2,1,0:T(8,128)(2,1)S(1)}, bf16[2,64,128]{2,1,0:T(8,128)(2,1)S(1)}, u32[]{:S(2)}, u32[]{:S(2)}) collective-permute-start(bf16[2,64,128]{2,1,0:T(8,128)(2,1)S(1)} %get-tuple-element.49), channel_id=1, source_target_pairs={{56,80},{57,81},{58,82},{59,83},{60,84},{61,85},{62,86},{63,87},{4... | collective-permute-start | bytes 98312 | tf_op jit(solution)/shard_map/ppermute | solution.py:339
  22.8 1.9 %collective-permute-start.1 = (bf16[2,64,128]{2,1,0:T(8,128)(2,1)S(1)}, bf16[2,64,128]{2,1,0:T(8,128)(2,1)S(1)}, u32[]{:S(2)}, u32[]{:S(2)}) collective-permute-start(bf16[2,64,128]{2,1,0:T(8,128)(2,1)S(1)} %get-tuple-element.50), channel_id=1, source_target_pairs={{0,8},{8,0},{16,24},{24,16},{32,40},{40,32},{48,56},{56,48},{64,72... | collective-permute-start | bytes 98312 | tf_op jit(solution)/shard_map/ppermute | solution.py:335
  24.8 1.0 slice_bitcast_fusion.14
  26.0 4.0 %collective-permute-start.2 = (bf16[2,2,64,128]{3,2,1,0:T(8,128)(2,1)S(1)}, bf16[2,2,64,128]{3,2,1,0:T(8,128)(2,1)S(1)}, u32[]{:S(2)}, u32[]{:S(2)}) collective-permute-start(bf16[2,2,64,128]{3,2,1,0:T(8,128)(2,1)S(1)} %broadcast_select_fusion.4), channel_id=1, source_target_pairs={{0,4},{1,5},{2,6},{3,7},{4,0},{5,1},{6,2},{7,3},{8,12},{9,13},{10,... | collective-permute-start | bytes 196616 | tf_op jit(solution)/shard_map/ppermute | solution.py:336
  30.0 4.8 %collective-permute-done.3 = bf16[2,64,128]{2,1,0:T(8,128)(2,1)S(1)} collective-permute-done((bf16[2,64,128]{2,1,0:T(8,128)(2,1)S(1)}, bf16[2,64,128]{2,1,0:T(8,128)(2,1)S(1)}, u32[]{:S(2)}, u32[]{:S(2)}) %collective-permute-start.3) | collective-permute-done | bytes 32800 | tf_op jit(solution)/shard_map/ppermute | solution.py:339
  35.1 4.6 %collective-permute-start.5 = (bf16[3,2,2,64,128]{4,3,2,1,0:T(8,128)(2,1)S(1)}, bf16[3,2,2,64,128]{4,3,2,1,0:T(8,128)(2,1)S(1)}, u32[]{:S(2)}, u32[]{:S(2)}) collective-permute-start(bf16[3,2,2,64,128]{4,3,2,1,0:T(8,128)(2,1)S(1)} %pad_maximum_fusion.2), channel_id=1, source_target_pairs={{0,2},{1,3},{2,0},{3,1},{4,6},{5,7},{6,4},{7,5},{8,10},{9,11},{10,... | collective-permute-start | bytes 589832 | tf_op jit(solution)/shard_map/ppermute | solution.py:345
  39.7 8.1 %collective-permute-done.5 = bf16[3,2,2,64,128]{4,3,2,1,0:T(8,128)(2,1)S(1)} collective-permute-done((bf16[3,2,2,64,128]{4,3,2,1,0:T(8,128)(2,1)S(1)}, bf16[3,2,2,64,128]{4,3,2,1,0:T(8,128)(2,1)S(1)}, u32[]{:S(2)}, u32[]{:S(2)}) %collective-permute-start.5) | collective-permute-done | bytes 196640 | tf_op jit(solution)/shard_map/ppermute | solution.py:345
  48.0 3.8 %collective-permute-start.6 = (bf16[3,2,2,2,64,128]{5,4,3,2,1,0:T(8,128)(2,1)S(1)}, bf16[3,2,2,2,64,128]{5,4,3,2,1,0:T(8,128)(2,1)S(1)}, u32[]{:S(2)}, u32[]{:S(2)}) collective-permute-start(bf16[3,2,2,2,64,128]{5,4,3,2,1,0:T(8,128)(2,1)S(1)} %broadcast_select_fusion.1), channel_id=1, source_target_pairs={{0,1},{1,0},{2,3},{3,2},{4,5},{5,4},{6,7},{7,6},{8,9},{9,8},{10,11... | collective-permute-start | bytes 1179656 | tf_op jit(solution)/shard_map/ppermute | solution.py:345
  51.8 2.7 %collective-permute-start = (bf16[2,512,128]{2,1,0:T(8,128)(2,1)S(1)}, bf16[2,512,128]{2,1,0:T(8,128)(2,1)S(1)}, u32[]{:S(2)}, u32[]{:S(2)}) collective-permute-start(bf16[2,512,128]{2,1,0:T(8,128)(2,1)S(1)} %maximum_select_fusion), channel_id=1, source_target_pairs={{0,8},{8,0},{16,24},{24,16},{32,40},{40,32},{48,56},{56,48},{64,72... | collective-permute-start | bytes 786440 | tf_op jit(solution)/shard_map/ppermute | solution.py:351
  54.7 5.0 %collective-permute-done.6 = bf16[3,2,2,2,64,128]{5,4,3,2,1,0:T(8,128)(2,1)S(1)} collective-permute-done((bf16[3,2,2,2,64,128]{5,4,3,2,1,0:T(8,128)(2,1)S(1)}, bf16[3,2,2,2,64,128]{5,4,3,2,1,0:T(8,128)(2,1)S(1)}, u32[]{:S(2)}, u32[]{:S(2)}) %collective-permute-start.6) | collective-permute-done | bytes 393248 | tf_op jit(solution)/shard_map/ppermute | solution.py:345
  59.9 1.3 collective-permute-start.7
  61.2 1.3 collective-permute-start.9
  62.5 1.5 convert_reduce_fusion
  64.1 8.0 %collective-permute-start.8 = (bf16[8,2,64,128]{3,2,1,0:T(8,128)(2,1)S(1)}, bf16[8,2,64,128]{3,2,1,0:T(8,128)(2,1)S(1)}, u32[]{:S(2)}, u32[]{:S(2)}) collective-permute-start(bf16[8,2,64,128]{3,2,1,0:T(8,128)(2,1)S(1)} %bitcast.167), channel_id=1, source_target_pairs={{8,0},{48,56},{72,64},{112,120},{136,128},{176,184},{200,192},{240... | collective-permute-start | bytes 786440 | tf_op jit(solution)/shard_map/ppermute | solution.py:364
  72.8 3.3 %own_forward.1 = (f32[1,1024]{1,0:T(1,128)S(1)}, f32[1,1024]{1,0:T(1,128)S(1)}, f32[4,128,256]{2,1,0:T(8,128)S(1)}) custom-call(s32[4]{0:T(128)S(1)} %and_select_fusion.lo_ref, s32[1]{0:T(128)} %bitcast.place_ref, s32[1,1024]{1,0:T(1,128)S(1)} %bitcast.159, bf16[2,512,128]{2,1,0:T(8,128)(2,1)S(1)} %bitcast.154, ...), custom_call_target="tpu_custom_call" | custom-call | flops 201326592 | bytes 4194304 | tf_op jit(solution)/shard_map/own_forward/pallas_call | solution.py:291
  76.5 3.1 %earlier.1 = (bf16[2,512,128]{2,1,0:T(8,128)(2,1)S(1)}, f32[1,1024]{1,0:T(1,128)S(1)}, f32[1,1024]{1,0:T(1,128)S(1)}, f32[4,128,256]{2,1,0:T(8,128)S(1)}, bf16[2...) custom-call(s32[4]{0:T(128)S(1)} %and_select_fusion.lo_ref, s32[1]{0:T(128)} %bitcast.place_ref, ...), custom_call_target="tpu_custom_call" | custom-call | flops 603979776 | bytes 4194304 | tf_op jit(solution)/shard_map/earlier/pallas_call | solution.py:291
  79.6 9.3 %collective-permute-start.12 = (bf16[2,8,2,64,128]{4,3,2,1,0:T(8,128)(2,1)S(1)}, bf16[2,8,2,64,128]{4,3,2,1,0:T(8,128)(2,1)S(1)}, u32[]{:S(2)}, u32[]{:S(2)}) collective-permute-start(bf16[2,8,2,64,128]{4,3,2,1,0:T(8,128)(2,1)S(1)} %get-tuple-element.26), channel_id=1, source_target_pairs={{16,0},{32,16},{48,32},{8,24},{24,40},{40,56},{80,64},{96,80},{112... | collective-permute-start | bytes 1572872 | tf_op jit(solution)/shard_map/ppermute | solution.py:420
  89.7 1.3 collective-permute-start.15
  91.0 1.3 collective-permute-start.13
  92.3 4.3 %own_backward.1 = (bf16[2,512,128]{2,1,0:T(8,128)(2,1)S(1)}, bf16[2,512,128]{2,1,0:T(8,128)(2,1)S(1)}, f32[2,8,2,64,128]{4,3,2,1,0:T(8,128)S(1)}) custom-call(s32[4]{0:T(128)S(1)} %and_select_fusion.lo_ref, s32[1]{0:T(128)} %bitcast.place_ref, s32[1,1024]{1,0:T(1,128)S(1)} %bitcast.161, bf16[2,512,128]{2,1,0:T(8,128)(2,1)S(1)} %bitcast.156, ...), custom_call_target="tpu_custom_call" | custom-call | flops 503316480 | bytes 4194304 | tf_op jit(solution)/shard_map/own_backward/pallas_call | solution.py:291
  97.7 2.3 %collective-permute-done.13 = bf16[8,2,64,128]{3,2,1,0:T(8,128)(2,1)S(1)} collective-permute-done((bf16[8,2,64,128]{3,2,1,0:T(8,128)(2,1)S(1)}, bf16[8,2,64,128]{3,2,1,0:T(8,128)(2,1)S(1)}, u32[]{:S(2)}, u32[]{:S(2)}) %collective-permute-start.13) | collective-permute-done | bytes 262176 | tf_op jit(solution)/shard_map/ppermute | solution.py:419
  100.3 4.9 %collective-permute-start.16 = (bf16[3,4,2,64,128]{4,3,2,1,0:T(8,128)(2,1)S(1)}, bf16[3,4,2,64,128]{4,3,2,1,0:T(8,128)(2,1)S(1)}, u32[]{:S(2)}, u32[]{:S(2)}) collective-permute-start(bf16[3,4,2,64,128]{4,3,2,1,0:T(8,128)(2,1)S(1)} %fusion.3), channel_id=1, source_target_pairs={{0,1},{1,0},{2,3},{3,2},{4,5},{5,4},{6,7},{7,6},{8,9},{9,8},{10,11... | collective-permute-start | bytes 1179656 | tf_op jit(solution)/shard_map/ppermute | solution.py:439
  105.2 6.9 %collective-permute-start.11 = (bf16[2,512,128]{2,1,0:T(8,128)(2,1)S(1)}, bf16[2,512,128]{2,1,0:T(8,128)(2,1)S(1)}, u32[]{:S(2)}, u32[]{:S(2)}) collective-permute-start(bf16[2,512,128]{2,1,0:T(8,128)(2,1)S(1)} %get-tuple-element.24), channel_id=1, source_target_pairs={{0,8},{8,0},{16,24},{24,16},{32,40},{40,32},{48,56},{56,48},{64,72... | collective-permute-start | bytes 786440 | tf_op jit(solution)/shard_map/ppermute | solution.py:455
  112.3 5.0 %collective-permute-start.17 = (bf16[3,2,2,64,128]{4,3,2,1,0:T(8,128)(2,1)S(1)}, bf16[3,2,2,64,128]{4,3,2,1,0:T(8,128)(2,1)S(1)}, u32[]{:S(2)}, u32[]{:S(2)}) collective-permute-start(bf16[3,2,2,64,128]{4,3,2,1,0:T(8,128)(2,1)S(1)} %fusion.10), channel_id=1, source_target_pairs={{0,2},{1,3},{2,0},{3,1},{4,6},{5,7},{6,4},{7,5},{8,10},{9,11},{10,... | collective-permute-start | bytes 589832 | tf_op jit(solution)/shard_map/ppermute | solution.py:439
  117.4 5.0 %collective-permute-done.17 = bf16[3,2,2,64,128]{4,3,2,1,0:T(8,128)(2,1)S(1)} collective-permute-done((bf16[3,2,2,64,128]{4,3,2,1,0:T(8,128)(2,1)S(1)}, bf16[3,2,2,64,128]{4,3,2,1,0:T(8,128)(2,1)S(1)}, u32[]{:S(2)}, u32[]{:S(2)}) %collective-permute-start.17) | collective-permute-done | bytes 196640 | tf_op jit(solution)/shard_map/ppermute | solution.py:439
  122.6 5.0 %collective-permute-start.18 = (bf16[2,2,64,128]{3,2,1,0:T(8,128)(2,1)S(1)}, bf16[2,2,64,128]{3,2,1,0:T(8,128)(2,1)S(1)}, u32[]{:S(2)}, u32[]{:S(2)}) collective-permute-start(bf16[2,2,64,128]{3,2,1,0:T(8,128)(2,1)S(1)} %slice_bitcast_fusion.17), channel_id=1, source_target_pairs={{0,4},{1,5},{2,6},{3,7},{4,0},{5,1},{6,2},{7,3},{8,12},{9,13},{10,... | collective-permute-start | bytes 196616 | tf_op jit(solution)/shard_map/ppermute | solution.py:443
  127.7 21.8 %collective-permute-start.20 = (bf16[2,64,128]{2,1,0:T(8,128)(2,1)S(1)}, bf16[2,64,128]{2,1,0:T(8,128)(2,1)S(1)}, u32[]{:S(2)}, u32[]{:S(2)}) collective-permute-start(bf16[2,64,128]{2,1,0:T(8,128)(2,1)S(1)} %fusion.19), channel_id=1, source_target_pairs={{80,56},{81,57},{82,58},{83,59},{84,60},{85,61},{86,62},{87,63},{7... | collective-permute-start | bytes 98312 | tf_op jit(solution)/shard_map/ppermute | solution.py:444
  149.5 1.9 %collective-permute-start.21 = (bf16[2,64,128]{2,1,0:T(8,128)(2,1)S(1)}, bf16[2,64,128]{2,1,0:T(8,128)(2,1)S(1)}, u32[]{:S(2)}, u32[]{:S(2)}) collective-permute-start(bf16[2,64,128]{2,1,0:T(8,128)(2,1)S(1)} %slice_bitcast_fusion.18), channel_id=1, source_target_pairs={{84,56},{85,57},{86,58},{87,59},{80,60},{81,61},{82,62},{83,63},{7... | collective-permute-start | bytes 98312 | tf_op jit(solution)/shard_map/ppermute | solution.py:445
  151.5 1.9 %collective-permute-start.19 = (bf16[2,64,128]{2,1,0:T(8,128)(2,1)S(1)}, bf16[2,64,128]{2,1,0:T(8,128)(2,1)S(1)}, u32[]{:S(2)}, u32[]{:S(2)}) collective-permute-start(bf16[2,64,128]{2,1,0:T(8,128)(2,1)S(1)} %fusion.16), channel_id=1, source_target_pairs={{0,8},{8,0},{16,24},{24,16},{32,40},{40,32},{48,56},{56,48},{64,72... | collective-permute-start | bytes 98312 | tf_op jit(solution)/shard_map/ppermute | solution.py:448
  153.4 0.9 maximum_select_fusion.1
  154.3 7.4 %collective-permute-done.21 = bf16[2,64,128]{2,1,0:T(8,128)(2,1)S(1)} collective-permute-done((bf16[2,64,128]{2,1,0:T(8,128)(2,1)S(1)}, bf16[2,64,128]{2,1,0:T(8,128)(2,1)S(1)}, u32[]{:S(2)}, u32[]{:S(2)}) %collective-permute-start.21) | collective-permute-done | bytes 32800 | tf_op jit(solution)/shard_map/ppermute | solution.py:445
  (70 shorter events, 6.9 us)
Async XLA Ops:
  0.6 39.1 %copy-start.1 = (bf16[1,2,512,128]{3,2,1,0:T(8,128)(2,1)S(1)}, bf16[1,2,512,128]{3,2,1,0:T(8,128)(2,1)}, u32[]{:S(2)}) copy-start(bf16[1,2,512,128]{3,2,1,0:T(8,128)(2,1)} %param.8) | copy-start | bytes 786436
  2.2 27.8 %collective-permute-start.4 = (bf16[2,64,128]{2,1,0:T(8,128)(2,1)S(1)}, bf16[2,64,128]{2,1,0:T(8,128)(2,1)S(1)}, u32[]{:S(2)}, u32[]{:S(2)}) collective-permute-start(bf16[2,64,128]{2,1,0:T(8,128)(2,1)S(1)} %get-tuple-element.49), channel_id=1, source_target_pairs={{56,84},{57,85},{58,86},{59,87},{60,80},{61,81},{62,82},{63,83},{4... | collective-permute-start | bytes 98312 | tf_op jit(solution)/shard_map/ppermute | solution.py:340
  17.9 17.0 %collective-permute-start.3 = (bf16[2,64,128]{2,1,0:T(8,128)(2,1)S(1)}, bf16[2,64,128]{2,1,0:T(8,128)(2,1)S(1)}, u32[]{:S(2)}, u32[]{:S(2)}) collective-permute-start(bf16[2,64,128]{2,1,0:T(8,128)(2,1)S(1)} %get-tuple-element.49), channel_id=1, source_target_pairs={{56,80},{57,81},{58,82},{59,83},{60,84},{61,85},{62,86},{63,87},{4... | collective-permute-start | bytes 98312 | tf_op jit(solution)/shard_map/ppermute | solution.py:339
  22.8 3.1 %collective-permute-start.1 = (bf16[2,64,128]{2,1,0:T(8,128)(2,1)S(1)}, bf16[2,64,128]{2,1,0:T(8,128)(2,1)S(1)}, u32[]{:S(2)}, u32[]{:S(2)}) collective-permute-start(bf16[2,64,128]{2,1,0:T(8,128)(2,1)S(1)} %get-tuple-element.50), channel_id=1, source_target_pairs={{0,8},{8,0},{16,24},{24,16},{32,40},{40,32},{48,56},{56,48},{64,72... | collective-permute-start | bytes 98312 | tf_op jit(solution)/shard_map/ppermute | solution.py:335
  25.8 28.7 %copy-start.2 = (s32[65536]{0:T(1024)S(1)}, s32[65536]{0:T(1024)}, u32[]{:S(2)}) copy-start(s32[65536]{0:T(1024)} %param.9) | copy-start | bytes 786436
  26.0 8.9 %collective-permute-start.2 = (bf16[2,2,64,128]{3,2,1,0:T(8,128)(2,1)S(1)}, bf16[2,2,64,128]{3,2,1,0:T(8,128)(2,1)S(1)}, u32[]{:S(2)}, u32[]{:S(2)}) collective-permute-start(bf16[2,2,64,128]{3,2,1,0:T(8,128)(2,1)S(1)} %broadcast_select_fusion.4), channel_id=1, source_target_pairs={{0,4},{1,5},{2,6},{3,7},{4,0},{5,1},{6,2},{7,3},{8,12},{9,13},{10,... | collective-permute-start | bytes 196616 | tf_op jit(solution)/shard_map/ppermute | solution.py:336
  35.1 12.8 %collective-permute-start.5 = (bf16[3,2,2,64,128]{4,3,2,1,0:T(8,128)(2,1)S(1)}, bf16[3,2,2,64,128]{4,3,2,1,0:T(8,128)(2,1)S(1)}, u32[]{:S(2)}, u32[]{:S(2)}) collective-permute-start(bf16[3,2,2,64,128]{4,3,2,1,0:T(8,128)(2,1)S(1)} %pad_maximum_fusion.2), channel_id=1, source_target_pairs={{0,2},{1,3},{2,0},{3,1},{4,6},{5,7},{6,4},{7,5},{8,10},{9,11},{10,... | collective-permute-start | bytes 589832 | tf_op jit(solution)/shard_map/ppermute | solution.py:345
  48.0 11.7 %collective-permute-start.6 = (bf16[3,2,2,2,64,128]{5,4,3,2,1,0:T(8,128)(2,1)S(1)}, bf16[3,2,2,2,64,128]{5,4,3,2,1,0:T(8,128)(2,1)S(1)}, u32[]{:S(2)}, u32[]{:S(2)}) collective-permute-start(bf16[3,2,2,2,64,128]{5,4,3,2,1,0:T(8,128)(2,1)S(1)} %broadcast_select_fusion.1), channel_id=1, source_target_pairs={{0,1},{1,0},{2,3},{3,2},{4,5},{5,4},{6,7},{7,6},{8,9},{9,8},{10,11... | collective-permute-start | bytes 1179656 | tf_op jit(solution)/shard_map/ppermute | solution.py:345
  51.8 21.0 %collective-permute-start = (bf16[2,512,128]{2,1,0:T(8,128)(2,1)S(1)}, bf16[2,512,128]{2,1,0:T(8,128)(2,1)S(1)}, u32[]{:S(2)}, u32[]{:S(2)}) collective-permute-start(bf16[2,512,128]{2,1,0:T(8,128)(2,1)S(1)} %maximum_select_fusion), channel_id=1, source_target_pairs={{0,8},{8,0},{16,24},{24,16},{32,40},{40,32},{48,56},{56,48},{64,72... | collective-permute-start | bytes 786440 | tf_op jit(solution)/shard_map/ppermute | solution.py:351
  59.8 13.0 %copy-start = (bf16[1,2,512,128]{3,2,1,0:T(8,128)(2,1)S(1)}, bf16[1,2,512,128]{3,2,1,0:T(8,128)(2,1)}, u32[]{:S(2)}) copy-start(bf16[1,2,512,128]{3,2,1,0:T(8,128)(2,1)} %param.5) | copy-start | bytes 786436
  59.9 16.2 %collective-permute-start.7 = (bf16[8,2,64,128]{3,2,1,0:T(8,128)(2,1)S(1)}, bf16[8,2,64,128]{3,2,1,0:T(8,128)(2,1)S(1)}, u32[]{:S(2)}, u32[]{:S(2)}) collective-permute-start(bf16[8,2,64,128]{3,2,1,0:T(8,128)(2,1)S(1)} %bitcast.169), channel_id=1, source_target_pairs={{0,32},{16,48},{40,8},{56,24},{64,96},{80,112},{104,72},{120,88},{... | collective-permute-start | bytes 786440 | tf_op jit(solution)/shard_map/ppermute | solution.py:361
  61.2 14.9 %collective-permute-start.9 = (bf16[2,8,2,64,128]{4,3,2,1,0:T(8,128)(2,1)S(1)}, bf16[2,8,2,64,128]{4,3,2,1,0:T(8,128)(2,1)S(1)}, u32[]{:S(2)}, u32[]{:S(2)}) collective-permute-start(bf16[2,8,2,64,128]{4,3,2,1,0:T(8,128)(2,1)S(1)} %bitcast.151), channel_id=1, source_target_pairs={{0,16},{16,32},{32,48},{24,8},{40,24},{56,40},{64,80},{80,96},{96,... | collective-permute-start | bytes 1572872 | tf_op jit(solution)/shard_map/ppermute | solution.py:362
  64.1 12.2 %collective-permute-start.8 = (bf16[8,2,64,128]{3,2,1,0:T(8,128)(2,1)S(1)}, bf16[8,2,64,128]{3,2,1,0:T(8,128)(2,1)S(1)}, u32[]{:S(2)}, u32[]{:S(2)}) collective-permute-start(bf16[8,2,64,128]{3,2,1,0:T(8,128)(2,1)S(1)} %bitcast.167), channel_id=1, source_target_pairs={{8,0},{48,56},{72,64},{112,120},{136,128},{176,184},{200,192},{240... | collective-permute-start | bytes 786440 | tf_op jit(solution)/shard_map/ppermute | solution.py:364
  72.1 4.3 %collective-permute-start.10 = (bf16[8,2,64,128]{3,2,1,0:T(8,128)(2,1)S(1)}, bf16[8,2,64,128]{3,2,1,0:T(8,128)(2,1)S(1)}, u32[]{:S(2)}, u32[]{:S(2)}) collective-permute-start(bf16[8,2,64,128]{3,2,1,0:T(8,128)(2,1)S(1)} %bitcast.168), channel_id=1, source_target_pairs={{16,0},{40,56},{80,64},{104,120},{144,128},{168,184},{208,192},{23... | collective-permute-start | bytes 786440 | tf_op jit(solution)/shard_map/ppermute | solution.py:363
  79.6 17.9 %collective-permute-start.12 = (bf16[2,8,2,64,128]{4,3,2,1,0:T(8,128)(2,1)S(1)}, bf16[2,8,2,64,128]{4,3,2,1,0:T(8,128)(2,1)S(1)}, u32[]{:S(2)}, u32[]{:S(2)}) collective-permute-start(bf16[2,8,2,64,128]{4,3,2,1,0:T(8,128)(2,1)S(1)} %get-tuple-element.26), channel_id=1, source_target_pairs={{16,0},{32,16},{48,32},{8,24},{24,40},{40,56},{80,64},{96,80},{112... | collective-permute-start | bytes 1572872 | tf_op jit(solution)/shard_map/ppermute | solution.py:420
  89.0 7.6 %collective-permute-start.14 = (bf16[8,2,64,128]{3,2,1,0:T(8,128)(2,1)S(1)}, bf16[8,2,64,128]{3,2,1,0:T(8,128)(2,1)S(1)}, u32[]{:S(2)}, u32[]{:S(2)}) collective-permute-start(bf16[8,2,64,128]{3,2,1,0:T(8,128)(2,1)S(1)} %get-tuple-element.32), channel_id=1, source_target_pairs={{0,16},{56,40},{64,80},{120,104},{128,144},{184,168},{192,208},{24... | collective-permute-start | bytes 786440 | tf_op jit(solution)/shard_map/ppermute | solution.py:417
  89.7 7.7 %collective-permute-start.15 = (bf16[8,2,64,128]{3,2,1,0:T(8,128)(2,1)S(1)}, bf16[8,2,64,128]{3,2,1,0:T(8,128)(2,1)S(1)}, u32[]{:S(2)}, u32[]{:S(2)}) collective-permute-start(bf16[8,2,64,128]{3,2,1,0:T(8,128)(2,1)S(1)} %get-tuple-element.33), channel_id=1, source_target_pairs={{0,8},{56,48},{64,72},{120,112},{128,136},{184,176},{192,200},{248... | collective-permute-start | bytes 786440 | tf_op jit(solution)/shard_map/ppermute | solution.py:418
  91.0 8.9 %collective-permute-start.13 = (bf16[8,2,64,128]{3,2,1,0:T(8,128)(2,1)S(1)}, bf16[8,2,64,128]{3,2,1,0:T(8,128)(2,1)S(1)}, u32[]{:S(2)}, u32[]{:S(2)}) collective-permute-start(bf16[8,2,64,128]{3,2,1,0:T(8,128)(2,1)S(1)} %get-tuple-element.27), channel_id=1, source_target_pairs={{32,0},{48,16},{8,40},{24,56},{96,64},{112,80},{72,104},{88,120},{... | collective-permute-start | bytes 786440 | tf_op jit(solution)/shard_map/ppermute | solution.py:419
  100.3 11.8 %collective-permute-start.16 = (bf16[3,4,2,64,128]{4,3,2,1,0:T(8,128)(2,1)S(1)}, bf16[3,4,2,64,128]{4,3,2,1,0:T(8,128)(2,1)S(1)}, u32[]{:S(2)}, u32[]{:S(2)}) collective-permute-start(bf16[3,4,2,64,128]{4,3,2,1,0:T(8,128)(2,1)S(1)} %fusion.3), channel_id=1, source_target_pairs={{0,1},{1,0},{2,3},{3,2},{4,5},{5,4},{6,7},{7,6},{8,9},{9,8},{10,11... | collective-permute-start | bytes 1179656 | tf_op jit(solution)/shard_map/ppermute | solution.py:439
  105.2 12.2 %collective-permute-start.11 = (bf16[2,512,128]{2,1,0:T(8,128)(2,1)S(1)}, bf16[2,512,128]{2,1,0:T(8,128)(2,1)S(1)}, u32[]{:S(2)}, u32[]{:S(2)}) collective-permute-start(bf16[2,512,128]{2,1,0:T(8,128)(2,1)S(1)} %get-tuple-element.24), channel_id=1, source_target_pairs={{0,8},{8,0},{16,24},{24,16},{32,40},{40,32},{48,56},{56,48},{64,72... | collective-permute-start | bytes 786440 | tf_op jit(solution)/shard_map/ppermute | solution.py:455
  112.3 10.1 %collective-permute-start.17 = (bf16[3,2,2,64,128]{4,3,2,1,0:T(8,128)(2,1)S(1)}, bf16[3,2,2,64,128]{4,3,2,1,0:T(8,128)(2,1)S(1)}, u32[]{:S(2)}, u32[]{:S(2)}) collective-permute-start(bf16[3,2,2,64,128]{4,3,2,1,0:T(8,128)(2,1)S(1)} %fusion.10), channel_id=1, source_target_pairs={{0,2},{1,3},{2,0},{3,1},{4,6},{5,7},{6,4},{7,5},{8,10},{9,11},{10,... | collective-permute-start | bytes 589832 | tf_op jit(solution)/shard_map/ppermute | solution.py:439
  122.6 28.8 %collective-permute-start.18 = (bf16[2,2,64,128]{3,2,1,0:T(8,128)(2,1)S(1)}, bf16[2,2,64,128]{3,2,1,0:T(8,128)(2,1)S(1)}, u32[]{:S(2)}, u32[]{:S(2)}) collective-permute-start(bf16[2,2,64,128]{3,2,1,0:T(8,128)(2,1)S(1)} %slice_bitcast_fusion.17), channel_id=1, source_target_pairs={{0,4},{1,5},{2,6},{3,7},{4,0},{5,1},{6,2},{7,3},{8,12},{9,13},{10,... | collective-permute-start | bytes 196616 | tf_op jit(solution)/shard_map/ppermute | solution.py:443
  127.7 26.6 %collective-permute-start.20 = (bf16[2,64,128]{2,1,0:T(8,128)(2,1)S(1)}, bf16[2,64,128]{2,1,0:T(8,128)(2,1)S(1)}, u32[]{:S(2)}, u32[]{:S(2)}) collective-permute-start(bf16[2,64,128]{2,1,0:T(8,128)(2,1)S(1)} %fusion.19), channel_id=1, source_target_pairs={{80,56},{81,57},{82,58},{83,59},{84,60},{85,61},{86,62},{87,63},{7... | collective-permute-start | bytes 98312 | tf_op jit(solution)/shard_map/ppermute | solution.py:444
  149.5 12.2 %collective-permute-start.21 = (bf16[2,64,128]{2,1,0:T(8,128)(2,1)S(1)}, bf16[2,64,128]{2,1,0:T(8,128)(2,1)S(1)}, u32[]{:S(2)}, u32[]{:S(2)}) collective-permute-start(bf16[2,64,128]{2,1,0:T(8,128)(2,1)S(1)} %slice_bitcast_fusion.18), channel_id=1, source_target_pairs={{84,56},{85,57},{86,58},{87,59},{80,60},{81,61},{82,62},{83,63},{7... | collective-permute-start | bytes 98312 | tf_op jit(solution)/shard_map/ppermute | solution.py:445
  151.5 10.2 %collective-permute-start.19 = (bf16[2,64,128]{2,1,0:T(8,128)(2,1)S(1)}, bf16[2,64,128]{2,1,0:T(8,128)(2,1)S(1)}, u32[]{:S(2)}, u32[]{:S(2)}) collective-permute-start(bf16[2,64,128]{2,1,0:T(8,128)(2,1)S(1)} %fusion.16), channel_id=1, source_target_pairs={{0,8},{8,0},{16,24},{24,16},{32,40},{40,32},{48,56},{56,48},{64,72... | collective-permute-start | bytes 98312 | tf_op jit(solution)/shard_map/ppermute | solution.py:448

commit v6 on v5

--- a/solution.py
+++ b/solution.py
@@ -36,7 +36,17 @@
     return [(d, d ^ bit) for d in range(ctx * heads)]
 
 
-def edge_pairs(ctx, heads, flip):
+def holder_pairs(ctx, heads, bit):
+    holders = [r for r in range(GROUP) if r < REACH or r >= GROUP - REACH]
+    return [
+        ((base + r) * heads + h, (base + r) * heads + (h ^ bit))
+        for base in range(0, ctx, GROUP)
+        for r in holders
+        for h in range(heads)
+    ]
+
+
+def edge_pairs(ctx, heads):
     moves = []
     for base in range(0, ctx, GROUP):
         for k in range(REACH):
@@ -48,7 +58,7 @@
             if base > 0:
                 moves.append((base + k, base - REACH + k))
     return [
-        (a * heads + h, b * heads + (h ^ flip)) for a, b in moves for h in range(heads)
+        (a * heads + h, b * heads + heads - 1 - h) for a, b in moves for h in range(heads)
     ]
 
 
@@ -325,27 +335,23 @@
     sends_lower = place >= GROUP - REACH
     head = lax.axis_index("head")
     bits = folds(heads)
-    far_bit = bits[0]
     high = {bit: (head & bit) != 0 for bit in bits}
-    straight, crossing = edge_pairs(ctx, heads, 0), edge_pairs(ctx, heads, far_bit)
+    edge = edge_pairs(ctx, heads)
 
     lower = jnp.stack([key_states[0, 0], value_states[0, 0]])
     upper = jnp.stack([key_states[0, 1], value_states[0, 1]])
     leaving = pick(sends_lower, upper, lower)
     half = by_bit(core, pick(even, upper, lower), lax.ppermute(pick(even, lower, upper), CTX, swap), 0)
-    kv_own = by_bit(high[far_bit], half, lax.ppermute(half, everywhere, head_pairs(ctx, heads, far_bit)), 1)
-    kv_edge = by_bit(
-        high[far_bit],
-        lax.ppermute(leaving, everywhere, straight),
-        lax.ppermute(leaving, everywhere, crossing),
-        0,
-    )
-    kv_all = jnp.concatenate([kv_own, kv_edge[None]])
-    for k, bit in enumerate(bits[1:]):
-        other = lax.ppermute(kv_all, everywhere, head_pairs(ctx, heads, bit))
-        kv_all = by_bit(high[bit], kv_all, other, 2 + k)
-    kv_all = kv_all.reshape((3, heads) + half.shape[1:])
-    kv_own, kv_edge = kv_all[:2], kv_all[2]
+    half, leaving = lax.optimization_barrier((half, leaving))
+    kv_own, kv_edge = half, lax.ppermute(leaving, everywhere, edge)
+    for k, bit in enumerate(bits):
+        other = lax.ppermute(kv_own, everywhere, head_pairs(ctx, heads, bit))
+        kv_own = by_bit(high[bit], kv_own, other, 1 + k)
+    for k, bit in enumerate(bits):
+        other = lax.ppermute(kv_edge, everywhere, holder_pairs(ctx, heads, bit))
+        kv_edge = by_bit(~high[bit], kv_edge, other, k)
+    kv_own = kv_own.reshape((2, heads) + half.shape[1:])
+    kv_edge = kv_edge.reshape((heads,) + half.shape[1:])
 
     queries, out_grad = queries[0], out_grad[0]
     far = lax.ppermute(
@@ -428,22 +434,22 @@
     )(lo, places, start, queries, out_grad, far, kv_own, attended, lse, delta, acc)
 
     edge_sum = jnp.where(edge_next, p_next.astype(f32), 0.0) + r_edge1 + r_edge2
+    for bit in reversed(bits):
+        halves = edge_sum.reshape((-1, 2) + half.shape[1:])
+        away = pick(high[bit], halves[:, 0], halves[:, 1]).astype(bf16)
+        other = lax.ppermute(away, everywhere, holder_pairs(ctx, heads, bit))
+        edge_sum = pick(high[bit], halves[:, 1], halves[:, 0]) + other.astype(f32)
+    returned = lax.ppermute(edge_sum[0].astype(bf16), everywhere, inverse(edge)).astype(f32)
+
     sums = p_own + r_near
     first_sum, second_sum = sums[0], sums[1] + r_next
-    sums = jnp.stack(
-        [pick(even, second_sum, first_sum), pick(even, first_sum, second_sum), edge_sum]
-    )
-    for bit in reversed(bits[1:]):
-        halves = sums.reshape((3, -1, 2) + half.shape[1:])
+    sums = jnp.stack([pick(even, second_sum, first_sum), pick(even, first_sum, second_sum)])
+    for bit in reversed(bits):
+        halves = sums.reshape((2, -1, 2) + half.shape[1:])
         away = pick(high[bit], halves[:, :, 1], halves[:, :, 0]).astype(bf16)
         other = lax.ppermute(away, everywhere, head_pairs(ctx, heads, bit))
         sums = pick(high[bit], halves[:, :, 0], halves[:, :, 1]) + other.astype(f32)
-    stays, away = pick(high[far_bit], sums[:, 0], sums[:, 1]), pick(high[far_bit], sums[:, 1], sums[:, 0])
-    away = away.astype(bf16)
-    other = lax.ppermute(away[:2], everywhere, head_pairs(ctx, heads, far_bit))
-    returned = lax.ppermute(stays[2].astype(bf16), everywhere, inverse(straight)).astype(f32)
-    returned += lax.ppermute(away[2], everywhere, inverse(crossing)).astype(f32)
-    stays = stays[:2] + other.astype(f32)
+    stays = sums[:, 0]
     own_half = pick(even, stays[1], stays[0])
     far_half = lax.ppermute(
         pick(even, stays[0], stays[1]).astype(bf16), CTX, swap

time: 163 us -> 158 us (0.969)
  the two profiles are of different devices: /device:TPU:7 before, /device:TPU:6 now
where the time goes in v6:
time: 158 us; the launch traced here: 156 us
  starting transfers between devices  103 us (65%)
  waiting for transfers between devices  32.3 us (20%)
  Pallas kernels  11.5 us (7%)
  other arithmetic  4.96 us (3%)
  local copies, waits for them, and re-layouts  3.31 us (2%)
    ppermute x3, starting transfers between devices, body(): other = lax.ppermute(kv_own, everywhere, head_pairs(ctx, heads, bit))  19.6 us
    ppermute x3, starting transfers between devices, body(): other = lax.ppermute(kv_edge, everywhere, holder_pairs(ctx, heads, bit))  16.2 us
    ppermute x3, waiting for transfers between devices, body(): other = lax.ppermute(away, everywhere, head_pairs(ctx, heads, bit))  13.8 us
    ppermute x1, starting transfers between devices, body(): kv_own, kv_edge = (half, lax.ppermute(leaving, everywhere, edge))  11.7 us
    pallas_call x3, Pallas kernels, call(): pl.pallas_call(kernel, out_shape=outputs, in_specs=[pl.BlockSpec(memory_s...  11.5 us
    ppermute x3, starting transfers between devices, body(): other = lax.ppermute(away, everywhere, head_pairs(ctx, heads, bit))  11.4 us
    ppermute x3, starting transfers between devices, body(): other = lax.ppermute(away, everywhere, holder_pairs(ctx, heads, bit))  8.53 us
    ppermute x1, starting transfers between devices, body(): back = lax.ppermute(out_far, CTX, swap)  6.6 us
  transfers between devices with their start and end apart: 26, of which 9 were waited for; matrix products, arithmetic and copies ran while one was open for 4% of the time, Pallas kernels for 5%

profile of v6, /device:TPU:6, one launch (start us, length us, event | category | flops | bytes accessed | tf_op | source)
XLA Modules:
  0.0 156.1 jit_solution(6883737022129976575)
XLA Ops:
  2.2 1.9 %collective-permute-start.1 = (bf16[2,64,128]{2,1,0:T(8,128)(2,1)S(1)}, bf16[2,64,128]{2,1,0:T(8,128)(2,1)S(1)}, u32[]{:S(2)}, u32[]{:S(2)}) collective-permute-start(bf16[2,64,128]{2,1,0:T(8,128)(2,1)S(1)} %get-tuple-element.53), channel_id=1, source_target_pairs={{0,8},{8,0},{16,24},{24,16},{32,40},{40,32},{48,56},{56,48},{64,72... | collective-permute-start | bytes 98312 | tf_op jit(solution)/shard_map/ppermute | solution.py:344
  5.2 2.4 %collective-permute-start = (bf16[2,512,128]{2,1,0:T(8,128)(2,1)S(1)}, bf16[2,512,128]{2,1,0:T(8,128)(2,1)S(1)}, u32[]{:S(2)}, u32[]{:S(2)}) collective-permute-start(bf16[2,512,128]{2,1,0:T(8,128)(2,1)S(1)} %maximum_select_fusion), channel_id=1, source_target_pairs={{0,8},{8,0},{16,24},{24,16},{32,40},{40,32},{48,56},{56,48},{64,72... | collective-permute-start | bytes 786440 | tf_op jit(solution)/shard_map/ppermute | solution.py:357
  9.4 9.1 %collective-permute-start.2 = (bf16[2,2,64,128]{3,2,1,0:T(8,128)(2,1)S(1)}, bf16[2,2,64,128]{3,2,1,0:T(8,128)(2,1)S(1)}, u32[]{:S(2)}, u32[]{:S(2)}) collective-permute-start(bf16[2,2,64,128]{3,2,1,0:T(8,128)(2,1)S(1)} %broadcast_select_fusion.6), channel_id=1, source_target_pairs={{0,4},{1,5},{2,6},{3,7},{4,0},{5,1},{6,2},{7,3},{8,12},{9,13},{10,... | collective-permute-start | bytes 196616 | tf_op jit(solution)/shard_map/ppermute | solution.py:348
  18.6 2.2 %collective-permute-done.2 = bf16[2,2,64,128]{3,2,1,0:T(8,128)(2,1)S(1)} collective-permute-done((bf16[2,2,64,128]{3,2,1,0:T(8,128)(2,1)S(1)}, bf16[2,2,64,128]{3,2,1,0:T(8,128)(2,1)S(1)}, u32[]{:S(2)}, u32[]{:S(2)}) %collective-permute-start.2) | collective-permute-done | bytes 65568 | tf_op jit(solution)/shard_map/ppermute | solution.py:348
  20.9 6.4 %collective-permute-start.3 = (bf16[2,2,2,64,128]{4,3,2,1,0:T(8,128)(2,1)S(1)}, bf16[2,2,2,64,128]{4,3,2,1,0:T(8,128)(2,1)S(1)}, u32[]{:S(2)}, u32[]{:S(2)}) collective-permute-start(bf16[2,2,2,64,128]{4,3,2,1,0:T(8,128)(2,1)S(1)} %broadcast_select_fusion.4), channel_id=1, source_target_pairs={{0,2},{1,3},{2,0},{3,1},{4,6},{5,7},{6,4},{7,5},{8,10},{9,11},{10,... | collective-permute-start | bytes 393224 | tf_op jit(solution)/shard_map/ppermute | solution.py:348
  27.3 11.7 %collective-permute-start.5 = (bf16[2,64,128]{2,1,0:T(8,128)(2,1)S(1)}, bf16[2,64,128]{2,1,0:T(8,128)(2,1)S(1)}, u32[]{:S(2)}, u32[]{:S(2)}) collective-permute-start(bf16[2,64,128]{2,1,0:T(8,128)(2,1)S(1)} %get-tuple-element.22), channel_id=1, source_target_pairs={{56,87},{57,86},{58,85},{59,84},{60,83},{61,82},{62,81},{63,80},{4... | collective-permute-start | bytes 98312 | tf_op jit(solution)/shard_map/ppermute | solution.py:346
  39.0 2.3 %collective-permute-done.5 = bf16[2,64,128]{2,1,0:T(8,128)(2,1)S(1)} collective-permute-done((bf16[2,64,128]{2,1,0:T(8,128)(2,1)S(1)}, bf16[2,64,128]{2,1,0:T(8,128)(2,1)S(1)}, u32[]{:S(2)}, u32[]{:S(2)}) %collective-permute-start.5) | collective-permute-done | bytes 32800 | tf_op jit(solution)/shard_map/ppermute | solution.py:346
  41.3 9.7 %collective-permute-start.6 = (bf16[2,64,128]{2,1,0:T(8,128)(2,1)S(1)}, bf16[2,64,128]{2,1,0:T(8,128)(2,1)S(1)}, u32[]{:S(2)}, u32[]{:S(2)}) collective-permute-start(bf16[2,64,128]{2,1,0:T(8,128)(2,1)S(1)} %collective-permute-done.5), channel_id=1, source_target_pairs={{0,4},{1,5},{2,6},{3,7},{4,0},{5,1},{6,2},{7,3},{8,12},{9,13},{10,... | collective-permute-start | bytes 98312 | tf_op jit(solution)/shard_map/ppermute | solution.py:351
  51.1 4.2 %collective-permute-start.4 = (bf16[2,2,2,2,64,128]{5,4,3,2,1,0:T(8,128)(2,1)S(1)}, bf16[2,2,2,2,64,128]{5,4,3,2,1,0:T(8,128)(2,1)S(1)}, u32[]{:S(2)}, u32[]{:S(2)}) collective-permute-start(bf16[2,2,2,2,64,128]{5,4,3,2,1,0:T(8,128)(2,1)S(1)} %broadcast_select_fusion.2), channel_id=1, source_target_pairs={{0,1},{1,0},{2,3},{3,2},{4,5},{5,4},{6,7},{7,6},{8,9},{9,8},{10,11... | collective-permute-start | bytes 786440 | tf_op jit(solution)/shard_map/ppermute | solution.py:348
  55.7 4.2 %collective-permute-start.7 = (bf16[2,2,64,128]{3,2,1,0:T(8,128)(2,1)S(1)}, bf16[2,2,64,128]{3,2,1,0:T(8,128)(2,1)S(1)}, u32[]{:S(2)}, u32[]{:S(2)}) collective-permute-start(bf16[2,2,64,128]{3,2,1,0:T(8,128)(2,1)S(1)} %broadcast_select_fusion.5), channel_id=1, source_target_pairs={{0,2},{1,3},{2,0},{3,1},{4,6},{5,7},{6,4},{7,5},{8,10},{9,11},{10,... | collective-permute-start | bytes 196616 | tf_op jit(solution)/shard_map/ppermute | solution.py:351
  59.9 2.3 %collective-permute-done.4 = bf16[2,2,2,2,64,128]{5,4,3,2,1,0:T(8,128)(2,1)S(1)} collective-permute-done((bf16[2,2,2,2,64,128]{5,4,3,2,1,0:T(8,128)(2,1)S(1)}, bf16[2,2,2,2,64,128]{5,4,3,2,1,0:T(8,128)(2,1)S(1)}, u32[]{:S(2)}, u32[]{:S(2)}) %collective-permute-start.4) | collective-permute-done | bytes 262176 | tf_op jit(solution)/shard_map/ppermute | solution.py:348
  64.0 6.1 %collective-permute-start.9 = (bf16[8,2,64,128]{3,2,1,0:T(8,128)(2,1)S(1)}, bf16[8,2,64,128]{3,2,1,0:T(8,128)(2,1)S(1)}, u32[]{:S(2)}, u32[]{:S(2)}) collective-permute-start(bf16[8,2,64,128]{3,2,1,0:T(8,128)(2,1)S(1)} %bitcast.247), channel_id=1, source_target_pairs={{0,32},{16,48},{40,8},{56,24},{64,96},{80,112},{104,72},{120,88},{... | collective-permute-start | bytes 786440 | tf_op jit(solution)/shard_map/ppermute | solution.py:367
  70.2 2.3 %collective-permute-start.8 = (bf16[2,2,2,64,128]{4,3,2,1,0:T(8,128)(2,1)S(1)}, bf16[2,2,2,64,128]{4,3,2,1,0:T(8,128)(2,1)S(1)}, u32[]{:S(2)}, u32[]{:S(2)}) collective-permute-start(bf16[2,2,2,64,128]{4,3,2,1,0:T(8,128)(2,1)S(1)} %broadcast_select_fusion.3), channel_id=1, source_target_pairs={{0,1},{1,0},{2,3},{3,2},{4,5},{5,4},{6,7},{7,6},{8,9},{9,8},{10,11... | collective-permute-start | bytes 393224 | tf_op jit(solution)/shard_map/ppermute | solution.py:351
  72.5 4.6 %collective-permute-done.8 = bf16[2,2,2,64,128]{4,3,2,1,0:T(8,128)(2,1)S(1)} collective-permute-done((bf16[2,2,2,64,128]{4,3,2,1,0:T(8,128)(2,1)S(1)}, bf16[2,2,2,64,128]{4,3,2,1,0:T(8,128)(2,1)S(1)}, u32[]{:S(2)}, u32[]{:S(2)}) %collective-permute-start.8) | collective-permute-done | bytes 131104 | tf_op jit(solution)/shard_map/ppermute | solution.py:351
  79.8 3.3 %own_forward.1 = (f32[1,1024]{1,0:T(1,128)S(1)}, f32[1,1024]{1,0:T(1,128)S(1)}, f32[4,128,256]{2,1,0:T(8,128)S(1)}) custom-call(s32[4]{0:T(128)S(1)} %and_select_fusion.lo_ref, s32[1]{0:T(128)} %bitcast.place_ref, s32[1,1024]{1,0:T(1,128)S(1)} %bitcast.230, bf16[2,512,128]{2,1,0:T(8,128)(2,1)S(1)} %bitcast.225, ...), custom_call_target="tpu_custom_call" | custom-call | flops 201326592 | bytes 4194304 | tf_op jit(solution)/shard_map/own_forward/pallas_call | solution.py:301
  83.3 3.5 %collective-permute-done.12 = bf16[8,2,64,128]{3,2,1,0:T(8,128)(2,1)S(1)} collective-permute-done((bf16[8,2,64,128]{3,2,1,0:T(8,128)(2,1)S(1)}, bf16[8,2,64,128]{3,2,1,0:T(8,128)(2,1)S(1)}, u32[]{:S(2)}, u32[]{:S(2)}) %collective-permute-start.12) | collective-permute-done | bytes 262176 | tf_op jit(solution)/shard_map/ppermute | solution.py:369
  86.9 3.9 %earlier.1 = (bf16[2,512,128]{2,1,0:T(8,128)(2,1)S(1)}, f32[1,1024]{1,0:T(1,128)S(1)}, f32[1,1024]{1,0:T(1,128)S(1)}, f32[4,128,256]{2,1,0:T(8,128)S(1)}, bf16[2...) custom-call(s32[4]{0:T(128)S(1)} %and_select_fusion.lo_ref, s32[1]{0:T(128)} %bitcast.place_ref, ...), custom_call_target="tpu_custom_call" | custom-call | flops 603979776 | bytes 4194304 | tf_op jit(solution)/shard_map/earlier/pallas_call | solution.py:301
  90.9 2.9 %collective-permute-start.20 = (bf16[8,2,64,128]{3,2,1,0:T(8,128)(2,1)S(1)}, bf16[8,2,64,128]{3,2,1,0:T(8,128)(2,1)S(1)}, u32[]{:S(2)}, u32[]{:S(2)}) collective-permute-start(bf16[8,2,64,128]{3,2,1,0:T(8,128)(2,1)S(1)} %get-tuple-element.36), channel_id=1, source_target_pairs={{0,16},{56,40},{64,80},{120,104},{128,144},{184,168},{192,208},{24... | collective-permute-start | bytes 786440 | tf_op jit(solution)/shard_map/ppermute | solution.py:423
  97.7 4.3 %own_backward.1 = (bf16[2,512,128]{2,1,0:T(8,128)(2,1)S(1)}, bf16[2,512,128]{2,1,0:T(8,128)(2,1)S(1)}, f32[2,8,2,64,128]{4,3,2,1,0:T(8,128)S(1)}) custom-call(s32[4]{0:T(128)S(1)} %and_select_fusion.lo_ref, s32[1]{0:T(128)} %bitcast.place_ref, s32[1,1024]{1,0:T(1,128)S(1)} %bitcast.232, bf16[2,512,128]{2,1,0:T(8,128)(2,1)S(1)} %bitcast.227, ...), custom_call_target="tpu_custom_call" | custom-call | flops 503316480 | bytes 4194304 | tf_op jit(solution)/shard_map/own_backward/pallas_call | solution.py:301
  102.2 2.3 %collective-permute-start.22 = (bf16[4,2,64,128]{3,2,1,0:T(8,128)(2,1)S(1)}, bf16[4,2,64,128]{3,2,1,0:T(8,128)(2,1)S(1)}, u32[]{:S(2)}, u32[]{:S(2)}) collective-permute-start(bf16[4,2,64,128]{3,2,1,0:T(8,128)(2,1)S(1)} %fusion.15), channel_id=1, source_target_pairs={{0,1},{1,0},{2,3},{3,2},{4,5},{5,4},{6,7},{7,6},{8,9},{9,8},{10,11... | collective-permute-start | bytes 393224 | tf_op jit(solution)/shard_map/ppermute | solution.py:440
  104.5 6.6 %collective-permute-start.13 = (bf16[2,512,128]{2,1,0:T(8,128)(2,1)S(1)}, bf16[2,512,128]{2,1,0:T(8,128)(2,1)S(1)}, u32[]{:S(2)}, u32[]{:S(2)}) collective-permute-start(bf16[2,512,128]{2,1,0:T(8,128)(2,1)S(1)} %get-tuple-element.28), channel_id=1, source_target_pairs={{0,8},{8,0},{16,24},{24,16},{32,40},{40,32},{48,56},{56,48},{64,72... | collective-permute-start | bytes 786440 | tf_op jit(solution)/shard_map/ppermute | solution.py:461
  111.2 2.9 %collective-permute-start.23 = (bf16[2,2,64,128]{3,2,1,0:T(8,128)(2,1)S(1)}, bf16[2,2,64,128]{3,2,1,0:T(8,128)(2,1)S(1)}, u32[]{:S(2)}, u32[]{:S(2)}) collective-permute-start(bf16[2,2,64,128]{3,2,1,0:T(8,128)(2,1)S(1)} %fusion.24), channel_id=1, source_target_pairs={{0,2},{1,3},{2,0},{3,1},{4,6},{5,7},{6,4},{7,5},{8,10},{9,11},{10,... | collective-permute-start | bytes 196616 | tf_op jit(solution)/shard_map/ppermute | solution.py:440
  114.5 2.4 %collective-permute-start.16 = (bf16[2,4,2,64,128]{4,3,2,1,0:T(8,128)(2,1)S(1)}, bf16[2,4,2,64,128]{4,3,2,1,0:T(8,128)(2,1)S(1)}, u32[]{:S(2)}, u32[]{:S(2)}) collective-permute-start(bf16[2,4,2,64,128]{4,3,2,1,0:T(8,128)(2,1)S(1)} %fusion.6), channel_id=1, source_target_pairs={{0,1},{1,0},{2,3},{3,2},{4,5},{5,4},{6,7},{7,6},{8,9},{9,8},{10,11... | collective-permute-start | bytes 786440 | tf_op jit(solution)/shard_map/ppermute | solution.py:450
  116.9 3.5 %collective-permute-done.23 = bf16[2,2,64,128]{3,2,1,0:T(8,128)(2,1)S(1)} collective-permute-done((bf16[2,2,64,128]{3,2,1,0:T(8,128)(2,1)S(1)}, bf16[2,2,64,128]{3,2,1,0:T(8,128)(2,1)S(1)}, u32[]{:S(2)}, u32[]{:S(2)}) %collective-permute-start.23) | collective-permute-done | bytes 65568 | tf_op jit(solution)/shard_map/ppermute | solution.py:440
  120.5 5.4 %collective-permute-done.16 = bf16[2,4,2,64,128]{4,3,2,1,0:T(8,128)(2,1)S(1)} collective-permute-done((bf16[2,4,2,64,128]{4,3,2,1,0:T(8,128)(2,1)S(1)}, bf16[2,4,2,64,128]{4,3,2,1,0:T(8,128)(2,1)S(1)}, u32[]{:S(2)}, u32[]{:S(2)}) %collective-permute-start.16) | collective-permute-done | bytes 262176 | tf_op jit(solution)/shard_map/ppermute | solution.py:450
  125.9 3.4 %collective-permute-start.17 = (bf16[2,2,2,64,128]{4,3,2,1,0:T(8,128)(2,1)S(1)}, bf16[2,2,2,64,128]{4,3,2,1,0:T(8,128)(2,1)S(1)}, u32[]{:S(2)}, u32[]{:S(2)}) collective-permute-start(bf16[2,2,2,64,128]{4,3,2,1,0:T(8,128)(2,1)S(1)} %fusion.14), channel_id=1, source_target_pairs={{0,2},{1,3},{2,0},{3,1},{4,6},{5,7},{6,4},{7,5},{8,10},{9,11},{10,... | collective-permute-start | bytes 393224 | tf_op jit(solution)/shard_map/ppermute | solution.py:450
  129.3 3.4 %collective-permute-start.24 = (bf16[1,2,64,128]{3,2,1,0:T(8,128)(2,1)S(1)}, bf16[1,2,64,128]{3,2,1,0:T(8,128)(2,1)S(1)}, u32[]{:S(2)}, u32[]{:S(2)}) collective-permute-start(bf16[1,2,64,128]{3,2,1,0:T(8,128)(2,1)S(1)} %fusion.27), channel_id=1, source_target_pairs={{0,4},{1,5},{2,6},{3,7},{4,0},{5,1},{6,2},{7,3},{8,12},{9,13},{10,... | collective-permute-start | bytes 98312 | tf_op jit(solution)/shard_map/ppermute | solution.py:440
  132.7 3.7 %collective-permute-done.17 = bf16[2,2,2,64,128]{4,3,2,1,0:T(8,128)(2,1)S(1)} collective-permute-done((bf16[2,2,2,64,128]{4,3,2,1,0:T(8,128)(2,1)S(1)}, bf16[2,2,2,64,128]{4,3,2,1,0:T(8,128)(2,1)S(1)}, u32[]{:S(2)}, u32[]{:S(2)}) %collective-permute-start.17) | collective-permute-done | bytes 131104 | tf_op jit(solution)/shard_map/ppermute | solution.py:450
  136.5 5.7 %collective-permute-start.18 = (bf16[2,1,2,64,128]{4,3,2,0,1:T(8,128)(2,1)S(1)}, bf16[2,1,2,64,128]{4,3,2,0,1:T(8,128)(2,1)S(1)}, u32[]{:S(2)}, u32[]{:S(2)}) collective-permute-start(bf16[2,1,2,64,128]{4,3,2,0,1:T(8,128)(2,1)S(1)} %fusion.23), channel_id=1, source_target_pairs={{0,4},{1,5},{2,6},{3,7},{4,0},{5,1},{6,2},{7,3},{8,12},{9,13},{10,... | collective-permute-start | bytes 196616 | tf_op jit(solution)/shard_map/ppermute | solution.py:450
  142.2 1.9 %collective-permute-start.25 = (bf16[2,64,128]{2,1,0:T(8,128)(2,1)S(1)}, bf16[2,64,128]{2,1,0:T(8,128)(2,1)S(1)}, u32[]{:S(2)}, u32[]{:S(2)}) collective-permute-start(bf16[2,64,128]{2,1,0:T(8,128)(2,1)S(1)} %fusion.29), channel_id=1, source_target_pairs={{87,56},{86,57},{85,58},{84,59},{83,60},{82,61},{81,62},{80,63},{7... | collective-permute-start | bytes 98312 | tf_op jit(solution)/shard_map/ppermute | solution.py:442
  144.1 4.8 %collective-permute-done.18 = bf16[2,1,2,64,128]{4,3,2,0,1:T(8,128)(2,1)S(1)} collective-permute-done((bf16[2,1,2,64,128]{4,3,2,0,1:T(8,128)(2,1)S(1)}, bf16[2,1,2,64,128]{4,3,2,0,1:T(8,128)(2,1)S(1)}, u32[]{:S(2)}, u32[]{:S(2)}) %collective-permute-start.18) | collective-permute-done | bytes 65568 | tf_op jit(solution)/shard_map/ppermute | solution.py:450
  149.0 5.6 %collective-permute-start.19 = (bf16[2,64,128]{2,1,0:T(8,128)(2,1)S(1)}, bf16[2,64,128]{2,1,0:T(8,128)(2,1)S(1)}, u32[]{:S(2)}, u32[]{:S(2)}) collective-permute-start(bf16[2,64,128]{2,1,0:T(8,128)(2,1)S(1)} %fusion.28), channel_id=1, source_target_pairs={{0,8},{8,0},{16,24},{24,16},{32,40},{40,32},{48,56},{56,48},{64,72... | collective-permute-start | bytes 98312 | tf_op jit(solution)/shard_map/ppermute | solution.py:454
  (87 shorter events, 16.1 us)
Async XLA Ops:
  0.6 4.5 %copy-start.1 = (bf16[1,2,512,128]{3,2,1,0:T(8,128)(2,1)S(1)}, bf16[1,2,512,128]{3,2,1,0:T(8,128)(2,1)}, u32[]{:S(2)}) copy-start(bf16[1,2,512,128]{3,2,1,0:T(8,128)(2,1)} %param.8) | copy-start | bytes 786436
  1.4 6.3 %copy-start.2 = (s32[65536]{0:T(1024)S(1)}, s32[65536]{0:T(1024)}, u32[]{:S(2)}) copy-start(s32[65536]{0:T(1024)} %param.9) | copy-start | bytes 786436
  2.2 7.1 %collective-permute-start.1 = (bf16[2,64,128]{2,1,0:T(8,128)(2,1)S(1)}, bf16[2,64,128]{2,1,0:T(8,128)(2,1)S(1)}, u32[]{:S(2)}, u32[]{:S(2)}) collective-permute-start(bf16[2,64,128]{2,1,0:T(8,128)(2,1)S(1)} %get-tuple-element.53), channel_id=1, source_target_pairs={{0,8},{8,0},{16,24},{24,16},{32,40},{40,32},{48,56},{56,48},{64,72... | collective-permute-start | bytes 98312 | tf_op jit(solution)/shard_map/ppermute | solution.py:344
  5.2 74.6 %collective-permute-start = (bf16[2,512,128]{2,1,0:T(8,128)(2,1)S(1)}, bf16[2,512,128]{2,1,0:T(8,128)(2,1)S(1)}, u32[]{:S(2)}, u32[]{:S(2)}) collective-permute-start(bf16[2,512,128]{2,1,0:T(8,128)(2,1)S(1)} %maximum_select_fusion), channel_id=1, source_target_pairs={{0,8},{8,0},{16,24},{24,16},{32,40},{40,32},{48,56},{56,48},{64,72... | collective-permute-start | bytes 786440 | tf_op jit(solution)/shard_map/ppermute | solution.py:357
  9.4 11.4 %collective-permute-start.2 = (bf16[2,2,64,128]{3,2,1,0:T(8,128)(2,1)S(1)}, bf16[2,2,64,128]{3,2,1,0:T(8,128)(2,1)S(1)}, u32[]{:S(2)}, u32[]{:S(2)}) collective-permute-start(bf16[2,2,64,128]{3,2,1,0:T(8,128)(2,1)S(1)} %broadcast_select_fusion.6), channel_id=1, source_target_pairs={{0,4},{1,5},{2,6},{3,7},{4,0},{5,1},{6,2},{7,3},{8,12},{9,13},{10,... | collective-permute-start | bytes 196616 | tf_op jit(solution)/shard_map/ppermute | solution.py:348
  20.9 30.1 %collective-permute-start.3 = (bf16[2,2,2,64,128]{4,3,2,1,0:T(8,128)(2,1)S(1)}, bf16[2,2,2,64,128]{4,3,2,1,0:T(8,128)(2,1)S(1)}, u32[]{:S(2)}, u32[]{:S(2)}) collective-permute-start(bf16[2,2,2,64,128]{4,3,2,1,0:T(8,128)(2,1)S(1)} %broadcast_select_fusion.4), channel_id=1, source_target_pairs={{0,2},{1,3},{2,0},{3,1},{4,6},{5,7},{6,4},{7,5},{8,10},{9,11},{10,... | collective-permute-start | bytes 393224 | tf_op jit(solution)/shard_map/ppermute | solution.py:348
  27.3 14.0 %collective-permute-start.5 = (bf16[2,64,128]{2,1,0:T(8,128)(2,1)S(1)}, bf16[2,64,128]{2,1,0:T(8,128)(2,1)S(1)}, u32[]{:S(2)}, u32[]{:S(2)}) collective-permute-start(bf16[2,64,128]{2,1,0:T(8,128)(2,1)S(1)} %get-tuple-element.22), channel_id=1, source_target_pairs={{56,87},{57,86},{58,85},{59,84},{60,83},{61,82},{62,81},{63,80},{4... | collective-permute-start | bytes 98312 | tf_op jit(solution)/shard_map/ppermute | solution.py:346
  41.3 14.3 %collective-permute-start.6 = (bf16[2,64,128]{2,1,0:T(8,128)(2,1)S(1)}, bf16[2,64,128]{2,1,0:T(8,128)(2,1)S(1)}, u32[]{:S(2)}, u32[]{:S(2)}) collective-permute-start(bf16[2,64,128]{2,1,0:T(8,128)(2,1)S(1)} %collective-permute-done.5), channel_id=1, source_target_pairs={{0,4},{1,5},{2,6},{3,7},{4,0},{5,1},{6,2},{7,3},{8,12},{9,13},{10,... | collective-permute-start | bytes 98312 | tf_op jit(solution)/shard_map/ppermute | solution.py:351
  51.1 11.1 %collective-permute-start.4 = (bf16[2,2,2,2,64,128]{5,4,3,2,1,0:T(8,128)(2,1)S(1)}, bf16[2,2,2,2,64,128]{5,4,3,2,1,0:T(8,128)(2,1)S(1)}, u32[]{:S(2)}, u32[]{:S(2)}) collective-permute-start(bf16[2,2,2,2,64,128]{5,4,3,2,1,0:T(8,128)(2,1)S(1)} %broadcast_select_fusion.2), channel_id=1, source_target_pairs={{0,1},{1,0},{2,3},{3,2},{4,5},{5,4},{6,7},{7,6},{8,9},{9,8},{10,11... | collective-permute-start | bytes 786440 | tf_op jit(solution)/shard_map/ppermute | solution.py:348
  55.7 14.5 %collective-permute-start.7 = (bf16[2,2,64,128]{3,2,1,0:T(8,128)(2,1)S(1)}, bf16[2,2,64,128]{3,2,1,0:T(8,128)(2,1)S(1)}, u32[]{:S(2)}, u32[]{:S(2)}) collective-permute-start(bf16[2,2,64,128]{3,2,1,0:T(8,128)(2,1)S(1)} %broadcast_select_fusion.5), channel_id=1, source_target_pairs={{0,2},{1,3},{2,0},{3,1},{4,6},{5,7},{6,4},{7,5},{8,10},{9,11},{10,... | collective-permute-start | bytes 196616 | tf_op jit(solution)/shard_map/ppermute | solution.py:351
  62.5 20.6 %collective-permute-start.11 = (bf16[2,8,2,64,128]{4,3,2,1,0:T(8,128)(2,1)S(1)}, bf16[2,8,2,64,128]{4,3,2,1,0:T(8,128)(2,1)S(1)}, u32[]{:S(2)}, u32[]{:S(2)}) collective-permute-start(bf16[2,8,2,64,128]{4,3,2,1,0:T(8,128)(2,1)S(1)} %broadcast_select_fusion.1.kv_own), channel_id=1, source_target_pairs={{0,16},{16,32},{32,48},{24,8},{40,24},{56,40},{64,80},{80,96},{96,... | collective-permute-start | bytes 1572872 | tf_op jit(solution)/shard_map/ppermute | solution.py:368
  64.0 15.8 %copy-start = (bf16[1,2,512,128]{3,2,1,0:T(8,128)(2,1)S(1)}, bf16[1,2,512,128]{3,2,1,0:T(8,128)(2,1)}, u32[]{:S(2)}) copy-start(bf16[1,2,512,128]{3,2,1,0:T(8,128)(2,1)} %param.5) | copy-start | bytes 786436
  64.0 13.0 %collective-permute-start.9 = (bf16[8,2,64,128]{3,2,1,0:T(8,128)(2,1)S(1)}, bf16[8,2,64,128]{3,2,1,0:T(8,128)(2,1)S(1)}, u32[]{:S(2)}, u32[]{:S(2)}) collective-permute-start(bf16[8,2,64,128]{3,2,1,0:T(8,128)(2,1)S(1)} %bitcast.247), channel_id=1, source_target_pairs={{0,32},{16,48},{40,8},{56,24},{64,96},{80,112},{104,72},{120,88},{... | collective-permute-start | bytes 786440 | tf_op jit(solution)/shard_map/ppermute | solution.py:367
  70.2 6.9 %collective-permute-start.8 = (bf16[2,2,2,64,128]{4,3,2,1,0:T(8,128)(2,1)S(1)}, bf16[2,2,2,64,128]{4,3,2,1,0:T(8,128)(2,1)S(1)}, u32[]{:S(2)}, u32[]{:S(2)}) collective-permute-start(bf16[2,2,2,64,128]{4,3,2,1,0:T(8,128)(2,1)S(1)} %broadcast_select_fusion.3), channel_id=1, source_target_pairs={{0,1},{1,0},{2,3},{3,2},{4,5},{5,4},{6,7},{7,6},{8,9},{9,8},{10,11... | collective-permute-start | bytes 393224 | tf_op jit(solution)/shard_map/ppermute | solution.py:351
  77.2 6.1 %collective-permute-start.10 = (bf16[8,2,64,128]{3,2,1,0:T(8,128)(2,1)S(1)}, bf16[8,2,64,128]{3,2,1,0:T(8,128)(2,1)S(1)}, u32[]{:S(2)}, u32[]{:S(2)}) collective-permute-start(bf16[8,2,64,128]{3,2,1,0:T(8,128)(2,1)S(1)} %get-tuple-element.33), channel_id=1, source_target_pairs={{8,0},{48,56},{72,64},{112,120},{136,128},{176,184},{200,192},{240... | collective-permute-start | bytes 786440 | tf_op jit(solution)/shard_map/ppermute | solution.py:370
  78.5 8.3 %collective-permute-start.12 = (bf16[8,2,64,128]{3,2,1,0:T(8,128)(2,1)S(1)}, bf16[8,2,64,128]{3,2,1,0:T(8,128)(2,1)S(1)}, u32[]{:S(2)}, u32[]{:S(2)}) collective-permute-start(bf16[8,2,64,128]{3,2,1,0:T(8,128)(2,1)S(1)} %get-tuple-element.33), channel_id=1, source_target_pairs={{16,0},{40,56},{80,64},{104,120},{144,128},{168,184},{208,192},{23... | collective-permute-start | bytes 786440 | tf_op jit(solution)/shard_map/ppermute | solution.py:369
  90.9 11.1 %collective-permute-start.20 = (bf16[8,2,64,128]{3,2,1,0:T(8,128)(2,1)S(1)}, bf16[8,2,64,128]{3,2,1,0:T(8,128)(2,1)S(1)}, u32[]{:S(2)}, u32[]{:S(2)}) collective-permute-start(bf16[8,2,64,128]{3,2,1,0:T(8,128)(2,1)S(1)} %get-tuple-element.36), channel_id=1, source_target_pairs={{0,16},{56,40},{64,80},{120,104},{128,144},{184,168},{192,208},{24... | collective-permute-start | bytes 786440 | tf_op jit(solution)/shard_map/ppermute | solution.py:423
  93.8 8.2 %collective-permute-start.21 = (bf16[8,2,64,128]{3,2,1,0:T(8,128)(2,1)S(1)}, bf16[8,2,64,128]{3,2,1,0:T(8,128)(2,1)S(1)}, u32[]{:S(2)}, u32[]{:S(2)}) collective-permute-start(bf16[8,2,64,128]{3,2,1,0:T(8,128)(2,1)S(1)} %get-tuple-element.37), channel_id=1, source_target_pairs={{0,8},{56,48},{64,72},{120,112},{128,136},{184,176},{192,200},{248... | collective-permute-start | bytes 786440 | tf_op jit(solution)/shard_map/ppermute | solution.py:424
  95.1 19.0 %collective-permute-start.14 = (bf16[2,8,2,64,128]{4,3,2,1,0:T(8,128)(2,1)S(1)}, bf16[2,8,2,64,128]{4,3,2,1,0:T(8,128)(2,1)S(1)}, u32[]{:S(2)}, u32[]{:S(2)}) collective-permute-start(bf16[2,8,2,64,128]{4,3,2,1,0:T(8,128)(2,1)S(1)} %get-tuple-element.30), channel_id=1, source_target_pairs={{16,0},{32,16},{48,32},{8,24},{24,40},{40,56},{80,64},{96,80},{112... | collective-permute-start | bytes 1572872 | tf_op jit(solution)/shard_map/ppermute | solution.py:426
  96.4 17.8 %collective-permute-start.15 = (bf16[8,2,64,128]{3,2,1,0:T(8,128)(2,1)S(1)}, bf16[8,2,64,128]{3,2,1,0:T(8,128)(2,1)S(1)}, u32[]{:S(2)}, u32[]{:S(2)}) collective-permute-start(bf16[8,2,64,128]{3,2,1,0:T(8,128)(2,1)S(1)} %get-tuple-element.31), channel_id=1, source_target_pairs={{32,0},{48,16},{8,40},{24,56},{96,64},{112,80},{72,104},{88,120},{... | collective-permute-start | bytes 786440 | tf_op jit(solution)/shard_map/ppermute | solution.py:425
  102.2 8.9 %collective-permute-start.22 = (bf16[4,2,64,128]{3,2,1,0:T(8,128)(2,1)S(1)}, bf16[4,2,64,128]{3,2,1,0:T(8,128)(2,1)S(1)}, u32[]{:S(2)}, u32[]{:S(2)}) collective-permute-start(bf16[4,2,64,128]{3,2,1,0:T(8,128)(2,1)S(1)} %fusion.15), channel_id=1, source_target_pairs={{0,1},{1,0},{2,3},{3,2},{4,5},{5,4},{6,7},{7,6},{8,9},{9,8},{10,11... | collective-permute-start | bytes 393224 | tf_op jit(solution)/shard_map/ppermute | solution.py:440
  104.5 12.3 %collective-permute-start.13 = (bf16[2,512,128]{2,1,0:T(8,128)(2,1)S(1)}, bf16[2,512,128]{2,1,0:T(8,128)(2,1)S(1)}, u32[]{:S(2)}, u32[]{:S(2)}) collective-permute-start(bf16[2,512,128]{2,1,0:T(8,128)(2,1)S(1)} %get-tuple-element.28), channel_id=1, source_target_pairs={{0,8},{8,0},{16,24},{24,16},{32,40},{40,32},{48,56},{56,48},{64,72... | collective-permute-start | bytes 786440 | tf_op jit(solution)/shard_map/ppermute | solution.py:461
  111.2 9.2 %collective-permute-start.23 = (bf16[2,2,64,128]{3,2,1,0:T(8,128)(2,1)S(1)}, bf16[2,2,64,128]{3,2,1,0:T(8,128)(2,1)S(1)}, u32[]{:S(2)}, u32[]{:S(2)}) collective-permute-start(bf16[2,2,64,128]{3,2,1,0:T(8,128)(2,1)S(1)} %fusion.24), channel_id=1, source_target_pairs={{0,2},{1,3},{2,0},{3,1},{4,6},{5,7},{6,4},{7,5},{8,10},{9,11},{10,... | collective-permute-start | bytes 196616 | tf_op jit(solution)/shard_map/ppermute | solution.py:440
  114.5 11.3 %collective-permute-start.16 = (bf16[2,4,2,64,128]{4,3,2,1,0:T(8,128)(2,1)S(1)}, bf16[2,4,2,64,128]{4,3,2,1,0:T(8,128)(2,1)S(1)}, u32[]{:S(2)}, u32[]{:S(2)}) collective-permute-start(bf16[2,4,2,64,128]{4,3,2,1,0:T(8,128)(2,1)S(1)} %fusion.6), channel_id=1, source_target_pairs={{0,1},{1,0},{2,3},{3,2},{4,5},{5,4},{6,7},{7,6},{8,9},{9,8},{10,11... | collective-permute-start | bytes 786440 | tf_op jit(solution)/shard_map/ppermute | solution.py:450
  125.9 10.5 %collective-permute-start.17 = (bf16[2,2,2,64,128]{4,3,2,1,0:T(8,128)(2,1)S(1)}, bf16[2,2,2,64,128]{4,3,2,1,0:T(8,128)(2,1)S(1)}, u32[]{:S(2)}, u32[]{:S(2)}) collective-permute-start(bf16[2,2,2,64,128]{4,3,2,1,0:T(8,128)(2,1)S(1)} %fusion.14), channel_id=1, source_target_pairs={{0,2},{1,3},{2,0},{3,1},{4,6},{5,7},{6,4},{7,5},{8,10},{9,11},{10,... | collective-permute-start | bytes 393224 | tf_op jit(solution)/shard_map/ppermute | solution.py:450
  129.3 12.8 %collective-permute-start.24 = (bf16[1,2,64,128]{3,2,1,0:T(8,128)(2,1)S(1)}, bf16[1,2,64,128]{3,2,1,0:T(8,128)(2,1)S(1)}, u32[]{:S(2)}, u32[]{:S(2)}) collective-permute-start(bf16[1,2,64,128]{3,2,1,0:T(8,128)(2,1)S(1)} %fusion.27), channel_id=1, source_target_pairs={{0,4},{1,5},{2,6},{3,7},{4,0},{5,1},{6,2},{7,3},{8,12},{9,13},{10,... | collective-permute-start | bytes 98312 | tf_op jit(solution)/shard_map/ppermute | solution.py:440
  136.5 12.4 %collective-permute-start.18 = (bf16[2,1,2,64,128]{4,3,2,0,1:T(8,128)(2,1)S(1)}, bf16[2,1,2,64,128]{4,3,2,0,1:T(8,128)(2,1)S(1)}, u32[]{:S(2)}, u32[]{:S(2)}) collective-permute-start(bf16[2,1,2,64,128]{4,3,2,0,1:T(8,128)(2,1)S(1)} %fusion.23), channel_id=1, source_target_pairs={{0,4},{1,5},{2,6},{3,7},{4,0},{5,1},{6,2},{7,3},{8,12},{9,13},{10,... | collective-permute-start | bytes 196616 | tf_op jit(solution)/shard_map/ppermute | solution.py:450
  142.2 13.3 %collective-permute-start.25 = (bf16[2,64,128]{2,1,0:T(8,128)(2,1)S(1)}, bf16[2,64,128]{2,1,0:T(8,128)(2,1)S(1)}, u32[]{:S(2)}, u32[]{:S(2)}) collective-permute-start(bf16[2,64,128]{2,1,0:T(8,128)(2,1)S(1)} %fusion.29), channel_id=1, source_target_pairs={{87,56},{86,57},{85,58},{84,59},{83,60},{82,61},{81,62},{80,63},{7... | collective-permute-start | bytes 98312 | tf_op jit(solution)/shard_map/ppermute | solution.py:442
  149.0 6.5 %collective-permute-start.19 = (bf16[2,64,128]{2,1,0:T(8,128)(2,1)S(1)}, bf16[2,64,128]{2,1,0:T(8,128)(2,1)S(1)}, u32[]{:S(2)}, u32[]{:S(2)}) collective-permute-start(bf16[2,64,128]{2,1,0:T(8,128)(2,1)S(1)} %fusion.28), channel_id=1, source_target_pairs={{0,8},{8,0},{16,24},{24,16},{32,40},{40,32},{48,56},{56,48},{64,72... | collective-permute-start | bytes 98312 | tf_op jit(solution)/shard_map/ppermute | solution.py:454

commit v7 on v6

--- a/solution.py
+++ b/solution.py
@@ -342,14 +342,18 @@
     upper = jnp.stack([key_states[0, 1], value_states[0, 1]])
     leaving = pick(sends_lower, upper, lower)
     half = by_bit(core, pick(even, upper, lower), lax.ppermute(pick(even, lower, upper), CTX, swap), 0)
-    half, leaving = lax.optimization_barrier((half, leaving))
-    kv_own, kv_edge = half, lax.ppermute(leaving, everywhere, edge)
+    kv_own = half
     for k, bit in enumerate(bits):
         other = lax.ppermute(kv_own, everywhere, head_pairs(ctx, heads, bit))
+        if k == 0:
+            arrived = lax.ppermute(leaving, everywhere, edge)
+        else:
+            arrived = lax.ppermute(kv_edge, everywhere, holder_pairs(ctx, heads, bits[k - 1]))
+        other, arrived = lax.optimization_barrier((other, arrived))
         kv_own = by_bit(high[bit], kv_own, other, 1 + k)
-    for k, bit in enumerate(bits):
-        other = lax.ppermute(kv_edge, everywhere, holder_pairs(ctx, heads, bit))
-        kv_edge = by_bit(~high[bit], kv_edge, other, k)
+        kv_edge = arrived if k == 0 else by_bit(~high[bits[k - 1]], kv_edge, arrived, k - 1)
+    arrived = lax.ppermute(kv_edge, everywhere, holder_pairs(ctx, heads, bits[-1]))
+    kv_edge = by_bit(~high[bits[-1]], kv_edge, arrived, len(bits) - 1)
     kv_own = kv_own.reshape((2, heads) + half.shape[1:])
     kv_edge = kv_edge.reshape((heads,) + half.shape[1:])
 

time: 158 us -> 158 us (level)
  the two profiles are of different devices: /device:TPU:6 before, /device:TPU:98 now
where the time goes in v7:
time: 158 us; the launch traced here: 157 us
  starting transfers between devices  82.2 us (52%)
  waiting for transfers between devices  46.9 us (30%)
  Pallas kernels  18.1 us (11%)
  other arithmetic  4.98 us (3%)
  local copies, waits for them, and re-layouts  3.32 us (2%)
    pallas_call x3, Pallas kernels, call(): pl.pallas_call(kernel, out_shape=outputs, in_specs=[pl.BlockSpec(memory_s...  18.1 us
    ppermute x1, starting transfers between devices, body(): arrived = lax.ppermute(leaving, everywhere, edge)  13.4 us
    ppermute x3, starting transfers between devices, body(): other = lax.ppermute(away, everywhere, head_pairs(ctx, heads, bit))  11.8 us
    ppermute x3, starting transfers between devices, body(): other = lax.ppermute(away, everywhere, holder_pairs(ctx, heads, bit))  11.3 us
    ppermute x2, waiting for transfers between devices, body(): lax.ppermute(kv_edge, everywhere, holder_pairs(ctx, heads, bits[k - 1]))  11.3 us
    ppermute x3, starting transfers between devices, body(): other = lax.ppermute(kv_own, everywhere, head_pairs(ctx, heads, bit))  11 us
    ppermute x3, waiting for transfers between devices, body(): other = lax.ppermute(away, everywhere, head_pairs(ctx, heads, bit))  9.4 us
    ppermute x1, waiting for transfers between devices, body(): lax.ppermute(edge_sum[0].astype(bf16), everywhere, inverse(edge))  8.63 us
  transfers between devices with their start and end apart: 26, of which 11 were waited for; matrix products, arithmetic and copies ran while one was open for 4% of the time, Pallas kernels for 7%

profile of v7, /device:TPU:98, one launch (start us, length us, event | category | flops | bytes accessed | tf_op | source)
XLA Modules:
  0.0 156.8 jit_solution(8903941387849130611)
XLA Ops:
  2.2 13.4 %collective-permute-start.3 = (bf16[2,64,128]{2,1,0:T(8,128)(2,1)S(1)}, bf16[2,64,128]{2,1,0:T(8,128)(2,1)S(1)}, u32[]{:S(2)}, u32[]{:S(2)}) collective-permute-start(bf16[2,64,128]{2,1,0:T(8,128)(2,1)S(1)} %get-tuple-element.60), channel_id=1, source_target_pairs={{56,87},{57,86},{58,85},{59,84},{60,83},{61,82},{62,81},{63,80},{4... | collective-permute-start | bytes 98312 | tf_op jit(solution)/shard_map/ppermute | solution.py:349
  15.7 2.4 %collective-permute-start.1 = (bf16[2,64,128]{2,1,0:T(8,128)(2,1)S(1)}, bf16[2,64,128]{2,1,0:T(8,128)(2,1)S(1)}, u32[]{:S(2)}, u32[]{:S(2)}) collective-permute-start(bf16[2,64,128]{2,1,0:T(8,128)(2,1)S(1)} %get-tuple-element.61), channel_id=1, source_target_pairs={{0,8},{8,0},{16,24},{24,16},{32,40},{40,32},{48,56},{56,48},{64,72... | collective-permute-start | bytes 98312 | tf_op jit(solution)/shard_map/ppermute | solution.py:344
  19.2 1.9 %collective-permute-start = (bf16[2,512,128]{2,1,0:T(8,128)(2,1)S(1)}, bf16[2,512,128]{2,1,0:T(8,128)(2,1)S(1)}, u32[]{:S(2)}, u32[]{:S(2)}) collective-permute-start(bf16[2,512,128]{2,1,0:T(8,128)(2,1)S(1)} %maximum_select_fusion), channel_id=1, source_target_pairs={{0,8},{8,0},{16,24},{24,16},{32,40},{40,32},{48,56},{56,48},{64,72... | collective-permute-start | bytes 786440 | tf_op jit(solution)/shard_map/ppermute | solution.py:361
  22.9 2.8 %collective-permute-start.2 = (bf16[2,2,64,128]{3,2,1,0:T(8,128)(2,1)S(1)}, bf16[2,2,64,128]{3,2,1,0:T(8,128)(2,1)S(1)}, u32[]{:S(2)}, u32[]{:S(2)}) collective-permute-start(bf16[2,2,64,128]{3,2,1,0:T(8,128)(2,1)S(1)} %broadcast_select_fusion.6), channel_id=1, source_target_pairs={{0,4},{1,5},{2,6},{3,7},{4,0},{5,1},{6,2},{7,3},{8,12},{9,13},{10,... | collective-permute-start | bytes 196616 | tf_op jit(solution)/shard_map/ppermute | solution.py:347
  25.7 7.7 %collective-permute-done.2 = bf16[2,2,64,128]{3,2,1,0:T(8,128)(2,1)S(1)} collective-permute-done((bf16[2,2,64,128]{3,2,1,0:T(8,128)(2,1)S(1)}, bf16[2,2,64,128]{3,2,1,0:T(8,128)(2,1)S(1)}, u32[]{:S(2)}, u32[]{:S(2)}) %collective-permute-start.2) | collective-permute-done | bytes 65568 | tf_op jit(solution)/shard_map/ppermute | solution.py:347
  33.4 4.3 %collective-permute-start.4 = (bf16[2,2,2,64,128]{4,3,2,1,0:T(8,128)(2,1)S(1)}, bf16[2,2,2,64,128]{4,3,2,1,0:T(8,128)(2,1)S(1)}, u32[]{:S(2)}, u32[]{:S(2)}) collective-permute-start(bf16[2,2,2,64,128]{4,3,2,1,0:T(8,128)(2,1)S(1)} %broadcast_select_fusion.4), channel_id=1, source_target_pairs={{0,2},{1,3},{2,0},{3,1},{4,6},{5,7},{6,4},{7,5},{8,10},{9,11},{10,... | collective-permute-start | bytes 393224 | tf_op jit(solution)/shard_map/ppermute | solution.py:347
  37.8 3.6 %collective-permute-start.5 = (bf16[2,64,128]{2,1,0:T(8,128)(2,1)S(1)}, bf16[2,64,128]{2,1,0:T(8,128)(2,1)S(1)}, u32[]{:S(2)}, u32[]{:S(2)}) collective-permute-start(bf16[2,64,128]{2,1,0:T(8,128)(2,1)S(1)} %collective-permute-done.3), channel_id=1, source_target_pairs={{0,4},{1,5},{2,6},{3,7},{4,0},{5,1},{6,2},{7,3},{8,12},{9,13},{10,... | collective-permute-start | bytes 98312 | tf_op jit(solution)/shard_map/ppermute | solution.py:351
  41.6 5.8 %collective-permute-done.5 = bf16[2,64,128]{2,1,0:T(8,128)(2,1)S(1)} collective-permute-done((bf16[2,64,128]{2,1,0:T(8,128)(2,1)S(1)}, bf16[2,64,128]{2,1,0:T(8,128)(2,1)S(1)}, u32[]{:S(2)}, u32[]{:S(2)}) %collective-permute-start.5) | collective-permute-done | bytes 32800 | tf_op jit(solution)/shard_map/ppermute | solution.py:351
  47.6 3.9 %collective-permute-start.6 = (bf16[2,2,2,2,64,128]{5,4,3,2,1,0:T(8,128)(2,1)S(1)}, bf16[2,2,2,2,64,128]{5,4,3,2,1,0:T(8,128)(2,1)S(1)}, u32[]{:S(2)}, u32[]{:S(2)}) collective-permute-start(bf16[2,2,2,2,64,128]{5,4,3,2,1,0:T(8,128)(2,1)S(1)} %broadcast_select_fusion.2), channel_id=1, source_target_pairs={{0,1},{1,0},{2,3},{3,2},{4,5},{5,4},{6,7},{7,6},{8,9},{9,8},{10,11... | collective-permute-start | bytes 786440 | tf_op jit(solution)/shard_map/ppermute | solution.py:347
  51.6 1.9 %collective-permute-start.7 = (bf16[2,2,64,128]{3,2,1,0:T(8,128)(2,1)S(1)}, bf16[2,2,64,128]{3,2,1,0:T(8,128)(2,1)S(1)}, u32[]{:S(2)}, u32[]{:S(2)}) collective-permute-start(bf16[2,2,64,128]{3,2,1,0:T(8,128)(2,1)S(1)} %broadcast_select_fusion.5), channel_id=1, source_target_pairs={{0,2},{1,3},{2,0},{3,1},{4,6},{5,7},{6,4},{7,5},{8,10},{9,11},{10,... | collective-permute-start | bytes 196616 | tf_op jit(solution)/shard_map/ppermute | solution.py:351
  53.5 5.4 %collective-permute-done.7 = bf16[2,2,64,128]{3,2,1,0:T(8,128)(2,1)S(1)} collective-permute-done((bf16[2,2,64,128]{3,2,1,0:T(8,128)(2,1)S(1)}, bf16[2,2,64,128]{3,2,1,0:T(8,128)(2,1)S(1)}, u32[]{:S(2)}, u32[]{:S(2)}) %collective-permute-start.7) | collective-permute-done | bytes 65568 | tf_op jit(solution)/shard_map/ppermute | solution.py:351
  59.5 2.7 %collective-permute-start.11 = (bf16[2,8,2,64,128]{4,3,2,1,0:T(8,128)(2,1)S(1)}, bf16[2,8,2,64,128]{4,3,2,1,0:T(8,128)(2,1)S(1)}, u32[]{:S(2)}, u32[]{:S(2)}) collective-permute-start(bf16[2,8,2,64,128]{4,3,2,1,0:T(8,128)(2,1)S(1)} %broadcast_select_fusion.1.kv_own), channel_id=1, source_target_pairs={{0,16},{16,32},{32,48},{24,8},{40,24},{56,40},{64,80},{80,96},{96,... | collective-permute-start | bytes 1572872 | tf_op jit(solution)/shard_map/ppermute | solution.py:372
  62.3 4.0 %collective-permute-start.9 = (bf16[8,2,64,128]{3,2,1,0:T(8,128)(2,1)S(1)}, bf16[8,2,64,128]{3,2,1,0:T(8,128)(2,1)S(1)}, u32[]{:S(2)}, u32[]{:S(2)}) collective-permute-start(bf16[8,2,64,128]{3,2,1,0:T(8,128)(2,1)S(1)} %bitcast.247), channel_id=1, source_target_pairs={{0,32},{16,48},{40,8},{56,24},{64,96},{80,112},{104,72},{120,88},{... | collective-permute-start | bytes 786440 | tf_op jit(solution)/shard_map/ppermute | solution.py:371
  66.3 3.2 %collective-permute-start.8 = (bf16[2,2,2,64,128]{4,3,2,1,0:T(8,128)(2,1)S(1)}, bf16[2,2,2,64,128]{4,3,2,1,0:T(8,128)(2,1)S(1)}, u32[]{:S(2)}, u32[]{:S(2)}) collective-permute-start(bf16[2,2,2,64,128]{4,3,2,1,0:T(8,128)(2,1)S(1)} %broadcast_select_fusion.3), channel_id=1, source_target_pairs={{0,1},{1,0},{2,3},{3,2},{4,5},{5,4},{6,7},{7,6},{8,9},{9,8},{10,11... | collective-permute-start | bytes 393224 | tf_op jit(solution)/shard_map/ppermute | solution.py:355
  69.5 3.7 %collective-permute-done.8 = bf16[2,2,2,64,128]{4,3,2,1,0:T(8,128)(2,1)S(1)} collective-permute-done((bf16[2,2,2,64,128]{4,3,2,1,0:T(8,128)(2,1)S(1)}, bf16[2,2,2,64,128]{4,3,2,1,0:T(8,128)(2,1)S(1)}, u32[]{:S(2)}, u32[]{:S(2)}) %collective-permute-start.8) | collective-permute-done | bytes 131104 | tf_op jit(solution)/shard_map/ppermute | solution.py:355
  75.9 4.5 %own_forward.1 = (f32[1,1024]{1,0:T(1,128)S(1)}, f32[1,1024]{1,0:T(1,128)S(1)}, f32[4,128,256]{2,1,0:T(8,128)S(1)}) custom-call(s32[4]{0:T(128)S(1)} %and_select_fusion.lo_ref, s32[1]{0:T(128)} %bitcast.place_ref, s32[1,1024]{1,0:T(1,128)S(1)} %bitcast.230, bf16[2,512,128]{2,1,0:T(8,128)(2,1)S(1)} %bitcast.225, ...), custom_call_target="tpu_custom_call" | custom-call | flops 201326592 | bytes 4194304 | tf_op jit(solution)/shard_map/own_forward/pallas_call | solution.py:301
  80.5 2.3 %collective-permute-done.12 = bf16[8,2,64,128]{3,2,1,0:T(8,128)(2,1)S(1)} collective-permute-done((bf16[8,2,64,128]{3,2,1,0:T(8,128)(2,1)S(1)}, bf16[8,2,64,128]{3,2,1,0:T(8,128)(2,1)S(1)}, u32[]{:S(2)}, u32[]{:S(2)}) %collective-permute-start.12) | collective-permute-done | bytes 262176 | tf_op jit(solution)/shard_map/ppermute | solution.py:373
  83.0 7.7 %earlier.1 = (bf16[2,512,128]{2,1,0:T(8,128)(2,1)S(1)}, f32[1,1024]{1,0:T(1,128)S(1)}, f32[1,1024]{1,0:T(1,128)S(1)}, f32[4,128,256]{2,1,0:T(8,128)S(1)}, bf16[2...) custom-call(s32[4]{0:T(128)S(1)} %and_select_fusion.lo_ref, s32[1]{0:T(128)} %bitcast.place_ref, ...), custom_call_target="tpu_custom_call" | custom-call | flops 603979776 | bytes 4194304 | tf_op jit(solution)/shard_map/earlier/pallas_call | solution.py:301
  96.0 5.9 %own_backward.1 = (bf16[2,512,128]{2,1,0:T(8,128)(2,1)S(1)}, bf16[2,512,128]{2,1,0:T(8,128)(2,1)S(1)}, f32[2,8,2,64,128]{4,3,2,1,0:T(8,128)S(1)}) custom-call(s32[4]{0:T(128)S(1)} %and_select_fusion.lo_ref, s32[1]{0:T(128)} %bitcast.place_ref, s32[1,1024]{1,0:T(1,128)S(1)} %bitcast.232, bf16[2,512,128]{2,1,0:T(8,128)(2,1)S(1)} %bitcast.227, ...), custom_call_target="tpu_custom_call" | custom-call | flops 503316480 | bytes 4194304 | tf_op jit(solution)/shard_map/own_backward/pallas_call | solution.py:301
  102.1 3.2 %collective-permute-start.22 = (bf16[4,2,64,128]{3,2,1,0:T(8,128)(2,1)S(1)}, bf16[4,2,64,128]{3,2,1,0:T(8,128)(2,1)S(1)}, u32[]{:S(2)}, u32[]{:S(2)}) collective-permute-start(bf16[4,2,64,128]{3,2,1,0:T(8,128)(2,1)S(1)} %fusion.15), channel_id=1, source_target_pairs={{0,1},{1,0},{2,3},{3,2},{4,5},{5,4},{6,7},{7,6},{8,9},{9,8},{10,11... | collective-permute-start | bytes 393224 | tf_op jit(solution)/shard_map/ppermute | solution.py:444
  105.3 3.5 %collective-permute-start.13 = (bf16[2,512,128]{2,1,0:T(8,128)(2,1)S(1)}, bf16[2,512,128]{2,1,0:T(8,128)(2,1)S(1)}, u32[]{:S(2)}, u32[]{:S(2)}) collective-permute-start(bf16[2,512,128]{2,1,0:T(8,128)(2,1)S(1)} %get-tuple-element.36), channel_id=1, source_target_pairs={{0,8},{8,0},{16,24},{24,16},{32,40},{40,32},{48,56},{56,48},{64,72... | collective-permute-start | bytes 786440 | tf_op jit(solution)/shard_map/ppermute | solution.py:465
  110.1 3.4 %collective-permute-start.23 = (bf16[2,2,64,128]{3,2,1,0:T(8,128)(2,1)S(1)}, bf16[2,2,64,128]{3,2,1,0:T(8,128)(2,1)S(1)}, u32[]{:S(2)}, u32[]{:S(2)}) collective-permute-start(bf16[2,2,64,128]{3,2,1,0:T(8,128)(2,1)S(1)} %fusion.24), channel_id=1, source_target_pairs={{0,2},{1,3},{2,0},{3,1},{4,6},{5,7},{6,4},{7,5},{8,10},{9,11},{10,... | collective-permute-start | bytes 196616 | tf_op jit(solution)/shard_map/ppermute | solution.py:444
  114.0 1.9 %collective-permute-start.16 = (bf16[2,4,2,64,128]{4,3,2,1,0:T(8,128)(2,1)S(1)}, bf16[2,4,2,64,128]{4,3,2,1,0:T(8,128)(2,1)S(1)}, u32[]{:S(2)}, u32[]{:S(2)}) collective-permute-start(bf16[2,4,2,64,128]{4,3,2,1,0:T(8,128)(2,1)S(1)} %fusion.6), channel_id=1, source_target_pairs={{0,1},{1,0},{2,3},{3,2},{4,5},{5,4},{6,7},{7,6},{8,9},{9,8},{10,11... | collective-permute-start | bytes 786440 | tf_op jit(solution)/shard_map/ppermute | solution.py:454
  115.9 2.6 %collective-permute-done.23 = bf16[2,2,64,128]{3,2,1,0:T(8,128)(2,1)S(1)} collective-permute-done((bf16[2,2,64,128]{3,2,1,0:T(8,128)(2,1)S(1)}, bf16[2,2,64,128]{3,2,1,0:T(8,128)(2,1)S(1)}, u32[]{:S(2)}, u32[]{:S(2)}) %collective-permute-start.23) | collective-permute-done | bytes 65568 | tf_op jit(solution)/shard_map/ppermute | solution.py:444
  118.5 5.6 %collective-permute-done.16 = bf16[2,4,2,64,128]{4,3,2,1,0:T(8,128)(2,1)S(1)} collective-permute-done((bf16[2,4,2,64,128]{4,3,2,1,0:T(8,128)(2,1)S(1)}, bf16[2,4,2,64,128]{4,3,2,1,0:T(8,128)(2,1)S(1)}, u32[]{:S(2)}, u32[]{:S(2)}) %collective-permute-start.16) | collective-permute-done | bytes 262176 | tf_op jit(solution)/shard_map/ppermute | solution.py:454
  124.2 3.1 %collective-permute-start.17 = (bf16[2,2,2,64,128]{4,3,2,1,0:T(8,128)(2,1)S(1)}, bf16[2,2,2,64,128]{4,3,2,1,0:T(8,128)(2,1)S(1)}, u32[]{:S(2)}, u32[]{:S(2)}) collective-permute-start(bf16[2,2,2,64,128]{4,3,2,1,0:T(8,128)(2,1)S(1)} %fusion.14), channel_id=1, source_target_pairs={{0,2},{1,3},{2,0},{3,1},{4,6},{5,7},{6,4},{7,5},{8,10},{9,11},{10,... | collective-permute-start | bytes 393224 | tf_op jit(solution)/shard_map/ppermute | solution.py:454
  127.4 4.7 %collective-permute-start.24 = (bf16[1,2,64,128]{3,2,1,0:T(8,128)(2,1)S(1)}, bf16[1,2,64,128]{3,2,1,0:T(8,128)(2,1)S(1)}, u32[]{:S(2)}, u32[]{:S(2)}) collective-permute-start(bf16[1,2,64,128]{3,2,1,0:T(8,128)(2,1)S(1)} %fusion.27), channel_id=1, source_target_pairs={{0,4},{1,5},{2,6},{3,7},{4,0},{5,1},{6,2},{7,3},{8,12},{9,13},{10,... | collective-permute-start | bytes 98312 | tf_op jit(solution)/shard_map/ppermute | solution.py:444
  132.1 2.1 %collective-permute-done.17 = bf16[2,2,2,64,128]{4,3,2,1,0:T(8,128)(2,1)S(1)} collective-permute-done((bf16[2,2,2,64,128]{4,3,2,1,0:T(8,128)(2,1)S(1)}, bf16[2,2,2,64,128]{4,3,2,1,0:T(8,128)(2,1)S(1)}, u32[]{:S(2)}, u32[]{:S(2)}) %collective-permute-start.17) | collective-permute-done | bytes 131104 | tf_op jit(solution)/shard_map/ppermute | solution.py:454
  134.3 6.7 %collective-permute-start.18 = (bf16[2,1,2,64,128]{4,3,2,0,1:T(8,128)(2,1)S(1)}, bf16[2,1,2,64,128]{4,3,2,0,1:T(8,128)(2,1)S(1)}, u32[]{:S(2)}, u32[]{:S(2)}) collective-permute-start(bf16[2,1,2,64,128]{4,3,2,0,1:T(8,128)(2,1)S(1)} %fusion.23), channel_id=1, source_target_pairs={{0,4},{1,5},{2,6},{3,7},{4,0},{5,1},{6,2},{7,3},{8,12},{9,13},{10,... | collective-permute-start | bytes 196616 | tf_op jit(solution)/shard_map/ppermute | solution.py:454
  141.0 1.9 %collective-permute-start.25 = (bf16[2,64,128]{2,1,0:T(8,128)(2,1)S(1)}, bf16[2,64,128]{2,1,0:T(8,128)(2,1)S(1)}, u32[]{:S(2)}, u32[]{:S(2)}) collective-permute-start(bf16[2,64,128]{2,1,0:T(8,128)(2,1)S(1)} %fusion.29), channel_id=1, source_target_pairs={{87,56},{86,57},{85,58},{84,59},{83,60},{82,61},{81,62},{80,63},{7... | collective-permute-start | bytes 98312 | tf_op jit(solution)/shard_map/ppermute | solution.py:446
  144.7 1.9 %collective-permute-start.19 = (bf16[2,64,128]{2,1,0:T(8,128)(2,1)S(1)}, bf16[2,64,128]{2,1,0:T(8,128)(2,1)S(1)}, u32[]{:S(2)}, u32[]{:S(2)}) collective-permute-start(bf16[2,64,128]{2,1,0:T(8,128)(2,1)S(1)} %fusion.28), channel_id=1, source_target_pairs={{0,8},{8,0},{16,24},{24,16},{32,40},{40,32},{48,56},{56,48},{64,72... | collective-permute-start | bytes 98312 | tf_op jit(solution)/shard_map/ppermute | solution.py:458
  147.5 8.6 %collective-permute-done.25 = bf16[2,64,128]{2,1,0:T(8,128)(2,1)S(1)} collective-permute-done((bf16[2,64,128]{2,1,0:T(8,128)(2,1)S(1)}, bf16[2,64,128]{2,1,0:T(8,128)(2,1)S(1)}, u32[]{:S(2)}, u32[]{:S(2)}) %collective-permute-start.25) | collective-permute-done | bytes 32800 | tf_op jit(solution)/shard_map/ppermute | solution.py:446
  (87 shorter events, 19.1 us)
Async XLA Ops:
  0.6 18.4 %copy-start.1 = (bf16[1,2,512,128]{3,2,1,0:T(8,128)(2,1)S(1)}, bf16[1,2,512,128]{3,2,1,0:T(8,128)(2,1)}, u32[]{:S(2)}) copy-start(bf16[1,2,512,128]{3,2,1,0:T(8,128)(2,1)} %param.8) | copy-start | bytes 786436
  1.4 19.7 %copy-start.2 = (s32[65536]{0:T(1024)S(1)}, s32[65536]{0:T(1024)}, u32[]{:S(2)}) copy-start(s32[65536]{0:T(1024)} %param.9) | copy-start | bytes 786436
  2.2 23.4 %collective-permute-start.3 = (bf16[2,64,128]{2,1,0:T(8,128)(2,1)S(1)}, bf16[2,64,128]{2,1,0:T(8,128)(2,1)S(1)}, u32[]{:S(2)}, u32[]{:S(2)}) collective-permute-start(bf16[2,64,128]{2,1,0:T(8,128)(2,1)S(1)} %get-tuple-element.60), channel_id=1, source_target_pairs={{56,87},{57,86},{58,85},{59,84},{60,83},{61,82},{62,81},{63,80},{4... | collective-permute-start | bytes 98312 | tf_op jit(solution)/shard_map/ppermute | solution.py:349
  15.7 7.1 %collective-permute-start.1 = (bf16[2,64,128]{2,1,0:T(8,128)(2,1)S(1)}, bf16[2,64,128]{2,1,0:T(8,128)(2,1)S(1)}, u32[]{:S(2)}, u32[]{:S(2)}) collective-permute-start(bf16[2,64,128]{2,1,0:T(8,128)(2,1)S(1)} %get-tuple-element.61), channel_id=1, source_target_pairs={{0,8},{8,0},{16,24},{24,16},{32,40},{40,32},{48,56},{56,48},{64,72... | collective-permute-start | bytes 98312 | tf_op jit(solution)/shard_map/ppermute | solution.py:344
  19.2 56.7 %collective-permute-start = (bf16[2,512,128]{2,1,0:T(8,128)(2,1)S(1)}, bf16[2,512,128]{2,1,0:T(8,128)(2,1)S(1)}, u32[]{:S(2)}, u32[]{:S(2)}) collective-permute-start(bf16[2,512,128]{2,1,0:T(8,128)(2,1)S(1)} %maximum_select_fusion), channel_id=1, source_target_pairs={{0,8},{8,0},{16,24},{24,16},{32,40},{40,32},{48,56},{56,48},{64,72... | collective-permute-start | bytes 786440 | tf_op jit(solution)/shard_map/ppermute | solution.py:361
  22.9 10.5 %collective-permute-start.2 = (bf16[2,2,64,128]{3,2,1,0:T(8,128)(2,1)S(1)}, bf16[2,2,64,128]{3,2,1,0:T(8,128)(2,1)S(1)}, u32[]{:S(2)}, u32[]{:S(2)}) collective-permute-start(bf16[2,2,64,128]{3,2,1,0:T(8,128)(2,1)S(1)} %broadcast_select_fusion.6), channel_id=1, source_target_pairs={{0,4},{1,5},{2,6},{3,7},{4,0},{5,1},{6,2},{7,3},{8,12},{9,13},{10,... | collective-permute-start | bytes 196616 | tf_op jit(solution)/shard_map/ppermute | solution.py:347
  33.4 14.0 %collective-permute-start.4 = (bf16[2,2,2,64,128]{4,3,2,1,0:T(8,128)(2,1)S(1)}, bf16[2,2,2,64,128]{4,3,2,1,0:T(8,128)(2,1)S(1)}, u32[]{:S(2)}, u32[]{:S(2)}) collective-permute-start(bf16[2,2,2,64,128]{4,3,2,1,0:T(8,128)(2,1)S(1)} %broadcast_select_fusion.4), channel_id=1, source_target_pairs={{0,2},{1,3},{2,0},{3,1},{4,6},{5,7},{6,4},{7,5},{8,10},{9,11},{10,... | collective-permute-start | bytes 393224 | tf_op jit(solution)/shard_map/ppermute | solution.py:347
  37.8 9.7 %collective-permute-start.5 = (bf16[2,64,128]{2,1,0:T(8,128)(2,1)S(1)}, bf16[2,64,128]{2,1,0:T(8,128)(2,1)S(1)}, u32[]{:S(2)}, u32[]{:S(2)}) collective-permute-start(bf16[2,64,128]{2,1,0:T(8,128)(2,1)S(1)} %collective-permute-done.3), channel_id=1, source_target_pairs={{0,4},{1,5},{2,6},{3,7},{4,0},{5,1},{6,2},{7,3},{8,12},{9,13},{10,... | collective-permute-start | bytes 98312 | tf_op jit(solution)/shard_map/ppermute | solution.py:351
  47.6 11.4 %collective-permute-start.6 = (bf16[2,2,2,2,64,128]{5,4,3,2,1,0:T(8,128)(2,1)S(1)}, bf16[2,2,2,2,64,128]{5,4,3,2,1,0:T(8,128)(2,1)S(1)}, u32[]{:S(2)}, u32[]{:S(2)}) collective-permute-start(bf16[2,2,2,2,64,128]{5,4,3,2,1,0:T(8,128)(2,1)S(1)} %broadcast_select_fusion.2), channel_id=1, source_target_pairs={{0,1},{1,0},{2,3},{3,2},{4,5},{5,4},{6,7},{7,6},{8,9},{9,8},{10,11... | collective-permute-start | bytes 786440 | tf_op jit(solution)/shard_map/ppermute | solution.py:347
  51.6 7.4 %collective-permute-start.7 = (bf16[2,2,64,128]{3,2,1,0:T(8,128)(2,1)S(1)}, bf16[2,2,64,128]{3,2,1,0:T(8,128)(2,1)S(1)}, u32[]{:S(2)}, u32[]{:S(2)}) collective-permute-start(bf16[2,2,64,128]{3,2,1,0:T(8,128)(2,1)S(1)} %broadcast_select_fusion.5), channel_id=1, source_target_pairs={{0,2},{1,3},{2,0},{3,1},{4,6},{5,7},{6,4},{7,5},{8,10},{9,11},{10,... | collective-permute-start | bytes 196616 | tf_op jit(solution)/shard_map/ppermute | solution.py:351
  59.5 16.4 %copy-start = (bf16[1,2,512,128]{3,2,1,0:T(8,128)(2,1)S(1)}, bf16[1,2,512,128]{3,2,1,0:T(8,128)(2,1)}, u32[]{:S(2)}) copy-start(bf16[1,2,512,128]{3,2,1,0:T(8,128)(2,1)} %param.5) | copy-start | bytes 786436
  59.5 20.9 %collective-permute-start.11 = (bf16[2,8,2,64,128]{4,3,2,1,0:T(8,128)(2,1)S(1)}, bf16[2,8,2,64,128]{4,3,2,1,0:T(8,128)(2,1)S(1)}, u32[]{:S(2)}, u32[]{:S(2)}) collective-permute-start(bf16[2,8,2,64,128]{4,3,2,1,0:T(8,128)(2,1)S(1)} %broadcast_select_fusion.1.kv_own), channel_id=1, source_target_pairs={{0,16},{16,32},{32,48},{24,8},{40,24},{56,40},{64,80},{80,96},{96,... | collective-permute-start | bytes 1572872 | tf_op jit(solution)/shard_map/ppermute | solution.py:372
  62.3 10.9 %collective-permute-start.9 = (bf16[8,2,64,128]{3,2,1,0:T(8,128)(2,1)S(1)}, bf16[8,2,64,128]{3,2,1,0:T(8,128)(2,1)S(1)}, u32[]{:S(2)}, u32[]{:S(2)}) collective-permute-start(bf16[8,2,64,128]{3,2,1,0:T(8,128)(2,1)S(1)} %bitcast.247), channel_id=1, source_target_pairs={{0,32},{16,48},{40,8},{56,24},{64,96},{80,112},{104,72},{120,88},{... | collective-permute-start | bytes 786440 | tf_op jit(solution)/shard_map/ppermute | solution.py:371
  66.3 6.9 %collective-permute-start.8 = (bf16[2,2,2,64,128]{4,3,2,1,0:T(8,128)(2,1)S(1)}, bf16[2,2,2,64,128]{4,3,2,1,0:T(8,128)(2,1)S(1)}, u32[]{:S(2)}, u32[]{:S(2)}) collective-permute-start(bf16[2,2,2,64,128]{4,3,2,1,0:T(8,128)(2,1)S(1)} %broadcast_select_fusion.3), channel_id=1, source_target_pairs={{0,1},{1,0},{2,3},{3,2},{4,5},{5,4},{6,7},{7,6},{8,9},{9,8},{10,11... | collective-permute-start | bytes 393224 | tf_op jit(solution)/shard_map/ppermute | solution.py:355
  73.3 7.3 %collective-permute-start.10 = (bf16[8,2,64,128]{3,2,1,0:T(8,128)(2,1)S(1)}, bf16[8,2,64,128]{3,2,1,0:T(8,128)(2,1)S(1)}, u32[]{:S(2)}, u32[]{:S(2)}) collective-permute-start(bf16[8,2,64,128]{3,2,1,0:T(8,128)(2,1)S(1)} %get-tuple-element.41), channel_id=1, source_target_pairs={{8,0},{48,56},{72,64},{112,120},{136,128},{176,184},{200,192},{240... | collective-permute-start | bytes 786440 | tf_op jit(solution)/shard_map/ppermute | solution.py:374
  74.6 8.3 %collective-permute-start.12 = (bf16[8,2,64,128]{3,2,1,0:T(8,128)(2,1)S(1)}, bf16[8,2,64,128]{3,2,1,0:T(8,128)(2,1)S(1)}, u32[]{:S(2)}, u32[]{:S(2)}) collective-permute-start(bf16[8,2,64,128]{3,2,1,0:T(8,128)(2,1)S(1)} %get-tuple-element.41), channel_id=1, source_target_pairs={{16,0},{40,56},{80,64},{104,120},{144,128},{168,184},{208,192},{23... | collective-permute-start | bytes 786440 | tf_op jit(solution)/shard_map/ppermute | solution.py:373
  90.7 11.2 %collective-permute-start.20 = (bf16[8,2,64,128]{3,2,1,0:T(8,128)(2,1)S(1)}, bf16[8,2,64,128]{3,2,1,0:T(8,128)(2,1)S(1)}, u32[]{:S(2)}, u32[]{:S(2)}) collective-permute-start(bf16[8,2,64,128]{3,2,1,0:T(8,128)(2,1)S(1)} %get-tuple-element.44), channel_id=1, source_target_pairs={{0,16},{56,40},{64,80},{120,104},{128,144},{184,168},{192,208},{24... | collective-permute-start | bytes 786440 | tf_op jit(solution)/shard_map/ppermute | solution.py:427
  92.1 9.9 %collective-permute-start.21 = (bf16[8,2,64,128]{3,2,1,0:T(8,128)(2,1)S(1)}, bf16[8,2,64,128]{3,2,1,0:T(8,128)(2,1)S(1)}, u32[]{:S(2)}, u32[]{:S(2)}) collective-permute-start(bf16[8,2,64,128]{3,2,1,0:T(8,128)(2,1)S(1)} %get-tuple-element.45), channel_id=1, source_target_pairs={{0,8},{56,48},{64,72},{120,112},{128,136},{184,176},{192,200},{248... | collective-permute-start | bytes 786440 | tf_op jit(solution)/shard_map/ppermute | solution.py:428
  93.4 20.2 %collective-permute-start.14 = (bf16[2,8,2,64,128]{4,3,2,1,0:T(8,128)(2,1)S(1)}, bf16[2,8,2,64,128]{4,3,2,1,0:T(8,128)(2,1)S(1)}, u32[]{:S(2)}, u32[]{:S(2)}) collective-permute-start(bf16[2,8,2,64,128]{4,3,2,1,0:T(8,128)(2,1)S(1)} %get-tuple-element.38), channel_id=1, source_target_pairs={{16,0},{32,16},{48,32},{8,24},{24,40},{40,56},{80,64},{96,80},{112... | collective-permute-start | bytes 1572872 | tf_op jit(solution)/shard_map/ppermute | solution.py:430
  94.7 19.1 %collective-permute-start.15 = (bf16[8,2,64,128]{3,2,1,0:T(8,128)(2,1)S(1)}, bf16[8,2,64,128]{3,2,1,0:T(8,128)(2,1)S(1)}, u32[]{:S(2)}, u32[]{:S(2)}) collective-permute-start(bf16[8,2,64,128]{3,2,1,0:T(8,128)(2,1)S(1)} %get-tuple-element.39), channel_id=1, source_target_pairs={{32,0},{48,16},{8,40},{24,56},{96,64},{112,80},{72,104},{88,120},{... | collective-permute-start | bytes 786440 | tf_op jit(solution)/shard_map/ppermute | solution.py:429
  102.1 8.0 %collective-permute-start.22 = (bf16[4,2,64,128]{3,2,1,0:T(8,128)(2,1)S(1)}, bf16[4,2,64,128]{3,2,1,0:T(8,128)(2,1)S(1)}, u32[]{:S(2)}, u32[]{:S(2)}) collective-permute-start(bf16[4,2,64,128]{3,2,1,0:T(8,128)(2,1)S(1)} %fusion.15), channel_id=1, source_target_pairs={{0,1},{1,0},{2,3},{3,2},{4,5},{5,4},{6,7},{7,6},{8,9},{9,8},{10,11... | collective-permute-start | bytes 393224 | tf_op jit(solution)/shard_map/ppermute | solution.py:444
  105.3 10.6 %collective-permute-start.13 = (bf16[2,512,128]{2,1,0:T(8,128)(2,1)S(1)}, bf16[2,512,128]{2,1,0:T(8,128)(2,1)S(1)}, u32[]{:S(2)}, u32[]{:S(2)}) collective-permute-start(bf16[2,512,128]{2,1,0:T(8,128)(2,1)S(1)} %get-tuple-element.36), channel_id=1, source_target_pairs={{0,8},{8,0},{16,24},{24,16},{32,40},{40,32},{48,56},{56,48},{64,72... | collective-permute-start | bytes 786440 | tf_op jit(solution)/shard_map/ppermute | solution.py:465
  110.1 8.3 %collective-permute-start.23 = (bf16[2,2,64,128]{3,2,1,0:T(8,128)(2,1)S(1)}, bf16[2,2,64,128]{3,2,1,0:T(8,128)(2,1)S(1)}, u32[]{:S(2)}, u32[]{:S(2)}) collective-permute-start(bf16[2,2,64,128]{3,2,1,0:T(8,128)(2,1)S(1)} %fusion.24), channel_id=1, source_target_pairs={{0,2},{1,3},{2,0},{3,1},{4,6},{5,7},{6,4},{7,5},{8,10},{9,11},{10,... | collective-permute-start | bytes 196616 | tf_op jit(solution)/shard_map/ppermute | solution.py:444
  114.0 10.1 %collective-permute-start.16 = (bf16[2,4,2,64,128]{4,3,2,1,0:T(8,128)(2,1)S(1)}, bf16[2,4,2,64,128]{4,3,2,1,0:T(8,128)(2,1)S(1)}, u32[]{:S(2)}, u32[]{:S(2)}) collective-permute-start(bf16[2,4,2,64,128]{4,3,2,1,0:T(8,128)(2,1)S(1)} %fusion.6), channel_id=1, source_target_pairs={{0,1},{1,0},{2,3},{3,2},{4,5},{5,4},{6,7},{7,6},{8,9},{9,8},{10,11... | collective-permute-start | bytes 786440 | tf_op jit(solution)/shard_map/ppermute | solution.py:454
  124.2 10.0 %collective-permute-start.17 = (bf16[2,2,2,64,128]{4,3,2,1,0:T(8,128)(2,1)S(1)}, bf16[2,2,2,64,128]{4,3,2,1,0:T(8,128)(2,1)S(1)}, u32[]{:S(2)}, u32[]{:S(2)}) collective-permute-start(bf16[2,2,2,64,128]{4,3,2,1,0:T(8,128)(2,1)S(1)} %fusion.14), channel_id=1, source_target_pairs={{0,2},{1,3},{2,0},{3,1},{4,6},{5,7},{6,4},{7,5},{8,10},{9,11},{10,... | collective-permute-start | bytes 393224 | tf_op jit(solution)/shard_map/ppermute | solution.py:454
  127.4 13.6 %collective-permute-start.24 = (bf16[1,2,64,128]{3,2,1,0:T(8,128)(2,1)S(1)}, bf16[1,2,64,128]{3,2,1,0:T(8,128)(2,1)S(1)}, u32[]{:S(2)}, u32[]{:S(2)}) collective-permute-start(bf16[1,2,64,128]{3,2,1,0:T(8,128)(2,1)S(1)} %fusion.27), channel_id=1, source_target_pairs={{0,4},{1,5},{2,6},{3,7},{4,0},{5,1},{6,2},{7,3},{8,12},{9,13},{10,... | collective-permute-start | bytes 98312 | tf_op jit(solution)/shard_map/ppermute | solution.py:444
  134.3 10.4 %collective-permute-start.18 = (bf16[2,1,2,64,128]{4,3,2,0,1:T(8,128)(2,1)S(1)}, bf16[2,1,2,64,128]{4,3,2,0,1:T(8,128)(2,1)S(1)}, u32[]{:S(2)}, u32[]{:S(2)}) collective-permute-start(bf16[2,1,2,64,128]{4,3,2,0,1:T(8,128)(2,1)S(1)} %fusion.23), channel_id=1, source_target_pairs={{0,4},{1,5},{2,6},{3,7},{4,0},{5,1},{6,2},{7,3},{8,12},{9,13},{10,... | collective-permute-start | bytes 196616 | tf_op jit(solution)/shard_map/ppermute | solution.py:454
  141.0 15.1 %collective-permute-start.25 = (bf16[2,64,128]{2,1,0:T(8,128)(2,1)S(1)}, bf16[2,64,128]{2,1,0:T(8,128)(2,1)S(1)}, u32[]{:S(2)}, u32[]{:S(2)}) collective-permute-start(bf16[2,64,128]{2,1,0:T(8,128)(2,1)S(1)} %fusion.29), channel_id=1, source_target_pairs={{87,56},{86,57},{85,58},{84,59},{83,60},{82,61},{81,62},{80,63},{7... | collective-permute-start | bytes 98312 | tf_op jit(solution)/shard_map/ppermute | solution.py:446
  144.7 11.4 %collective-permute-start.19 = (bf16[2,64,128]{2,1,0:T(8,128)(2,1)S(1)}, bf16[2,64,128]{2,1,0:T(8,128)(2,1)S(1)}, u32[]{:S(2)}, u32[]{:S(2)}) collective-permute-start(bf16[2,64,128]{2,1,0:T(8,128)(2,1)S(1)} %fusion.28), channel_id=1, source_target_pairs={{0,8},{8,0},{16,24},{24,16},{32,40},{40,32},{48,56},{56,48},{64,72... | collective-permute-start | bytes 98312 | tf_op jit(solution)/shard_map/ppermute | solution.py:458

commit v8 on v5

--- a/solution.py
+++ b/solution.py
@@ -34,6 +34,12 @@
 
 def head_pairs(ctx, heads, bit):
     return [(d, d ^ bit) for d in range(ctx * heads)]
+
+
+def cross_pairs(ctx, heads, bit):
+    return [
+        (c * heads + h, (c ^ 1) * heads + (h ^ bit)) for c in range(ctx) for h in range(heads)
+    ]
 
 
 def edge_pairs(ctx, heads, flip):
@@ -327,24 +333,34 @@
     bits = folds(heads)
     far_bit = bits[0]
     high = {bit: (head & bit) != 0 for bit in bits}
-    straight, crossing = edge_pairs(ctx, heads, 0), edge_pairs(ctx, heads, far_bit)
+    cross = cross_pairs(ctx, heads, far_bit)
+    mirrored = edge_pairs(ctx, heads, heads - 1)
+    folded = edge_pairs(ctx, heads, heads - 1 - far_bit)
+    is_edge = lax.broadcasted_iota(jnp.int32, (3, 1, 1, 1, 1), 0) == 2
 
     lower = jnp.stack([key_states[0, 0], value_states[0, 0]])
     upper = jnp.stack([key_states[0, 1], value_states[0, 1]])
     leaving = pick(sends_lower, upper, lower)
-    half = by_bit(core, pick(even, upper, lower), lax.ppermute(pick(even, lower, upper), CTX, swap), 0)
-    kv_own = by_bit(high[far_bit], half, lax.ppermute(half, everywhere, head_pairs(ctx, heads, far_bit)), 1)
-    kv_edge = by_bit(
-        high[far_bit],
-        lax.ppermute(leaving, everywhere, straight),
-        lax.ppermute(leaving, everywhere, crossing),
+    mine, theirs = pick(even, upper, lower), pick(even, lower, upper)
+    edge_far = lax.ppermute(leaving, everywhere, mirrored)
+    near_core = lax.ppermute(theirs, CTX, swap)
+    near_head = lax.ppermute(mine, everywhere, head_pairs(ctx, heads, far_bit))
+    far_core = lax.ppermute(theirs, everywhere, cross)
+    leaving, near_core = lax.optimization_barrier((leaving, near_core))
+    edge_near = lax.ppermute(leaving, everywhere, folded)
+    kv_own = by_bit(
+        core,
+        by_bit(high[far_bit], mine, near_head, 0),
+        by_bit(high[far_bit], near_core, far_core, 0),
         0,
     )
-    kv_all = jnp.concatenate([kv_own, kv_edge[None]])
-    for k, bit in enumerate(bits[1:]):
+    kv_all = jnp.concatenate([kv_own, by_bit(high[far_bit], edge_near, edge_far, 0)[None]])
+    for bit in bits[1:]:
         other = lax.ppermute(kv_all, everywhere, head_pairs(ctx, heads, bit))
-        kv_all = by_bit(high[bit], kv_all, other, 2 + k)
-    kv_all = kv_all.reshape((3, heads) + half.shape[1:])
+        slot = lax.broadcasted_iota(jnp.int32, (2, 1, 1, 1), 0) == 1
+        stays = slot == (high[bit] ^ is_edge)[:, None]
+        kv_all = jnp.where(stays, kv_all[:, :, None], other[:, :, None])
+        kv_all = kv_all.reshape((3, -1) + mine.shape)
     kv_own, kv_edge = kv_all[:2], kv_all[2]
 
     queries, out_grad = queries[0], out_grad[0]
@@ -434,20 +450,26 @@
         [pick(even, second_sum, first_sum), pick(even, first_sum, second_sum), edge_sum]
     )
     for bit in reversed(bits[1:]):
-        halves = sums.reshape((3, -1, 2) + half.shape[1:])
-        away = pick(high[bit], halves[:, :, 1], halves[:, :, 0]).astype(bf16)
+        halves = sums.reshape((3, -1, 2) + mine.shape)
+        high_half = high[bit] ^ is_edge
+        away = jnp.where(high_half, halves[:, :, 0], halves[:, :, 1]).astype(bf16)
         other = lax.ppermute(away, everywhere, head_pairs(ctx, heads, bit))
-        sums = pick(high[bit], halves[:, :, 0], halves[:, :, 1]) + other.astype(f32)
-    stays, away = pick(high[far_bit], sums[:, 0], sums[:, 1]), pick(high[far_bit], sums[:, 1], sums[:, 0])
-    away = away.astype(bf16)
-    other = lax.ppermute(away[:2], everywhere, head_pairs(ctx, heads, far_bit))
-    returned = lax.ppermute(stays[2].astype(bf16), everywhere, inverse(straight)).astype(f32)
-    returned += lax.ppermute(away[2], everywhere, inverse(crossing)).astype(f32)
-    stays = stays[:2] + other.astype(f32)
+        sums = jnp.where(high_half, halves[:, :, 1], halves[:, :, 0]) + other.astype(f32)
+    stays = pick(high[far_bit], sums[:, 0], sums[:, 1])
+    away = pick(high[far_bit], sums[:, 1], sums[:, 0])
     own_half = pick(even, stays[1], stays[0])
-    far_half = lax.ppermute(
-        pick(even, stays[0], stays[1]).astype(bf16), CTX, swap
-    ).astype(f32)
+    sent_head = pick(even, away[1], away[0]).astype(bf16)
+    sent_core = pick(even, stays[0], stays[1]).astype(bf16)
+    sent_cross = pick(even, away[0], away[1]).astype(bf16)
+    from_far = lax.ppermute(away[2].astype(bf16), everywhere, inverse(mirrored))
+    far_half = lax.ppermute(sent_core, CTX, swap)
+    from_head = lax.ppermute(sent_head, everywhere, head_pairs(ctx, heads, far_bit))
+    from_cross = lax.ppermute(sent_cross, everywhere, cross)
+    folded_back, far_half = lax.optimization_barrier((stays[2].astype(bf16), far_half))
+    from_near = lax.ppermute(folded_back, everywhere, inverse(folded))
+    own_half = own_half + from_head.astype(f32)
+    far_half = far_half.astype(f32) + from_cross.astype(f32)
+    returned = from_near.astype(f32) + from_far.astype(f32)
     lower = pick(even, far_half, own_half) + jnp.where(sends_lower, returned, 0.0)
     upper = pick(even, own_half, far_half) + jnp.where(sends_lower, 0.0, returned)
     grads = jnp.stack([lower, upper]).astype(bf16)

time: 163 us -> 172 us (1.055)
  the two profiles are of different devices: /device:TPU:7 before, /device:TPU:6 now
where the time goes in v8:
time: 172 us; the launch traced here: 170 us
  starting transfers between devices  90 us (52%)
  waiting for transfers between devices  52.6 us (31%)
  Pallas kernels  18.1 us (11%)
  other arithmetic  5.28 us (3%)
  local copies, waits for them, and re-layouts  2.34 us (1%)
    pallas_call x3, Pallas kernels, call(): pl.pallas_call(kernel, out_shape=outputs, in_specs=[pl.BlockSpec(memory_s...  18.1 us
    ppermute x2, waiting for transfers between devices, body(): other = lax.ppermute(away, everywhere, head_pairs(ctx, heads, bit))  18 us
    ppermute x2, waiting for transfers between devices, body(): other = lax.ppermute(kv_all, everywhere, head_pairs(ctx, heads, bit))  17.6 us
    ppermute x1, starting transfers between devices, body(): edge_far = lax.ppermute(leaving, everywhere, mirrored)  12.4 us
    ppermute x1, starting transfers between devices, body(): from_near = lax.ppermute(folded_back, everywhere, inverse(folded))  10.5 us
    ppermute x2, starting transfers between devices, body(): other = lax.ppermute(kv_all, everywhere, head_pairs(ctx, heads, bit))  9.85 us
    ppermute x1, waiting for transfers between devices, body(): edge_near = lax.ppermute(leaving, everywhere, folded)  8.58 us
    ppermute x1, starting transfers between devices, body(): far_core = lax.ppermute(theirs, everywhere, cross)  8.54 us
  transfers between devices with their start and end apart: 24, of which 8 were waited for; matrix products, arithmetic and copies ran while one was open for 3% of the time, Pallas kernels for 6%

profile of v8, /device:TPU:6, one launch (start us, length us, event | category | flops | bytes accessed | tf_op | source)
XLA Modules:
  0.0 169.6 jit_solution(1679751464896818488)
XLA Ops:
  2.2 8.5 %collective-permute-start.3 = (bf16[2,64,128]{2,1,0:T(8,128)(2,1)S(1)}, bf16[2,64,128]{2,1,0:T(8,128)(2,1)S(1)}, u32[]{:S(2)}, u32[]{:S(2)}) collective-permute-start(bf16[2,64,128]{2,1,0:T(8,128)(2,1)S(1)} %get-tuple-element.63), channel_id=1, source_target_pairs={{0,12},{1,13},{2,14},{3,15},{4,8},{5,9},{6,10},{7,11},{8,4},{9,5},... | collective-permute-start | bytes 98312 | tf_op jit(solution)/shard_map/ppermute | solution.py:348
  10.7 2.6 %collective-permute-start.2 = (bf16[2,64,128]{2,1,0:T(8,128)(2,1)S(1)}, bf16[2,64,128]{2,1,0:T(8,128)(2,1)S(1)}, u32[]{:S(2)}, u32[]{:S(2)}) collective-permute-start(bf16[2,64,128]{2,1,0:T(8,128)(2,1)S(1)} %get-tuple-element.63), channel_id=1, source_target_pairs={{0,8},{8,0},{16,24},{24,16},{32,40},{40,32},{48,56},{56,48},{64,72... | collective-permute-start | bytes 98312 | tf_op jit(solution)/shard_map/ppermute | solution.py:346
  13.3 1.9 %collective-permute-start.1 = (bf16[2,64,128]{2,1,0:T(8,128)(2,1)S(1)}, bf16[2,64,128]{2,1,0:T(8,128)(2,1)S(1)}, u32[]{:S(2)}, u32[]{:S(2)}) collective-permute-start(bf16[2,64,128]{2,1,0:T(8,128)(2,1)S(1)} %get-tuple-element.61), channel_id=1, source_target_pairs={{0,4},{1,5},{2,6},{3,7},{4,0},{5,1},{6,2},{7,3},{8,12},{9,13},{10,... | collective-permute-start | bytes 98312 | tf_op jit(solution)/shard_map/ppermute | solution.py:347
  15.3 12.4 %collective-permute-start.5 = (bf16[2,64,128]{2,1,0:T(8,128)(2,1)S(1)}, bf16[2,64,128]{2,1,0:T(8,128)(2,1)S(1)}, u32[]{:S(2)}, u32[]{:S(2)}) collective-permute-start(bf16[2,64,128]{2,1,0:T(8,128)(2,1)S(1)} %get-tuple-element.21), channel_id=1, source_target_pairs={{56,87},{57,86},{58,85},{59,84},{60,83},{61,82},{62,81},{63,80},{4... | collective-permute-start | bytes 98312 | tf_op jit(solution)/shard_map/ppermute | solution.py:345
  27.9 5.8 %collective-permute-start.4 = (bf16[2,64,128]{2,1,0:T(8,128)(2,1)S(1)}, bf16[2,64,128]{2,1,0:T(8,128)(2,1)S(1)}, u32[]{:S(2)}, u32[]{:S(2)}) collective-permute-start(bf16[2,64,128]{2,1,0:T(8,128)(2,1)S(1)} %get-tuple-element.21), channel_id=1, source_target_pairs={{56,83},{57,82},{58,81},{59,80},{60,87},{61,86},{62,85},{63,84},{4... | collective-permute-start | bytes 98312 | tf_op jit(solution)/shard_map/ppermute | solution.py:350
  33.9 8.6 %collective-permute-done.4 = bf16[2,64,128]{2,1,0:T(8,128)(2,1)S(1)} collective-permute-done((bf16[2,64,128]{2,1,0:T(8,128)(2,1)S(1)}, bf16[2,64,128]{2,1,0:T(8,128)(2,1)S(1)}, u32[]{:S(2)}, u32[]{:S(2)}) %collective-permute-start.4) | collective-permute-done | bytes 32800 | tf_op jit(solution)/shard_map/ppermute | solution.py:350
  42.6 7.9 %collective-permute-start.6 = (bf16[3,2,2,64,128]{4,3,2,1,0:T(8,128)(2,1)S(1)}, bf16[3,2,2,64,128]{4,3,2,1,0:T(8,128)(2,1)S(1)}, u32[]{:S(2)}, u32[]{:S(2)}) collective-permute-start(bf16[3,2,2,64,128]{4,3,2,1,0:T(8,128)(2,1)S(1)} %pad_maximum_fusion.2), channel_id=1, source_target_pairs={{0,2},{1,3},{2,0},{3,1},{4,6},{5,7},{6,4},{7,5},{8,10},{9,11},{10,... | collective-permute-start | bytes 589832 | tf_op jit(solution)/shard_map/ppermute | solution.py:359
  50.5 9.3 %collective-permute-done.6 = bf16[3,2,2,64,128]{4,3,2,1,0:T(8,128)(2,1)S(1)} collective-permute-done((bf16[3,2,2,64,128]{4,3,2,1,0:T(8,128)(2,1)S(1)}, bf16[3,2,2,64,128]{4,3,2,1,0:T(8,128)(2,1)S(1)}, u32[]{:S(2)}, u32[]{:S(2)}) %collective-permute-start.6) | collective-permute-done | bytes 196640 | tf_op jit(solution)/shard_map/ppermute | solution.py:359
  60.1 1.9 %collective-permute-start.7 = (bf16[3,4,2,64,128]{4,3,2,1,0:T(8,128)(2,1)S(1)}, bf16[3,4,2,64,128]{4,3,2,1,0:T(8,128)(2,1)S(1)}, u32[]{:S(2)}, u32[]{:S(2)}) collective-permute-start(bf16[3,4,2,64,128]{4,3,2,1,0:T(8,128)(2,1)S(1)} %broadcast_select_fusion.1), channel_id=1, source_target_pairs={{0,1},{1,0},{2,3},{3,2},{4,5},{5,4},{6,7},{7,6},{8,9},{9,8},{10,11... | collective-permute-start | bytes 1179656 | tf_op jit(solution)/shard_map/ppermute | solution.py:359
  62.2 1.9 %collective-permute-start = (bf16[2,512,128]{2,1,0:T(8,128)(2,1)S(1)}, bf16[2,512,128]{2,1,0:T(8,128)(2,1)S(1)}, u32[]{:S(2)}, u32[]{:S(2)}) collective-permute-start(bf16[2,512,128]{2,1,0:T(8,128)(2,1)S(1)} %maximum_select_fusion), channel_id=1, source_target_pairs={{0,8},{8,0},{16,24},{24,16},{32,40},{40,32},{48,56},{56,48},{64,72... | collective-permute-start | bytes 786440 | tf_op jit(solution)/shard_map/ppermute | solution.py:367
  64.4 8.3 %collective-permute-done.7 = bf16[3,4,2,64,128]{4,3,2,1,0:T(8,128)(2,1)S(1)} collective-permute-done((bf16[3,4,2,64,128]{4,3,2,1,0:T(8,128)(2,1)S(1)}, bf16[3,4,2,64,128]{4,3,2,1,0:T(8,128)(2,1)S(1)}, u32[]{:S(2)}, u32[]{:S(2)}) %collective-permute-start.7) | collective-permute-done | bytes 393248 | tf_op jit(solution)/shard_map/ppermute | solution.py:359
  72.9 1.3 collective-permute-start.8
  74.2 1.6 collective-permute-start.10
  75.8 1.5 convert_reduce_fusion
  80.0 4.4 %own_forward.1 = (f32[1,1024]{1,0:T(1,128)S(1)}, f32[1,1024]{1,0:T(1,128)S(1)}, f32[4,128,256]{2,1,0:T(8,128)S(1)}) custom-call(s32[4]{0:T(128)S(1)} %and_select_fusion.lo_ref, s32[1]{0:T(128)} %bitcast.place_ref, s32[1,1024]{1,0:T(1,128)S(1)} %bitcast.138, bf16[2,512,128]{2,1,0:T(8,128)(2,1)S(1)} %bitcast.133, ...), custom_call_target="tpu_custom_call" | custom-call | flops 201326592 | bytes 4194304 | tf_op jit(solution)/shard_map/own_forward/pallas_call | solution.py:297
  84.7 2.3 %collective-permute-done.11 = bf16[8,2,64,128]{3,2,1,0:T(8,128)(2,1)S(1)} collective-permute-done((bf16[8,2,64,128]{3,2,1,0:T(8,128)(2,1)S(1)}, bf16[8,2,64,128]{3,2,1,0:T(8,128)(2,1)S(1)}, u32[]{:S(2)}, u32[]{:S(2)}) %collective-permute-start.11) | collective-permute-done | bytes 262176 | tf_op jit(solution)/shard_map/ppermute | solution.py:379
  87.1 7.7 %earlier.1 = (bf16[2,512,128]{2,1,0:T(8,128)(2,1)S(1)}, f32[1,1024]{1,0:T(1,128)S(1)}, f32[1,1024]{1,0:T(1,128)S(1)}, f32[4,128,256]{2,1,0:T(8,128)S(1)}, bf16[2...) custom-call(s32[4]{0:T(128)S(1)} %and_select_fusion.lo_ref, s32[1]{0:T(128)} %bitcast.place_ref, ...), custom_call_target="tpu_custom_call" | custom-call | flops 603979776 | bytes 4194304 | tf_op jit(solution)/shard_map/earlier/pallas_call | solution.py:297
  96.2 4.6 %collective-permute-start.15 = (bf16[8,2,64,128]{3,2,1,0:T(8,128)(2,1)S(1)}, bf16[8,2,64,128]{3,2,1,0:T(8,128)(2,1)S(1)}, u32[]{:S(2)}, u32[]{:S(2)}) collective-permute-start(bf16[8,2,64,128]{3,2,1,0:T(8,128)(2,1)S(1)} %get-tuple-element.40), channel_id=1, source_target_pairs={{0,16},{56,40},{64,80},{120,104},{128,144},{184,168},{192,208},{24... | collective-permute-start | bytes 786440 | tf_op jit(solution)/shard_map/ppermute | solution.py:433
  100.8 1.3 collective-permute-start.16
  103.4 5.9 %own_backward.1 = (bf16[2,512,128]{2,1,0:T(8,128)(2,1)S(1)}, bf16[2,512,128]{2,1,0:T(8,128)(2,1)S(1)}, f32[2,8,2,64,128]{4,3,2,1,0:T(8,128)S(1)}) custom-call(s32[4]{0:T(128)S(1)} %and_select_fusion.lo_ref, s32[1]{0:T(128)} %bitcast.place_ref, s32[1,1024]{1,0:T(1,128)S(1)} %bitcast.140, bf16[2,512,128]{2,1,0:T(8,128)(2,1)S(1)} %bitcast.135, ...), custom_call_target="tpu_custom_call" | custom-call | flops 503316480 | bytes 4194304 | tf_op jit(solution)/shard_map/own_backward/pallas_call | solution.py:297
  109.6 2.8 %collective-permute-done.14 = bf16[8,2,64,128]{3,2,1,0:T(8,128)(2,1)S(1)} collective-permute-done((bf16[8,2,64,128]{3,2,1,0:T(8,128)(2,1)S(1)}, bf16[8,2,64,128]{3,2,1,0:T(8,128)(2,1)S(1)}, u32[]{:S(2)}, u32[]{:S(2)}) %collective-permute-start.14) | collective-permute-done | bytes 262176 | tf_op jit(solution)/shard_map/ppermute | solution.py:435
  112.9 2.7 %collective-permute-start.17 = (bf16[3,4,2,64,128]{4,3,2,1,0:T(8,128)(2,1)S(1)}, bf16[3,4,2,64,128]{4,3,2,1,0:T(8,128)(2,1)S(1)}, u32[]{:S(2)}, u32[]{:S(2)}) collective-permute-start(bf16[3,4,2,64,128]{4,3,2,1,0:T(8,128)(2,1)S(1)} %select_convert_fusion), channel_id=1, source_target_pairs={{0,1},{1,0},{2,3},{3,2},{4,5},{5,4},{6,7},{7,6},{8,9},{9,8},{10,11... | collective-permute-start | bytes 1179656 | tf_op jit(solution)/shard_map/ppermute | solution.py:456
  115.6 2.3 %collective-permute-start.12 = (bf16[2,512,128]{2,1,0:T(8,128)(2,1)S(1)}, bf16[2,512,128]{2,1,0:T(8,128)(2,1)S(1)}, u32[]{:S(2)}, u32[]{:S(2)}) collective-permute-start(bf16[2,512,128]{2,1,0:T(8,128)(2,1)S(1)} %get-tuple-element.30), channel_id=1, source_target_pairs={{0,8},{8,0},{16,24},{24,16},{32,40},{40,32},{48,56},{56,48},{64,72... | collective-permute-start | bytes 786440 | tf_op jit(solution)/shard_map/ppermute | solution.py:477
  118.0 8.5 %collective-permute-done.17 = bf16[3,4,2,64,128]{4,3,2,1,0:T(8,128)(2,1)S(1)} collective-permute-done((bf16[3,4,2,64,128]{4,3,2,1,0:T(8,128)(2,1)S(1)}, bf16[3,4,2,64,128]{4,3,2,1,0:T(8,128)(2,1)S(1)}, u32[]{:S(2)}, u32[]{:S(2)}) %collective-permute-start.17) | collective-permute-done | bytes 393248 | tf_op jit(solution)/shard_map/ppermute | solution.py:456
  126.9 4.2 %collective-permute-start.18 = (bf16[3,2,2,64,128]{4,3,2,1,0:T(8,128)(2,1)S(1)}, bf16[3,2,2,64,128]{4,3,2,1,0:T(8,128)(2,1)S(1)}, u32[]{:S(2)}, u32[]{:S(2)}) collective-permute-start(bf16[3,2,2,64,128]{4,3,2,1,0:T(8,128)(2,1)S(1)} %select_convert_fusion.1), channel_id=1, source_target_pairs={{0,2},{1,3},{2,0},{3,1},{4,6},{5,7},{6,4},{7,5},{8,10},{9,11},{10,... | collective-permute-start | bytes 589832 | tf_op jit(solution)/shard_map/ppermute | solution.py:456
  131.1 9.5 %collective-permute-done.18 = bf16[3,2,2,64,128]{4,3,2,1,0:T(8,128)(2,1)S(1)} collective-permute-done((bf16[3,2,2,64,128]{4,3,2,1,0:T(8,128)(2,1)S(1)}, bf16[3,2,2,64,128]{4,3,2,1,0:T(8,128)(2,1)S(1)}, u32[]{:S(2)}, u32[]{:S(2)}) %collective-permute-start.18) | collective-permute-done | bytes 196640 | tf_op jit(solution)/shard_map/ppermute | solution.py:456
  140.8 1.9 %collective-permute-start.20 = (bf16[2,64,128]{2,1,0:T(8,128)(2,1)S(1)}, bf16[2,64,128]{2,1,0:T(8,128)(2,1)S(1)}, u32[]{:S(2)}, u32[]{:S(2)}) collective-permute-start(bf16[2,64,128]{2,1,0:T(8,128)(2,1)S(1)} %get-tuple-element.54), channel_id=1, source_target_pairs={{0,8},{8,0},{16,24},{24,16},{32,40},{40,32},{48,56},{56,48},{64,72... | collective-permute-start | bytes 98312 | tf_op jit(solution)/shard_map/ppermute | solution.py:465
  142.7 7.1 %collective-permute-start.19 = (bf16[2,64,128]{2,1,0:T(8,128)(2,1)S(1)}, bf16[2,64,128]{2,1,0:T(8,128)(2,1)S(1)}, u32[]{:S(2)}, u32[]{:S(2)}) collective-permute-start(bf16[2,64,128]{2,1,0:T(8,128)(2,1)S(1)} %get-tuple-element.56), channel_id=1, source_target_pairs={{0,4},{1,5},{2,6},{3,7},{4,0},{5,1},{6,2},{7,3},{8,12},{9,13},{10,... | collective-permute-start | bytes 98312 | tf_op jit(solution)/shard_map/ppermute | solution.py:466
  149.8 1.9 %collective-permute-start.23 = (bf16[2,64,128]{2,1,0:T(8,128)(2,1)S(1)}, bf16[2,64,128]{2,1,0:T(8,128)(2,1)S(1)}, u32[]{:S(2)}, u32[]{:S(2)}) collective-permute-start(bf16[2,64,128]{2,1,0:T(8,128)(2,1)S(1)} %get-tuple-element.57), channel_id=1, source_target_pairs={{87,56},{86,57},{85,58},{84,59},{83,60},{82,61},{81,62},{80,63},{7... | collective-permute-start | bytes 98312 | tf_op jit(solution)/shard_map/ppermute | solution.py:464
  151.7 2.5 %collective-permute-start.21 = (bf16[2,64,128]{2,1,0:T(8,128)(2,1)S(1)}, bf16[2,64,128]{2,1,0:T(8,128)(2,1)S(1)}, u32[]{:S(2)}, u32[]{:S(2)}) collective-permute-start(bf16[2,64,128]{2,1,0:T(8,128)(2,1)S(1)} %get-tuple-element.58), channel_id=1, source_target_pairs={{0,12},{1,13},{2,14},{3,15},{4,8},{5,9},{6,10},{7,11},{8,4},{9,5},... | collective-permute-start | bytes 98312 | tf_op jit(solution)/shard_map/ppermute | solution.py:467
  154.2 10.5 %collective-permute-start.22 = (bf16[2,64,128]{2,1,0:T(8,128)(2,1)S(1)}, bf16[2,64,128]{2,1,0:T(8,128)(2,1)S(1)}, u32[]{:S(2)}, u32[]{:S(2)}) collective-permute-start(bf16[2,64,128]{2,1,0:T(8,128)(2,1)S(1)} %get-tuple-element.35), channel_id=1, source_target_pairs={{83,56},{82,57},{81,58},{80,59},{87,60},{86,61},{85,62},{84,63},{7... | collective-permute-start | bytes 98312 | tf_op jit(solution)/shard_map/ppermute | solution.py:469
  165.6 3.3 %collective-permute-done.22 = bf16[2,64,128]{2,1,0:T(8,128)(2,1)S(1)} collective-permute-done((bf16[2,64,128]{2,1,0:T(8,128)(2,1)S(1)}, bf16[2,64,128]{2,1,0:T(8,128)(2,1)S(1)}, u32[]{:S(2)}, u32[]{:S(2)}) %collective-permute-start.22) | collective-permute-done | bytes 32800 | tf_op jit(solution)/shard_map/ppermute | solution.py:469
  (78 shorter events, 11.4 us)
Async XLA Ops:
  0.6 49.9 %copy-start = (bf16[1,2,512,128]{3,2,1,0:T(8,128)(2,1)S(1)}, bf16[1,2,512,128]{3,2,1,0:T(8,128)(2,1)}, u32[]{:S(2)}) copy-start(bf16[1,2,512,128]{3,2,1,0:T(8,128)(2,1)} %param.5) | copy-start | bytes 786436
  2.2 31.5 %collective-permute-start.3 = (bf16[2,64,128]{2,1,0:T(8,128)(2,1)S(1)}, bf16[2,64,128]{2,1,0:T(8,128)(2,1)S(1)}, u32[]{:S(2)}, u32[]{:S(2)}) collective-permute-start(bf16[2,64,128]{2,1,0:T(8,128)(2,1)S(1)} %get-tuple-element.63), channel_id=1, source_target_pairs={{0,12},{1,13},{2,14},{3,15},{4,8},{5,9},{6,10},{7,11},{8,4},{9,5},... | collective-permute-start | bytes 98312 | tf_op jit(solution)/shard_map/ppermute | solution.py:348
  10.7 17.2 %collective-permute-start.2 = (bf16[2,64,128]{2,1,0:T(8,128)(2,1)S(1)}, bf16[2,64,128]{2,1,0:T(8,128)(2,1)S(1)}, u32[]{:S(2)}, u32[]{:S(2)}) collective-permute-start(bf16[2,64,128]{2,1,0:T(8,128)(2,1)S(1)} %get-tuple-element.63), channel_id=1, source_target_pairs={{0,8},{8,0},{16,24},{24,16},{32,40},{40,32},{48,56},{56,48},{64,72... | collective-permute-start | bytes 98312 | tf_op jit(solution)/shard_map/ppermute | solution.py:346
  13.3 20.3 %collective-permute-start.1 = (bf16[2,64,128]{2,1,0:T(8,128)(2,1)S(1)}, bf16[2,64,128]{2,1,0:T(8,128)(2,1)S(1)}, u32[]{:S(2)}, u32[]{:S(2)}) collective-permute-start(bf16[2,64,128]{2,1,0:T(8,128)(2,1)S(1)} %get-tuple-element.61), channel_id=1, source_target_pairs={{0,4},{1,5},{2,6},{3,7},{4,0},{5,1},{6,2},{7,3},{8,12},{9,13},{10,... | collective-permute-start | bytes 98312 | tf_op jit(solution)/shard_map/ppermute | solution.py:347
  15.3 18.6 %collective-permute-start.5 = (bf16[2,64,128]{2,1,0:T(8,128)(2,1)S(1)}, bf16[2,64,128]{2,1,0:T(8,128)(2,1)S(1)}, u32[]{:S(2)}, u32[]{:S(2)}) collective-permute-start(bf16[2,64,128]{2,1,0:T(8,128)(2,1)S(1)} %get-tuple-element.21), channel_id=1, source_target_pairs={{56,87},{57,86},{58,85},{59,84},{60,83},{61,82},{62,81},{63,80},{4... | collective-permute-start | bytes 98312 | tf_op jit(solution)/shard_map/ppermute | solution.py:345
  27.9 14.5 %collective-permute-start.4 = (bf16[2,64,128]{2,1,0:T(8,128)(2,1)S(1)}, bf16[2,64,128]{2,1,0:T(8,128)(2,1)S(1)}, u32[]{:S(2)}, u32[]{:S(2)}) collective-permute-start(bf16[2,64,128]{2,1,0:T(8,128)(2,1)S(1)} %get-tuple-element.21), channel_id=1, source_target_pairs={{56,83},{57,82},{58,81},{59,80},{60,87},{61,86},{62,85},{63,84},{4... | collective-permute-start | bytes 98312 | tf_op jit(solution)/shard_map/ppermute | solution.py:350
  42.5 19.5 %copy-start.1 = (bf16[1,2,512,128]{3,2,1,0:T(8,128)(2,1)S(1)}, bf16[1,2,512,128]{3,2,1,0:T(8,128)(2,1)}, u32[]{:S(2)}) copy-start(bf16[1,2,512,128]{3,2,1,0:T(8,128)(2,1)} %param.8) | copy-start | bytes 786436
  42.6 17.3 %collective-permute-start.6 = (bf16[3,2,2,64,128]{4,3,2,1,0:T(8,128)(2,1)S(1)}, bf16[3,2,2,64,128]{4,3,2,1,0:T(8,128)(2,1)S(1)}, u32[]{:S(2)}, u32[]{:S(2)}) collective-permute-start(bf16[3,2,2,64,128]{4,3,2,1,0:T(8,128)(2,1)S(1)} %pad_maximum_fusion.2), channel_id=1, source_target_pairs={{0,2},{1,3},{2,0},{3,1},{4,6},{5,7},{6,4},{7,5},{8,10},{9,11},{10,... | collective-permute-start | bytes 589832 | tf_op jit(solution)/shard_map/ppermute | solution.py:359
  59.9 4.3 %copy-start.2 = (s32[65536]{0:T(1024)S(1)}, s32[65536]{0:T(1024)}, u32[]{:S(2)}) copy-start(s32[65536]{0:T(1024)} %param.9) | copy-start | bytes 786436
  60.1 12.6 %collective-permute-start.7 = (bf16[3,4,2,64,128]{4,3,2,1,0:T(8,128)(2,1)S(1)}, bf16[3,4,2,64,128]{4,3,2,1,0:T(8,128)(2,1)S(1)}, u32[]{:S(2)}, u32[]{:S(2)}) collective-permute-start(bf16[3,4,2,64,128]{4,3,2,1,0:T(8,128)(2,1)S(1)} %broadcast_select_fusion.1), channel_id=1, source_target_pairs={{0,1},{1,0},{2,3},{3,2},{4,5},{5,4},{6,7},{7,6},{8,9},{9,8},{10,11... | collective-permute-start | bytes 1179656 | tf_op jit(solution)/shard_map/ppermute | solution.py:359
  62.2 17.9 %collective-permute-start = (bf16[2,512,128]{2,1,0:T(8,128)(2,1)S(1)}, bf16[2,512,128]{2,1,0:T(8,128)(2,1)S(1)}, u32[]{:S(2)}, u32[]{:S(2)}) collective-permute-start(bf16[2,512,128]{2,1,0:T(8,128)(2,1)S(1)} %maximum_select_fusion), channel_id=1, source_target_pairs={{0,8},{8,0},{16,24},{24,16},{32,40},{40,32},{48,56},{56,48},{64,72... | collective-permute-start | bytes 786440 | tf_op jit(solution)/shard_map/ppermute | solution.py:367
  72.9 11.6 %collective-permute-start.8 = (bf16[8,2,64,128]{3,2,1,0:T(8,128)(2,1)S(1)}, bf16[8,2,64,128]{3,2,1,0:T(8,128)(2,1)S(1)}, u32[]{:S(2)}, u32[]{:S(2)}) collective-permute-start(bf16[8,2,64,128]{3,2,1,0:T(8,128)(2,1)S(1)} %bitcast.150), channel_id=1, source_target_pairs={{0,32},{16,48},{40,8},{56,24},{64,96},{80,112},{104,72},{120,88},{... | collective-permute-start | bytes 786440 | tf_op jit(solution)/shard_map/ppermute | solution.py:377
  74.2 10.3 %collective-permute-start.10 = (bf16[2,8,2,64,128]{4,3,2,1,0:T(8,128)(2,1)S(1)}, bf16[2,8,2,64,128]{4,3,2,1,0:T(8,128)(2,1)S(1)}, u32[]{:S(2)}, u32[]{:S(2)}) collective-permute-start(bf16[2,8,2,64,128]{4,3,2,1,0:T(8,128)(2,1)S(1)} %bitcast.130), channel_id=1, source_target_pairs={{0,16},{16,32},{32,48},{24,8},{40,24},{56,40},{64,80},{80,96},{96,... | collective-permute-start | bytes 1572872 | tf_op jit(solution)/shard_map/ppermute | solution.py:378
  77.4 7.3 %collective-permute-start.9 = (bf16[8,2,64,128]{3,2,1,0:T(8,128)(2,1)S(1)}, bf16[8,2,64,128]{3,2,1,0:T(8,128)(2,1)S(1)}, u32[]{:S(2)}, u32[]{:S(2)}) collective-permute-start(bf16[8,2,64,128]{3,2,1,0:T(8,128)(2,1)S(1)} %bitcast.148), channel_id=1, source_target_pairs={{8,0},{48,56},{72,64},{112,120},{136,128},{176,184},{200,192},{240... | collective-permute-start | bytes 786440 | tf_op jit(solution)/shard_map/ppermute | solution.py:380
  78.7 8.3 %collective-permute-start.11 = (bf16[8,2,64,128]{3,2,1,0:T(8,128)(2,1)S(1)}, bf16[8,2,64,128]{3,2,1,0:T(8,128)(2,1)S(1)}, u32[]{:S(2)}, u32[]{:S(2)}) collective-permute-start(bf16[8,2,64,128]{3,2,1,0:T(8,128)(2,1)S(1)} %bitcast.149), channel_id=1, source_target_pairs={{16,0},{40,56},{80,64},{104,120},{144,128},{168,184},{208,192},{23... | collective-permute-start | bytes 786440 | tf_op jit(solution)/shard_map/ppermute | solution.py:379
  94.8 14.6 %collective-permute-start.13 = (bf16[2,8,2,64,128]{4,3,2,1,0:T(8,128)(2,1)S(1)}, bf16[2,8,2,64,128]{4,3,2,1,0:T(8,128)(2,1)S(1)}, u32[]{:S(2)}, u32[]{:S(2)}) collective-permute-start(bf16[2,8,2,64,128]{4,3,2,1,0:T(8,128)(2,1)S(1)} %get-tuple-element.32), channel_id=1, source_target_pairs={{16,0},{32,16},{48,32},{8,24},{24,40},{40,56},{80,64},{96,80},{112... | collective-permute-start | bytes 1572872 | tf_op jit(solution)/shard_map/ppermute | solution.py:436
  96.2 13.1 %collective-permute-start.15 = (bf16[8,2,64,128]{3,2,1,0:T(8,128)(2,1)S(1)}, bf16[8,2,64,128]{3,2,1,0:T(8,128)(2,1)S(1)}, u32[]{:S(2)}, u32[]{:S(2)}) collective-permute-start(bf16[8,2,64,128]{3,2,1,0:T(8,128)(2,1)S(1)} %get-tuple-element.40), channel_id=1, source_target_pairs={{0,16},{56,40},{64,80},{120,104},{128,144},{184,168},{192,208},{24... | collective-permute-start | bytes 786440 | tf_op jit(solution)/shard_map/ppermute | solution.py:433
  100.8 8.6 %collective-permute-start.16 = (bf16[8,2,64,128]{3,2,1,0:T(8,128)(2,1)S(1)}, bf16[8,2,64,128]{3,2,1,0:T(8,128)(2,1)S(1)}, u32[]{:S(2)}, u32[]{:S(2)}) collective-permute-start(bf16[8,2,64,128]{3,2,1,0:T(8,128)(2,1)S(1)} %get-tuple-element.41), channel_id=1, source_target_pairs={{0,8},{56,48},{64,72},{120,112},{128,136},{184,176},{192,200},{248... | collective-permute-start | bytes 786440 | tf_op jit(solution)/shard_map/ppermute | solution.py:434
  102.1 10.4 %collective-permute-start.14 = (bf16[8,2,64,128]{3,2,1,0:T(8,128)(2,1)S(1)}, bf16[8,2,64,128]{3,2,1,0:T(8,128)(2,1)S(1)}, u32[]{:S(2)}, u32[]{:S(2)}) collective-permute-start(bf16[8,2,64,128]{3,2,1,0:T(8,128)(2,1)S(1)} %get-tuple-element.33), channel_id=1, source_target_pairs={{32,0},{48,16},{8,40},{24,56},{96,64},{112,80},{72,104},{88,120},{... | collective-permute-start | bytes 786440 | tf_op jit(solution)/shard_map/ppermute | solution.py:435
  112.9 13.6 %collective-permute-start.17 = (bf16[3,4,2,64,128]{4,3,2,1,0:T(8,128)(2,1)S(1)}, bf16[3,4,2,64,128]{4,3,2,1,0:T(8,128)(2,1)S(1)}, u32[]{:S(2)}, u32[]{:S(2)}) collective-permute-start(bf16[3,4,2,64,128]{4,3,2,1,0:T(8,128)(2,1)S(1)} %select_convert_fusion), channel_id=1, source_target_pairs={{0,1},{1,0},{2,3},{3,2},{4,5},{5,4},{6,7},{7,6},{8,9},{9,8},{10,11... | collective-permute-start | bytes 1179656 | tf_op jit(solution)/shard_map/ppermute | solution.py:456
  115.6 15.4 %collective-permute-start.12 = (bf16[2,512,128]{2,1,0:T(8,128)(2,1)S(1)}, bf16[2,512,128]{2,1,0:T(8,128)(2,1)S(1)}, u32[]{:S(2)}, u32[]{:S(2)}) collective-permute-start(bf16[2,512,128]{2,1,0:T(8,128)(2,1)S(1)} %get-tuple-element.30), channel_id=1, source_target_pairs={{0,8},{8,0},{16,24},{24,16},{32,40},{40,32},{48,56},{56,48},{64,72... | collective-permute-start | bytes 786440 | tf_op jit(solution)/shard_map/ppermute | solution.py:477
  126.9 13.7 %collective-permute-start.18 = (bf16[3,2,2,64,128]{4,3,2,1,0:T(8,128)(2,1)S(1)}, bf16[3,2,2,64,128]{4,3,2,1,0:T(8,128)(2,1)S(1)}, u32[]{:S(2)}, u32[]{:S(2)}) collective-permute-start(bf16[3,2,2,64,128]{4,3,2,1,0:T(8,128)(2,1)S(1)} %select_convert_fusion.1), channel_id=1, source_target_pairs={{0,2},{1,3},{2,0},{3,1},{4,6},{5,7},{6,4},{7,5},{8,10},{9,11},{10,... | collective-permute-start | bytes 589832 | tf_op jit(solution)/shard_map/ppermute | solution.py:456
  140.8 13.5 %collective-permute-start.20 = (bf16[2,64,128]{2,1,0:T(8,128)(2,1)S(1)}, bf16[2,64,128]{2,1,0:T(8,128)(2,1)S(1)}, u32[]{:S(2)}, u32[]{:S(2)}) collective-permute-start(bf16[2,64,128]{2,1,0:T(8,128)(2,1)S(1)} %get-tuple-element.54), channel_id=1, source_target_pairs={{0,8},{8,0},{16,24},{24,16},{32,40},{40,32},{48,56},{56,48},{64,72... | collective-permute-start | bytes 98312 | tf_op jit(solution)/shard_map/ppermute | solution.py:465
  142.7 22.9 %collective-permute-start.19 = (bf16[2,64,128]{2,1,0:T(8,128)(2,1)S(1)}, bf16[2,64,128]{2,1,0:T(8,128)(2,1)S(1)}, u32[]{:S(2)}, u32[]{:S(2)}) collective-permute-start(bf16[2,64,128]{2,1,0:T(8,128)(2,1)S(1)} %get-tuple-element.56), channel_id=1, source_target_pairs={{0,4},{1,5},{2,6},{3,7},{4,0},{5,1},{6,2},{7,3},{8,12},{9,13},{10,... | collective-permute-start | bytes 98312 | tf_op jit(solution)/shard_map/ppermute | solution.py:466
  149.8 15.8 %collective-permute-start.23 = (bf16[2,64,128]{2,1,0:T(8,128)(2,1)S(1)}, bf16[2,64,128]{2,1,0:T(8,128)(2,1)S(1)}, u32[]{:S(2)}, u32[]{:S(2)}) collective-permute-start(bf16[2,64,128]{2,1,0:T(8,128)(2,1)S(1)} %get-tuple-element.57), channel_id=1, source_target_pairs={{87,56},{86,57},{85,58},{84,59},{83,60},{82,61},{81,62},{80,63},{7... | collective-permute-start | bytes 98312 | tf_op jit(solution)/shard_map/ppermute | solution.py:464
  151.7 13.9 %collective-permute-start.21 = (bf16[2,64,128]{2,1,0:T(8,128)(2,1)S(1)}, bf16[2,64,128]{2,1,0:T(8,128)(2,1)S(1)}, u32[]{:S(2)}, u32[]{:S(2)}) collective-permute-start(bf16[2,64,128]{2,1,0:T(8,128)(2,1)S(1)} %get-tuple-element.58), channel_id=1, source_target_pairs={{0,12},{1,13},{2,14},{3,15},{4,8},{5,9},{6,10},{7,11},{8,4},{9,5},... | collective-permute-start | bytes 98312 | tf_op jit(solution)/shard_map/ppermute | solution.py:467
  154.2 14.7 %collective-permute-start.22 = (bf16[2,64,128]{2,1,0:T(8,128)(2,1)S(1)}, bf16[2,64,128]{2,1,0:T(8,128)(2,1)S(1)}, u32[]{:S(2)}, u32[]{:S(2)}) collective-permute-start(bf16[2,64,128]{2,1,0:T(8,128)(2,1)S(1)} %get-tuple-element.35), channel_id=1, source_target_pairs={{83,56},{82,57},{81,58},{80,59},{87,60},{86,61},{85,62},{84,63},{7... | collective-permute-start | bytes 98312 | tf_op jit(solution)/shard_map/ppermute | solution.py:469

commit v9 on v6

--- a/solution.py
+++ b/solution.py
@@ -342,16 +342,16 @@
     upper = jnp.stack([key_states[0, 1], value_states[0, 1]])
     leaving = pick(sends_lower, upper, lower)
     half = by_bit(core, pick(even, upper, lower), lax.ppermute(pick(even, lower, upper), CTX, swap), 0)
-    half, leaving = lax.optimization_barrier((half, leaving))
-    kv_own, kv_edge = half, lax.ppermute(leaving, everywhere, edge)
-    for k, bit in enumerate(bits):
-        other = lax.ppermute(kv_own, everywhere, head_pairs(ctx, heads, bit))
-        kv_own = by_bit(high[bit], kv_own, other, 1 + k)
-    for k, bit in enumerate(bits):
-        other = lax.ppermute(kv_edge, everywhere, holder_pairs(ctx, heads, bit))
-        kv_edge = by_bit(~high[bit], kv_edge, other, k)
-    kv_own = kv_own.reshape((2, heads) + half.shape[1:])
-    kv_edge = kv_edge.reshape((heads,) + half.shape[1:])
+    crossed = lax.ppermute(leaving, everywhere, edge)
+    kv_all = jnp.concatenate([half, crossed[None]])[:, None]
+    is_edge = lax.broadcasted_iota(jnp.int32, (3, 1, 1, 1, 1, 1), 0) == 2
+    slot = lax.broadcasted_iota(jnp.int32, (1, 1, 2, 1, 1, 1), 2) == 1
+    for bit in bits:
+        other = lax.ppermute(kv_all, everywhere, head_pairs(ctx, heads, bit))
+        stays = slot == (high[bit] ^ is_edge)
+        kv_all = jnp.where(stays, kv_all[:, :, None], other[:, :, None])
+        kv_all = kv_all.reshape((3, -1) + half.shape[1:])
+    kv_own, kv_edge = kv_all[:2], kv_all[2]
 
     queries, out_grad = queries[0], out_grad[0]
     far = lax.ppermute(

time: 158 us -> 151 us (0.956)
  the two profiles are of different devices: /device:TPU:6 before, /device:TPU:100 now
where the time goes in v9:
time: 151 us; the launch traced here: 150 us
  starting transfers between devices  79.5 us (53%)
  waiting for transfers between devices  49.7 us (33%)
  Pallas kernels  12.3 us (8%)
  other arithmetic  4.78 us (3%)
  local copies, waits for them, and re-layouts  2.45 us (2%)
    ppermute x3, waiting for transfers between devices, body(): other = lax.ppermute(kv_all, everywhere, head_pairs(ctx, heads, bit))  24.3 us
    ppermute x3, starting transfers between devices, body(): other = lax.ppermute(away, everywhere, holder_pairs(ctx, heads, bit))  15.2 us
    ppermute x3, waiting for transfers between devices, body(): other = lax.ppermute(away, everywhere, head_pairs(ctx, heads, bit))  14.4 us
    ppermute x1, starting transfers between devices, body(): crossed = lax.ppermute(leaving, everywhere, edge)  13.4 us
    pallas_call x3, Pallas kernels, call(): pl.pallas_call(kernel, out_shape=outputs, in_specs=[pl.BlockSpec(memory_s...  12.3 us
    ppermute x3, starting transfers between devices, body(): other = lax.ppermute(kv_all, everywhere, head_pairs(ctx, heads, bit))  10.5 us
    ppermute x1, starting transfers between devices, body(): back = lax.ppermute(out_far, CTX, swap)  10.2 us
    ppermute x3, starting transfers between devices, body(): other = lax.ppermute(away, everywhere, head_pairs(ctx, heads, bit))  8.25 us
  transfers between devices with their start and end apart: 23, of which 10 were waited for; matrix products, arithmetic and copies ran while one was open for 3% of the time, Pallas kernels for 6%

profile of v9, /device:TPU:100, one launch (start us, length us, event | category | flops | bytes accessed | tf_op | source)
XLA Modules:
  0.0 150.0 jit_solution(2111240938552932630)
XLA Ops:
  2.2 13.4 %collective-permute-start.2 = (bf16[2,64,128]{2,1,0:T(8,128)(2,1)S(1)}, bf16[2,64,128]{2,1,0:T(8,128)(2,1)S(1)}, u32[]{:S(2)}, u32[]{:S(2)}) collective-permute-start(bf16[2,64,128]{2,1,0:T(8,128)(2,1)S(1)} %get-tuple-element.51), channel_id=1, source_target_pairs={{56,87},{57,86},{58,85},{59,84},{60,83},{61,82},{62,81},{63,80},{4... | collective-permute-start | bytes 98312 | tf_op jit(solution)/shard_map/ppermute | solution.py:345
  15.6 2.4 %collective-permute-start.1 = (bf16[2,64,128]{2,1,0:T(8,128)(2,1)S(1)}, bf16[2,64,128]{2,1,0:T(8,128)(2,1)S(1)}, u32[]{:S(2)}, u32[]{:S(2)}) collective-permute-start(bf16[2,64,128]{2,1,0:T(8,128)(2,1)S(1)} %get-tuple-element.52), channel_id=1, source_target_pairs={{0,8},{8,0},{16,24},{24,16},{32,40},{40,32},{48,56},{56,48},{64,72... | collective-permute-start | bytes 98312 | tf_op jit(solution)/shard_map/ppermute | solution.py:344
  19.0 2.8 %collective-permute-start.3 = (bf16[3,1,2,64,128]{4,3,2,0,1:T(8,128)(2,1)S(1)}, bf16[3,1,2,64,128]{4,3,2,0,1:T(8,128)(2,1)S(1)}, u32[]{:S(2)}, u32[]{:S(2)}) collective-permute-start(bf16[3,1,2,64,128]{4,3,2,0,1:T(8,128)(2,1)S(1)} %get-tuple-element.47), channel_id=1, source_target_pairs={{0,4},{1,5},{2,6},{3,7},{4,0},{5,1},{6,2},{7,3},{8,12},{9,13},{10,... | collective-permute-start | bytes 294920 | tf_op jit(solution)/shard_map/ppermute | solution.py:350
  22.1 8.6 %collective-permute-done.3 = bf16[3,1,2,64,128]{4,3,2,0,1:T(8,128)(2,1)S(1)} collective-permute-done((bf16[3,1,2,64,128]{4,3,2,0,1:T(8,128)(2,1)S(1)}, bf16[3,1,2,64,128]{4,3,2,0,1:T(8,128)(2,1)S(1)}, u32[]{:S(2)}, u32[]{:S(2)}) %collective-permute-start.3) | collective-permute-done | bytes 98336 | tf_op jit(solution)/shard_map/ppermute | solution.py:350
  30.7 5.1 %collective-permute-start.4 = (bf16[3,2,2,64,128]{4,3,2,1,0:T(8,128)(2,1)S(1)}, bf16[3,2,2,64,128]{4,3,2,1,0:T(8,128)(2,1)S(1)}, u32[]{:S(2)}, u32[]{:S(2)}) collective-permute-start(bf16[3,2,2,64,128]{4,3,2,1,0:T(8,128)(2,1)S(1)} %broadcast_select_fusion.2), channel_id=1, source_target_pairs={{0,2},{1,3},{2,0},{3,1},{4,6},{5,7},{6,4},{7,5},{8,10},{9,11},{10,... | collective-permute-start | bytes 589832 | tf_op jit(solution)/shard_map/ppermute | solution.py:350
  35.9 8.7 %collective-permute-done.4 = bf16[3,2,2,64,128]{4,3,2,1,0:T(8,128)(2,1)S(1)} collective-permute-done((bf16[3,2,2,64,128]{4,3,2,1,0:T(8,128)(2,1)S(1)}, bf16[3,2,2,64,128]{4,3,2,1,0:T(8,128)(2,1)S(1)}, u32[]{:S(2)}, u32[]{:S(2)}) %collective-permute-start.4) | collective-permute-done | bytes 196640 | tf_op jit(solution)/shard_map/ppermute | solution.py:350
  44.9 2.6 %collective-permute-start.5 = (bf16[3,4,2,64,128]{4,3,2,1,0:T(8,128)(2,1)S(1)}, bf16[3,4,2,64,128]{4,3,2,1,0:T(8,128)(2,1)S(1)}, u32[]{:S(2)}, u32[]{:S(2)}) collective-permute-start(bf16[3,4,2,64,128]{4,3,2,1,0:T(8,128)(2,1)S(1)} %broadcast_select_fusion.1), channel_id=1, source_target_pairs={{0,1},{1,0},{2,3},{3,2},{4,5},{5,4},{6,7},{7,6},{8,9},{9,8},{10,11... | collective-permute-start | bytes 1179656 | tf_op jit(solution)/shard_map/ppermute | solution.py:350
  47.6 1.9 %collective-permute-start = (bf16[2,512,128]{2,1,0:T(8,128)(2,1)S(1)}, bf16[2,512,128]{2,1,0:T(8,128)(2,1)S(1)}, u32[]{:S(2)}, u32[]{:S(2)}) collective-permute-start(bf16[2,512,128]{2,1,0:T(8,128)(2,1)S(1)} %maximum_select_fusion), channel_id=1, source_target_pairs={{0,8},{8,0},{16,24},{24,16},{32,40},{40,32},{48,56},{56,48},{64,72... | collective-permute-start | bytes 786440 | tf_op jit(solution)/shard_map/ppermute | solution.py:357
  49.8 7.0 %collective-permute-done.5 = bf16[3,4,2,64,128]{4,3,2,1,0:T(8,128)(2,1)S(1)} collective-permute-done((bf16[3,4,2,64,128]{4,3,2,1,0:T(8,128)(2,1)S(1)}, bf16[3,4,2,64,128]{4,3,2,1,0:T(8,128)(2,1)S(1)}, u32[]{:S(2)}, u32[]{:S(2)}) %collective-permute-start.5) | collective-permute-done | bytes 393248 | tf_op jit(solution)/shard_map/ppermute | solution.py:350
  57.0 3.9 %collective-permute-start.6 = (bf16[8,2,64,128]{3,2,1,0:T(8,128)(2,1)S(1)}, bf16[8,2,64,128]{3,2,1,0:T(8,128)(2,1)S(1)}, u32[]{:S(2)}, u32[]{:S(2)}) collective-permute-start(bf16[8,2,64,128]{3,2,1,0:T(8,128)(2,1)S(1)} %bitcast.255), channel_id=1, source_target_pairs={{0,32},{16,48},{40,8},{56,24},{64,96},{80,112},{104,72},{120,88},{... | collective-permute-start | bytes 786440 | tf_op jit(solution)/shard_map/ppermute | solution.py:367
  61.0 2.0 %collective-permute-start.8 = (bf16[2,8,2,64,128]{4,3,2,1,0:T(8,128)(2,1)S(1)}, bf16[2,8,2,64,128]{4,3,2,1,0:T(8,128)(2,1)S(1)}, u32[]{:S(2)}, u32[]{:S(2)}) collective-permute-start(bf16[2,8,2,64,128]{4,3,2,1,0:T(8,128)(2,1)S(1)} %bitcast.228), channel_id=1, source_target_pairs={{0,16},{16,32},{32,48},{24,8},{40,24},{56,40},{64,80},{80,96},{96,... | collective-permute-start | bytes 1572872 | tf_op jit(solution)/shard_map/ppermute | solution.py:368
  63.0 1.5 convert_reduce_fusion
  67.2 3.7 %own_forward.1 = (f32[1,1024]{1,0:T(1,128)S(1)}, f32[1,1024]{1,0:T(1,128)S(1)}, f32[4,128,256]{2,1,0:T(8,128)S(1)}) custom-call(s32[4]{0:T(128)S(1)} %and_select_fusion.lo_ref, s32[1]{0:T(128)} %bitcast.place_ref, s32[1,1024]{1,0:T(1,128)S(1)} %bitcast.236, bf16[2,512,128]{2,1,0:T(8,128)(2,1)S(1)} %bitcast.231, ...), custom_call_target="tpu_custom_call" | custom-call | flops 201326592 | bytes 4194304 | tf_op jit(solution)/shard_map/own_forward/pallas_call | solution.py:301
  71.1 3.0 %collective-permute-done.9 = bf16[8,2,64,128]{3,2,1,0:T(8,128)(2,1)S(1)} collective-permute-done((bf16[8,2,64,128]{3,2,1,0:T(8,128)(2,1)S(1)}, bf16[8,2,64,128]{3,2,1,0:T(8,128)(2,1)S(1)}, u32[]{:S(2)}, u32[]{:S(2)}) %collective-permute-start.9) | collective-permute-done | bytes 262176 | tf_op jit(solution)/shard_map/ppermute | solution.py:369
  74.3 3.8 %earlier.1 = (bf16[2,512,128]{2,1,0:T(8,128)(2,1)S(1)}, f32[1,1024]{1,0:T(1,128)S(1)}, f32[1,1024]{1,0:T(1,128)S(1)}, f32[4,128,256]{2,1,0:T(8,128)S(1)}, bf16[2...) custom-call(s32[4]{0:T(128)S(1)} %and_select_fusion.lo_ref, s32[1]{0:T(128)} %bitcast.place_ref, ...), custom_call_target="tpu_custom_call" | custom-call | flops 603979776 | bytes 4194304 | tf_op jit(solution)/shard_map/earlier/pallas_call | solution.py:301
  78.1 1.3 collective-permute-start.17
  79.5 1.3 collective-permute-start.18
  83.4 4.8 %own_backward.1 = (bf16[2,512,128]{2,1,0:T(8,128)(2,1)S(1)}, bf16[2,512,128]{2,1,0:T(8,128)(2,1)S(1)}, f32[2,8,2,64,128]{4,3,2,1,0:T(8,128)S(1)}) custom-call(s32[4]{0:T(128)S(1)} %and_select_fusion.lo_ref, s32[1]{0:T(128)} %bitcast.place_ref, s32[1,1024]{1,0:T(1,128)S(1)} %bitcast.238, bf16[2,512,128]{2,1,0:T(8,128)(2,1)S(1)} %bitcast.233, ...), custom_call_target="tpu_custom_call" | custom-call | flops 503316480 | bytes 4194304 | tf_op jit(solution)/shard_map/own_backward/pallas_call | solution.py:301
  88.4 3.6 %collective-permute-start.19 = (bf16[4,2,64,128]{3,2,1,0:T(8,128)(2,1)S(1)}, bf16[4,2,64,128]{3,2,1,0:T(8,128)(2,1)S(1)}, u32[]{:S(2)}, u32[]{:S(2)}) collective-permute-start(bf16[4,2,64,128]{3,2,1,0:T(8,128)(2,1)S(1)} %fusion.15), channel_id=1, source_target_pairs={{0,1},{1,0},{2,3},{3,2},{4,5},{5,4},{6,7},{7,6},{8,9},{9,8},{10,11... | collective-permute-start | bytes 393224 | tf_op jit(solution)/shard_map/ppermute | solution.py:440
  92.1 10.2 %collective-permute-start.10 = (bf16[2,512,128]{2,1,0:T(8,128)(2,1)S(1)}, bf16[2,512,128]{2,1,0:T(8,128)(2,1)S(1)}, u32[]{:S(2)}, u32[]{:S(2)}) collective-permute-start(bf16[2,512,128]{2,1,0:T(8,128)(2,1)S(1)} %get-tuple-element.24), channel_id=1, source_target_pairs={{0,8},{8,0},{16,24},{24,16},{32,40},{40,32},{48,56},{56,48},{64,72... | collective-permute-start | bytes 786440 | tf_op jit(solution)/shard_map/ppermute | solution.py:461
  102.4 5.3 %collective-permute-start.20 = (bf16[2,2,64,128]{3,2,1,0:T(8,128)(2,1)S(1)}, bf16[2,2,64,128]{3,2,1,0:T(8,128)(2,1)S(1)}, u32[]{:S(2)}, u32[]{:S(2)}) collective-permute-start(bf16[2,2,64,128]{3,2,1,0:T(8,128)(2,1)S(1)} %fusion.24), channel_id=1, source_target_pairs={{0,2},{1,3},{2,0},{3,1},{4,6},{5,7},{6,4},{7,5},{8,10},{9,11},{10,... | collective-permute-start | bytes 196616 | tf_op jit(solution)/shard_map/ppermute | solution.py:440
  108.1 2.5 %collective-permute-start.13 = (bf16[2,4,2,64,128]{4,3,2,1,0:T(8,128)(2,1)S(1)}, bf16[2,4,2,64,128]{4,3,2,1,0:T(8,128)(2,1)S(1)}, u32[]{:S(2)}, u32[]{:S(2)}) collective-permute-start(bf16[2,4,2,64,128]{4,3,2,1,0:T(8,128)(2,1)S(1)} %fusion.6), channel_id=1, source_target_pairs={{0,1},{1,0},{2,3},{3,2},{4,5},{5,4},{6,7},{7,6},{8,9},{9,8},{10,11... | collective-permute-start | bytes 786440 | tf_op jit(solution)/shard_map/ppermute | solution.py:450
  110.6 1.4 collective-permute-done.20
  112.0 6.6 %collective-permute-done.13 = bf16[2,4,2,64,128]{4,3,2,1,0:T(8,128)(2,1)S(1)} collective-permute-done((bf16[2,4,2,64,128]{4,3,2,1,0:T(8,128)(2,1)S(1)}, bf16[2,4,2,64,128]{4,3,2,1,0:T(8,128)(2,1)S(1)}, u32[]{:S(2)}, u32[]{:S(2)}) %collective-permute-start.13) | collective-permute-done | bytes 262176 | tf_op jit(solution)/shard_map/ppermute | solution.py:450
  118.7 2.2 %collective-permute-start.14 = (bf16[2,2,2,64,128]{4,3,2,1,0:T(8,128)(2,1)S(1)}, bf16[2,2,2,64,128]{4,3,2,1,0:T(8,128)(2,1)S(1)}, u32[]{:S(2)}, u32[]{:S(2)}) collective-permute-start(bf16[2,2,2,64,128]{4,3,2,1,0:T(8,128)(2,1)S(1)} %fusion.14), channel_id=1, source_target_pairs={{0,2},{1,3},{2,0},{3,1},{4,6},{5,7},{6,4},{7,5},{8,10},{9,11},{10,... | collective-permute-start | bytes 393224 | tf_op jit(solution)/shard_map/ppermute | solution.py:450
  121.0 6.3 %collective-permute-start.21 = (bf16[1,2,64,128]{3,2,1,0:T(8,128)(2,1)S(1)}, bf16[1,2,64,128]{3,2,1,0:T(8,128)(2,1)S(1)}, u32[]{:S(2)}, u32[]{:S(2)}) collective-permute-start(bf16[1,2,64,128]{3,2,1,0:T(8,128)(2,1)S(1)} %fusion.27), channel_id=1, source_target_pairs={{0,4},{1,5},{2,6},{3,7},{4,0},{5,1},{6,2},{7,3},{8,12},{9,13},{10,... | collective-permute-start | bytes 98312 | tf_op jit(solution)/shard_map/ppermute | solution.py:440
  127.3 3.3 %collective-permute-done.14 = bf16[2,2,2,64,128]{4,3,2,1,0:T(8,128)(2,1)S(1)} collective-permute-done((bf16[2,2,2,64,128]{4,3,2,1,0:T(8,128)(2,1)S(1)}, bf16[2,2,2,64,128]{4,3,2,1,0:T(8,128)(2,1)S(1)}, u32[]{:S(2)}, u32[]{:S(2)}) %collective-permute-start.14) | collective-permute-done | bytes 131104 | tf_op jit(solution)/shard_map/ppermute | solution.py:450
  130.6 3.6 %collective-permute-start.15 = (bf16[2,1,2,64,128]{4,3,2,0,1:T(8,128)(2,1)S(1)}, bf16[2,1,2,64,128]{4,3,2,0,1:T(8,128)(2,1)S(1)}, u32[]{:S(2)}, u32[]{:S(2)}) collective-permute-start(bf16[2,1,2,64,128]{4,3,2,0,1:T(8,128)(2,1)S(1)} %fusion.23), channel_id=1, source_target_pairs={{0,4},{1,5},{2,6},{3,7},{4,0},{5,1},{6,2},{7,3},{8,12},{9,13},{10,... | collective-permute-start | bytes 196616 | tf_op jit(solution)/shard_map/ppermute | solution.py:450
  134.2 1.9 %collective-permute-start.22 = (bf16[2,64,128]{2,1,0:T(8,128)(2,1)S(1)}, bf16[2,64,128]{2,1,0:T(8,128)(2,1)S(1)}, u32[]{:S(2)}, u32[]{:S(2)}) collective-permute-start(bf16[2,64,128]{2,1,0:T(8,128)(2,1)S(1)} %fusion.29), channel_id=1, source_target_pairs={{87,56},{86,57},{85,58},{84,59},{83,60},{82,61},{81,62},{80,63},{7... | collective-permute-start | bytes 98312 | tf_op jit(solution)/shard_map/ppermute | solution.py:442
  136.1 4.5 %collective-permute-done.15 = bf16[2,1,2,64,128]{4,3,2,0,1:T(8,128)(2,1)S(1)} collective-permute-done((bf16[2,1,2,64,128]{4,3,2,0,1:T(8,128)(2,1)S(1)}, bf16[2,1,2,64,128]{4,3,2,0,1:T(8,128)(2,1)S(1)}, u32[]{:S(2)}, u32[]{:S(2)}) %collective-permute-start.15) | collective-permute-done | bytes 65568 | tf_op jit(solution)/shard_map/ppermute | solution.py:450
  140.7 1.9 %collective-permute-start.16 = (bf16[2,64,128]{2,1,0:T(8,128)(2,1)S(1)}, bf16[2,64,128]{2,1,0:T(8,128)(2,1)S(1)}, u32[]{:S(2)}, u32[]{:S(2)}) collective-permute-start(bf16[2,64,128]{2,1,0:T(8,128)(2,1)S(1)} %fusion.28), channel_id=1, source_target_pairs={{0,8},{8,0},{16,24},{24,16},{32,40},{40,32},{48,56},{56,48},{64,72... | collective-permute-start | bytes 98312 | tf_op jit(solution)/shard_map/ppermute | solution.py:454
  143.5 5.8 %collective-permute-done.22 = bf16[2,64,128]{2,1,0:T(8,128)(2,1)S(1)} collective-permute-done((bf16[2,64,128]{2,1,0:T(8,128)(2,1)S(1)}, bf16[2,64,128]{2,1,0:T(8,128)(2,1)S(1)}, u32[]{:S(2)}, u32[]{:S(2)}) %collective-permute-start.22) | collective-permute-done | bytes 32800 | tf_op jit(solution)/shard_map/ppermute | solution.py:442
  (80 shorter events, 11.7 us)
Async XLA Ops:
  0.6 35.2 %copy-start = (bf16[1,2,512,128]{3,2,1,0:T(8,128)(2,1)S(1)}, bf16[1,2,512,128]{3,2,1,0:T(8,128)(2,1)}, u32[]{:S(2)}) copy-start(bf16[1,2,512,128]{3,2,1,0:T(8,128)(2,1)} %param.5) | copy-start | bytes 786436
  2.2 16.8 %collective-permute-start.2 = (bf16[2,64,128]{2,1,0:T(8,128)(2,1)S(1)}, bf16[2,64,128]{2,1,0:T(8,128)(2,1)S(1)}, u32[]{:S(2)}, u32[]{:S(2)}) collective-permute-start(bf16[2,64,128]{2,1,0:T(8,128)(2,1)S(1)} %get-tuple-element.51), channel_id=1, source_target_pairs={{56,87},{57,86},{58,85},{59,84},{60,83},{61,82},{62,81},{63,80},{4... | collective-permute-start | bytes 98312 | tf_op jit(solution)/shard_map/ppermute | solution.py:345
  15.6 3.2 %collective-permute-start.1 = (bf16[2,64,128]{2,1,0:T(8,128)(2,1)S(1)}, bf16[2,64,128]{2,1,0:T(8,128)(2,1)S(1)}, u32[]{:S(2)}, u32[]{:S(2)}) collective-permute-start(bf16[2,64,128]{2,1,0:T(8,128)(2,1)S(1)} %get-tuple-element.52), channel_id=1, source_target_pairs={{0,8},{8,0},{16,24},{24,16},{32,40},{40,32},{48,56},{56,48},{64,72... | collective-permute-start | bytes 98312 | tf_op jit(solution)/shard_map/ppermute | solution.py:344
  19.0 11.7 %collective-permute-start.3 = (bf16[3,1,2,64,128]{4,3,2,0,1:T(8,128)(2,1)S(1)}, bf16[3,1,2,64,128]{4,3,2,0,1:T(8,128)(2,1)S(1)}, u32[]{:S(2)}, u32[]{:S(2)}) collective-permute-start(bf16[3,1,2,64,128]{4,3,2,0,1:T(8,128)(2,1)S(1)} %get-tuple-element.47), channel_id=1, source_target_pairs={{0,4},{1,5},{2,6},{3,7},{4,0},{5,1},{6,2},{7,3},{8,12},{9,13},{10,... | collective-permute-start | bytes 294920 | tf_op jit(solution)/shard_map/ppermute | solution.py:350
  30.7 13.8 %collective-permute-start.4 = (bf16[3,2,2,64,128]{4,3,2,1,0:T(8,128)(2,1)S(1)}, bf16[3,2,2,64,128]{4,3,2,1,0:T(8,128)(2,1)S(1)}, u32[]{:S(2)}, u32[]{:S(2)}) collective-permute-start(bf16[3,2,2,64,128]{4,3,2,1,0:T(8,128)(2,1)S(1)} %broadcast_select_fusion.2), channel_id=1, source_target_pairs={{0,2},{1,3},{2,0},{3,1},{4,6},{5,7},{6,4},{7,5},{8,10},{9,11},{10,... | collective-permute-start | bytes 589832 | tf_op jit(solution)/shard_map/ppermute | solution.py:350
  35.8 11.7 %copy-start.1 = (bf16[1,2,512,128]{3,2,1,0:T(8,128)(2,1)S(1)}, bf16[1,2,512,128]{3,2,1,0:T(8,128)(2,1)}, u32[]{:S(2)}) copy-start(bf16[1,2,512,128]{3,2,1,0:T(8,128)(2,1)} %param.8) | copy-start | bytes 786436
  44.7 4.9 %copy-start.2 = (s32[65536]{0:T(1024)S(1)}, s32[65536]{0:T(1024)}, u32[]{:S(2)}) copy-start(s32[65536]{0:T(1024)} %param.9) | copy-start | bytes 786436
  44.9 11.9 %collective-permute-start.5 = (bf16[3,4,2,64,128]{4,3,2,1,0:T(8,128)(2,1)S(1)}, bf16[3,4,2,64,128]{4,3,2,1,0:T(8,128)(2,1)S(1)}, u32[]{:S(2)}, u32[]{:S(2)}) collective-permute-start(bf16[3,4,2,64,128]{4,3,2,1,0:T(8,128)(2,1)S(1)} %broadcast_select_fusion.1), channel_id=1, source_target_pairs={{0,1},{1,0},{2,3},{3,2},{4,5},{5,4},{6,7},{7,6},{8,9},{9,8},{10,11... | collective-permute-start | bytes 1179656 | tf_op jit(solution)/shard_map/ppermute | solution.py:350
  47.6 19.6 %collective-permute-start = (bf16[2,512,128]{2,1,0:T(8,128)(2,1)S(1)}, bf16[2,512,128]{2,1,0:T(8,128)(2,1)S(1)}, u32[]{:S(2)}, u32[]{:S(2)}) collective-permute-start(bf16[2,512,128]{2,1,0:T(8,128)(2,1)S(1)} %maximum_select_fusion), channel_id=1, source_target_pairs={{0,8},{8,0},{16,24},{24,16},{32,40},{40,32},{48,56},{56,48},{64,72... | collective-permute-start | bytes 786440 | tf_op jit(solution)/shard_map/ppermute | solution.py:357
  57.0 13.9 %collective-permute-start.6 = (bf16[8,2,64,128]{3,2,1,0:T(8,128)(2,1)S(1)}, bf16[8,2,64,128]{3,2,1,0:T(8,128)(2,1)S(1)}, u32[]{:S(2)}, u32[]{:S(2)}) collective-permute-start(bf16[8,2,64,128]{3,2,1,0:T(8,128)(2,1)S(1)} %bitcast.255), channel_id=1, source_target_pairs={{0,32},{16,48},{40,8},{56,24},{64,96},{80,112},{104,72},{120,88},{... | collective-permute-start | bytes 786440 | tf_op jit(solution)/shard_map/ppermute | solution.py:367
  61.0 10.0 %collective-permute-start.8 = (bf16[2,8,2,64,128]{4,3,2,1,0:T(8,128)(2,1)S(1)}, bf16[2,8,2,64,128]{4,3,2,1,0:T(8,128)(2,1)S(1)}, u32[]{:S(2)}, u32[]{:S(2)}) collective-permute-start(bf16[2,8,2,64,128]{4,3,2,1,0:T(8,128)(2,1)S(1)} %bitcast.228), channel_id=1, source_target_pairs={{0,16},{16,32},{32,48},{24,8},{40,24},{56,40},{64,80},{80,96},{96,... | collective-permute-start | bytes 1572872 | tf_op jit(solution)/shard_map/ppermute | solution.py:368
  64.6 6.5 %collective-permute-start.7 = (bf16[8,2,64,128]{3,2,1,0:T(8,128)(2,1)S(1)}, bf16[8,2,64,128]{3,2,1,0:T(8,128)(2,1)S(1)}, u32[]{:S(2)}, u32[]{:S(2)}) collective-permute-start(bf16[8,2,64,128]{3,2,1,0:T(8,128)(2,1)S(1)} %bitcast.251), channel_id=1, source_target_pairs={{8,0},{48,56},{72,64},{112,120},{136,128},{176,184},{200,192},{240... | collective-permute-start | bytes 786440 | tf_op jit(solution)/shard_map/ppermute | solution.py:370
  65.9 8.3 %collective-permute-start.9 = (bf16[8,2,64,128]{3,2,1,0:T(8,128)(2,1)S(1)}, bf16[8,2,64,128]{3,2,1,0:T(8,128)(2,1)S(1)}, u32[]{:S(2)}, u32[]{:S(2)}) collective-permute-start(bf16[8,2,64,128]{3,2,1,0:T(8,128)(2,1)S(1)} %bitcast.252), channel_id=1, source_target_pairs={{16,0},{40,56},{80,64},{104,120},{144,128},{168,184},{208,192},{23... | collective-permute-start | bytes 786440 | tf_op jit(solution)/shard_map/ppermute | solution.py:369
  78.1 10.1 %collective-permute-start.17 = (bf16[8,2,64,128]{3,2,1,0:T(8,128)(2,1)S(1)}, bf16[8,2,64,128]{3,2,1,0:T(8,128)(2,1)S(1)}, u32[]{:S(2)}, u32[]{:S(2)}) collective-permute-start(bf16[8,2,64,128]{3,2,1,0:T(8,128)(2,1)S(1)} %get-tuple-element.32), channel_id=1, source_target_pairs={{0,16},{56,40},{64,80},{120,104},{128,144},{184,168},{192,208},{24... | collective-permute-start | bytes 786440 | tf_op jit(solution)/shard_map/ppermute | solution.py:423
  79.5 8.8 %collective-permute-start.18 = (bf16[8,2,64,128]{3,2,1,0:T(8,128)(2,1)S(1)}, bf16[8,2,64,128]{3,2,1,0:T(8,128)(2,1)S(1)}, u32[]{:S(2)}, u32[]{:S(2)}) collective-permute-start(bf16[8,2,64,128]{3,2,1,0:T(8,128)(2,1)S(1)} %get-tuple-element.33), channel_id=1, source_target_pairs={{0,8},{56,48},{64,72},{120,112},{128,136},{184,176},{192,200},{248... | collective-permute-start | bytes 786440 | tf_op jit(solution)/shard_map/ppermute | solution.py:424
  80.8 26.9 %collective-permute-start.11 = (bf16[2,8,2,64,128]{4,3,2,1,0:T(8,128)(2,1)S(1)}, bf16[2,8,2,64,128]{4,3,2,1,0:T(8,128)(2,1)S(1)}, u32[]{:S(2)}, u32[]{:S(2)}) collective-permute-start(bf16[2,8,2,64,128]{4,3,2,1,0:T(8,128)(2,1)S(1)} %get-tuple-element.26), channel_id=1, source_target_pairs={{16,0},{32,16},{48,32},{8,24},{24,40},{40,56},{80,64},{96,80},{112... | collective-permute-start | bytes 1572872 | tf_op jit(solution)/shard_map/ppermute | solution.py:426
  82.1 25.8 %collective-permute-start.12 = (bf16[8,2,64,128]{3,2,1,0:T(8,128)(2,1)S(1)}, bf16[8,2,64,128]{3,2,1,0:T(8,128)(2,1)S(1)}, u32[]{:S(2)}, u32[]{:S(2)}) collective-permute-start(bf16[8,2,64,128]{3,2,1,0:T(8,128)(2,1)S(1)} %get-tuple-element.27), channel_id=1, source_target_pairs={{32,0},{48,16},{8,40},{24,56},{96,64},{112,80},{72,104},{88,120},{... | collective-permute-start | bytes 786440 | tf_op jit(solution)/shard_map/ppermute | solution.py:425
  88.4 13.9 %collective-permute-start.19 = (bf16[4,2,64,128]{3,2,1,0:T(8,128)(2,1)S(1)}, bf16[4,2,64,128]{3,2,1,0:T(8,128)(2,1)S(1)}, u32[]{:S(2)}, u32[]{:S(2)}) collective-permute-start(bf16[4,2,64,128]{3,2,1,0:T(8,128)(2,1)S(1)} %fusion.15), channel_id=1, source_target_pairs={{0,1},{1,0},{2,3},{3,2},{4,5},{5,4},{6,7},{7,6},{8,9},{9,8},{10,11... | collective-permute-start | bytes 393224 | tf_op jit(solution)/shard_map/ppermute | solution.py:440
  92.1 18.5 %collective-permute-start.10 = (bf16[2,512,128]{2,1,0:T(8,128)(2,1)S(1)}, bf16[2,512,128]{2,1,0:T(8,128)(2,1)S(1)}, u32[]{:S(2)}, u32[]{:S(2)}) collective-permute-start(bf16[2,512,128]{2,1,0:T(8,128)(2,1)S(1)} %get-tuple-element.24), channel_id=1, source_target_pairs={{0,8},{8,0},{16,24},{24,16},{32,40},{40,32},{48,56},{56,48},{64,72... | collective-permute-start | bytes 786440 | tf_op jit(solution)/shard_map/ppermute | solution.py:461
  102.4 9.6 %collective-permute-start.20 = (bf16[2,2,64,128]{3,2,1,0:T(8,128)(2,1)S(1)}, bf16[2,2,64,128]{3,2,1,0:T(8,128)(2,1)S(1)}, u32[]{:S(2)}, u32[]{:S(2)}) collective-permute-start(bf16[2,2,64,128]{3,2,1,0:T(8,128)(2,1)S(1)} %fusion.24), channel_id=1, source_target_pairs={{0,2},{1,3},{2,0},{3,1},{4,6},{5,7},{6,4},{7,5},{8,10},{9,11},{10,... | collective-permute-start | bytes 196616 | tf_op jit(solution)/shard_map/ppermute | solution.py:440
  108.1 10.5 %collective-permute-start.13 = (bf16[2,4,2,64,128]{4,3,2,1,0:T(8,128)(2,1)S(1)}, bf16[2,4,2,64,128]{4,3,2,1,0:T(8,128)(2,1)S(1)}, u32[]{:S(2)}, u32[]{:S(2)}) collective-permute-start(bf16[2,4,2,64,128]{4,3,2,1,0:T(8,128)(2,1)S(1)} %fusion.6), channel_id=1, source_target_pairs={{0,1},{1,0},{2,3},{3,2},{4,5},{5,4},{6,7},{7,6},{8,9},{9,8},{10,11... | collective-permute-start | bytes 786440 | tf_op jit(solution)/shard_map/ppermute | solution.py:450
  118.7 11.8 %collective-permute-start.14 = (bf16[2,2,2,64,128]{4,3,2,1,0:T(8,128)(2,1)S(1)}, bf16[2,2,2,64,128]{4,3,2,1,0:T(8,128)(2,1)S(1)}, u32[]{:S(2)}, u32[]{:S(2)}) collective-permute-start(bf16[2,2,2,64,128]{4,3,2,1,0:T(8,128)(2,1)S(1)} %fusion.14), channel_id=1, source_target_pairs={{0,2},{1,3},{2,0},{3,1},{4,6},{5,7},{6,4},{7,5},{8,10},{9,11},{10,... | collective-permute-start | bytes 393224 | tf_op jit(solution)/shard_map/ppermute | solution.py:450
  121.0 13.2 %collective-permute-start.21 = (bf16[1,2,64,128]{3,2,1,0:T(8,128)(2,1)S(1)}, bf16[1,2,64,128]{3,2,1,0:T(8,128)(2,1)S(1)}, u32[]{:S(2)}, u32[]{:S(2)}) collective-permute-start(bf16[1,2,64,128]{3,2,1,0:T(8,128)(2,1)S(1)} %fusion.27), channel_id=1, source_target_pairs={{0,4},{1,5},{2,6},{3,7},{4,0},{5,1},{6,2},{7,3},{8,12},{9,13},{10,... | collective-permute-start | bytes 98312 | tf_op jit(solution)/shard_map/ppermute | solution.py:440
  130.6 10.1 %collective-permute-start.15 = (bf16[2,1,2,64,128]{4,3,2,0,1:T(8,128)(2,1)S(1)}, bf16[2,1,2,64,128]{4,3,2,0,1:T(8,128)(2,1)S(1)}, u32[]{:S(2)}, u32[]{:S(2)}) collective-permute-start(bf16[2,1,2,64,128]{4,3,2,0,1:T(8,128)(2,1)S(1)} %fusion.23), channel_id=1, source_target_pairs={{0,4},{1,5},{2,6},{3,7},{4,0},{5,1},{6,2},{7,3},{8,12},{9,13},{10,... | collective-permute-start | bytes 196616 | tf_op jit(solution)/shard_map/ppermute | solution.py:450
  134.2 15.1 %collective-permute-start.22 = (bf16[2,64,128]{2,1,0:T(8,128)(2,1)S(1)}, bf16[2,64,128]{2,1,0:T(8,128)(2,1)S(1)}, u32[]{:S(2)}, u32[]{:S(2)}) collective-permute-start(bf16[2,64,128]{2,1,0:T(8,128)(2,1)S(1)} %fusion.29), channel_id=1, source_target_pairs={{87,56},{86,57},{85,58},{84,59},{83,60},{82,61},{81,62},{80,63},{7... | collective-permute-start | bytes 98312 | tf_op jit(solution)/shard_map/ppermute | solution.py:442
  140.7 8.6 %collective-permute-start.16 = (bf16[2,64,128]{2,1,0:T(8,128)(2,1)S(1)}, bf16[2,64,128]{2,1,0:T(8,128)(2,1)S(1)}, u32[]{:S(2)}, u32[]{:S(2)}) collective-permute-start(bf16[2,64,128]{2,1,0:T(8,128)(2,1)S(1)} %fusion.28), channel_id=1, source_target_pairs={{0,8},{8,0},{16,24},{24,16},{32,40},{40,32},{48,56},{56,48},{64,72... | collective-permute-start | bytes 98312 | tf_op jit(solution)/shard_map/ppermute | solution.py:454

commit v10 on v9

--- a/solution.py
+++ b/solution.py
@@ -434,21 +434,20 @@
     )(lo, places, start, queries, out_grad, far, kv_own, attended, lse, delta, acc)
 
     edge_sum = jnp.where(edge_next, p_next.astype(f32), 0.0) + r_edge1 + r_edge2
-    for bit in reversed(bits):
-        halves = edge_sum.reshape((-1, 2) + half.shape[1:])
-        away = pick(high[bit], halves[:, 0], halves[:, 1]).astype(bf16)
-        other = lax.ppermute(away, everywhere, holder_pairs(ctx, heads, bit))
-        edge_sum = pick(high[bit], halves[:, 1], halves[:, 0]) + other.astype(f32)
-    returned = lax.ppermute(edge_sum[0].astype(bf16), everywhere, inverse(edge)).astype(f32)
-
     sums = p_own + r_near
     first_sum, second_sum = sums[0], sums[1] + r_next
     sums = jnp.stack([pick(even, second_sum, first_sum), pick(even, first_sum, second_sum)])
     for bit in reversed(bits):
         halves = sums.reshape((2, -1, 2) + half.shape[1:])
+        edge_halves = edge_sum.reshape((-1, 2) + half.shape[1:])
         away = pick(high[bit], halves[:, :, 1], halves[:, :, 0]).astype(bf16)
+        edge_away = pick(high[bit], edge_halves[:, 0], edge_halves[:, 1]).astype(bf16)
         other = lax.ppermute(away, everywhere, head_pairs(ctx, heads, bit))
+        edge_other = lax.ppermute(edge_away, everywhere, holder_pairs(ctx, heads, bit))
+        other, edge_other = lax.optimization_barrier((other, edge_other))
         sums = pick(high[bit], halves[:, :, 0], halves[:, :, 1]) + other.astype(f32)
+        edge_sum = pick(high[bit], edge_halves[:, 1], edge_halves[:, 0]) + edge_other.astype(f32)
+    returned = lax.ppermute(edge_sum[0].astype(bf16), everywhere, inverse(edge)).astype(f32)
     stays = sums[:, 0]
     own_half = pick(even, stays[1], stays[0])
     far_half = lax.ppermute(

time: 151 us -> 157 us (1.040)
  the two profiles are of different devices: /device:TPU:100 before, /device:TPU:98 now
where the time goes in v10:
time: 157 us; the launch traced here: 156 us
  starting transfers between devices  83.6 us (53%)
  waiting for transfers between devices  53.2 us (34%)
  Pallas kernels  10.6 us (7%)
  other arithmetic  4.81 us (3%)
  local copies, waits for them, and re-layouts  2.46 us (2%)
    ppermute x3, waiting for transfers between devices, body(): other = lax.ppermute(kv_all, everywhere, head_pairs(ctx, heads, bit))  24.3 us
    ppermute x3, starting transfers between devices, body(): other = lax.ppermute(away, everywhere, head_pairs(ctx, heads, bit))  17.3 us
    ppermute x3, waiting for transfers between devices, body(): lax.ppermute(edge_away, everywhere, holder_pairs(ctx, heads, bit))  16.7 us
    ppermute x1, starting transfers between devices, body(): crossed = lax.ppermute(leaving, everywhere, edge)  13.4 us
    pallas_call x3, Pallas kernels, call(): pl.pallas_call(kernel, out_shape=outputs, in_specs=[pl.BlockSpec(memory_s...  10.6 us
    ppermute x3, starting transfers between devices, body(): other = lax.ppermute(kv_all, everywhere, head_pairs(ctx, heads, bit))  10.5 us
    ppermute x1, starting transfers between devices, body(): r_edge1 = lax.ppermute(p_near[1], CTX, inverse(edge1)).astype(f32)  7 us
    ppermute x3, starting transfers between devices, body(): lax.ppermute(edge_away, everywhere, holder_pairs(ctx, heads, bit))  6.04 us
  transfers between devices with their start and end apart: 23, of which 10 were waited for; matrix products, arithmetic and copies ran while one was open for 3% of the time, Pallas kernels for 5%

profile of v10, /device:TPU:98, one launch (start us, length us, event | category | flops | bytes accessed | tf_op | source)
XLA Modules:
  0.0 155.9 jit_solution(15370641448831865555)
XLA Ops:
  2.2 13.4 %collective-permute-start.2 = (bf16[2,64,128]{2,1,0:T(8,128)(2,1)S(1)}, bf16[2,64,128]{2,1,0:T(8,128)(2,1)S(1)}, u32[]{:S(2)}, u32[]{:S(2)}) collective-permute-start(bf16[2,64,128]{2,1,0:T(8,128)(2,1)S(1)} %get-tuple-element.63), channel_id=1, source_target_pairs={{56,87},{57,86},{58,85},{59,84},{60,83},{61,82},{62,81},{63,80},{4... | collective-permute-start | bytes 98312 | tf_op jit(solution)/shard_map/ppermute | solution.py:345
  15.6 2.4 %collective-permute-start.1 = (bf16[2,64,128]{2,1,0:T(8,128)(2,1)S(1)}, bf16[2,64,128]{2,1,0:T(8,128)(2,1)S(1)}, u32[]{:S(2)}, u32[]{:S(2)}) collective-permute-start(bf16[2,64,128]{2,1,0:T(8,128)(2,1)S(1)} %get-tuple-element.64), channel_id=1, source_target_pairs={{0,8},{8,0},{16,24},{24,16},{32,40},{40,32},{48,56},{56,48},{64,72... | collective-permute-start | bytes 98312 | tf_op jit(solution)/shard_map/ppermute | solution.py:344
  19.0 2.8 %collective-permute-start.3 = (bf16[3,1,2,64,128]{4,3,2,0,1:T(8,128)(2,1)S(1)}, bf16[3,1,2,64,128]{4,3,2,0,1:T(8,128)(2,1)S(1)}, u32[]{:S(2)}, u32[]{:S(2)}) collective-permute-start(bf16[3,1,2,64,128]{4,3,2,0,1:T(8,128)(2,1)S(1)} %get-tuple-element.59), channel_id=1, source_target_pairs={{0,4},{1,5},{2,6},{3,7},{4,0},{5,1},{6,2},{7,3},{8,12},{9,13},{10,... | collective-permute-start | bytes 294920 | tf_op jit(solution)/shard_map/ppermute | solution.py:350
  22.1 8.6 %collective-permute-done.3 = bf16[3,1,2,64,128]{4,3,2,0,1:T(8,128)(2,1)S(1)} collective-permute-done((bf16[3,1,2,64,128]{4,3,2,0,1:T(8,128)(2,1)S(1)}, bf16[3,1,2,64,128]{4,3,2,0,1:T(8,128)(2,1)S(1)}, u32[]{:S(2)}, u32[]{:S(2)}) %collective-permute-start.3) | collective-permute-done | bytes 98336 | tf_op jit(solution)/shard_map/ppermute | solution.py:350
  30.7 5.1 %collective-permute-start.4 = (bf16[3,2,2,64,128]{4,3,2,1,0:T(8,128)(2,1)S(1)}, bf16[3,2,2,64,128]{4,3,2,1,0:T(8,128)(2,1)S(1)}, u32[]{:S(2)}, u32[]{:S(2)}) collective-permute-start(bf16[3,2,2,64,128]{4,3,2,1,0:T(8,128)(2,1)S(1)} %broadcast_select_fusion.2), channel_id=1, source_target_pairs={{0,2},{1,3},{2,0},{3,1},{4,6},{5,7},{6,4},{7,5},{8,10},{9,11},{10,... | collective-permute-start | bytes 589832 | tf_op jit(solution)/shard_map/ppermute | solution.py:350
  35.9 8.7 %collective-permute-done.4 = bf16[3,2,2,64,128]{4,3,2,1,0:T(8,128)(2,1)S(1)} collective-permute-done((bf16[3,2,2,64,128]{4,3,2,1,0:T(8,128)(2,1)S(1)}, bf16[3,2,2,64,128]{4,3,2,1,0:T(8,128)(2,1)S(1)}, u32[]{:S(2)}, u32[]{:S(2)}) %collective-permute-start.4) | collective-permute-done | bytes 196640 | tf_op jit(solution)/shard_map/ppermute | solution.py:350
  44.9 2.6 %collective-permute-start.5 = (bf16[3,4,2,64,128]{4,3,2,1,0:T(8,128)(2,1)S(1)}, bf16[3,4,2,64,128]{4,3,2,1,0:T(8,128)(2,1)S(1)}, u32[]{:S(2)}, u32[]{:S(2)}) collective-permute-start(bf16[3,4,2,64,128]{4,3,2,1,0:T(8,128)(2,1)S(1)} %broadcast_select_fusion.1), channel_id=1, source_target_pairs={{0,1},{1,0},{2,3},{3,2},{4,5},{5,4},{6,7},{7,6},{8,9},{9,8},{10,11... | collective-permute-start | bytes 1179656 | tf_op jit(solution)/shard_map/ppermute | solution.py:350
  47.6 1.9 %collective-permute-start = (bf16[2,512,128]{2,1,0:T(8,128)(2,1)S(1)}, bf16[2,512,128]{2,1,0:T(8,128)(2,1)S(1)}, u32[]{:S(2)}, u32[]{:S(2)}) collective-permute-start(bf16[2,512,128]{2,1,0:T(8,128)(2,1)S(1)} %maximum_select_fusion), channel_id=1, source_target_pairs={{0,8},{8,0},{16,24},{24,16},{32,40},{40,32},{48,56},{56,48},{64,72... | collective-permute-start | bytes 786440 | tf_op jit(solution)/shard_map/ppermute | solution.py:357
  49.8 7.0 %collective-permute-done.5 = bf16[3,4,2,64,128]{4,3,2,1,0:T(8,128)(2,1)S(1)} collective-permute-done((bf16[3,4,2,64,128]{4,3,2,1,0:T(8,128)(2,1)S(1)}, bf16[3,4,2,64,128]{4,3,2,1,0:T(8,128)(2,1)S(1)}, u32[]{:S(2)}, u32[]{:S(2)}) %collective-permute-start.5) | collective-permute-done | bytes 393248 | tf_op jit(solution)/shard_map/ppermute | solution.py:350
  57.0 1.3 collective-permute-start.8
  58.4 5.2 %collective-permute-start.6 = (bf16[8,2,64,128]{3,2,1,0:T(8,128)(2,1)S(1)}, bf16[8,2,64,128]{3,2,1,0:T(8,128)(2,1)S(1)}, u32[]{:S(2)}, u32[]{:S(2)}) collective-permute-start(bf16[8,2,64,128]{3,2,1,0:T(8,128)(2,1)S(1)} %bitcast.255), channel_id=1, source_target_pairs={{0,32},{16,48},{40,8},{56,24},{64,96},{80,112},{104,72},{120,88},{... | collective-permute-start | bytes 786440 | tf_op jit(solution)/shard_map/ppermute | solution.py:367
  63.6 1.5 convert_reduce_fusion
  67.8 3.3 %own_forward.1 = (f32[1,1024]{1,0:T(1,128)S(1)}, f32[1,1024]{1,0:T(1,128)S(1)}, f32[4,128,256]{2,1,0:T(8,128)S(1)}) custom-call(s32[4]{0:T(128)S(1)} %and_select_fusion.lo_ref, s32[1]{0:T(128)} %bitcast.place_ref, s32[1,1024]{1,0:T(1,128)S(1)} %bitcast.236, bf16[2,512,128]{2,1,0:T(8,128)(2,1)S(1)} %bitcast.231, ...), custom_call_target="tpu_custom_call" | custom-call | flops 201326592 | bytes 4194304 | tf_op jit(solution)/shard_map/own_forward/pallas_call | solution.py:301
  71.3 3.4 %collective-permute-done.9 = bf16[8,2,64,128]{3,2,1,0:T(8,128)(2,1)S(1)} collective-permute-done((bf16[8,2,64,128]{3,2,1,0:T(8,128)(2,1)S(1)}, bf16[8,2,64,128]{3,2,1,0:T(8,128)(2,1)S(1)}, u32[]{:S(2)}, u32[]{:S(2)}) %collective-permute-start.9) | collective-permute-done | bytes 262176 | tf_op jit(solution)/shard_map/ppermute | solution.py:369
  74.9 3.0 %earlier.1 = (bf16[2,512,128]{2,1,0:T(8,128)(2,1)S(1)}, f32[1,1024]{1,0:T(1,128)S(1)}, f32[1,1024]{1,0:T(1,128)S(1)}, f32[4,128,256]{2,1,0:T(8,128)S(1)}, bf16[2...) custom-call(s32[4]{0:T(128)S(1)} %and_select_fusion.lo_ref, s32[1]{0:T(128)} %bitcast.place_ref, ...), custom_call_target="tpu_custom_call" | custom-call | flops 603979776 | bytes 4194304 | tf_op jit(solution)/shard_map/earlier/pallas_call | solution.py:301
  79.3 1.3 collective-permute-start.15
  80.6 7.0 %collective-permute-start.14 = (bf16[8,2,64,128]{3,2,1,0:T(8,128)(2,1)S(1)}, bf16[8,2,64,128]{3,2,1,0:T(8,128)(2,1)S(1)}, u32[]{:S(2)}, u32[]{:S(2)}) collective-permute-start(bf16[8,2,64,128]{3,2,1,0:T(8,128)(2,1)S(1)} %get-tuple-element.44), channel_id=1, source_target_pairs={{0,16},{56,40},{64,80},{120,104},{128,144},{184,168},{192,208},{24... | collective-permute-start | bytes 786440 | tf_op jit(solution)/shard_map/ppermute | solution.py:423
  88.9 4.3 %own_backward.1 = (bf16[2,512,128]{2,1,0:T(8,128)(2,1)S(1)}, bf16[2,512,128]{2,1,0:T(8,128)(2,1)S(1)}, f32[2,8,2,64,128]{4,3,2,1,0:T(8,128)S(1)}) custom-call(s32[4]{0:T(128)S(1)} %and_select_fusion.lo_ref, s32[1]{0:T(128)} %bitcast.place_ref, s32[1,1024]{1,0:T(1,128)S(1)} %bitcast.238, bf16[2,512,128]{2,1,0:T(8,128)(2,1)S(1)} %bitcast.233, ...), custom_call_target="tpu_custom_call" | custom-call | flops 503316480 | bytes 4194304 | tf_op jit(solution)/shard_map/own_backward/pallas_call | solution.py:301
  93.5 3.9 %collective-permute-done.12 = bf16[8,2,64,128]{3,2,1,0:T(8,128)(2,1)S(1)} collective-permute-done((bf16[8,2,64,128]{3,2,1,0:T(8,128)(2,1)S(1)}, bf16[8,2,64,128]{3,2,1,0:T(8,128)(2,1)S(1)}, u32[]{:S(2)}, u32[]{:S(2)}) %collective-permute-start.12) | collective-permute-done | bytes 262176 | tf_op jit(solution)/shard_map/ppermute | solution.py:425
  97.6 3.6 %collective-permute-start.13 = (bf16[2,4,2,64,128]{4,3,2,1,0:T(8,128)(2,1)S(1)}, bf16[2,4,2,64,128]{4,3,2,1,0:T(8,128)(2,1)S(1)}, u32[]{:S(2)}, u32[]{:S(2)}) collective-permute-start(bf16[2,4,2,64,128]{4,3,2,1,0:T(8,128)(2,1)S(1)} %fusion.6), channel_id=1, source_target_pairs={{0,1},{1,0},{2,3},{3,2},{4,5},{5,4},{6,7},{7,6},{8,9},{9,8},{10,11... | collective-permute-start | bytes 786440 | tf_op jit(solution)/shard_map/ppermute | solution.py:445
  101.2 2.2 %collective-permute-start.16 = (bf16[4,2,64,128]{3,2,1,0:T(8,128)(2,1)S(1)}, bf16[4,2,64,128]{3,2,1,0:T(8,128)(2,1)S(1)}, u32[]{:S(2)}, u32[]{:S(2)}) collective-permute-start(bf16[4,2,64,128]{3,2,1,0:T(8,128)(2,1)S(1)} %fusion.14), channel_id=1, source_target_pairs={{0,1},{1,0},{2,3},{3,2},{4,5},{5,4},{6,7},{7,6},{8,9},{9,8},{10,11... | collective-permute-start | bytes 393224 | tf_op jit(solution)/shard_map/ppermute | solution.py:446
  103.5 1.9 %collective-permute-start.10 = (bf16[2,512,128]{2,1,0:T(8,128)(2,1)S(1)}, bf16[2,512,128]{2,1,0:T(8,128)(2,1)S(1)}, u32[]{:S(2)}, u32[]{:S(2)}) collective-permute-start(bf16[2,512,128]{2,1,0:T(8,128)(2,1)S(1)} %get-tuple-element.30), channel_id=1, source_target_pairs={{0,8},{8,0},{16,24},{24,16},{32,40},{40,32},{48,56},{56,48},{64,72... | collective-permute-start | bytes 786440 | tf_op jit(solution)/shard_map/ppermute | solution.py:460
  105.4 3.8 %collective-permute-done.16 = bf16[4,2,64,128]{3,2,1,0:T(8,128)(2,1)S(1)} collective-permute-done((bf16[4,2,64,128]{3,2,1,0:T(8,128)(2,1)S(1)}, bf16[4,2,64,128]{3,2,1,0:T(8,128)(2,1)S(1)}, u32[]{:S(2)}, u32[]{:S(2)}) %collective-permute-start.16) | collective-permute-done | bytes 131104 | tf_op jit(solution)/shard_map/ppermute | solution.py:446
  109.4 5.6 %collective-permute-start.17 = (bf16[2,2,2,64,128]{4,3,2,1,0:T(8,128)(2,1)S(1)}, bf16[2,2,2,64,128]{4,3,2,1,0:T(8,128)(2,1)S(1)}, u32[]{:S(2)}, u32[]{:S(2)}) collective-permute-start(bf16[2,2,2,64,128]{4,3,2,1,0:T(8,128)(2,1)S(1)} %fusion.15), channel_id=1, source_target_pairs={{0,2},{1,3},{2,0},{3,1},{4,6},{5,7},{6,4},{7,5},{8,10},{9,11},{10,... | collective-permute-start | bytes 393224 | tf_op jit(solution)/shard_map/ppermute | solution.py:445
  115.1 1.9 %collective-permute-start.18 = (bf16[2,2,64,128]{3,2,1,0:T(8,128)(2,1)S(1)}, bf16[2,2,64,128]{3,2,1,0:T(8,128)(2,1)S(1)}, u32[]{:S(2)}, u32[]{:S(2)}) collective-permute-start(bf16[2,2,64,128]{3,2,1,0:T(8,128)(2,1)S(1)} %fusion.23), channel_id=1, source_target_pairs={{0,2},{1,3},{2,0},{3,1},{4,6},{5,7},{6,4},{7,5},{8,10},{9,11},{10,... | collective-permute-start | bytes 196616 | tf_op jit(solution)/shard_map/ppermute | solution.py:446
  117.0 5.1 %collective-permute-done.18 = bf16[2,2,64,128]{3,2,1,0:T(8,128)(2,1)S(1)} collective-permute-done((bf16[2,2,64,128]{3,2,1,0:T(8,128)(2,1)S(1)}, bf16[2,2,64,128]{3,2,1,0:T(8,128)(2,1)S(1)}, u32[]{:S(2)}, u32[]{:S(2)}) %collective-permute-start.18) | collective-permute-done | bytes 65568 | tf_op jit(solution)/shard_map/ppermute | solution.py:446
  122.2 8.1 %collective-permute-start.19 = (bf16[2,1,2,64,128]{4,3,2,0,1:T(8,128)(2,1)S(1)}, bf16[2,1,2,64,128]{4,3,2,0,1:T(8,128)(2,1)S(1)}, u32[]{:S(2)}, u32[]{:S(2)}) collective-permute-start(bf16[2,1,2,64,128]{4,3,2,0,1:T(8,128)(2,1)S(1)} %fusion.24), channel_id=1, source_target_pairs={{0,4},{1,5},{2,6},{3,7},{4,0},{5,1},{6,2},{7,3},{8,12},{9,13},{10,... | collective-permute-start | bytes 196616 | tf_op jit(solution)/shard_map/ppermute | solution.py:445
  130.3 1.9 %collective-permute-start.20 = (bf16[1,2,64,128]{3,2,1,0:T(8,128)(2,1)S(1)}, bf16[1,2,64,128]{3,2,1,0:T(8,128)(2,1)S(1)}, u32[]{:S(2)}, u32[]{:S(2)}) collective-permute-start(bf16[1,2,64,128]{3,2,1,0:T(8,128)(2,1)S(1)} %fusion.27), channel_id=1, source_target_pairs={{0,4},{1,5},{2,6},{3,7},{4,0},{5,1},{6,2},{7,3},{8,12},{9,13},{10,... | collective-permute-start | bytes 98312 | tf_op jit(solution)/shard_map/ppermute | solution.py:446
  132.3 7.7 %collective-permute-done.20 = bf16[1,2,64,128]{3,2,1,0:T(8,128)(2,1)S(1)} collective-permute-done((bf16[1,2,64,128]{3,2,1,0:T(8,128)(2,1)S(1)}, bf16[1,2,64,128]{3,2,1,0:T(8,128)(2,1)S(1)}, u32[]{:S(2)}, u32[]{:S(2)}) %collective-permute-start.20) | collective-permute-done | bytes 32800 | tf_op jit(solution)/shard_map/ppermute | solution.py:446
  140.1 5.4 %collective-permute-start.22 = (bf16[2,64,128]{2,1,0:T(8,128)(2,1)S(1)}, bf16[2,64,128]{2,1,0:T(8,128)(2,1)S(1)}, u32[]{:S(2)}, u32[]{:S(2)}) collective-permute-start(bf16[2,64,128]{2,1,0:T(8,128)(2,1)S(1)} %fusion.29), channel_id=1, source_target_pairs={{87,56},{86,57},{85,58},{84,59},{83,60},{82,61},{81,62},{80,63},{7... | collective-permute-start | bytes 98312 | tf_op jit(solution)/shard_map/ppermute | solution.py:450
  145.6 4.6 %collective-permute-start.21 = (bf16[2,64,128]{2,1,0:T(8,128)(2,1)S(1)}, bf16[2,64,128]{2,1,0:T(8,128)(2,1)S(1)}, u32[]{:S(2)}, u32[]{:S(2)}) collective-permute-start(bf16[2,64,128]{2,1,0:T(8,128)(2,1)S(1)} %fusion.28), channel_id=1, source_target_pairs={{0,8},{8,0},{16,24},{24,16},{32,40},{40,32},{48,56},{56,48},{64,72... | collective-permute-start | bytes 98312 | tf_op jit(solution)/shard_map/ppermute | solution.py:453
  151.1 4.2 %collective-permute-done.22 = bf16[2,64,128]{2,1,0:T(8,128)(2,1)S(1)} collective-permute-done((bf16[2,64,128]{2,1,0:T(8,128)(2,1)S(1)}, bf16[2,64,128]{2,1,0:T(8,128)(2,1)S(1)}, u32[]{:S(2)}, u32[]{:S(2)}) %collective-permute-start.22) | collective-permute-done | bytes 32800 | tf_op jit(solution)/shard_map/ppermute | solution.py:450
  (80 shorter events, 11.8 us)
Async XLA Ops:
  0.6 35.2 %copy-start.1 = (bf16[1,2,512,128]{3,2,1,0:T(8,128)(2,1)S(1)}, bf16[1,2,512,128]{3,2,1,0:T(8,128)(2,1)}, u32[]{:S(2)}) copy-start(bf16[1,2,512,128]{3,2,1,0:T(8,128)(2,1)} %param.8) | copy-start | bytes 786436
  2.2 16.8 %collective-permute-start.2 = (bf16[2,64,128]{2,1,0:T(8,128)(2,1)S(1)}, bf16[2,64,128]{2,1,0:T(8,128)(2,1)S(1)}, u32[]{:S(2)}, u32[]{:S(2)}) collective-permute-start(bf16[2,64,128]{2,1,0:T(8,128)(2,1)S(1)} %get-tuple-element.63), channel_id=1, source_target_pairs={{56,87},{57,86},{58,85},{59,84},{60,83},{61,82},{62,81},{63,80},{4... | collective-permute-start | bytes 98312 | tf_op jit(solution)/shard_map/ppermute | solution.py:345
  15.6 3.2 %collective-permute-start.1 = (bf16[2,64,128]{2,1,0:T(8,128)(2,1)S(1)}, bf16[2,64,128]{2,1,0:T(8,128)(2,1)S(1)}, u32[]{:S(2)}, u32[]{:S(2)}) collective-permute-start(bf16[2,64,128]{2,1,0:T(8,128)(2,1)S(1)} %get-tuple-element.64), channel_id=1, source_target_pairs={{0,8},{8,0},{16,24},{24,16},{32,40},{40,32},{48,56},{56,48},{64,72... | collective-permute-start | bytes 98312 | tf_op jit(solution)/shard_map/ppermute | solution.py:344
  19.0 11.7 %collective-permute-start.3 = (bf16[3,1,2,64,128]{4,3,2,0,1:T(8,128)(2,1)S(1)}, bf16[3,1,2,64,128]{4,3,2,0,1:T(8,128)(2,1)S(1)}, u32[]{:S(2)}, u32[]{:S(2)}) collective-permute-start(bf16[3,1,2,64,128]{4,3,2,0,1:T(8,128)(2,1)S(1)} %get-tuple-element.59), channel_id=1, source_target_pairs={{0,4},{1,5},{2,6},{3,7},{4,0},{5,1},{6,2},{7,3},{8,12},{9,13},{10,... | collective-permute-start | bytes 294920 | tf_op jit(solution)/shard_map/ppermute | solution.py:350
  30.7 13.8 %collective-permute-start.4 = (bf16[3,2,2,64,128]{4,3,2,1,0:T(8,128)(2,1)S(1)}, bf16[3,2,2,64,128]{4,3,2,1,0:T(8,128)(2,1)S(1)}, u32[]{:S(2)}, u32[]{:S(2)}) collective-permute-start(bf16[3,2,2,64,128]{4,3,2,1,0:T(8,128)(2,1)S(1)} %broadcast_select_fusion.2), channel_id=1, source_target_pairs={{0,2},{1,3},{2,0},{3,1},{4,6},{5,7},{6,4},{7,5},{8,10},{9,11},{10,... | collective-permute-start | bytes 589832 | tf_op jit(solution)/shard_map/ppermute | solution.py:350
  35.9 11.7 %copy-start = (bf16[1,2,512,128]{3,2,1,0:T(8,128)(2,1)S(1)}, bf16[1,2,512,128]{3,2,1,0:T(8,128)(2,1)}, u32[]{:S(2)}) copy-start(bf16[1,2,512,128]{3,2,1,0:T(8,128)(2,1)} %param.5) | copy-start | bytes 786436
  44.8 4.9 %copy-start.2 = (s32[65536]{0:T(1024)S(1)}, s32[65536]{0:T(1024)}, u32[]{:S(2)}) copy-start(s32[65536]{0:T(1024)} %param.9) | copy-start | bytes 786436
  44.9 11.9 %collective-permute-start.5 = (bf16[3,4,2,64,128]{4,3,2,1,0:T(8,128)(2,1)S(1)}, bf16[3,4,2,64,128]{4,3,2,1,0:T(8,128)(2,1)S(1)}, u32[]{:S(2)}, u32[]{:S(2)}) collective-permute-start(bf16[3,4,2,64,128]{4,3,2,1,0:T(8,128)(2,1)S(1)} %broadcast_select_fusion.1), channel_id=1, source_target_pairs={{0,1},{1,0},{2,3},{3,2},{4,5},{5,4},{6,7},{7,6},{8,9},{9,8},{10,11... | collective-permute-start | bytes 1179656 | tf_op jit(solution)/shard_map/ppermute | solution.py:350
  47.6 20.2 %collective-permute-start = (bf16[2,512,128]{2,1,0:T(8,128)(2,1)S(1)}, bf16[2,512,128]{2,1,0:T(8,128)(2,1)S(1)}, u32[]{:S(2)}, u32[]{:S(2)}) collective-permute-start(bf16[2,512,128]{2,1,0:T(8,128)(2,1)S(1)} %maximum_select_fusion), channel_id=1, source_target_pairs={{0,8},{8,0},{16,24},{24,16},{32,40},{40,32},{48,56},{56,48},{64,72... | collective-permute-start | bytes 786440 | tf_op jit(solution)/shard_map/ppermute | solution.py:357
  57.0 14.1 %collective-permute-start.8 = (bf16[2,8,2,64,128]{4,3,2,1,0:T(8,128)(2,1)S(1)}, bf16[2,8,2,64,128]{4,3,2,1,0:T(8,128)(2,1)S(1)}, u32[]{:S(2)}, u32[]{:S(2)}) collective-permute-start(bf16[2,8,2,64,128]{4,3,2,1,0:T(8,128)(2,1)S(1)} %bitcast.228), channel_id=1, source_target_pairs={{0,16},{16,32},{32,48},{24,8},{40,24},{56,40},{64,80},{80,96},{96,... | collective-permute-start | bytes 1572872 | tf_op jit(solution)/shard_map/ppermute | solution.py:368
  58.4 12.7 %collective-permute-start.6 = (bf16[8,2,64,128]{3,2,1,0:T(8,128)(2,1)S(1)}, bf16[8,2,64,128]{3,2,1,0:T(8,128)(2,1)S(1)}, u32[]{:S(2)}, u32[]{:S(2)}) collective-permute-start(bf16[8,2,64,128]{3,2,1,0:T(8,128)(2,1)S(1)} %bitcast.255), channel_id=1, source_target_pairs={{0,32},{16,48},{40,8},{56,24},{64,96},{80,112},{104,72},{120,88},{... | collective-permute-start | bytes 786440 | tf_op jit(solution)/shard_map/ppermute | solution.py:367
  65.2 6.2 %collective-permute-start.7 = (bf16[8,2,64,128]{3,2,1,0:T(8,128)(2,1)S(1)}, bf16[8,2,64,128]{3,2,1,0:T(8,128)(2,1)S(1)}, u32[]{:S(2)}, u32[]{:S(2)}) collective-permute-start(bf16[8,2,64,128]{3,2,1,0:T(8,128)(2,1)S(1)} %bitcast.251), channel_id=1, source_target_pairs={{8,0},{48,56},{72,64},{112,120},{136,128},{176,184},{200,192},{240... | collective-permute-start | bytes 786440 | tf_op jit(solution)/shard_map/ppermute | solution.py:370
  66.5 8.3 %collective-permute-start.9 = (bf16[8,2,64,128]{3,2,1,0:T(8,128)(2,1)S(1)}, bf16[8,2,64,128]{3,2,1,0:T(8,128)(2,1)S(1)}, u32[]{:S(2)}, u32[]{:S(2)}) collective-permute-start(bf16[8,2,64,128]{3,2,1,0:T(8,128)(2,1)S(1)} %bitcast.252), channel_id=1, source_target_pairs={{16,0},{40,56},{80,64},{104,120},{144,128},{168,184},{208,192},{23... | collective-permute-start | bytes 786440 | tf_op jit(solution)/shard_map/ppermute | solution.py:369
  77.9 15.4 %collective-permute-start.11 = (bf16[2,8,2,64,128]{4,3,2,1,0:T(8,128)(2,1)S(1)}, bf16[2,8,2,64,128]{4,3,2,1,0:T(8,128)(2,1)S(1)}, u32[]{:S(2)}, u32[]{:S(2)}) collective-permute-start(bf16[2,8,2,64,128]{4,3,2,1,0:T(8,128)(2,1)S(1)} %get-tuple-element.32), channel_id=1, source_target_pairs={{16,0},{32,16},{48,32},{8,24},{24,40},{40,56},{80,64},{96,80},{112... | collective-permute-start | bytes 1572872 | tf_op jit(solution)/shard_map/ppermute | solution.py:426
  79.3 13.9 %collective-permute-start.15 = (bf16[8,2,64,128]{3,2,1,0:T(8,128)(2,1)S(1)}, bf16[8,2,64,128]{3,2,1,0:T(8,128)(2,1)S(1)}, u32[]{:S(2)}, u32[]{:S(2)}) collective-permute-start(bf16[8,2,64,128]{3,2,1,0:T(8,128)(2,1)S(1)} %get-tuple-element.45), channel_id=1, source_target_pairs={{0,8},{56,48},{64,72},{120,112},{128,136},{184,176},{192,200},{248... | collective-permute-start | bytes 786440 | tf_op jit(solution)/shard_map/ppermute | solution.py:424
  80.6 12.6 %collective-permute-start.14 = (bf16[8,2,64,128]{3,2,1,0:T(8,128)(2,1)S(1)}, bf16[8,2,64,128]{3,2,1,0:T(8,128)(2,1)S(1)}, u32[]{:S(2)}, u32[]{:S(2)}) collective-permute-start(bf16[8,2,64,128]{3,2,1,0:T(8,128)(2,1)S(1)} %get-tuple-element.44), channel_id=1, source_target_pairs={{0,16},{56,40},{64,80},{120,104},{128,144},{184,168},{192,208},{24... | collective-permute-start | bytes 786440 | tf_op jit(solution)/shard_map/ppermute | solution.py:423
  87.6 9.8 %collective-permute-start.12 = (bf16[8,2,64,128]{3,2,1,0:T(8,128)(2,1)S(1)}, bf16[8,2,64,128]{3,2,1,0:T(8,128)(2,1)S(1)}, u32[]{:S(2)}, u32[]{:S(2)}) collective-permute-start(bf16[8,2,64,128]{3,2,1,0:T(8,128)(2,1)S(1)} %get-tuple-element.33), channel_id=1, source_target_pairs={{32,0},{48,16},{8,40},{24,56},{96,64},{112,80},{72,104},{88,120},{... | collective-permute-start | bytes 786440 | tf_op jit(solution)/shard_map/ppermute | solution.py:425
  97.6 11.7 %collective-permute-start.13 = (bf16[2,4,2,64,128]{4,3,2,1,0:T(8,128)(2,1)S(1)}, bf16[2,4,2,64,128]{4,3,2,1,0:T(8,128)(2,1)S(1)}, u32[]{:S(2)}, u32[]{:S(2)}) collective-permute-start(bf16[2,4,2,64,128]{4,3,2,1,0:T(8,128)(2,1)S(1)} %fusion.6), channel_id=1, source_target_pairs={{0,1},{1,0},{2,3},{3,2},{4,5},{5,4},{6,7},{7,6},{8,9},{9,8},{10,11... | collective-permute-start | bytes 786440 | tf_op jit(solution)/shard_map/ppermute | solution.py:445
  101.2 8.0 %collective-permute-start.16 = (bf16[4,2,64,128]{3,2,1,0:T(8,128)(2,1)S(1)}, bf16[4,2,64,128]{3,2,1,0:T(8,128)(2,1)S(1)}, u32[]{:S(2)}, u32[]{:S(2)}) collective-permute-start(bf16[4,2,64,128]{3,2,1,0:T(8,128)(2,1)S(1)} %fusion.14), channel_id=1, source_target_pairs={{0,1},{1,0},{2,3},{3,2},{4,5},{5,4},{6,7},{7,6},{8,9},{9,8},{10,11... | collective-permute-start | bytes 393224 | tf_op jit(solution)/shard_map/ppermute | solution.py:446
  103.5 28.8 %collective-permute-start.10 = (bf16[2,512,128]{2,1,0:T(8,128)(2,1)S(1)}, bf16[2,512,128]{2,1,0:T(8,128)(2,1)S(1)}, u32[]{:S(2)}, u32[]{:S(2)}) collective-permute-start(bf16[2,512,128]{2,1,0:T(8,128)(2,1)S(1)} %get-tuple-element.30), channel_id=1, source_target_pairs={{0,8},{8,0},{16,24},{24,16},{32,40},{40,32},{48,56},{56,48},{64,72... | collective-permute-start | bytes 786440 | tf_op jit(solution)/shard_map/ppermute | solution.py:460
  109.4 12.8 %collective-permute-start.17 = (bf16[2,2,2,64,128]{4,3,2,1,0:T(8,128)(2,1)S(1)}, bf16[2,2,2,64,128]{4,3,2,1,0:T(8,128)(2,1)S(1)}, u32[]{:S(2)}, u32[]{:S(2)}) collective-permute-start(bf16[2,2,2,64,128]{4,3,2,1,0:T(8,128)(2,1)S(1)} %fusion.15), channel_id=1, source_target_pairs={{0,2},{1,3},{2,0},{3,1},{4,6},{5,7},{6,4},{7,5},{8,10},{9,11},{10,... | collective-permute-start | bytes 393224 | tf_op jit(solution)/shard_map/ppermute | solution.py:445
  115.1 7.1 %collective-permute-start.18 = (bf16[2,2,64,128]{3,2,1,0:T(8,128)(2,1)S(1)}, bf16[2,2,64,128]{3,2,1,0:T(8,128)(2,1)S(1)}, u32[]{:S(2)}, u32[]{:S(2)}) collective-permute-start(bf16[2,2,64,128]{3,2,1,0:T(8,128)(2,1)S(1)} %fusion.23), channel_id=1, source_target_pairs={{0,2},{1,3},{2,0},{3,1},{4,6},{5,7},{6,4},{7,5},{8,10},{9,11},{10,... | collective-permute-start | bytes 196616 | tf_op jit(solution)/shard_map/ppermute | solution.py:446
  122.2 17.9 %collective-permute-start.19 = (bf16[2,1,2,64,128]{4,3,2,0,1:T(8,128)(2,1)S(1)}, bf16[2,1,2,64,128]{4,3,2,0,1:T(8,128)(2,1)S(1)}, u32[]{:S(2)}, u32[]{:S(2)}) collective-permute-start(bf16[2,1,2,64,128]{4,3,2,0,1:T(8,128)(2,1)S(1)} %fusion.24), channel_id=1, source_target_pairs={{0,4},{1,5},{2,6},{3,7},{4,0},{5,1},{6,2},{7,3},{8,12},{9,13},{10,... | collective-permute-start | bytes 196616 | tf_op jit(solution)/shard_map/ppermute | solution.py:445
  130.3 9.7 %collective-permute-start.20 = (bf16[1,2,64,128]{3,2,1,0:T(8,128)(2,1)S(1)}, bf16[1,2,64,128]{3,2,1,0:T(8,128)(2,1)S(1)}, u32[]{:S(2)}, u32[]{:S(2)}) collective-permute-start(bf16[1,2,64,128]{3,2,1,0:T(8,128)(2,1)S(1)} %fusion.27), channel_id=1, source_target_pairs={{0,4},{1,5},{2,6},{3,7},{4,0},{5,1},{6,2},{7,3},{8,12},{9,13},{10,... | collective-permute-start | bytes 98312 | tf_op jit(solution)/shard_map/ppermute | solution.py:446
  140.1 15.1 %collective-permute-start.22 = (bf16[2,64,128]{2,1,0:T(8,128)(2,1)S(1)}, bf16[2,64,128]{2,1,0:T(8,128)(2,1)S(1)}, u32[]{:S(2)}, u32[]{:S(2)}) collective-permute-start(bf16[2,64,128]{2,1,0:T(8,128)(2,1)S(1)} %fusion.29), channel_id=1, source_target_pairs={{87,56},{86,57},{85,58},{84,59},{83,60},{82,61},{81,62},{80,63},{7... | collective-permute-start | bytes 98312 | tf_op jit(solution)/shard_map/ppermute | solution.py:450
  145.6 9.7 %collective-permute-start.21 = (bf16[2,64,128]{2,1,0:T(8,128)(2,1)S(1)}, bf16[2,64,128]{2,1,0:T(8,128)(2,1)S(1)}, u32[]{:S(2)}, u32[]{:S(2)}) collective-permute-start(bf16[2,64,128]{2,1,0:T(8,128)(2,1)S(1)} %fusion.28), channel_id=1, source_target_pairs={{0,8},{8,0},{16,24},{24,16},{32,40},{40,32},{48,56},{56,48},{64,72... | collective-permute-start | bytes 98312 | tf_op jit(solution)/shard_map/ppermute | solution.py:453

commit v11 on v9

--- a/solution.py
+++ b/solution.py
@@ -364,10 +364,11 @@
         swap,
     )
 
-    kv_next = lax.ppermute(jnp.where(even, kv_own[1], kv_own[0]), CTX, far_chip)
+    hands_edge = (place == 1) | (place == GROUP - 2)
+    kv_next = jnp.where(hands_edge, kv_edge, jnp.where(even, kv_own[1], kv_own[0]))
+    kv_next = lax.ppermute(kv_next, CTX, far_chip + edge2)
     kv_near = lax.ppermute(kv_own, CTX, near)
     kv_edge1 = lax.ppermute(kv_edge, CTX, edge1)
-    kv_edge2 = lax.ppermute(kv_edge, CTX, edge2)
 
     first = jnp.where(even, position, 2 * ctx - 1 - position)
     window = (REACH + 2) * width
@@ -388,7 +389,7 @@
     kv_prev = jnp.stack(
         [
             jnp.where(edge_next, kv_edge, kv_next),
-            jnp.where(edge_near, kv_edge2, near_ordered[0]),
+            jnp.where(edge_near, kv_next, near_ordered[0]),
             jnp.where(edge_near, kv_edge1, near_ordered[1]),
         ]
     )
@@ -420,10 +421,10 @@
         6, tile, head_dim, 6,
     )(lo, places, start, queries, out_grad, far, top, total, acc, kv_prev)
 
-    r_edge1 = lax.ppermute(p_near[1], CTX, inverse(edge1)).astype(f32)
-    r_edge2 = lax.ppermute(p_near[0], CTX, inverse(edge2)).astype(f32)
-    r_next = lax.ppermute(p_next, CTX, inverse(far_chip)).astype(f32)
-    r_near = lax.ppermute(p_near, CTX, inverse(near)).astype(f32)
+    r_edge1 = lax.ppermute(p_near[1], CTX, inverse(edge1))
+    r_edge2 = lax.ppermute(p_near[0], CTX, inverse(edge2))
+    r_next = lax.ppermute(p_next, CTX, inverse(far_chip))
+    r_near = lax.ppermute(p_near, CTX, inverse(near))
 
     out_own, out_far, p_own = vmem_kernel(
         own_backward_kernel, "own_backward",
@@ -433,7 +434,11 @@
         6, tile, head_dim, 5,
     )(lo, places, start, queries, out_grad, far, kv_own, attended, lse, delta, acc)
 
-    edge_sum = jnp.where(edge_next, p_next.astype(f32), 0.0) + r_edge1 + r_edge2
+    r_edge1, r_edge2, r_next, r_near, p_own = lax.optimization_barrier(
+        (r_edge1, r_edge2, r_next, r_near, p_own)
+    )
+    edge_sum = jnp.where(edge_next, p_next.astype(f32), 0.0) + r_edge1.astype(f32)
+    edge_sum = edge_sum + r_edge2.astype(f32)
     for bit in reversed(bits):
         halves = edge_sum.reshape((-1, 2) + half.shape[1:])
         away = pick(high[bit], halves[:, 0], halves[:, 1]).astype(bf16)
@@ -441,13 +446,18 @@
         edge_sum = pick(high[bit], halves[:, 1], halves[:, 0]) + other.astype(f32)
     returned = lax.ppermute(edge_sum[0].astype(bf16), everywhere, inverse(edge)).astype(f32)
 
-    sums = p_own + r_near
-    first_sum, second_sum = sums[0], sums[1] + r_next
+    sums = p_own + r_near.astype(f32)
+    first_sum, second_sum = sums[0], sums[1] + r_next.astype(f32)
     sums = jnp.stack([pick(even, second_sum, first_sum), pick(even, first_sum, second_sum)])
     for bit in reversed(bits):
         halves = sums.reshape((2, -1, 2) + half.shape[1:])
         away = pick(high[bit], halves[:, :, 1], halves[:, :, 0]).astype(bf16)
         other = lax.ppermute(away, everywhere, head_pairs(ctx, heads, bit))
+        if bit == bits[-1]:
+            other, out_far = lax.optimization_barrier((other, out_far))
+            back = lax.ppermute(out_far, CTX, swap)
+        elif bit == bits[0]:
+            other, back = lax.optimization_barrier((other, back))
         sums = pick(high[bit], halves[:, :, 0], halves[:, :, 1]) + other.astype(f32)
     stays = sums[:, 0]
     own_half = pick(even, stays[1], stays[0])
@@ -458,7 +468,6 @@
     upper = pick(even, own_half, far_half) + jnp.where(sends_lower, 0.0, returned)
     grads = jnp.stack([lower, upper]).astype(bf16)
 
-    back = lax.ppermute(out_far, CTX, swap)
     results = []
     for k in range(2):
         results.append(

time: 151 us -> 147 us (0.974)
  the two profiles are of different devices: /device:TPU:100 before, /device:TPU:76 now
where the time goes in v11:
time: 147 us
  starting transfers between devices  77.4 us (53%)
  waiting for transfers between devices  48 us (33%)
  Pallas kernels  11.6 us (8%)
  other arithmetic  4.87 us (3%)
  local copies, waits for them, and re-layouts  3.43 us (2%)
    ppermute x3, waiting for transfers between devices, body(): other = lax.ppermute(kv_all, everywhere, head_pairs(ctx, heads, bit))  19.7 us
    ppermute x3, starting transfers between devices, body(): other = lax.ppermute(away, everywhere, head_pairs(ctx, heads, bit))  15.7 us
    ppermute x3, starting transfers between devices, body(): other = lax.ppermute(kv_all, everywhere, head_pairs(ctx, heads, bit))  15.3 us
    ppermute x1, waiting for transfers between devices, body(): r_next = lax.ppermute(p_next, CTX, inverse(far_chip))  14.8 us
    ppermute x1, starting transfers between devices, body(): crossed = lax.ppermute(leaving, everywhere, edge)  12.5 us
    pallas_call x3, Pallas kernels, call(): pl.pallas_call(kernel, out_shape=outputs, in_specs=[pl.BlockSpec(memory_s...  11.6 us
    ppermute x3, starting transfers between devices, body(): other = lax.ppermute(away, everywhere, holder_pairs(ctx, heads, bit))  10.3 us
    ppermute x1, waiting for transfers between devices, body(): lax.ppermute(edge_sum[0].astype(bf16), everywhere, inverse(edge))  7.02 us
  transfers between devices with their start and end apart: 22, of which 10 were waited for; matrix products, arithmetic and copies ran while one was open for 4% of the time, Pallas kernels for 6%

profile of v11, /device:TPU:76, one launch (start us, length us, event | category | flops | bytes accessed | tf_op | source)
XLA Modules:
  0.0 146.5 jit_solution(16520033014611566103)
XLA Ops:
  2.2 12.5 %collective-permute-start.2 = (bf16[2,64,128]{2,1,0:T(8,128)(2,1)S(1)}, bf16[2,64,128]{2,1,0:T(8,128)(2,1)S(1)}, u32[]{:S(2)}, u32[]{:S(2)}) collective-permute-start(bf16[2,64,128]{2,1,0:T(8,128)(2,1)S(1)} %get-tuple-element.70), channel_id=1, source_target_pairs={{56,87},{57,86},{58,85},{59,84},{60,83},{61,82},{62,81},{63,80},{4... | collective-permute-start | bytes 98312 | tf_op jit(solution)/shard_map/ppermute | solution.py:345
  14.7 1.9 %collective-permute-start.1 = (bf16[2,64,128]{2,1,0:T(8,128)(2,1)S(1)}, bf16[2,64,128]{2,1,0:T(8,128)(2,1)S(1)}, u32[]{:S(2)}, u32[]{:S(2)}) collective-permute-start(bf16[2,64,128]{2,1,0:T(8,128)(2,1)S(1)} %get-tuple-element.71), channel_id=1, source_target_pairs={{0,8},{8,0},{16,24},{24,16},{32,40},{40,32},{48,56},{56,48},{64,72... | collective-permute-start | bytes 98312 | tf_op jit(solution)/shard_map/ppermute | solution.py:344
  17.9 5.9 %collective-permute-start.3 = (bf16[3,1,2,64,128]{4,3,2,0,1:T(8,128)(2,1)S(1)}, bf16[3,1,2,64,128]{4,3,2,0,1:T(8,128)(2,1)S(1)}, u32[]{:S(2)}, u32[]{:S(2)}) collective-permute-start(bf16[3,1,2,64,128]{4,3,2,0,1:T(8,128)(2,1)S(1)} %get-tuple-element.66), channel_id=1, source_target_pairs={{0,4},{1,5},{2,6},{3,7},{4,0},{5,1},{6,2},{7,3},{8,12},{9,13},{10,... | collective-permute-start | bytes 294920 | tf_op jit(solution)/shard_map/ppermute | solution.py:350
  24.0 7.1 %collective-permute-done.3 = bf16[3,1,2,64,128]{4,3,2,0,1:T(8,128)(2,1)S(1)} collective-permute-done((bf16[3,1,2,64,128]{4,3,2,0,1:T(8,128)(2,1)S(1)}, bf16[3,1,2,64,128]{4,3,2,0,1:T(8,128)(2,1)S(1)}, u32[]{:S(2)}, u32[]{:S(2)}) %collective-permute-start.3) | collective-permute-done | bytes 98336 | tf_op jit(solution)/shard_map/ppermute | solution.py:350
  31.2 6.2 %collective-permute-start.4 = (bf16[3,2,2,64,128]{4,3,2,1,0:T(8,128)(2,1)S(1)}, bf16[3,2,2,64,128]{4,3,2,1,0:T(8,128)(2,1)S(1)}, u32[]{:S(2)}, u32[]{:S(2)}) collective-permute-start(bf16[3,2,2,64,128]{4,3,2,1,0:T(8,128)(2,1)S(1)} %broadcast_select_fusion.2), channel_id=1, source_target_pairs={{0,2},{1,3},{2,0},{3,1},{4,6},{5,7},{6,4},{7,5},{8,10},{9,11},{10,... | collective-permute-start | bytes 589832 | tf_op jit(solution)/shard_map/ppermute | solution.py:350
  37.5 1.9 %collective-permute-start = (bf16[2,512,128]{2,1,0:T(8,128)(2,1)S(1)}, bf16[2,512,128]{2,1,0:T(8,128)(2,1)S(1)}, u32[]{:S(2)}, u32[]{:S(2)}) collective-permute-start(bf16[2,512,128]{2,1,0:T(8,128)(2,1)S(1)} %maximum_select_fusion), channel_id=1, source_target_pairs={{0,8},{8,0},{16,24},{24,16},{32,40},{40,32},{48,56},{56,48},{64,72... | collective-permute-start | bytes 786440 | tf_op jit(solution)/shard_map/ppermute | solution.py:357
  39.6 4.7 %collective-permute-done.4 = bf16[3,2,2,64,128]{4,3,2,1,0:T(8,128)(2,1)S(1)} collective-permute-done((bf16[3,2,2,64,128]{4,3,2,1,0:T(8,128)(2,1)S(1)}, bf16[3,2,2,64,128]{4,3,2,1,0:T(8,128)(2,1)S(1)}, u32[]{:S(2)}, u32[]{:S(2)}) %collective-permute-start.4) | collective-permute-done | bytes 196640 | tf_op jit(solution)/shard_map/ppermute | solution.py:350
  44.6 3.2 %collective-permute-start.5 = (bf16[3,4,2,64,128]{4,3,2,1,0:T(8,128)(2,1)S(1)}, bf16[3,4,2,64,128]{4,3,2,1,0:T(8,128)(2,1)S(1)}, u32[]{:S(2)}, u32[]{:S(2)}) collective-permute-start(bf16[3,4,2,64,128]{4,3,2,1,0:T(8,128)(2,1)S(1)} %broadcast_select_fusion.1), channel_id=1, source_target_pairs={{0,1},{1,0},{2,3},{3,2},{4,5},{5,4},{6,7},{7,6},{8,9},{9,8},{10,11... | collective-permute-start | bytes 1179656 | tf_op jit(solution)/shard_map/ppermute | solution.py:350
  48.1 1.4 convert_reduce_fusion
  49.7 7.9 %collective-permute-done.5 = bf16[3,4,2,64,128]{4,3,2,1,0:T(8,128)(2,1)S(1)} collective-permute-done((bf16[3,4,2,64,128]{4,3,2,1,0:T(8,128)(2,1)S(1)}, bf16[3,4,2,64,128]{4,3,2,1,0:T(8,128)(2,1)S(1)}, u32[]{:S(2)}, u32[]{:S(2)}) %collective-permute-start.5) | collective-permute-done | bytes 393248 | tf_op jit(solution)/shard_map/ppermute | solution.py:350
  57.7 2.4 %collective-permute-start.7 = (bf16[2,8,2,64,128]{4,3,2,1,0:T(8,128)(2,1)S(1)}, bf16[2,8,2,64,128]{4,3,2,1,0:T(8,128)(2,1)S(1)}, u32[]{:S(2)}, u32[]{:S(2)}) collective-permute-start(bf16[2,8,2,64,128]{4,3,2,1,0:T(8,128)(2,1)S(1)} %bitcast.228), channel_id=1, source_target_pairs={{0,16},{16,32},{32,48},{24,8},{40,24},{56,40},{64,80},{80,96},{96,... | collective-permute-start | bytes 1572872 | tf_op jit(solution)/shard_map/ppermute | solution.py:370
  60.2 3.6 %collective-permute-start.8 = (bf16[8,2,64,128]{3,2,1,0:T(8,128)(2,1)S(1)}, bf16[8,2,64,128]{3,2,1,0:T(8,128)(2,1)S(1)}, u32[]{:S(2)}, u32[]{:S(2)}) collective-permute-start(bf16[8,2,64,128]{3,2,1,0:T(8,128)(2,1)S(1)} %bitcast.247), channel_id=1, source_target_pairs={{16,0},{40,56},{80,64},{104,120},{144,128},{168,184},{208,192},{23... | collective-permute-start | bytes 786440 | tf_op jit(solution)/shard_map/ppermute | solution.py:371
  63.9 1.3 collective-permute-start.6
  65.3 3.7 %own_forward.1 = (f32[1,1024]{1,0:T(1,128)S(1)}, f32[1,1024]{1,0:T(1,128)S(1)}, f32[4,128,256]{2,1,0:T(8,128)S(1)}) custom-call(s32[4]{0:T(128)S(1)} %and_select_fusion.lo_ref, s32[1]{0:T(128)} %bitcast.place_ref, s32[1,1024]{1,0:T(1,128)S(1)} %bitcast.236, bf16[2,512,128]{2,1,0:T(8,128)(2,1)S(1)} %bitcast.231, ...), custom_call_target="tpu_custom_call" | custom-call | flops 201326592 | bytes 4194304 | tf_op jit(solution)/shard_map/own_forward/pallas_call | solution.py:301
  69.1 1.4 collective-permute-done.6
  70.8 3.1 %earlier.1 = (bf16[2,512,128]{2,1,0:T(8,128)(2,1)S(1)}, f32[1,1024]{1,0:T(1,128)S(1)}, f32[1,1024]{1,0:T(1,128)S(1)}, f32[4,128,256]{2,1,0:T(8,128)S(1)}, bf16[2...) custom-call(s32[4]{0:T(128)S(1)} %and_select_fusion.lo_ref, s32[1]{0:T(128)} %bitcast.place_ref, ...), custom_call_target="tpu_custom_call" | custom-call | flops 603979776 | bytes 4194304 | tf_op jit(solution)/shard_map/earlier/pallas_call | solution.py:301
  73.9 3.4 %collective-permute-start.12 = (bf16[2,8,2,64,128]{4,3,2,1,0:T(8,128)(2,1)S(1)}, bf16[2,8,2,64,128]{4,3,2,1,0:T(8,128)(2,1)S(1)}, u32[]{:S(2)}, u32[]{:S(2)}) collective-permute-start(bf16[2,8,2,64,128]{4,3,2,1,0:T(8,128)(2,1)S(1)} %get-tuple-element.33), channel_id=1, source_target_pairs={{16,0},{32,16},{48,32},{8,24},{24,40},{40,56},{80,64},{96,80},{112... | collective-permute-start | bytes 1572872 | tf_op jit(solution)/shard_map/ppermute | solution.py:427
  79.3 1.3 collective-permute-start.9
  80.6 4.8 %own_backward.1 = (bf16[2,512,128]{2,1,0:T(8,128)(2,1)S(1)}, bf16[2,512,128]{2,1,0:T(8,128)(2,1)S(1)}, f32[2,8,2,64,128]{4,3,2,1,0:T(8,128)S(1)}) custom-call(s32[4]{0:T(128)S(1)} %and_select_fusion.lo_ref, s32[1]{0:T(128)} %bitcast.place_ref, s32[1,1024]{1,0:T(1,128)S(1)} %bitcast.238, bf16[2,512,128]{2,1,0:T(8,128)(2,1)S(1)} %bitcast.233, ...), custom_call_target="tpu_custom_call" | custom-call | flops 503316480 | bytes 4194304 | tf_op jit(solution)/shard_map/own_backward/pallas_call | solution.py:301
  85.4 14.8 %collective-permute-done.11 = bf16[8,2,64,128]{3,2,1,0:T(8,128)(2,1)S(1)} collective-permute-done((bf16[8,2,64,128]{3,2,1,0:T(8,128)(2,1)S(1)}, bf16[8,2,64,128]{3,2,1,0:T(8,128)(2,1)S(1)}, u32[]{:S(2)}, u32[]{:S(2)}) %collective-permute-start.11) | collective-permute-done | bytes 262176 | tf_op jit(solution)/shard_map/ppermute | solution.py:426
  100.4 2.7 %collective-permute-start.18 = (bf16[4,2,64,128]{3,2,1,0:T(8,128)(2,1)S(1)}, bf16[4,2,64,128]{3,2,1,0:T(8,128)(2,1)S(1)}, u32[]{:S(2)}, u32[]{:S(2)}) collective-permute-start(bf16[4,2,64,128]{3,2,1,0:T(8,128)(2,1)S(1)} %fusion.15), channel_id=1, source_target_pairs={{0,1},{1,0},{2,3},{3,2},{4,5},{5,4},{6,7},{7,6},{8,9},{9,8},{10,11... | collective-permute-start | bytes 393224 | tf_op jit(solution)/shard_map/ppermute | solution.py:445
  103.5 3.2 %collective-permute-start.13 = (bf16[2,4,2,64,128]{4,3,2,1,0:T(8,128)(2,1)S(1)}, bf16[2,4,2,64,128]{4,3,2,1,0:T(8,128)(2,1)S(1)}, u32[]{:S(2)}, u32[]{:S(2)}) collective-permute-start(bf16[2,4,2,64,128]{4,3,2,1,0:T(8,128)(2,1)S(1)} %fusion.6), channel_id=1, source_target_pairs={{0,1},{1,0},{2,3},{3,2},{4,5},{5,4},{6,7},{7,6},{8,9},{9,8},{10,11... | collective-permute-start | bytes 786440 | tf_op jit(solution)/shard_map/ppermute | solution.py:455
  107.4 5.3 %collective-permute-start.19 = (bf16[2,2,64,128]{3,2,1,0:T(8,128)(2,1)S(1)}, bf16[2,2,64,128]{3,2,1,0:T(8,128)(2,1)S(1)}, u32[]{:S(2)}, u32[]{:S(2)}) collective-permute-start(bf16[2,2,64,128]{3,2,1,0:T(8,128)(2,1)S(1)} %fusion.22), channel_id=1, source_target_pairs={{0,2},{1,3},{2,0},{3,1},{4,6},{5,7},{6,4},{7,5},{8,10},{9,11},{10,... | collective-permute-start | bytes 196616 | tf_op jit(solution)/shard_map/ppermute | solution.py:445
  112.7 2.4 %collective-permute-done.19 = bf16[2,2,64,128]{3,2,1,0:T(8,128)(2,1)S(1)} collective-permute-done((bf16[2,2,64,128]{3,2,1,0:T(8,128)(2,1)S(1)}, bf16[2,2,64,128]{3,2,1,0:T(8,128)(2,1)S(1)}, u32[]{:S(2)}, u32[]{:S(2)}) %collective-permute-start.19) | collective-permute-done | bytes 65568 | tf_op jit(solution)/shard_map/ppermute | solution.py:445
  115.3 5.1 %collective-permute-start.14 = (bf16[2,2,2,64,128]{4,3,2,1,0:T(8,128)(2,1)S(1)}, bf16[2,2,2,64,128]{4,3,2,1,0:T(8,128)(2,1)S(1)}, u32[]{:S(2)}, u32[]{:S(2)}) collective-permute-start(bf16[2,2,2,64,128]{4,3,2,1,0:T(8,128)(2,1)S(1)} %fusion.14), channel_id=1, source_target_pairs={{0,2},{1,3},{2,0},{3,1},{4,6},{5,7},{6,4},{7,5},{8,10},{9,11},{10,... | collective-permute-start | bytes 393224 | tf_op jit(solution)/shard_map/ppermute | solution.py:455
  120.4 2.3 %collective-permute-start.20 = (bf16[1,2,64,128]{3,2,1,0:T(8,128)(2,1)S(1)}, bf16[1,2,64,128]{3,2,1,0:T(8,128)(2,1)S(1)}, u32[]{:S(2)}, u32[]{:S(2)}) collective-permute-start(bf16[1,2,64,128]{3,2,1,0:T(8,128)(2,1)S(1)} %fusion.26), channel_id=1, source_target_pairs={{0,4},{1,5},{2,6},{3,7},{4,0},{5,1},{6,2},{7,3},{8,12},{9,13},{10,... | collective-permute-start | bytes 98312 | tf_op jit(solution)/shard_map/ppermute | solution.py:445
  122.7 1.9 %collective-permute-start.16 = (bf16[2,512,128]{2,1,0:T(8,128)(2,1)S(1)}, bf16[2,512,128]{2,1,0:T(8,128)(2,1)S(1)}, u32[]{:S(2)}, u32[]{:S(2)}) collective-permute-start(bf16[2,512,128]{2,1,0:T(8,128)(2,1)S(1)} %get-tuple-element.41), channel_id=1, source_target_pairs={{0,8},{8,0},{16,24},{24,16},{32,40},{40,32},{48,56},{56,48},{64,72... | collective-permute-start | bytes 786440 | tf_op jit(solution)/shard_map/ppermute | solution.py:458
  124.7 7.4 %collective-permute-start.15 = (bf16[2,1,2,64,128]{4,3,2,0,1:T(8,128)(2,1)S(1)}, bf16[2,1,2,64,128]{4,3,2,0,1:T(8,128)(2,1)S(1)}, u32[]{:S(2)}, u32[]{:S(2)}) collective-permute-start(bf16[2,1,2,64,128]{4,3,2,0,1:T(8,128)(2,1)S(1)} %fusion.23), channel_id=1, source_target_pairs={{0,4},{1,5},{2,6},{3,7},{4,0},{5,1},{6,2},{7,3},{8,12},{9,13},{10,... | collective-permute-start | bytes 196616 | tf_op jit(solution)/shard_map/ppermute | solution.py:455
  132.2 1.9 %collective-permute-start.21 = (bf16[2,64,128]{2,1,0:T(8,128)(2,1)S(1)}, bf16[2,64,128]{2,1,0:T(8,128)(2,1)S(1)}, u32[]{:S(2)}, u32[]{:S(2)}) collective-permute-start(bf16[2,64,128]{2,1,0:T(8,128)(2,1)S(1)} %fusion.28), channel_id=1, source_target_pairs={{87,56},{86,57},{85,58},{84,59},{83,60},{82,61},{81,62},{80,63},{7... | collective-permute-start | bytes 98312 | tf_op jit(solution)/shard_map/ppermute | solution.py:447
  134.1 1.9 %collective-permute-done.15 = bf16[2,1,2,64,128]{4,3,2,0,1:T(8,128)(2,1)S(1)} collective-permute-done((bf16[2,1,2,64,128]{4,3,2,0,1:T(8,128)(2,1)S(1)}, bf16[2,1,2,64,128]{4,3,2,0,1:T(8,128)(2,1)S(1)}, u32[]{:S(2)}, u32[]{:S(2)}) %collective-permute-start.15) | collective-permute-done | bytes 65568 | tf_op jit(solution)/shard_map/ppermute | solution.py:455
  136.1 1.9 %collective-permute-start.17 = (bf16[2,64,128]{2,1,0:T(8,128)(2,1)S(1)}, bf16[2,64,128]{2,1,0:T(8,128)(2,1)S(1)}, u32[]{:S(2)}, u32[]{:S(2)}) collective-permute-start(bf16[2,64,128]{2,1,0:T(8,128)(2,1)S(1)} %fusion.27), channel_id=1, source_target_pairs={{0,8},{8,0},{16,24},{24,16},{32,40},{40,32},{48,56},{56,48},{64,72... | collective-permute-start | bytes 98312 | tf_op jit(solution)/shard_map/ppermute | solution.py:464
  138.8 7.0 %collective-permute-done.21 = bf16[2,64,128]{2,1,0:T(8,128)(2,1)S(1)} collective-permute-done((bf16[2,64,128]{2,1,0:T(8,128)(2,1)S(1)}, bf16[2,64,128]{2,1,0:T(8,128)(2,1)S(1)}, u32[]{:S(2)}, u32[]{:S(2)}) %collective-permute-start.21) | collective-permute-done | bytes 32800 | tf_op jit(solution)/shard_map/ppermute | solution.py:447
  (78 shorter events, 9.6 us)
Async XLA Ops:
  0.6 36.8 %copy-start.1 = (bf16[1,2,512,128]{3,2,1,0:T(8,128)(2,1)S(1)}, bf16[1,2,512,128]{3,2,1,0:T(8,128)(2,1)}, u32[]{:S(2)}) copy-start(bf16[1,2,512,128]{3,2,1,0:T(8,128)(2,1)} %param.8) | copy-start | bytes 786436
  2.2 15.7 %collective-permute-start.2 = (bf16[2,64,128]{2,1,0:T(8,128)(2,1)S(1)}, bf16[2,64,128]{2,1,0:T(8,128)(2,1)S(1)}, u32[]{:S(2)}, u32[]{:S(2)}) collective-permute-start(bf16[2,64,128]{2,1,0:T(8,128)(2,1)S(1)} %get-tuple-element.70), channel_id=1, source_target_pairs={{56,87},{57,86},{58,85},{59,84},{60,83},{61,82},{62,81},{63,80},{4... | collective-permute-start | bytes 98312 | tf_op jit(solution)/shard_map/ppermute | solution.py:345
  14.7 3.1 %collective-permute-start.1 = (bf16[2,64,128]{2,1,0:T(8,128)(2,1)S(1)}, bf16[2,64,128]{2,1,0:T(8,128)(2,1)S(1)}, u32[]{:S(2)}, u32[]{:S(2)}) collective-permute-start(bf16[2,64,128]{2,1,0:T(8,128)(2,1)S(1)} %get-tuple-element.71), channel_id=1, source_target_pairs={{0,8},{8,0},{16,24},{24,16},{32,40},{40,32},{48,56},{56,48},{64,72... | collective-permute-start | bytes 98312 | tf_op jit(solution)/shard_map/ppermute | solution.py:344
  17.9 13.2 %collective-permute-start.3 = (bf16[3,1,2,64,128]{4,3,2,0,1:T(8,128)(2,1)S(1)}, bf16[3,1,2,64,128]{4,3,2,0,1:T(8,128)(2,1)S(1)}, u32[]{:S(2)}, u32[]{:S(2)}) collective-permute-start(bf16[3,1,2,64,128]{4,3,2,0,1:T(8,128)(2,1)S(1)} %get-tuple-element.66), channel_id=1, source_target_pairs={{0,4},{1,5},{2,6},{3,7},{4,0},{5,1},{6,2},{7,3},{8,12},{9,13},{10,... | collective-permute-start | bytes 294920 | tf_op jit(solution)/shard_map/ppermute | solution.py:350
  31.2 13.1 %collective-permute-start.4 = (bf16[3,2,2,64,128]{4,3,2,1,0:T(8,128)(2,1)S(1)}, bf16[3,2,2,64,128]{4,3,2,1,0:T(8,128)(2,1)S(1)}, u32[]{:S(2)}, u32[]{:S(2)}) collective-permute-start(bf16[3,2,2,64,128]{4,3,2,1,0:T(8,128)(2,1)S(1)} %broadcast_select_fusion.2), channel_id=1, source_target_pairs={{0,2},{1,3},{2,0},{3,1},{4,6},{5,7},{6,4},{7,5},{8,10},{9,11},{10,... | collective-permute-start | bytes 589832 | tf_op jit(solution)/shard_map/ppermute | solution.py:350
  37.5 27.7 %collective-permute-start = (bf16[2,512,128]{2,1,0:T(8,128)(2,1)S(1)}, bf16[2,512,128]{2,1,0:T(8,128)(2,1)S(1)}, u32[]{:S(2)}, u32[]{:S(2)}) collective-permute-start(bf16[2,512,128]{2,1,0:T(8,128)(2,1)S(1)} %maximum_select_fusion), channel_id=1, source_target_pairs={{0,8},{8,0},{16,24},{24,16},{32,40},{40,32},{48,56},{56,48},{64,72... | collective-permute-start | bytes 786440 | tf_op jit(solution)/shard_map/ppermute | solution.py:357
  39.6 8.2 %copy-start.2 = (s32[65536]{0:T(1024)S(1)}, s32[65536]{0:T(1024)}, u32[]{:S(2)}) copy-start(s32[65536]{0:T(1024)} %param.9) | copy-start | bytes 786436
  44.6 12.9 %collective-permute-start.5 = (bf16[3,4,2,64,128]{4,3,2,1,0:T(8,128)(2,1)S(1)}, bf16[3,4,2,64,128]{4,3,2,1,0:T(8,128)(2,1)S(1)}, u32[]{:S(2)}, u32[]{:S(2)}) collective-permute-start(bf16[3,4,2,64,128]{4,3,2,1,0:T(8,128)(2,1)S(1)} %broadcast_select_fusion.1), channel_id=1, source_target_pairs={{0,1},{1,0},{2,3},{3,2},{4,5},{5,4},{6,7},{7,6},{8,9},{9,8},{10,11... | collective-permute-start | bytes 1179656 | tf_op jit(solution)/shard_map/ppermute | solution.py:350
  57.7 11.2 %collective-permute-start.7 = (bf16[2,8,2,64,128]{4,3,2,1,0:T(8,128)(2,1)S(1)}, bf16[2,8,2,64,128]{4,3,2,1,0:T(8,128)(2,1)S(1)}, u32[]{:S(2)}, u32[]{:S(2)}) collective-permute-start(bf16[2,8,2,64,128]{4,3,2,1,0:T(8,128)(2,1)S(1)} %bitcast.228), channel_id=1, source_target_pairs={{0,16},{16,32},{32,48},{24,8},{40,24},{56,40},{64,80},{80,96},{96,... | collective-permute-start | bytes 1572872 | tf_op jit(solution)/shard_map/ppermute | solution.py:370
  60.2 5.1 %copy-start = (bf16[1,2,512,128]{3,2,1,0:T(8,128)(2,1)S(1)}, bf16[1,2,512,128]{3,2,1,0:T(8,128)(2,1)}, u32[]{:S(2)}) copy-start(bf16[1,2,512,128]{3,2,1,0:T(8,128)(2,1)} %param.5) | copy-start | bytes 786436
  60.2 8.9 %collective-permute-start.8 = (bf16[8,2,64,128]{3,2,1,0:T(8,128)(2,1)S(1)}, bf16[8,2,64,128]{3,2,1,0:T(8,128)(2,1)S(1)}, u32[]{:S(2)}, u32[]{:S(2)}) collective-permute-start(bf16[8,2,64,128]{3,2,1,0:T(8,128)(2,1)S(1)} %bitcast.247), channel_id=1, source_target_pairs={{16,0},{40,56},{80,64},{104,120},{144,128},{168,184},{208,192},{23... | collective-permute-start | bytes 786440 | tf_op jit(solution)/shard_map/ppermute | solution.py:371
  63.9 6.6 %collective-permute-start.6 = (bf16[8,2,64,128]{3,2,1,0:T(8,128)(2,1)S(1)}, bf16[8,2,64,128]{3,2,1,0:T(8,128)(2,1)S(1)}, u32[]{:S(2)}, u32[]{:S(2)}) collective-permute-start(bf16[8,2,64,128]{3,2,1,0:T(8,128)(2,1)S(1)} %bitcast_select_fusion.1), channel_id=1, source_target_pairs={{0,32},{16,48},{40,8},{56,24},{64,96},{80,112},{104,72},{120,88},{... | collective-permute-start | bytes 786440 | tf_op jit(solution)/shard_map/ppermute | solution.py:369
  73.9 26.4 %collective-permute-start.12 = (bf16[2,8,2,64,128]{4,3,2,1,0:T(8,128)(2,1)S(1)}, bf16[2,8,2,64,128]{4,3,2,1,0:T(8,128)(2,1)S(1)}, u32[]{:S(2)}, u32[]{:S(2)}) collective-permute-start(bf16[2,8,2,64,128]{4,3,2,1,0:T(8,128)(2,1)S(1)} %get-tuple-element.33), channel_id=1, source_target_pairs={{16,0},{32,16},{48,32},{8,24},{24,40},{40,56},{80,64},{96,80},{112... | collective-permute-start | bytes 1572872 | tf_op jit(solution)/shard_map/ppermute | solution.py:427
  77.3 23.0 %collective-permute-start.11 = (bf16[8,2,64,128]{3,2,1,0:T(8,128)(2,1)S(1)}, bf16[8,2,64,128]{3,2,1,0:T(8,128)(2,1)S(1)}, u32[]{:S(2)}, u32[]{:S(2)}) collective-permute-start(bf16[8,2,64,128]{3,2,1,0:T(8,128)(2,1)S(1)} %get-tuple-element.34), channel_id=1, source_target_pairs={{32,0},{48,16},{8,40},{24,56},{96,64},{112,80},{72,104},{88,120},{... | collective-permute-start | bytes 786440 | tf_op jit(solution)/shard_map/ppermute | solution.py:426
  78.6 21.7 %collective-permute-start.10 = (bf16[8,2,64,128]{3,2,1,0:T(8,128)(2,1)S(1)}, bf16[8,2,64,128]{3,2,1,0:T(8,128)(2,1)S(1)}, u32[]{:S(2)}, u32[]{:S(2)}) collective-permute-start(bf16[8,2,64,128]{3,2,1,0:T(8,128)(2,1)S(1)} %get-tuple-element.50), channel_id=1, source_target_pairs={{0,8},{56,48},{64,72},{120,112},{128,136},{184,176},{192,200},{248... | collective-permute-start | bytes 786440 | tf_op jit(solution)/shard_map/ppermute | solution.py:425
  79.3 21.0 %collective-permute-start.9 = (bf16[8,2,64,128]{3,2,1,0:T(8,128)(2,1)S(1)}, bf16[8,2,64,128]{3,2,1,0:T(8,128)(2,1)S(1)}, u32[]{:S(2)}, u32[]{:S(2)}) collective-permute-start(bf16[8,2,64,128]{3,2,1,0:T(8,128)(2,1)S(1)} %get-tuple-element.51), channel_id=1, source_target_pairs={{0,16},{56,40},{64,80},{120,104},{128,144},{184,168},{192,208},{24... | collective-permute-start | bytes 786440 | tf_op jit(solution)/shard_map/ppermute | solution.py:424
  100.4 6.9 %collective-permute-start.18 = (bf16[4,2,64,128]{3,2,1,0:T(8,128)(2,1)S(1)}, bf16[4,2,64,128]{3,2,1,0:T(8,128)(2,1)S(1)}, u32[]{:S(2)}, u32[]{:S(2)}) collective-permute-start(bf16[4,2,64,128]{3,2,1,0:T(8,128)(2,1)S(1)} %fusion.15), channel_id=1, source_target_pairs={{0,1},{1,0},{2,3},{3,2},{4,5},{5,4},{6,7},{7,6},{8,9},{9,8},{10,11... | collective-permute-start | bytes 393224 | tf_op jit(solution)/shard_map/ppermute | solution.py:445
  103.5 11.6 %collective-permute-start.13 = (bf16[2,4,2,64,128]{4,3,2,1,0:T(8,128)(2,1)S(1)}, bf16[2,4,2,64,128]{4,3,2,1,0:T(8,128)(2,1)S(1)}, u32[]{:S(2)}, u32[]{:S(2)}) collective-permute-start(bf16[2,4,2,64,128]{4,3,2,1,0:T(8,128)(2,1)S(1)} %fusion.6), channel_id=1, source_target_pairs={{0,1},{1,0},{2,3},{3,2},{4,5},{5,4},{6,7},{7,6},{8,9},{9,8},{10,11... | collective-permute-start | bytes 786440 | tf_op jit(solution)/shard_map/ppermute | solution.py:455
  107.4 7.7 %collective-permute-start.19 = (bf16[2,2,64,128]{3,2,1,0:T(8,128)(2,1)S(1)}, bf16[2,2,64,128]{3,2,1,0:T(8,128)(2,1)S(1)}, u32[]{:S(2)}, u32[]{:S(2)}) collective-permute-start(bf16[2,2,64,128]{3,2,1,0:T(8,128)(2,1)S(1)} %fusion.22), channel_id=1, source_target_pairs={{0,2},{1,3},{2,0},{3,1},{4,6},{5,7},{6,4},{7,5},{8,10},{9,11},{10,... | collective-permute-start | bytes 196616 | tf_op jit(solution)/shard_map/ppermute | solution.py:445
  115.3 9.4 %collective-permute-start.14 = (bf16[2,2,2,64,128]{4,3,2,1,0:T(8,128)(2,1)S(1)}, bf16[2,2,2,64,128]{4,3,2,1,0:T(8,128)(2,1)S(1)}, u32[]{:S(2)}, u32[]{:S(2)}) collective-permute-start(bf16[2,2,2,64,128]{4,3,2,1,0:T(8,128)(2,1)S(1)} %fusion.14), channel_id=1, source_target_pairs={{0,2},{1,3},{2,0},{3,1},{4,6},{5,7},{6,4},{7,5},{8,10},{9,11},{10,... | collective-permute-start | bytes 393224 | tf_op jit(solution)/shard_map/ppermute | solution.py:455
  120.4 11.8 %collective-permute-start.20 = (bf16[1,2,64,128]{3,2,1,0:T(8,128)(2,1)S(1)}, bf16[1,2,64,128]{3,2,1,0:T(8,128)(2,1)S(1)}, u32[]{:S(2)}, u32[]{:S(2)}) collective-permute-start(bf16[1,2,64,128]{3,2,1,0:T(8,128)(2,1)S(1)} %fusion.26), channel_id=1, source_target_pairs={{0,4},{1,5},{2,6},{3,7},{4,0},{5,1},{6,2},{7,3},{8,12},{9,13},{10,... | collective-permute-start | bytes 98312 | tf_op jit(solution)/shard_map/ppermute | solution.py:445
  122.7 13.3 %collective-permute-start.16 = (bf16[2,512,128]{2,1,0:T(8,128)(2,1)S(1)}, bf16[2,512,128]{2,1,0:T(8,128)(2,1)S(1)}, u32[]{:S(2)}, u32[]{:S(2)}) collective-permute-start(bf16[2,512,128]{2,1,0:T(8,128)(2,1)S(1)} %get-tuple-element.41), channel_id=1, source_target_pairs={{0,8},{8,0},{16,24},{24,16},{32,40},{40,32},{48,56},{56,48},{64,72... | collective-permute-start | bytes 786440 | tf_op jit(solution)/shard_map/ppermute | solution.py:458
  124.7 11.3 %collective-permute-start.15 = (bf16[2,1,2,64,128]{4,3,2,0,1:T(8,128)(2,1)S(1)}, bf16[2,1,2,64,128]{4,3,2,0,1:T(8,128)(2,1)S(1)}, u32[]{:S(2)}, u32[]{:S(2)}) collective-permute-start(bf16[2,1,2,64,128]{4,3,2,0,1:T(8,128)(2,1)S(1)} %fusion.23), channel_id=1, source_target_pairs={{0,4},{1,5},{2,6},{3,7},{4,0},{5,1},{6,2},{7,3},{8,12},{9,13},{10,... | collective-permute-start | bytes 196616 | tf_op jit(solution)/shard_map/ppermute | solution.py:455
  132.2 13.7 %collective-permute-start.21 = (bf16[2,64,128]{2,1,0:T(8,128)(2,1)S(1)}, bf16[2,64,128]{2,1,0:T(8,128)(2,1)S(1)}, u32[]{:S(2)}, u32[]{:S(2)}) collective-permute-start(bf16[2,64,128]{2,1,0:T(8,128)(2,1)S(1)} %fusion.28), channel_id=1, source_target_pairs={{87,56},{86,57},{85,58},{84,59},{83,60},{82,61},{81,62},{80,63},{7... | collective-permute-start | bytes 98312 | tf_op jit(solution)/shard_map/ppermute | solution.py:447
  136.1 9.8 %collective-permute-start.17 = (bf16[2,64,128]{2,1,0:T(8,128)(2,1)S(1)}, bf16[2,64,128]{2,1,0:T(8,128)(2,1)S(1)}, u32[]{:S(2)}, u32[]{:S(2)}) collective-permute-start(bf16[2,64,128]{2,1,0:T(8,128)(2,1)S(1)} %fusion.27), channel_id=1, source_target_pairs={{0,8},{8,0},{16,24},{24,16},{32,40},{40,32},{48,56},{56,48},{64,72... | collective-permute-start | bytes 98312 | tf_op jit(solution)/shard_map/ppermute | solution.py:464

commit v12 on v11

--- a/solution.py
+++ b/solution.py
@@ -422,8 +422,9 @@
     )(lo, places, start, queries, out_grad, far, top, total, acc, kv_prev)
 
     r_edge1 = lax.ppermute(p_near[1], CTX, inverse(edge1))
-    r_edge2 = lax.ppermute(p_near[0], CTX, inverse(edge2))
-    r_next = lax.ppermute(p_next, CTX, inverse(far_chip))
+    r_next = lax.ppermute(
+        jnp.where(edge_near, p_near[0], p_next), CTX, inverse(far_chip + edge2)
+    )
     r_near = lax.ppermute(p_near, CTX, inverse(near))
 
     out_own, out_far, p_own = vmem_kernel(
@@ -434,11 +435,10 @@
         6, tile, head_dim, 5,
     )(lo, places, start, queries, out_grad, far, kv_own, attended, lse, delta, acc)
 
-    r_edge1, r_edge2, r_next, r_near, p_own = lax.optimization_barrier(
-        (r_edge1, r_edge2, r_next, r_near, p_own)
-    )
+    r_edge1, r_next, r_near, p_own = lax.optimization_barrier((r_edge1, r_next, r_near, p_own))
     edge_sum = jnp.where(edge_next, p_next.astype(f32), 0.0) + r_edge1.astype(f32)
-    edge_sum = edge_sum + r_edge2.astype(f32)
+    r_next = r_next.astype(f32)
+    edge_sum = edge_sum + jnp.where(hands_edge, r_next, 0.0)
     for bit in reversed(bits):
         halves = edge_sum.reshape((-1, 2) + half.shape[1:])
         away = pick(high[bit], halves[:, 0], halves[:, 1]).astype(bf16)
@@ -447,7 +447,7 @@
     returned = lax.ppermute(edge_sum[0].astype(bf16), everywhere, inverse(edge)).astype(f32)
 
     sums = p_own + r_near.astype(f32)
-    first_sum, second_sum = sums[0], sums[1] + r_next.astype(f32)
+    first_sum, second_sum = sums[0], sums[1] + jnp.where(hands_edge, 0.0, r_next)
     sums = jnp.stack([pick(even, second_sum, first_sum), pick(even, first_sum, second_sum)])
     for bit in reversed(bits):
         halves = sums.reshape((2, -1, 2) + half.shape[1:])

time: 147 us -> 147 us (level)
  the two profiles are of different devices: /device:TPU:76 before, /device:TPU:67 now
where the time goes in v12:
time: 147 us; the launch traced here: 146 us
  starting transfers between devices  83.5 us (57%)
  waiting for transfers between devices  34.6 us (24%)
  Pallas kernels  18.1 us (12%)
  other arithmetic  4.89 us (3%)
  local copies, waits for them, and re-layouts  3.41 us (2%)
    pallas_call x3, Pallas kernels, call(): pl.pallas_call(kernel, out_shape=outputs, in_specs=[pl.BlockSpec(memory_s...  18.1 us
    ppermute x3, waiting for transfers between devices, body(): other = lax.ppermute(kv_all, everywhere, head_pairs(ctx, heads, bit))  16.8 us
    ppermute x3, starting transfers between devices, body(): other = lax.ppermute(kv_all, everywhere, head_pairs(ctx, heads, bit))  14.7 us
    ppermute x1, starting transfers between devices, body(): crossed = lax.ppermute(leaving, everywhere, edge)  14.1 us
    ppermute x3, starting transfers between devices, body(): other = lax.ppermute(away, everywhere, holder_pairs(ctx, heads, bit))  11.8 us
    ppermute x3, starting transfers between devices, body(): other = lax.ppermute(away, everywhere, head_pairs(ctx, heads, bit))  11.6 us
    ppermute x1, waiting for transfers between devices, body(): lax.ppermute(edge_sum[0].astype(bf16), everywhere, inverse(edge))  6.99 us
    ppermute x1, starting transfers between devices, body(): back = lax.ppermute(out_far, CTX, swap)  6.94 us
  transfers between devices with their start and end apart: 21, of which 10 were waited for; matrix products, arithmetic and copies ran while one was open for 4% of the time, Pallas kernels for 7%

profile of v12, /device:TPU:67, one launch (start us, length us, event | category | flops | bytes accessed | tf_op | source)
XLA Modules:
  0.0 145.8 jit_solution(11593121128706423300)
XLA Ops:
  2.2 14.1 %collective-permute-start.2 = (bf16[2,64,128]{2,1,0:T(8,128)(2,1)S(1)}, bf16[2,64,128]{2,1,0:T(8,128)(2,1)S(1)}, u32[]{:S(2)}, u32[]{:S(2)}) collective-permute-start(bf16[2,64,128]{2,1,0:T(8,128)(2,1)S(1)} %get-tuple-element.67), channel_id=1, source_target_pairs={{56,87},{57,86},{58,85},{59,84},{60,83},{61,82},{62,81},{63,80},{4... | collective-permute-start | bytes 98312 | tf_op jit(solution)/shard_map/ppermute | solution.py:345
  16.3 1.9 %collective-permute-start.1 = (bf16[2,64,128]{2,1,0:T(8,128)(2,1)S(1)}, bf16[2,64,128]{2,1,0:T(8,128)(2,1)S(1)}, u32[]{:S(2)}, u32[]{:S(2)}) collective-permute-start(bf16[2,64,128]{2,1,0:T(8,128)(2,1)S(1)} %get-tuple-element.68), channel_id=1, source_target_pairs={{0,8},{8,0},{16,24},{24,16},{32,40},{40,32},{48,56},{56,48},{64,72... | collective-permute-start | bytes 98312 | tf_op jit(solution)/shard_map/ppermute | solution.py:344
  18.3 1.0 slice_bitcast_fusion.14
  19.5 4.3 %collective-permute-start.3 = (bf16[3,1,2,64,128]{4,3,2,0,1:T(8,128)(2,1)S(1)}, bf16[3,1,2,64,128]{4,3,2,0,1:T(8,128)(2,1)S(1)}, u32[]{:S(2)}, u32[]{:S(2)}) collective-permute-start(bf16[3,1,2,64,128]{4,3,2,0,1:T(8,128)(2,1)S(1)} %get-tuple-element.63), channel_id=1, source_target_pairs={{0,4},{1,5},{2,6},{3,7},{4,0},{5,1},{6,2},{7,3},{8,12},{9,13},{10,... | collective-permute-start | bytes 294920 | tf_op jit(solution)/shard_map/ppermute | solution.py:350
  24.0 5.3 %collective-permute-done.3 = bf16[3,1,2,64,128]{4,3,2,0,1:T(8,128)(2,1)S(1)} collective-permute-done((bf16[3,1,2,64,128]{4,3,2,0,1:T(8,128)(2,1)S(1)}, bf16[3,1,2,64,128]{4,3,2,0,1:T(8,128)(2,1)S(1)}, u32[]{:S(2)}, u32[]{:S(2)}) %collective-permute-start.3) | collective-permute-done | bytes 98336 | tf_op jit(solution)/shard_map/ppermute | solution.py:350
  29.4 8.5 %collective-permute-start.4 = (bf16[3,2,2,64,128]{4,3,2,1,0:T(8,128)(2,1)S(1)}, bf16[3,2,2,64,128]{4,3,2,1,0:T(8,128)(2,1)S(1)}, u32[]{:S(2)}, u32[]{:S(2)}) collective-permute-start(bf16[3,2,2,64,128]{4,3,2,1,0:T(8,128)(2,1)S(1)} %broadcast_select_fusion.2), channel_id=1, source_target_pairs={{0,2},{1,3},{2,0},{3,1},{4,6},{5,7},{6,4},{7,5},{8,10},{9,11},{10,... | collective-permute-start | bytes 589832 | tf_op jit(solution)/shard_map/ppermute | solution.py:350
  38.0 3.1 %collective-permute-start = (bf16[2,512,128]{2,1,0:T(8,128)(2,1)S(1)}, bf16[2,512,128]{2,1,0:T(8,128)(2,1)S(1)}, u32[]{:S(2)}, u32[]{:S(2)}) collective-permute-start(bf16[2,512,128]{2,1,0:T(8,128)(2,1)S(1)} %maximum_select_fusion), channel_id=1, source_target_pairs={{0,8},{8,0},{16,24},{24,16},{32,40},{40,32},{48,56},{56,48},{64,72... | collective-permute-start | bytes 786440 | tf_op jit(solution)/shard_map/ppermute | solution.py:357
  41.3 3.2 %collective-permute-done.4 = bf16[3,2,2,64,128]{4,3,2,1,0:T(8,128)(2,1)S(1)} collective-permute-done((bf16[3,2,2,64,128]{4,3,2,1,0:T(8,128)(2,1)S(1)}, bf16[3,2,2,64,128]{4,3,2,1,0:T(8,128)(2,1)S(1)}, u32[]{:S(2)}, u32[]{:S(2)}) %collective-permute-start.4) | collective-permute-done | bytes 196640 | tf_op jit(solution)/shard_map/ppermute | solution.py:350
  44.8 1.9 %collective-permute-start.5 = (bf16[3,4,2,64,128]{4,3,2,1,0:T(8,128)(2,1)S(1)}, bf16[3,4,2,64,128]{4,3,2,1,0:T(8,128)(2,1)S(1)}, u32[]{:S(2)}, u32[]{:S(2)}) collective-permute-start(bf16[3,4,2,64,128]{4,3,2,1,0:T(8,128)(2,1)S(1)} %broadcast_select_fusion.1), channel_id=1, source_target_pairs={{0,1},{1,0},{2,3},{3,2},{4,5},{5,4},{6,7},{7,6},{8,9},{9,8},{10,11... | collective-permute-start | bytes 1179656 | tf_op jit(solution)/shard_map/ppermute | solution.py:350
  47.0 1.4 convert_reduce_fusion
  48.6 8.2 %collective-permute-done.5 = bf16[3,4,2,64,128]{4,3,2,1,0:T(8,128)(2,1)S(1)} collective-permute-done((bf16[3,4,2,64,128]{4,3,2,1,0:T(8,128)(2,1)S(1)}, bf16[3,4,2,64,128]{4,3,2,1,0:T(8,128)(2,1)S(1)}, u32[]{:S(2)}, u32[]{:S(2)}) %collective-permute-start.5) | collective-permute-done | bytes 393248 | tf_op jit(solution)/shard_map/ppermute | solution.py:350
  56.9 1.3 collective-permute-start.7
  59.2 6.2 %collective-permute-start.6 = (bf16[8,2,64,128]{3,2,1,0:T(8,128)(2,1)S(1)}, bf16[8,2,64,128]{3,2,1,0:T(8,128)(2,1)S(1)}, u32[]{:S(2)}, u32[]{:S(2)}) collective-permute-start(bf16[8,2,64,128]{3,2,1,0:T(8,128)(2,1)S(1)} %bitcast_select_fusion.2), channel_id=1, source_target_pairs={{0,32},{16,48},{40,8},{56,24},{64,96},{80,112},{104,72},{120,88},{... | collective-permute-start | bytes 786440 | tf_op jit(solution)/shard_map/ppermute | solution.py:369
  65.5 4.5 %own_forward.1 = (f32[1,1024]{1,0:T(1,128)S(1)}, f32[1,1024]{1,0:T(1,128)S(1)}, f32[4,128,256]{2,1,0:T(8,128)S(1)}) custom-call(s32[4]{0:T(128)S(1)} %and_select_fusion.lo_ref, s32[1]{0:T(128)} %bitcast.place_ref, s32[1,1024]{1,0:T(1,128)S(1)} %bitcast.236, bf16[2,512,128]{2,1,0:T(8,128)(2,1)S(1)} %bitcast.231, ...), custom_call_target="tpu_custom_call" | custom-call | flops 201326592 | bytes 4194304 | tf_op jit(solution)/shard_map/own_forward/pallas_call | solution.py:301
  70.1 4.4 %collective-permute-done.6 = bf16[8,2,64,128]{3,2,1,0:T(8,128)(2,1)S(1)} collective-permute-done((bf16[8,2,64,128]{3,2,1,0:T(8,128)(2,1)S(1)}, bf16[8,2,64,128]{3,2,1,0:T(8,128)(2,1)S(1)}, u32[]{:S(2)}, u32[]{:S(2)}) %collective-permute-start.6) | collective-permute-done | bytes 262176 | tf_op jit(solution)/shard_map/ppermute | solution.py:369
  74.8 7.7 %earlier.1 = (bf16[2,512,128]{2,1,0:T(8,128)(2,1)S(1)}, f32[1,1024]{1,0:T(1,128)S(1)}, f32[1,1024]{1,0:T(1,128)S(1)}, f32[4,128,256]{2,1,0:T(8,128)S(1)}, bf16[2...) custom-call(s32[4]{0:T(128)S(1)} %and_select_fusion.lo_ref, s32[1]{0:T(128)} %bitcast.place_ref, ...), custom_call_target="tpu_custom_call" | custom-call | flops 603979776 | bytes 4194304 | tf_op jit(solution)/shard_map/earlier/pallas_call | solution.py:301
  82.4 1.3 collective-permute-start.11
  84.5 4.6 %collective-permute-start.10 = (bf16[8,2,64,128]{3,2,1,0:T(8,128)(2,1)S(1)}, bf16[8,2,64,128]{3,2,1,0:T(8,128)(2,1)S(1)}, u32[]{:S(2)}, u32[]{:S(2)}) collective-permute-start(bf16[8,2,64,128]{3,2,1,0:T(8,128)(2,1)S(1)} %bitcast_select_fusion.1), channel_id=1, source_target_pairs={{32,0},{48,16},{8,40},{24,56},{96,64},{112,80},{72,104},{88,120},{... | collective-permute-start | bytes 786440 | tf_op jit(solution)/shard_map/ppermute | solution.py:425
  89.2 5.9 %own_backward.1 = (bf16[2,512,128]{2,1,0:T(8,128)(2,1)S(1)}, bf16[2,512,128]{2,1,0:T(8,128)(2,1)S(1)}, f32[2,8,2,64,128]{4,3,2,1,0:T(8,128)S(1)}) custom-call(s32[4]{0:T(128)S(1)} %and_select_fusion.lo_ref, s32[1]{0:T(128)} %bitcast.place_ref, s32[1,1024]{1,0:T(1,128)S(1)} %bitcast.238, bf16[2,512,128]{2,1,0:T(8,128)(2,1)S(1)} %bitcast.233, ...), custom_call_target="tpu_custom_call" | custom-call | flops 503316480 | bytes 4194304 | tf_op jit(solution)/shard_map/own_backward/pallas_call | solution.py:301
  95.9 3.2 %collective-permute-start.17 = (bf16[4,2,64,128]{3,2,1,0:T(8,128)(2,1)S(1)}, bf16[4,2,64,128]{3,2,1,0:T(8,128)(2,1)S(1)}, u32[]{:S(2)}, u32[]{:S(2)}) collective-permute-start(bf16[4,2,64,128]{3,2,1,0:T(8,128)(2,1)S(1)} %fusion.16), channel_id=1, source_target_pairs={{0,1},{1,0},{2,3},{3,2},{4,5},{5,4},{6,7},{7,6},{8,9},{9,8},{10,11... | collective-permute-start | bytes 393224 | tf_op jit(solution)/shard_map/ppermute | solution.py:445
  99.2 2.1 %collective-permute-start.12 = (bf16[2,4,2,64,128]{4,3,2,1,0:T(8,128)(2,1)S(1)}, bf16[2,4,2,64,128]{4,3,2,1,0:T(8,128)(2,1)S(1)}, u32[]{:S(2)}, u32[]{:S(2)}) collective-permute-start(bf16[2,4,2,64,128]{4,3,2,1,0:T(8,128)(2,1)S(1)} %fusion.7), channel_id=1, source_target_pairs={{0,1},{1,0},{2,3},{3,2},{4,5},{5,4},{6,7},{7,6},{8,9},{9,8},{10,11... | collective-permute-start | bytes 786440 | tf_op jit(solution)/shard_map/ppermute | solution.py:455
  101.7 5.0 %collective-permute-start.18 = (bf16[2,2,64,128]{3,2,1,0:T(8,128)(2,1)S(1)}, bf16[2,2,64,128]{3,2,1,0:T(8,128)(2,1)S(1)}, u32[]{:S(2)}, u32[]{:S(2)}) collective-permute-start(bf16[2,2,64,128]{3,2,1,0:T(8,128)(2,1)S(1)} %fusion.23), channel_id=1, source_target_pairs={{0,2},{1,3},{2,0},{3,1},{4,6},{5,7},{6,4},{7,5},{8,10},{9,11},{10,... | collective-permute-start | bytes 196616 | tf_op jit(solution)/shard_map/ppermute | solution.py:445
  106.7 4.4 %collective-permute-done.18 = bf16[2,2,64,128]{3,2,1,0:T(8,128)(2,1)S(1)} collective-permute-done((bf16[2,2,64,128]{3,2,1,0:T(8,128)(2,1)S(1)}, bf16[2,2,64,128]{3,2,1,0:T(8,128)(2,1)S(1)}, u32[]{:S(2)}, u32[]{:S(2)}) %collective-permute-start.18) | collective-permute-done | bytes 65568 | tf_op jit(solution)/shard_map/ppermute | solution.py:445
  111.3 1.9 %collective-permute-start.13 = (bf16[2,2,2,64,128]{4,3,2,1,0:T(8,128)(2,1)S(1)}, bf16[2,2,2,64,128]{4,3,2,1,0:T(8,128)(2,1)S(1)}, u32[]{:S(2)}, u32[]{:S(2)}) collective-permute-start(bf16[2,2,2,64,128]{4,3,2,1,0:T(8,128)(2,1)S(1)} %fusion.15), channel_id=1, source_target_pairs={{0,2},{1,3},{2,0},{3,1},{4,6},{5,7},{6,4},{7,5},{8,10},{9,11},{10,... | collective-permute-start | bytes 393224 | tf_op jit(solution)/shard_map/ppermute | solution.py:455
  113.3 3.6 %collective-permute-start.19 = (bf16[1,2,64,128]{3,2,1,0:T(8,128)(2,1)S(1)}, bf16[1,2,64,128]{3,2,1,0:T(8,128)(2,1)S(1)}, u32[]{:S(2)}, u32[]{:S(2)}) collective-permute-start(bf16[1,2,64,128]{3,2,1,0:T(8,128)(2,1)S(1)} %fusion.27), channel_id=1, source_target_pairs={{0,4},{1,5},{2,6},{3,7},{4,0},{5,1},{6,2},{7,3},{8,12},{9,13},{10,... | collective-permute-start | bytes 98312 | tf_op jit(solution)/shard_map/ppermute | solution.py:445
  116.9 6.9 %collective-permute-start.15 = (bf16[2,512,128]{2,1,0:T(8,128)(2,1)S(1)}, bf16[2,512,128]{2,1,0:T(8,128)(2,1)S(1)}, u32[]{:S(2)}, u32[]{:S(2)}) collective-permute-start(bf16[2,512,128]{2,1,0:T(8,128)(2,1)S(1)} %get-tuple-element.40), channel_id=1, source_target_pairs={{0,8},{8,0},{16,24},{24,16},{32,40},{40,32},{48,56},{56,48},{64,72... | collective-permute-start | bytes 786440 | tf_op jit(solution)/shard_map/ppermute | solution.py:458
  123.9 7.5 %collective-permute-start.14 = (bf16[2,1,2,64,128]{4,3,2,0,1:T(8,128)(2,1)S(1)}, bf16[2,1,2,64,128]{4,3,2,0,1:T(8,128)(2,1)S(1)}, u32[]{:S(2)}, u32[]{:S(2)}) collective-permute-start(bf16[2,1,2,64,128]{4,3,2,0,1:T(8,128)(2,1)S(1)} %fusion.24), channel_id=1, source_target_pairs={{0,4},{1,5},{2,6},{3,7},{4,0},{5,1},{6,2},{7,3},{8,12},{9,13},{10,... | collective-permute-start | bytes 196616 | tf_op jit(solution)/shard_map/ppermute | solution.py:455
  131.5 1.9 %collective-permute-start.20 = (bf16[2,64,128]{2,1,0:T(8,128)(2,1)S(1)}, bf16[2,64,128]{2,1,0:T(8,128)(2,1)S(1)}, u32[]{:S(2)}, u32[]{:S(2)}) collective-permute-start(bf16[2,64,128]{2,1,0:T(8,128)(2,1)S(1)} %fusion.29), channel_id=1, source_target_pairs={{87,56},{86,57},{85,58},{84,59},{83,60},{82,61},{81,62},{80,63},{7... | collective-permute-start | bytes 98312 | tf_op jit(solution)/shard_map/ppermute | solution.py:447
  133.4 1.2 collective-permute-done.14
  134.7 2.5 %collective-permute-start.16 = (bf16[2,64,128]{2,1,0:T(8,128)(2,1)S(1)}, bf16[2,64,128]{2,1,0:T(8,128)(2,1)S(1)}, u32[]{:S(2)}, u32[]{:S(2)}) collective-permute-start(bf16[2,64,128]{2,1,0:T(8,128)(2,1)S(1)} %fusion.28), channel_id=1, source_target_pairs={{0,8},{8,0},{16,24},{24,16},{32,40},{40,32},{48,56},{56,48},{64,72... | collective-permute-start | bytes 98312 | tf_op jit(solution)/shard_map/ppermute | solution.py:464
  137.2 0.9 maximum_select_fusion.1
  138.1 7.0 %collective-permute-done.20 = bf16[2,64,128]{2,1,0:T(8,128)(2,1)S(1)} collective-permute-done((bf16[2,64,128]{2,1,0:T(8,128)(2,1)S(1)}, bf16[2,64,128]{2,1,0:T(8,128)(2,1)S(1)}, u32[]{:S(2)}, u32[]{:S(2)}) %collective-permute-start.20) | collective-permute-done | bytes 32800 | tf_op jit(solution)/shard_map/ppermute | solution.py:447
  (76 shorter events, 7.3 us)
Async XLA Ops:
  0.6 37.3 %copy-start.1 = (bf16[1,2,512,128]{3,2,1,0:T(8,128)(2,1)S(1)}, bf16[1,2,512,128]{3,2,1,0:T(8,128)(2,1)}, u32[]{:S(2)}) copy-start(bf16[1,2,512,128]{3,2,1,0:T(8,128)(2,1)} %param.8) | copy-start | bytes 786436
  2.2 17.3 %collective-permute-start.2 = (bf16[2,64,128]{2,1,0:T(8,128)(2,1)S(1)}, bf16[2,64,128]{2,1,0:T(8,128)(2,1)S(1)}, u32[]{:S(2)}, u32[]{:S(2)}) collective-permute-start(bf16[2,64,128]{2,1,0:T(8,128)(2,1)S(1)} %get-tuple-element.67), channel_id=1, source_target_pairs={{56,87},{57,86},{58,85},{59,84},{60,83},{61,82},{62,81},{63,80},{4... | collective-permute-start | bytes 98312 | tf_op jit(solution)/shard_map/ppermute | solution.py:345
  16.3 3.1 %collective-permute-start.1 = (bf16[2,64,128]{2,1,0:T(8,128)(2,1)S(1)}, bf16[2,64,128]{2,1,0:T(8,128)(2,1)S(1)}, u32[]{:S(2)}, u32[]{:S(2)}) collective-permute-start(bf16[2,64,128]{2,1,0:T(8,128)(2,1)S(1)} %get-tuple-element.68), channel_id=1, source_target_pairs={{0,8},{8,0},{16,24},{24,16},{32,40},{40,32},{48,56},{56,48},{64,72... | collective-permute-start | bytes 98312 | tf_op jit(solution)/shard_map/ppermute | solution.py:344
  19.5 9.8 %collective-permute-start.3 = (bf16[3,1,2,64,128]{4,3,2,0,1:T(8,128)(2,1)S(1)}, bf16[3,1,2,64,128]{4,3,2,0,1:T(8,128)(2,1)S(1)}, u32[]{:S(2)}, u32[]{:S(2)}) collective-permute-start(bf16[3,1,2,64,128]{4,3,2,0,1:T(8,128)(2,1)S(1)} %get-tuple-element.63), channel_id=1, source_target_pairs={{0,4},{1,5},{2,6},{3,7},{4,0},{5,1},{6,2},{7,3},{8,12},{9,13},{10,... | collective-permute-start | bytes 294920 | tf_op jit(solution)/shard_map/ppermute | solution.py:350
  29.4 15.1 %collective-permute-start.4 = (bf16[3,2,2,64,128]{4,3,2,1,0:T(8,128)(2,1)S(1)}, bf16[3,2,2,64,128]{4,3,2,1,0:T(8,128)(2,1)S(1)}, u32[]{:S(2)}, u32[]{:S(2)}) collective-permute-start(bf16[3,2,2,64,128]{4,3,2,1,0:T(8,128)(2,1)S(1)} %broadcast_select_fusion.2), channel_id=1, source_target_pairs={{0,2},{1,3},{2,0},{3,1},{4,6},{5,7},{6,4},{7,5},{8,10},{9,11},{10,... | collective-permute-start | bytes 589832 | tf_op jit(solution)/shard_map/ppermute | solution.py:350
  38.0 27.5 %collective-permute-start = (bf16[2,512,128]{2,1,0:T(8,128)(2,1)S(1)}, bf16[2,512,128]{2,1,0:T(8,128)(2,1)S(1)}, u32[]{:S(2)}, u32[]{:S(2)}) collective-permute-start(bf16[2,512,128]{2,1,0:T(8,128)(2,1)S(1)} %maximum_select_fusion), channel_id=1, source_target_pairs={{0,8},{8,0},{16,24},{24,16},{32,40},{40,32},{48,56},{56,48},{64,72... | collective-permute-start | bytes 786440 | tf_op jit(solution)/shard_map/ppermute | solution.py:357
  41.3 5.5 %copy-start.2 = (s32[65536]{0:T(1024)S(1)}, s32[65536]{0:T(1024)}, u32[]{:S(2)}) copy-start(s32[65536]{0:T(1024)} %param.9) | copy-start | bytes 786436
  44.8 12.0 %collective-permute-start.5 = (bf16[3,4,2,64,128]{4,3,2,1,0:T(8,128)(2,1)S(1)}, bf16[3,4,2,64,128]{4,3,2,1,0:T(8,128)(2,1)S(1)}, u32[]{:S(2)}, u32[]{:S(2)}) collective-permute-start(bf16[3,4,2,64,128]{4,3,2,1,0:T(8,128)(2,1)S(1)} %broadcast_select_fusion.1), channel_id=1, source_target_pairs={{0,1},{1,0},{2,3},{3,2},{4,5},{5,4},{6,7},{7,6},{8,9},{9,8},{10,11... | collective-permute-start | bytes 1179656 | tf_op jit(solution)/shard_map/ppermute | solution.py:350
  56.9 13.0 %collective-permute-start.7 = (bf16[2,8,2,64,128]{4,3,2,1,0:T(8,128)(2,1)S(1)}, bf16[2,8,2,64,128]{4,3,2,1,0:T(8,128)(2,1)S(1)}, u32[]{:S(2)}, u32[]{:S(2)}) collective-permute-start(bf16[2,8,2,64,128]{4,3,2,1,0:T(8,128)(2,1)S(1)} %bitcast.228), channel_id=1, source_target_pairs={{0,16},{16,32},{32,48},{24,8},{40,24},{56,40},{64,80},{80,96},{96,... | collective-permute-start | bytes 1572872 | tf_op jit(solution)/shard_map/ppermute | solution.py:370
  58.3 7.2 %copy-start = (bf16[1,2,512,128]{3,2,1,0:T(8,128)(2,1)S(1)}, bf16[1,2,512,128]{3,2,1,0:T(8,128)(2,1)}, u32[]{:S(2)}) copy-start(bf16[1,2,512,128]{3,2,1,0:T(8,128)(2,1)} %param.5) | copy-start | bytes 786436
  58.4 11.7 %collective-permute-start.8 = (bf16[8,2,64,128]{3,2,1,0:T(8,128)(2,1)S(1)}, bf16[8,2,64,128]{3,2,1,0:T(8,128)(2,1)S(1)}, u32[]{:S(2)}, u32[]{:S(2)}) collective-permute-start(bf16[8,2,64,128]{3,2,1,0:T(8,128)(2,1)S(1)} %bitcast.247), channel_id=1, source_target_pairs={{16,0},{40,56},{80,64},{104,120},{144,128},{168,184},{208,192},{23... | collective-permute-start | bytes 786440 | tf_op jit(solution)/shard_map/ppermute | solution.py:371
  59.2 15.3 %collective-permute-start.6 = (bf16[8,2,64,128]{3,2,1,0:T(8,128)(2,1)S(1)}, bf16[8,2,64,128]{3,2,1,0:T(8,128)(2,1)S(1)}, u32[]{:S(2)}, u32[]{:S(2)}) collective-permute-start(bf16[8,2,64,128]{3,2,1,0:T(8,128)(2,1)S(1)} %bitcast_select_fusion.2), channel_id=1, source_target_pairs={{0,32},{16,48},{40,8},{56,24},{64,96},{80,112},{104,72},{120,88},{... | collective-permute-start | bytes 786440 | tf_op jit(solution)/shard_map/ppermute | solution.py:369
  82.4 13.0 %collective-permute-start.11 = (bf16[2,8,2,64,128]{4,3,2,1,0:T(8,128)(2,1)S(1)}, bf16[2,8,2,64,128]{4,3,2,1,0:T(8,128)(2,1)S(1)}, u32[]{:S(2)}, u32[]{:S(2)}) collective-permute-start(bf16[2,8,2,64,128]{4,3,2,1,0:T(8,128)(2,1)S(1)} %get-tuple-element.32), channel_id=1, source_target_pairs={{16,0},{32,16},{48,32},{8,24},{24,40},{40,56},{80,64},{96,80},{112... | collective-permute-start | bytes 1572872 | tf_op jit(solution)/shard_map/ppermute | solution.py:428
  83.8 11.3 %collective-permute-start.9 = (bf16[8,2,64,128]{3,2,1,0:T(8,128)(2,1)S(1)}, bf16[8,2,64,128]{3,2,1,0:T(8,128)(2,1)S(1)}, u32[]{:S(2)}, u32[]{:S(2)}) collective-permute-start(bf16[8,2,64,128]{3,2,1,0:T(8,128)(2,1)S(1)} %slice_bitcast_fusion.6), channel_id=1, source_target_pairs={{0,16},{56,40},{64,80},{120,104},{128,144},{184,168},{192,208},{24... | collective-permute-start | bytes 786440 | tf_op jit(solution)/shard_map/ppermute | solution.py:424
  84.5 10.9 %collective-permute-start.10 = (bf16[8,2,64,128]{3,2,1,0:T(8,128)(2,1)S(1)}, bf16[8,2,64,128]{3,2,1,0:T(8,128)(2,1)S(1)}, u32[]{:S(2)}, u32[]{:S(2)}) collective-permute-start(bf16[8,2,64,128]{3,2,1,0:T(8,128)(2,1)S(1)} %bitcast_select_fusion.1), channel_id=1, source_target_pairs={{32,0},{48,16},{8,40},{24,56},{96,64},{112,80},{72,104},{88,120},{... | collective-permute-start | bytes 786440 | tf_op jit(solution)/shard_map/ppermute | solution.py:425
  95.9 5.7 %collective-permute-start.17 = (bf16[4,2,64,128]{3,2,1,0:T(8,128)(2,1)S(1)}, bf16[4,2,64,128]{3,2,1,0:T(8,128)(2,1)S(1)}, u32[]{:S(2)}, u32[]{:S(2)}) collective-permute-start(bf16[4,2,64,128]{3,2,1,0:T(8,128)(2,1)S(1)} %fusion.16), channel_id=1, source_target_pairs={{0,1},{1,0},{2,3},{3,2},{4,5},{5,4},{6,7},{7,6},{8,9},{9,8},{10,11... | collective-permute-start | bytes 393224 | tf_op jit(solution)/shard_map/ppermute | solution.py:445
  99.2 12.0 %collective-permute-start.12 = (bf16[2,4,2,64,128]{4,3,2,1,0:T(8,128)(2,1)S(1)}, bf16[2,4,2,64,128]{4,3,2,1,0:T(8,128)(2,1)S(1)}, u32[]{:S(2)}, u32[]{:S(2)}) collective-permute-start(bf16[2,4,2,64,128]{4,3,2,1,0:T(8,128)(2,1)S(1)} %fusion.7), channel_id=1, source_target_pairs={{0,1},{1,0},{2,3},{3,2},{4,5},{5,4},{6,7},{7,6},{8,9},{9,8},{10,11... | collective-permute-start | bytes 786440 | tf_op jit(solution)/shard_map/ppermute | solution.py:455
  101.7 9.4 %collective-permute-start.18 = (bf16[2,2,64,128]{3,2,1,0:T(8,128)(2,1)S(1)}, bf16[2,2,64,128]{3,2,1,0:T(8,128)(2,1)S(1)}, u32[]{:S(2)}, u32[]{:S(2)}) collective-permute-start(bf16[2,2,64,128]{3,2,1,0:T(8,128)(2,1)S(1)} %fusion.23), channel_id=1, source_target_pairs={{0,2},{1,3},{2,0},{3,1},{4,6},{5,7},{6,4},{7,5},{8,10},{9,11},{10,... | collective-permute-start | bytes 196616 | tf_op jit(solution)/shard_map/ppermute | solution.py:445
  111.3 12.5 %collective-permute-start.13 = (bf16[2,2,2,64,128]{4,3,2,1,0:T(8,128)(2,1)S(1)}, bf16[2,2,2,64,128]{4,3,2,1,0:T(8,128)(2,1)S(1)}, u32[]{:S(2)}, u32[]{:S(2)}) collective-permute-start(bf16[2,2,2,64,128]{4,3,2,1,0:T(8,128)(2,1)S(1)} %fusion.15), channel_id=1, source_target_pairs={{0,2},{1,3},{2,0},{3,1},{4,6},{5,7},{6,4},{7,5},{8,10},{9,11},{10,... | collective-permute-start | bytes 393224 | tf_op jit(solution)/shard_map/ppermute | solution.py:455
  113.3 18.2 %collective-permute-start.19 = (bf16[1,2,64,128]{3,2,1,0:T(8,128)(2,1)S(1)}, bf16[1,2,64,128]{3,2,1,0:T(8,128)(2,1)S(1)}, u32[]{:S(2)}, u32[]{:S(2)}) collective-permute-start(bf16[1,2,64,128]{3,2,1,0:T(8,128)(2,1)S(1)} %fusion.27), channel_id=1, source_target_pairs={{0,4},{1,5},{2,6},{3,7},{4,0},{5,1},{6,2},{7,3},{8,12},{9,13},{10,... | collective-permute-start | bytes 98312 | tf_op jit(solution)/shard_map/ppermute | solution.py:445
  116.9 17.8 %collective-permute-start.15 = (bf16[2,512,128]{2,1,0:T(8,128)(2,1)S(1)}, bf16[2,512,128]{2,1,0:T(8,128)(2,1)S(1)}, u32[]{:S(2)}, u32[]{:S(2)}) collective-permute-start(bf16[2,512,128]{2,1,0:T(8,128)(2,1)S(1)} %get-tuple-element.40), channel_id=1, source_target_pairs={{0,8},{8,0},{16,24},{24,16},{32,40},{40,32},{48,56},{56,48},{64,72... | collective-permute-start | bytes 786440 | tf_op jit(solution)/shard_map/ppermute | solution.py:458
  123.9 10.8 %collective-permute-start.14 = (bf16[2,1,2,64,128]{4,3,2,0,1:T(8,128)(2,1)S(1)}, bf16[2,1,2,64,128]{4,3,2,0,1:T(8,128)(2,1)S(1)}, u32[]{:S(2)}, u32[]{:S(2)}) collective-permute-start(bf16[2,1,2,64,128]{4,3,2,0,1:T(8,128)(2,1)S(1)} %fusion.24), channel_id=1, source_target_pairs={{0,4},{1,5},{2,6},{3,7},{4,0},{5,1},{6,2},{7,3},{8,12},{9,13},{10,... | collective-permute-start | bytes 196616 | tf_op jit(solution)/shard_map/ppermute | solution.py:455
  131.5 13.6 %collective-permute-start.20 = (bf16[2,64,128]{2,1,0:T(8,128)(2,1)S(1)}, bf16[2,64,128]{2,1,0:T(8,128)(2,1)S(1)}, u32[]{:S(2)}, u32[]{:S(2)}) collective-permute-start(bf16[2,64,128]{2,1,0:T(8,128)(2,1)S(1)} %fusion.29), channel_id=1, source_target_pairs={{87,56},{86,57},{85,58},{84,59},{83,60},{82,61},{81,62},{80,63},{7... | collective-permute-start | bytes 98312 | tf_op jit(solution)/shard_map/ppermute | solution.py:447
  134.7 10.4 %collective-permute-start.16 = (bf16[2,64,128]{2,1,0:T(8,128)(2,1)S(1)}, bf16[2,64,128]{2,1,0:T(8,128)(2,1)S(1)}, u32[]{:S(2)}, u32[]{:S(2)}) collective-permute-start(bf16[2,64,128]{2,1,0:T(8,128)(2,1)S(1)} %fusion.28), channel_id=1, source_target_pairs={{0,8},{8,0},{16,24},{24,16},{32,40},{40,32},{48,56},{56,48},{64,72... | collective-permute-start | bytes 98312 | tf_op jit(solution)/shard_map/ppermute | solution.py:464

commit v13 on v11

--- a/solution.py
+++ b/solution.py
@@ -120,7 +120,8 @@
 
 
 def own_forward_kernel(
-    lo_ref, place_ref, start_row, queries, far, kv_own, top_row, total_row, acc_out,
+    lo_ref, place_ref, start_row, queries, out_grad, far, kv_own, top_row, total_row, acc_out,
+    grad_out,
     keys, values, values_t, scores,
 ):
     tile, tiles = scores.shape[1], scores.shape[0]
@@ -157,10 +158,11 @@
         top_row[:, columns] = top
         total_row[:, columns] = total
         acc_out[i] = acc
+        grad_out[i] = query_tile(out_grad, far, 1, core, i, tile).T
 
 
 def earlier_kernel(
-    lo_ref, place_ref, start_row, queries, out_grad, far, top_row, total_row, acc_in, kv_prev,
+    lo_ref, place_ref, start_row, queries, out_grad, far, top_row, total_row, acc_in, grad_t, kv_prev,
     attended_out, lse_row, delta_row, acc_out, p_near, p_next,
     keys_t, values_t, scores, key_acc, value_acc,
 ):
@@ -210,7 +212,7 @@
         )
         inv = 1.0 / total
         attended_t = (acc * inv).astype(bf16).astype(f32)
-        delta = column_sum(grad.astype(f32).T * attended_t)
+        delta = column_sum(grad_t[i].astype(f32) * attended_t)
         half, part = divmod(i, tiles // 2)
         attended_out[half, pl.ds(part * tile, tile)] = attended_t.T.astype(bf16)
         lse_row[:, columns] = top + jnp.log2(total)
@@ -399,11 +401,11 @@
     part = jax.ShapeDtypeStruct((2, width, head_dim), bf16)
     span_like = kv_next.shape
     natural = ((tiles, tile, head_dim), bf16)
-    top, total, acc = vmem_kernel(
-        own_forward_kernel, "own_forward", (row, row, turned),
+    top, total, acc, grad_t = vmem_kernel(
+        own_forward_kernel, "own_forward", (row, row, turned, jax.ShapeDtypeStruct(turned.shape, bf16)),
         [natural, natural, ((tiles, head_dim, tile), bf16), ((tiles, tile, tile), f32)],
         6, tile, head_dim, 2,
-    )(lo, places, start, queries, far, kv_own)
+    )(lo, places, start, queries, out_grad, far, kv_own)
     attended, lse, delta, acc, p_near, p_next = vmem_kernel(
         earlier_kernel, "earlier",
         (
@@ -419,7 +421,7 @@
             ((earlier * tile, head_dim), f32),
         ],
         6, tile, head_dim, 6,
-    )(lo, places, start, queries, out_grad, far, top, total, acc, kv_prev)
+    )(lo, places, start, queries, out_grad, far, top, total, acc, grad_t, kv_prev)
 
     r_edge1 = lax.ppermute(p_near[1], CTX, inverse(edge1))
     r_edge2 = lax.ppermute(p_near[0], CTX, inverse(edge2))

time: 147 us -> 147 us (level)
  the two profiles are of different devices: /device:TPU:76 before, /device:TPU:74 now
where the time goes in v13:
time: 147 us
  starting transfers between devices  78.9 us (54%)
  waiting for transfers between devices  43.3 us (29%)
  Pallas kernels  15.1 us (10%)
  other arithmetic  4.83 us (3%)
  local copies, waits for them, and re-layouts  3.44 us (2%)
    ppermute x3, waiting for transfers between devices, body(): other = lax.ppermute(kv_all, everywhere, head_pairs(ctx, heads, bit))  19.7 us
    ppermute x3, starting transfers between devices, body(): other = lax.ppermute(kv_all, everywhere, head_pairs(ctx, heads, bit))  15.3 us
    ppermute x3, starting transfers between devices, body(): other = lax.ppermute(away, everywhere, head_pairs(ctx, heads, bit))  15.3 us
    pallas_call x3, Pallas kernels, call(): pl.pallas_call(kernel, out_shape=outputs, in_specs=[pl.BlockSpec(memory_s...  15.1 us
    ppermute x1, starting transfers between devices, body(): crossed = lax.ppermute(leaving, everywhere, edge)  12.5 us
    ppermute x1, waiting for transfers between devices, body(): r_next = lax.ppermute(p_next, CTX, inverse(far_chip))  11.1 us
    ppermute x3, starting transfers between devices, body(): other = lax.ppermute(away, everywhere, holder_pairs(ctx, heads, bit))  10.5 us
    ppermute x1, waiting for transfers between devices, body(): lax.ppermute(edge_sum[0].astype(bf16), everywhere, inverse(edge))  7.09 us
  transfers between devices with their start and end apart: 22, of which 10 were waited for; matrix products, arithmetic and copies ran while one was open for 4% of the time, Pallas kernels for 6%

profile of v13, /device:TPU:74, one launch (start us, length us, event | category | flops | bytes accessed | tf_op | source)
XLA Modules:
  0.0 146.7 jit_solution(18197002466039832418)
XLA Ops:
  2.2 12.5 %collective-permute-start.2 = (bf16[2,64,128]{2,1,0:T(8,128)(2,1)S(1)}, bf16[2,64,128]{2,1,0:T(8,128)(2,1)S(1)}, u32[]{:S(2)}, u32[]{:S(2)}) collective-permute-start(bf16[2,64,128]{2,1,0:T(8,128)(2,1)S(1)} %get-tuple-element.72), channel_id=1, source_target_pairs={{56,87},{57,86},{58,85},{59,84},{60,83},{61,82},{62,81},{63,80},{4... | collective-permute-start | bytes 98312 | tf_op jit(solution)/shard_map/ppermute | solution.py:347
  14.7 1.9 %collective-permute-start.1 = (bf16[2,64,128]{2,1,0:T(8,128)(2,1)S(1)}, bf16[2,64,128]{2,1,0:T(8,128)(2,1)S(1)}, u32[]{:S(2)}, u32[]{:S(2)}) collective-permute-start(bf16[2,64,128]{2,1,0:T(8,128)(2,1)S(1)} %get-tuple-element.73), channel_id=1, source_target_pairs={{0,8},{8,0},{16,24},{24,16},{32,40},{40,32},{48,56},{56,48},{64,72... | collective-permute-start | bytes 98312 | tf_op jit(solution)/shard_map/ppermute | solution.py:346
  17.9 5.9 %collective-permute-start.3 = (bf16[3,1,2,64,128]{4,3,2,0,1:T(8,128)(2,1)S(1)}, bf16[3,1,2,64,128]{4,3,2,0,1:T(8,128)(2,1)S(1)}, u32[]{:S(2)}, u32[]{:S(2)}) collective-permute-start(bf16[3,1,2,64,128]{4,3,2,0,1:T(8,128)(2,1)S(1)} %get-tuple-element.68), channel_id=1, source_target_pairs={{0,4},{1,5},{2,6},{3,7},{4,0},{5,1},{6,2},{7,3},{8,12},{9,13},{10,... | collective-permute-start | bytes 294920 | tf_op jit(solution)/shard_map/ppermute | solution.py:352
  24.0 7.1 %collective-permute-done.3 = bf16[3,1,2,64,128]{4,3,2,0,1:T(8,128)(2,1)S(1)} collective-permute-done((bf16[3,1,2,64,128]{4,3,2,0,1:T(8,128)(2,1)S(1)}, bf16[3,1,2,64,128]{4,3,2,0,1:T(8,128)(2,1)S(1)}, u32[]{:S(2)}, u32[]{:S(2)}) %collective-permute-start.3) | collective-permute-done | bytes 98336 | tf_op jit(solution)/shard_map/ppermute | solution.py:352
  31.2 6.2 %collective-permute-start.4 = (bf16[3,2,2,64,128]{4,3,2,1,0:T(8,128)(2,1)S(1)}, bf16[3,2,2,64,128]{4,3,2,1,0:T(8,128)(2,1)S(1)}, u32[]{:S(2)}, u32[]{:S(2)}) collective-permute-start(bf16[3,2,2,64,128]{4,3,2,1,0:T(8,128)(2,1)S(1)} %broadcast_select_fusion.2), channel_id=1, source_target_pairs={{0,2},{1,3},{2,0},{3,1},{4,6},{5,7},{6,4},{7,5},{8,10},{9,11},{10,... | collective-permute-start | bytes 589832 | tf_op jit(solution)/shard_map/ppermute | solution.py:352
  37.5 1.9 %collective-permute-start = (bf16[2,512,128]{2,1,0:T(8,128)(2,1)S(1)}, bf16[2,512,128]{2,1,0:T(8,128)(2,1)S(1)}, u32[]{:S(2)}, u32[]{:S(2)}) collective-permute-start(bf16[2,512,128]{2,1,0:T(8,128)(2,1)S(1)} %maximum_select_fusion), channel_id=1, source_target_pairs={{0,8},{8,0},{16,24},{24,16},{32,40},{40,32},{48,56},{56,48},{64,72... | collective-permute-start | bytes 786440 | tf_op jit(solution)/shard_map/ppermute | solution.py:359
  39.6 4.7 %collective-permute-done.4 = bf16[3,2,2,64,128]{4,3,2,1,0:T(8,128)(2,1)S(1)} collective-permute-done((bf16[3,2,2,64,128]{4,3,2,1,0:T(8,128)(2,1)S(1)}, bf16[3,2,2,64,128]{4,3,2,1,0:T(8,128)(2,1)S(1)}, u32[]{:S(2)}, u32[]{:S(2)}) %collective-permute-start.4) | collective-permute-done | bytes 196640 | tf_op jit(solution)/shard_map/ppermute | solution.py:352
  44.6 3.2 %collective-permute-start.5 = (bf16[3,4,2,64,128]{4,3,2,1,0:T(8,128)(2,1)S(1)}, bf16[3,4,2,64,128]{4,3,2,1,0:T(8,128)(2,1)S(1)}, u32[]{:S(2)}, u32[]{:S(2)}) collective-permute-start(bf16[3,4,2,64,128]{4,3,2,1,0:T(8,128)(2,1)S(1)} %broadcast_select_fusion.1), channel_id=1, source_target_pairs={{0,1},{1,0},{2,3},{3,2},{4,5},{5,4},{6,7},{7,6},{8,9},{9,8},{10,11... | collective-permute-start | bytes 1179656 | tf_op jit(solution)/shard_map/ppermute | solution.py:352
  48.1 1.4 convert_reduce_fusion
  49.7 7.9 %collective-permute-done.5 = bf16[3,4,2,64,128]{4,3,2,1,0:T(8,128)(2,1)S(1)} collective-permute-done((bf16[3,4,2,64,128]{4,3,2,1,0:T(8,128)(2,1)S(1)}, bf16[3,4,2,64,128]{4,3,2,1,0:T(8,128)(2,1)S(1)}, u32[]{:S(2)}, u32[]{:S(2)}) %collective-permute-start.5) | collective-permute-done | bytes 393248 | tf_op jit(solution)/shard_map/ppermute | solution.py:352
  57.7 2.4 %collective-permute-start.7 = (bf16[2,8,2,64,128]{4,3,2,1,0:T(8,128)(2,1)S(1)}, bf16[2,8,2,64,128]{4,3,2,1,0:T(8,128)(2,1)S(1)}, u32[]{:S(2)}, u32[]{:S(2)}) collective-permute-start(bf16[2,8,2,64,128]{4,3,2,1,0:T(8,128)(2,1)S(1)} %bitcast.228), channel_id=1, source_target_pairs={{0,16},{16,32},{32,48},{24,8},{40,24},{56,40},{64,80},{80,96},{96,... | collective-permute-start | bytes 1572872 | tf_op jit(solution)/shard_map/ppermute | solution.py:372
  60.2 3.6 %collective-permute-start.8 = (bf16[8,2,64,128]{3,2,1,0:T(8,128)(2,1)S(1)}, bf16[8,2,64,128]{3,2,1,0:T(8,128)(2,1)S(1)}, u32[]{:S(2)}, u32[]{:S(2)}) collective-permute-start(bf16[8,2,64,128]{3,2,1,0:T(8,128)(2,1)S(1)} %bitcast.248), channel_id=1, source_target_pairs={{16,0},{40,56},{80,64},{104,120},{144,128},{168,184},{208,192},{23... | collective-permute-start | bytes 786440 | tf_op jit(solution)/shard_map/ppermute | solution.py:373
  63.9 1.3 collective-permute-start.6
  65.3 3.7 %own_forward.1 = (f32[1,1024]{1,0:T(1,128)S(1)}, f32[1,1024]{1,0:T(1,128)S(1)}, f32[4,128,256]{2,1,0:T(8,128)S(1)}, bf16[4,128,256]{2,1,0:T(8,128)(2,1)S(1)}) custom-call(s32[4]{0:T(128)S(1)} %and_select_fusion.lo_ref, s32[1]{0:T(128)} %bitcast.place_ref, s32[1,1024]{1,0:T(1,128)S(1)} %bitcast.237, bf16[2,512,128]{2,1,0:T(8,128)(2,1)S(1)} %bitcast.231, ...), custom_call_target="tpu_custom_call" | custom-call | flops 201326592 | bytes 4194304 | tf_op jit(solution)/shard_map/own_forward/pallas_call | solution.py:303
  69.2 1.4 collective-permute-done.6
  70.7 6.5 %earlier.1 = (bf16[2,512,128]{2,1,0:T(8,128)(2,1)S(1)}, f32[1,1024]{1,0:T(1,128)S(1)}, f32[1,1024]{1,0:T(1,128)S(1)}, f32[4,128,256]{2,1,0:T(8,128)S(1)}, bf16[2...) custom-call(s32[4]{0:T(128)S(1)} %and_select_fusion.lo_ref, s32[1]{0:T(128)} %bitcast.place_ref, ...), custom_call_target="tpu_custom_call" | custom-call | flops 603979776 | bytes 4194304 | tf_op jit(solution)/shard_map/earlier/pallas_call | solution.py:303
  77.2 3.7 %collective-permute-start.12 = (bf16[2,8,2,64,128]{4,3,2,1,0:T(8,128)(2,1)S(1)}, bf16[2,8,2,64,128]{4,3,2,1,0:T(8,128)(2,1)S(1)}, u32[]{:S(2)}, u32[]{:S(2)}) collective-permute-start(bf16[2,8,2,64,128]{4,3,2,1,0:T(8,128)(2,1)S(1)} %get-tuple-element.35), channel_id=1, source_target_pairs={{16,0},{32,16},{48,32},{8,24},{24,40},{40,56},{80,64},{96,80},{112... | collective-permute-start | bytes 1572872 | tf_op jit(solution)/shard_map/ppermute | solution.py:429
  80.9 1.3 collective-permute-start.11
  84.3 4.8 %own_backward.1 = (bf16[2,512,128]{2,1,0:T(8,128)(2,1)S(1)}, bf16[2,512,128]{2,1,0:T(8,128)(2,1)S(1)}, f32[2,8,2,64,128]{4,3,2,1,0:T(8,128)S(1)}) custom-call(s32[4]{0:T(128)S(1)} %and_select_fusion.lo_ref, s32[1]{0:T(128)} %bitcast.place_ref, s32[1,1024]{1,0:T(1,128)S(1)} %bitcast.239, bf16[2,512,128]{2,1,0:T(8,128)(2,1)S(1)} %bitcast.233, ...), custom_call_target="tpu_custom_call" | custom-call | flops 503316480 | bytes 4194304 | tf_op jit(solution)/shard_map/own_backward/pallas_call | solution.py:303
  89.1 11.1 %collective-permute-done.11 = bf16[8,2,64,128]{3,2,1,0:T(8,128)(2,1)S(1)} collective-permute-done((bf16[8,2,64,128]{3,2,1,0:T(8,128)(2,1)S(1)}, bf16[8,2,64,128]{3,2,1,0:T(8,128)(2,1)S(1)}, u32[]{:S(2)}, u32[]{:S(2)}) %collective-permute-start.11) | collective-permute-done | bytes 262176 | tf_op jit(solution)/shard_map/ppermute | solution.py:428
  100.4 2.7 %collective-permute-start.18 = (bf16[4,2,64,128]{3,2,1,0:T(8,128)(2,1)S(1)}, bf16[4,2,64,128]{3,2,1,0:T(8,128)(2,1)S(1)}, u32[]{:S(2)}, u32[]{:S(2)}) collective-permute-start(bf16[4,2,64,128]{3,2,1,0:T(8,128)(2,1)S(1)} %fusion.15), channel_id=1, source_target_pairs={{0,1},{1,0},{2,3},{3,2},{4,5},{5,4},{6,7},{7,6},{8,9},{9,8},{10,11... | collective-permute-start | bytes 393224 | tf_op jit(solution)/shard_map/ppermute | solution.py:447
  103.4 3.2 %collective-permute-start.13 = (bf16[2,4,2,64,128]{4,3,2,1,0:T(8,128)(2,1)S(1)}, bf16[2,4,2,64,128]{4,3,2,1,0:T(8,128)(2,1)S(1)}, u32[]{:S(2)}, u32[]{:S(2)}) collective-permute-start(bf16[2,4,2,64,128]{4,3,2,1,0:T(8,128)(2,1)S(1)} %fusion.6), channel_id=1, source_target_pairs={{0,1},{1,0},{2,3},{3,2},{4,5},{5,4},{6,7},{7,6},{8,9},{9,8},{10,11... | collective-permute-start | bytes 786440 | tf_op jit(solution)/shard_map/ppermute | solution.py:457
  106.6 1.4 collective-permute-done.18
  108.1 5.3 %collective-permute-start.19 = (bf16[2,2,64,128]{3,2,1,0:T(8,128)(2,1)S(1)}, bf16[2,2,64,128]{3,2,1,0:T(8,128)(2,1)S(1)}, u32[]{:S(2)}, u32[]{:S(2)}) collective-permute-start(bf16[2,2,64,128]{3,2,1,0:T(8,128)(2,1)S(1)} %fusion.22), channel_id=1, source_target_pairs={{0,2},{1,3},{2,0},{3,1},{4,6},{5,7},{6,4},{7,5},{8,10},{9,11},{10,... | collective-permute-start | bytes 196616 | tf_op jit(solution)/shard_map/ppermute | solution.py:447
  113.5 2.2 %collective-permute-done.19 = bf16[2,2,64,128]{3,2,1,0:T(8,128)(2,1)S(1)} collective-permute-done((bf16[2,2,64,128]{3,2,1,0:T(8,128)(2,1)S(1)}, bf16[2,2,64,128]{3,2,1,0:T(8,128)(2,1)S(1)}, u32[]{:S(2)}, u32[]{:S(2)}) %collective-permute-start.19) | collective-permute-done | bytes 65568 | tf_op jit(solution)/shard_map/ppermute | solution.py:447
  115.8 4.8 %collective-permute-start.14 = (bf16[2,2,2,64,128]{4,3,2,1,0:T(8,128)(2,1)S(1)}, bf16[2,2,2,64,128]{4,3,2,1,0:T(8,128)(2,1)S(1)}, u32[]{:S(2)}, u32[]{:S(2)}) collective-permute-start(bf16[2,2,2,64,128]{4,3,2,1,0:T(8,128)(2,1)S(1)} %fusion.14), channel_id=1, source_target_pairs={{0,2},{1,3},{2,0},{3,1},{4,6},{5,7},{6,4},{7,5},{8,10},{9,11},{10,... | collective-permute-start | bytes 393224 | tf_op jit(solution)/shard_map/ppermute | solution.py:457
  120.7 2.5 %collective-permute-start.20 = (bf16[1,2,64,128]{3,2,1,0:T(8,128)(2,1)S(1)}, bf16[1,2,64,128]{3,2,1,0:T(8,128)(2,1)S(1)}, u32[]{:S(2)}, u32[]{:S(2)}) collective-permute-start(bf16[1,2,64,128]{3,2,1,0:T(8,128)(2,1)S(1)} %fusion.26), channel_id=1, source_target_pairs={{0,4},{1,5},{2,6},{3,7},{4,0},{5,1},{6,2},{7,3},{8,12},{9,13},{10,... | collective-permute-start | bytes 98312 | tf_op jit(solution)/shard_map/ppermute | solution.py:447
  123.2 1.9 %collective-permute-start.16 = (bf16[2,512,128]{2,1,0:T(8,128)(2,1)S(1)}, bf16[2,512,128]{2,1,0:T(8,128)(2,1)S(1)}, u32[]{:S(2)}, u32[]{:S(2)}) collective-permute-start(bf16[2,512,128]{2,1,0:T(8,128)(2,1)S(1)} %get-tuple-element.43), channel_id=1, source_target_pairs={{0,8},{8,0},{16,24},{24,16},{32,40},{40,32},{48,56},{56,48},{64,72... | collective-permute-start | bytes 786440 | tf_op jit(solution)/shard_map/ppermute | solution.py:460
  125.2 7.3 %collective-permute-start.15 = (bf16[2,1,2,64,128]{4,3,2,0,1:T(8,128)(2,1)S(1)}, bf16[2,1,2,64,128]{4,3,2,0,1:T(8,128)(2,1)S(1)}, u32[]{:S(2)}, u32[]{:S(2)}) collective-permute-start(bf16[2,1,2,64,128]{4,3,2,0,1:T(8,128)(2,1)S(1)} %fusion.23), channel_id=1, source_target_pairs={{0,4},{1,5},{2,6},{3,7},{4,0},{5,1},{6,2},{7,3},{8,12},{9,13},{10,... | collective-permute-start | bytes 196616 | tf_op jit(solution)/shard_map/ppermute | solution.py:457
  132.5 3.3 %collective-permute-start.21 = (bf16[2,64,128]{2,1,0:T(8,128)(2,1)S(1)}, bf16[2,64,128]{2,1,0:T(8,128)(2,1)S(1)}, u32[]{:S(2)}, u32[]{:S(2)}) collective-permute-start(bf16[2,64,128]{2,1,0:T(8,128)(2,1)S(1)} %fusion.28), channel_id=1, source_target_pairs={{87,56},{86,57},{85,58},{84,59},{83,60},{82,61},{81,62},{80,63},{7... | collective-permute-start | bytes 98312 | tf_op jit(solution)/shard_map/ppermute | solution.py:449
  136.2 1.9 %collective-permute-start.17 = (bf16[2,64,128]{2,1,0:T(8,128)(2,1)S(1)}, bf16[2,64,128]{2,1,0:T(8,128)(2,1)S(1)}, u32[]{:S(2)}, u32[]{:S(2)}) collective-permute-start(bf16[2,64,128]{2,1,0:T(8,128)(2,1)S(1)} %fusion.27), channel_id=1, source_target_pairs={{0,8},{8,0},{16,24},{24,16},{32,40},{40,32},{48,56},{56,48},{64,72... | collective-permute-start | bytes 98312 | tf_op jit(solution)/shard_map/ppermute | solution.py:466
  139.0 7.1 %collective-permute-done.21 = bf16[2,64,128]{2,1,0:T(8,128)(2,1)S(1)} collective-permute-done((bf16[2,64,128]{2,1,0:T(8,128)(2,1)S(1)}, bf16[2,64,128]{2,1,0:T(8,128)(2,1)S(1)}, u32[]{:S(2)}, u32[]{:S(2)}) %collective-permute-start.21) | collective-permute-done | bytes 32800 | tf_op jit(solution)/shard_map/ppermute | solution.py:449
  (78 shorter events, 9.2 us)
Async XLA Ops:
  0.6 36.8 %copy-start.1 = (bf16[1,2,512,128]{3,2,1,0:T(8,128)(2,1)S(1)}, bf16[1,2,512,128]{3,2,1,0:T(8,128)(2,1)}, u32[]{:S(2)}) copy-start(bf16[1,2,512,128]{3,2,1,0:T(8,128)(2,1)} %param.8) | copy-start | bytes 786436
  2.2 15.7 %collective-permute-start.2 = (bf16[2,64,128]{2,1,0:T(8,128)(2,1)S(1)}, bf16[2,64,128]{2,1,0:T(8,128)(2,1)S(1)}, u32[]{:S(2)}, u32[]{:S(2)}) collective-permute-start(bf16[2,64,128]{2,1,0:T(8,128)(2,1)S(1)} %get-tuple-element.72), channel_id=1, source_target_pairs={{56,87},{57,86},{58,85},{59,84},{60,83},{61,82},{62,81},{63,80},{4... | collective-permute-start | bytes 98312 | tf_op jit(solution)/shard_map/ppermute | solution.py:347
  14.7 3.1 %collective-permute-start.1 = (bf16[2,64,128]{2,1,0:T(8,128)(2,1)S(1)}, bf16[2,64,128]{2,1,0:T(8,128)(2,1)S(1)}, u32[]{:S(2)}, u32[]{:S(2)}) collective-permute-start(bf16[2,64,128]{2,1,0:T(8,128)(2,1)S(1)} %get-tuple-element.73), channel_id=1, source_target_pairs={{0,8},{8,0},{16,24},{24,16},{32,40},{40,32},{48,56},{56,48},{64,72... | collective-permute-start | bytes 98312 | tf_op jit(solution)/shard_map/ppermute | solution.py:346
  17.9 13.2 %collective-permute-start.3 = (bf16[3,1,2,64,128]{4,3,2,0,1:T(8,128)(2,1)S(1)}, bf16[3,1,2,64,128]{4,3,2,0,1:T(8,128)(2,1)S(1)}, u32[]{:S(2)}, u32[]{:S(2)}) collective-permute-start(bf16[3,1,2,64,128]{4,3,2,0,1:T(8,128)(2,1)S(1)} %get-tuple-element.68), channel_id=1, source_target_pairs={{0,4},{1,5},{2,6},{3,7},{4,0},{5,1},{6,2},{7,3},{8,12},{9,13},{10,... | collective-permute-start | bytes 294920 | tf_op jit(solution)/shard_map/ppermute | solution.py:352
  31.2 13.1 %collective-permute-start.4 = (bf16[3,2,2,64,128]{4,3,2,1,0:T(8,128)(2,1)S(1)}, bf16[3,2,2,64,128]{4,3,2,1,0:T(8,128)(2,1)S(1)}, u32[]{:S(2)}, u32[]{:S(2)}) collective-permute-start(bf16[3,2,2,64,128]{4,3,2,1,0:T(8,128)(2,1)S(1)} %broadcast_select_fusion.2), channel_id=1, source_target_pairs={{0,2},{1,3},{2,0},{3,1},{4,6},{5,7},{6,4},{7,5},{8,10},{9,11},{10,... | collective-permute-start | bytes 589832 | tf_op jit(solution)/shard_map/ppermute | solution.py:352
  37.5 27.7 %collective-permute-start = (bf16[2,512,128]{2,1,0:T(8,128)(2,1)S(1)}, bf16[2,512,128]{2,1,0:T(8,128)(2,1)S(1)}, u32[]{:S(2)}, u32[]{:S(2)}) collective-permute-start(bf16[2,512,128]{2,1,0:T(8,128)(2,1)S(1)} %maximum_select_fusion), channel_id=1, source_target_pairs={{0,8},{8,0},{16,24},{24,16},{32,40},{40,32},{48,56},{56,48},{64,72... | collective-permute-start | bytes 786440 | tf_op jit(solution)/shard_map/ppermute | solution.py:359
  39.6 8.2 %copy-start.2 = (s32[65536]{0:T(1024)S(1)}, s32[65536]{0:T(1024)}, u32[]{:S(2)}) copy-start(s32[65536]{0:T(1024)} %param.9) | copy-start | bytes 786436
  44.6 12.9 %collective-permute-start.5 = (bf16[3,4,2,64,128]{4,3,2,1,0:T(8,128)(2,1)S(1)}, bf16[3,4,2,64,128]{4,3,2,1,0:T(8,128)(2,1)S(1)}, u32[]{:S(2)}, u32[]{:S(2)}) collective-permute-start(bf16[3,4,2,64,128]{4,3,2,1,0:T(8,128)(2,1)S(1)} %broadcast_select_fusion.1), channel_id=1, source_target_pairs={{0,1},{1,0},{2,3},{3,2},{4,5},{5,4},{6,7},{7,6},{8,9},{9,8},{10,11... | collective-permute-start | bytes 1179656 | tf_op jit(solution)/shard_map/ppermute | solution.py:352
  57.7 11.3 %collective-permute-start.7 = (bf16[2,8,2,64,128]{4,3,2,1,0:T(8,128)(2,1)S(1)}, bf16[2,8,2,64,128]{4,3,2,1,0:T(8,128)(2,1)S(1)}, u32[]{:S(2)}, u32[]{:S(2)}) collective-permute-start(bf16[2,8,2,64,128]{4,3,2,1,0:T(8,128)(2,1)S(1)} %bitcast.228), channel_id=1, source_target_pairs={{0,16},{16,32},{32,48},{24,8},{40,24},{56,40},{64,80},{80,96},{96,... | collective-permute-start | bytes 1572872 | tf_op jit(solution)/shard_map/ppermute | solution.py:372
  60.2 5.1 %copy-start = (bf16[1,2,512,128]{3,2,1,0:T(8,128)(2,1)S(1)}, bf16[1,2,512,128]{3,2,1,0:T(8,128)(2,1)}, u32[]{:S(2)}) copy-start(bf16[1,2,512,128]{3,2,1,0:T(8,128)(2,1)} %param.5) | copy-start | bytes 786436
  60.2 8.9 %collective-permute-start.8 = (bf16[8,2,64,128]{3,2,1,0:T(8,128)(2,1)S(1)}, bf16[8,2,64,128]{3,2,1,0:T(8,128)(2,1)S(1)}, u32[]{:S(2)}, u32[]{:S(2)}) collective-permute-start(bf16[8,2,64,128]{3,2,1,0:T(8,128)(2,1)S(1)} %bitcast.248), channel_id=1, source_target_pairs={{16,0},{40,56},{80,64},{104,120},{144,128},{168,184},{208,192},{23... | collective-permute-start | bytes 786440 | tf_op jit(solution)/shard_map/ppermute | solution.py:373
  63.9 6.6 %collective-permute-start.6 = (bf16[8,2,64,128]{3,2,1,0:T(8,128)(2,1)S(1)}, bf16[8,2,64,128]{3,2,1,0:T(8,128)(2,1)S(1)}, u32[]{:S(2)}, u32[]{:S(2)}) collective-permute-start(bf16[8,2,64,128]{3,2,1,0:T(8,128)(2,1)S(1)} %bitcast_select_fusion.1), channel_id=1, source_target_pairs={{0,32},{16,48},{40,8},{56,24},{64,96},{80,112},{104,72},{120,88},{... | collective-permute-start | bytes 786440 | tf_op jit(solution)/shard_map/ppermute | solution.py:371
  77.2 23.0 %collective-permute-start.12 = (bf16[2,8,2,64,128]{4,3,2,1,0:T(8,128)(2,1)S(1)}, bf16[2,8,2,64,128]{4,3,2,1,0:T(8,128)(2,1)S(1)}, u32[]{:S(2)}, u32[]{:S(2)}) collective-permute-start(bf16[2,8,2,64,128]{4,3,2,1,0:T(8,128)(2,1)S(1)} %get-tuple-element.35), channel_id=1, source_target_pairs={{16,0},{32,16},{48,32},{8,24},{24,40},{40,56},{80,64},{96,80},{112... | collective-permute-start | bytes 1572872 | tf_op jit(solution)/shard_map/ppermute | solution.py:429
  80.9 19.3 %collective-permute-start.11 = (bf16[8,2,64,128]{3,2,1,0:T(8,128)(2,1)S(1)}, bf16[8,2,64,128]{3,2,1,0:T(8,128)(2,1)S(1)}, u32[]{:S(2)}, u32[]{:S(2)}) collective-permute-start(bf16[8,2,64,128]{3,2,1,0:T(8,128)(2,1)S(1)} %get-tuple-element.36), channel_id=1, source_target_pairs={{32,0},{48,16},{8,40},{24,56},{96,64},{112,80},{72,104},{88,120},{... | collective-permute-start | bytes 786440 | tf_op jit(solution)/shard_map/ppermute | solution.py:428
  82.3 17.9 %collective-permute-start.10 = (bf16[8,2,64,128]{3,2,1,0:T(8,128)(2,1)S(1)}, bf16[8,2,64,128]{3,2,1,0:T(8,128)(2,1)S(1)}, u32[]{:S(2)}, u32[]{:S(2)}) collective-permute-start(bf16[8,2,64,128]{3,2,1,0:T(8,128)(2,1)S(1)} %get-tuple-element.52), channel_id=1, source_target_pairs={{0,8},{56,48},{64,72},{120,112},{128,136},{184,176},{192,200},{248... | collective-permute-start | bytes 786440 | tf_op jit(solution)/shard_map/ppermute | solution.py:427
  83.0 17.2 %collective-permute-start.9 = (bf16[8,2,64,128]{3,2,1,0:T(8,128)(2,1)S(1)}, bf16[8,2,64,128]{3,2,1,0:T(8,128)(2,1)S(1)}, u32[]{:S(2)}, u32[]{:S(2)}) collective-permute-start(bf16[8,2,64,128]{3,2,1,0:T(8,128)(2,1)S(1)} %get-tuple-element.53), channel_id=1, source_target_pairs={{0,16},{56,40},{64,80},{120,104},{128,144},{184,168},{192,208},{24... | collective-permute-start | bytes 786440 | tf_op jit(solution)/shard_map/ppermute | solution.py:426
  100.4 7.6 %collective-permute-start.18 = (bf16[4,2,64,128]{3,2,1,0:T(8,128)(2,1)S(1)}, bf16[4,2,64,128]{3,2,1,0:T(8,128)(2,1)S(1)}, u32[]{:S(2)}, u32[]{:S(2)}) collective-permute-start(bf16[4,2,64,128]{3,2,1,0:T(8,128)(2,1)S(1)} %fusion.15), channel_id=1, source_target_pairs={{0,1},{1,0},{2,3},{3,2},{4,5},{5,4},{6,7},{7,6},{8,9},{9,8},{10,11... | collective-permute-start | bytes 393224 | tf_op jit(solution)/shard_map/ppermute | solution.py:447
  103.4 12.2 %collective-permute-start.13 = (bf16[2,4,2,64,128]{4,3,2,1,0:T(8,128)(2,1)S(1)}, bf16[2,4,2,64,128]{4,3,2,1,0:T(8,128)(2,1)S(1)}, u32[]{:S(2)}, u32[]{:S(2)}) collective-permute-start(bf16[2,4,2,64,128]{4,3,2,1,0:T(8,128)(2,1)S(1)} %fusion.6), channel_id=1, source_target_pairs={{0,1},{1,0},{2,3},{3,2},{4,5},{5,4},{6,7},{7,6},{8,9},{9,8},{10,11... | collective-permute-start | bytes 786440 | tf_op jit(solution)/shard_map/ppermute | solution.py:457
  108.1 7.6 %collective-permute-start.19 = (bf16[2,2,64,128]{3,2,1,0:T(8,128)(2,1)S(1)}, bf16[2,2,64,128]{3,2,1,0:T(8,128)(2,1)S(1)}, u32[]{:S(2)}, u32[]{:S(2)}) collective-permute-start(bf16[2,2,64,128]{3,2,1,0:T(8,128)(2,1)S(1)} %fusion.22), channel_id=1, source_target_pairs={{0,2},{1,3},{2,0},{3,1},{4,6},{5,7},{6,4},{7,5},{8,10},{9,11},{10,... | collective-permute-start | bytes 196616 | tf_op jit(solution)/shard_map/ppermute | solution.py:447
  115.8 9.3 %collective-permute-start.14 = (bf16[2,2,2,64,128]{4,3,2,1,0:T(8,128)(2,1)S(1)}, bf16[2,2,2,64,128]{4,3,2,1,0:T(8,128)(2,1)S(1)}, u32[]{:S(2)}, u32[]{:S(2)}) collective-permute-start(bf16[2,2,2,64,128]{4,3,2,1,0:T(8,128)(2,1)S(1)} %fusion.14), channel_id=1, source_target_pairs={{0,2},{1,3},{2,0},{3,1},{4,6},{5,7},{6,4},{7,5},{8,10},{9,11},{10,... | collective-permute-start | bytes 393224 | tf_op jit(solution)/shard_map/ppermute | solution.py:457
  120.7 11.8 %collective-permute-start.20 = (bf16[1,2,64,128]{3,2,1,0:T(8,128)(2,1)S(1)}, bf16[1,2,64,128]{3,2,1,0:T(8,128)(2,1)S(1)}, u32[]{:S(2)}, u32[]{:S(2)}) collective-permute-start(bf16[1,2,64,128]{3,2,1,0:T(8,128)(2,1)S(1)} %fusion.26), channel_id=1, source_target_pairs={{0,4},{1,5},{2,6},{3,7},{4,0},{5,1},{6,2},{7,3},{8,12},{9,13},{10,... | collective-permute-start | bytes 98312 | tf_op jit(solution)/shard_map/ppermute | solution.py:447
  123.2 12.9 %collective-permute-start.16 = (bf16[2,512,128]{2,1,0:T(8,128)(2,1)S(1)}, bf16[2,512,128]{2,1,0:T(8,128)(2,1)S(1)}, u32[]{:S(2)}, u32[]{:S(2)}) collective-permute-start(bf16[2,512,128]{2,1,0:T(8,128)(2,1)S(1)} %get-tuple-element.43), channel_id=1, source_target_pairs={{0,8},{8,0},{16,24},{24,16},{32,40},{40,32},{48,56},{56,48},{64,72... | collective-permute-start | bytes 786440 | tf_op jit(solution)/shard_map/ppermute | solution.py:460
  125.2 10.9 %collective-permute-start.15 = (bf16[2,1,2,64,128]{4,3,2,0,1:T(8,128)(2,1)S(1)}, bf16[2,1,2,64,128]{4,3,2,0,1:T(8,128)(2,1)S(1)}, u32[]{:S(2)}, u32[]{:S(2)}) collective-permute-start(bf16[2,1,2,64,128]{4,3,2,0,1:T(8,128)(2,1)S(1)} %fusion.23), channel_id=1, source_target_pairs={{0,4},{1,5},{2,6},{3,7},{4,0},{5,1},{6,2},{7,3},{8,12},{9,13},{10,... | collective-permute-start | bytes 196616 | tf_op jit(solution)/shard_map/ppermute | solution.py:457
  132.5 13.6 %collective-permute-start.21 = (bf16[2,64,128]{2,1,0:T(8,128)(2,1)S(1)}, bf16[2,64,128]{2,1,0:T(8,128)(2,1)S(1)}, u32[]{:S(2)}, u32[]{:S(2)}) collective-permute-start(bf16[2,64,128]{2,1,0:T(8,128)(2,1)S(1)} %fusion.28), channel_id=1, source_target_pairs={{87,56},{86,57},{85,58},{84,59},{83,60},{82,61},{81,62},{80,63},{7... | collective-permute-start | bytes 98312 | tf_op jit(solution)/shard_map/ppermute | solution.py:449
  136.2 9.9 %collective-permute-start.17 = (bf16[2,64,128]{2,1,0:T(8,128)(2,1)S(1)}, bf16[2,64,128]{2,1,0:T(8,128)(2,1)S(1)}, u32[]{:S(2)}, u32[]{:S(2)}) collective-permute-start(bf16[2,64,128]{2,1,0:T(8,128)(2,1)S(1)} %fusion.27), channel_id=1, source_target_pairs={{0,8},{8,0},{16,24},{24,16},{32,40},{40,32},{48,56},{56,48},{64,72... | collective-permute-start | bytes 98312 | tf_op jit(solution)/shard_map/ppermute | solution.py:466
